TPU v7x, 32 devices: a whole 2x2x4 slice. The times are simulated.
32 devices in a mesh: groups: 2 (over y), label: 4 (over x, core), dp: 4 (over z).
Axes of the slice: x: 2, y: 2, z: 4, core: 2. Of those that a mesh axis runs over, the one named last changes fastest.
Arguments:
- embeds: bfloat16 [24576, 1024], P(('groups', 'label', 'dp')), parts along dimension 0, may hold values from -6 to 6
- weights: bfloat16 [2048, 1024], P(('label', 'dp')), may hold values from -0.1875 to 0.1875
- pos_ids: int32 [24576, 8], P(('groups', 'label', 'dp')), parts along dimension 0, may hold values from 0 to 2047, as said below
- pos_count: int32 [24576], P(('groups', 'label', 'dp')), parts along dimension 0, may hold values from 1 to 8
Outputs:
- grad_weight: bfloat16 [4096, 1024], P(('groups', 'label', 'dp')), parts along dimension 0
- grad_embed: bfloat16 [24576, 1024], P(('groups', 'label', 'dp')), parts along dimension 0
There are 2 independent parts, one for each index of `groups`. A program takes and returns all parts, laid end to end along the dimension named above; an argument that names none is the same for every part. Nothing has to cross between parts.
Inputs may be any that keep to these rules, and one draw needn't show every extreme that they name: `pos_ids`: entry p of a row lies in [p * 256, (p + 1) * 256), so a row's entries are distinct.
All inputs are finite; a program needn't handle non-finite values.
Results may differ from a plain program's by a relative error of at most 0.012.
Values may be sent and summed in bfloat16 or wider, within the bound.
No kernel may reach another device: no remote copies, remote signals or barrier semaphores. Data moves between devices by JAX's collectives and lax.ppermute only.
A program may use at most 64 MiB of HBM per device.

v0:
```python
import math

import jax
import jax.numpy as jnp
from jax import lax
from jax.sharding import PartitionSpec as P

STEPS = 2


def passed_along(shard, axis, by):
    devices = lax.axis_size(axis)
    return lax.ppermute(shard, axis, [(i, (i + by) % devices) for i in range(devices)])


def local(embeds, weights, pos_ids, pos_count):
    n_label = lax.axis_size("label")
    n_dp = lax.axis_size("dp")
    me_label = lax.axis_index("label")
    rows_dev, width = embeds.shape
    ch_dev = weights.shape[0]
    stretch = ch_dev * n_dp
    scale = 1.0 / math.sqrt(rows_dev * n_dp)
    valid = jnp.arange(pos_ids.shape[1], dtype=jnp.int32)[None, :] < pos_count[:, None]
    grad_x = jnp.zeros((rows_dev, width), jnp.float32)
    grad_w = jnp.zeros((ch_dev, width), jnp.float32)
    shard = weights
    for step in range(STEPS):
        if step > 0:
            shard = passed_along(shard, "label", 1)
        current = lax.all_gather(shard, "dp", axis=0, tiled=True)
        owner = (me_label - step) % n_label
        labels = owner * stretch + jnp.arange(stretch, dtype=jnp.int32)
        hits = (pos_ids[:, :, None] == labels[None, None, :]) & valid[:, :, None]
        target = jnp.any(hits, axis=1).astype(jnp.float32)
        logits = lax.dot_general(
            embeds, current, (((1,), (1,)), ((), ())), preferred_element_type=jnp.float32
        )
        delta = (jax.nn.sigmoid(logits) - target).astype(jnp.bfloat16)
        grad_x = grad_x + jnp.dot(delta, current, preferred_element_type=jnp.float32)
        product = lax.dot_general(
            delta, embeds, (((0,), (0,)), ((), ())), preferred_element_type=jnp.float32
        )
        summed = lax.psum_scatter(
            (product * scale).astype(jnp.bfloat16), "dp", scatter_dimension=0, tiled=True
        ).astype(jnp.float32)
        if step > 0:
            summed = passed_along(summed.astype(jnp.bfloat16), "label", -step).astype(summed.dtype)
        grad_w = grad_w + summed
    return (grad_w.astype(jnp.bfloat16), grad_x.astype(jnp.bfloat16))


def solution(mesh):
    return jax.shard_map(
        local,
        mesh=mesh,
        in_specs=(
            P(("groups", "label", "dp"), None),
            P(("label", "dp"), None),
            P(("groups", "label", "dp"), None),
            P(("groups", "label", "dp")),
        ),
        out_specs=(P(("groups", "label", "dp"), None), P(("groups", "label", "dp"), None)),
        check_vma=False,
    )
```

profile of v0, /device:TPU:0, one launch (start us, length us, event | category | flops | bytes accessed | tf_op | source)
XLA Modules:
  0.0 139.7 jit_solution(12375719251068192768)
XLA Ops:
  7.2 0.0 copy-start
  7.2 0.0 all-gather.5.cloned.1.call-start
  7.2 0.5 collective-permute-start
  7.7 6.2 %collective-permute-done = bf16[128,1024]{1,0:T(8,128)(2,1)S(1)} collective-permute-done((bf16[128,1024]{1,0:T(8,128)(2,1)}, bf16[128,1024]{1,0:T(8,128)(2,1)S(1)}, u32[]{:S(2)}, u32[]{:S(2)}) %collective-permute-start) | collective-permute-done | bytes 262176 | tf_op jit(solution)/shard_map/ppermute | solution.py:13
  13.9 0.0 copy-start.3
  13.9 0.7 copy-done.3
  14.6 0.0 all-gather.5.cloned.1.call-update
  14.6 0.0 all-gather.3.cloned.1.call-start
  14.7 0.7 all-gather.3.cloned.1.call-update
  15.4 0.0 reduce-scatter.5.cloned.1.call-start
  15.4 0.9 iota_compare_fusion
  16.3 0.9 copy.7
  17.3 9.8 %and_reduce_fusion.1 = (pred[768,512]{1,0:T(8,128)(4,1)S(1)}, pred[768,512]{1,0:T(8,128)(4,1)S(1)}) fusion(s32[512]{0:T(512)S(1)} %get-tuple-element.5, s32[768,8]{1,0:T(8,128)S(1)} %copy.7, pred[768,8]{1,0:T(8,128)(4,1)S(1)} %iota_compare_fusion, s32[512]{0:T(512)S(1)} %get-tuple-element.4), kind=kLoop, calls=%fused_computation.1 | loop fusion | flops 18087936 | bytes 821248 | tf_op jit(solution)/shard_map/reduce_or | solution.py:35
  27.0 17.7 %all-gather.5.cloned.1.call-done = bf16[512,1024]{1,0:T(8,128)(2,1)} async-done(((bf16[128,1024]{1,0:T(8,128)(2,1)}), bf16[512,1024]{1,0:T(8,128)(2,1)}) %all-gather.5.cloned.1.call-update) | async-done | bytes 1048592 | tf_op jit(solution)/shard_map/all_gather | solution.py:31
  44.8 0.0 copy-done
  44.8 2.4 %subtract_convert_fusion = bf16[768,512]{1,0:T(8,128)(2,1)S(1)} fusion(pred[768,512]{1,0:T(8,128)(4,1)S(1)} %get-tuple-element.3, bf16[768,1024]{1,0:T(8,128)(2,1)S(1)} %copy-done, bf16[512,1024]{1,0:T(8,128)(2,1)} %all-gather.5.cloned.1.call-done), kind=kOutput, calls=%fused_computation.5 | convolution fusion | flops 807665664 | bytes 3801088 | tf_op jit(solution)/shard_map/dot_general | solution.py:36
  47.2 0.0 copy-start.2
  47.3 0.9 copy-done.2
  48.2 2.0 %multiply_convert_fusion = bf16[512,1024]{1,0:T(8,128)(2,1)} fusion(bf16[768,512]{1,0:T(8,128)(2,1)S(1)} %subtract_convert_fusion, bf16[768,1024]{1,0:T(8,128)(2,1)S(1)} %copy-done), kind=kOutput, calls=%fused_computation.3 | convolution fusion | flops 806354944 | bytes 3407872 | tf_op jit(solution)/shard_map/dot_general | solution.py:41
  50.1 0.0 reduce-scatter.5.cloned.1.call-update
  50.2 0.0 reduce-scatter.3.cloned.1.call-start
  50.2 23.6 %all-gather.3.cloned.1.call-done = bf16[512,1024]{1,0:T(8,128)(2,1)} async-done(((bf16[128,1024]{1,0:T(8,128)(2,1)}), bf16[512,1024]{1,0:T(8,128)(2,1)}) %all-gather.3.cloned.1.call-update) | async-done | bytes 1048592 | tf_op jit(solution)/shard_map/all_gather | solution.py:31
  73.8 2.4 %subtract_convert_fusion.1 = bf16[768,512]{1,0:T(8,128)(2,1)S(1)} fusion(pred[768,512]{1,0:T(8,128)(4,1)S(1)} %get-tuple-element.2, bf16[768,1024]{1,0:T(8,128)(2,1)S(1)} %copy-done, bf16[512,1024]{1,0:T(8,128)(2,1)} %all-gather.3.cloned.1.call-done), kind=kOutput, calls=%fused_computation.6 | convolution fusion | flops 807665664 | bytes 3801088 | tf_op jit(solution)/shard_map/dot_general | solution.py:36
  76.3 2.0 %multiply_convert_fusion.1 = bf16[512,1024]{1,0:T(8,128)(2,1)} fusion(bf16[768,512]{1,0:T(8,128)(2,1)S(1)} %subtract_convert_fusion.1, bf16[768,1024]{1,0:T(8,128)(2,1)S(1)} %copy-done), kind=kOutput, calls=%fused_computation.4 | convolution fusion | flops 806354944 | bytes 3407872 | tf_op jit(solution)/shard_map/dot_general | solution.py:41
  78.2 0.0 reduce-scatter.3.cloned.1.call-update
  78.3 0.0 copy-start.1
  78.3 3.9 %fusion = f32[768,1024]{1,0:T(8,128)} fusion(bf16[768,512]{1,0:T(8,128)(2,1)S(1)} %subtract_convert_fusion.1, bf16[512,1024]{1,0:T(8,128)(2,1)} %all-gather.3.cloned.1.call-done), kind=kOutput, calls=%fused_computation.11 | convolution fusion | flops 805306368 | bytes 4980736 | tf_op jit(solution)/shard_map/dot_general | solution.py:40
  82.2 21.2 %reduce-scatter.5.cloned.1.call-done = bf16[128,1024]{1,0:T(8,128)(2,1)} async-done(((bf16[512,1024]{1,0:T(8,128)(2,1)}), bf16[128,1024]{1,0:T(8,128)(2,1)}) %reduce-scatter.5.cloned.1.call-update) | async-done | bytes 262160 | tf_op jit(solution)/shard_map/reduce_scatter | solution.py:44
  103.4 0.7 collective-permute-start.1
  104.1 0.0 copy-done.1
  104.1 4.3 %add_convert_fusion = bf16[768,1024]{1,0:T(8,128)(2,1)} fusion(f32[768,1024]{1,0:T(8,128)} %fusion, bf16[768,512]{1,0:T(8,128)(2,1)} %copy-done.2, bf16[512,1024]{1,0:T(8,128)(2,1)S(1)} %copy-done.1), kind=kOutput, calls=%fused_computation.2 | convolution fusion | flops 806879232 | bytes 6553600 | tf_op jit(solution)/shard_map/dot_general | solution.py:40
  108.4 23.0 %reduce-scatter.3.cloned.1.call-done = bf16[128,1024]{1,0:T(8,128)(2,1)} async-done(((bf16[512,1024]{1,0:T(8,128)(2,1)}), bf16[128,1024]{1,0:T(8,128)(2,1)}) %reduce-scatter.3.cloned.1.call-update) | async-done | bytes 262160 | tf_op jit(solution)/shard_map/reduce_scatter | solution.py:44
  131.4 0.0 collective-permute-done.1
  131.4 1.7 %add_convert_fusion.1 = bf16[128,1024]{1,0:T(8,128)(2,1)} fusion(bf16[128,1024]{1,0:T(8,128)(2,1)S(1)} %collective-permute-done.1, bf16[128,1024]{1,0:T(8,128)(2,1)} %reduce-scatter.3.cloned.1.call-done), kind=kLoop, calls=%fused_computation.7 | loop fusion | flops 524288 | bytes 786432 | tf_op jit(solution)/shard_map/convert_element_type | solution.py:50
  (1 shorter events, 0.0 us)
Async XLA Ops:
  7.2 37.6 %copy-start = (bf16[768,1024]{1,0:T(8,128)(2,1)S(1)}, bf16[768,1024]{1,0:T(8,128)(2,1)}, u32[]{:S(2)}) copy-start(bf16[768,1024]{1,0:T(8,128)(2,1)} %param.4) | copy-start | bytes 4718596
  7.2 37.6 %all-gather.5.cloned.1.call-start = ((), (), s32[]{:S(2)}) async-start(), calls=%async_computation.4 | async-start | bytes 1310720 | tf_op jit(solution)/shard_map/all_gather | solution.py:31
  7.2 6.7 %collective-permute-start = (bf16[128,1024]{1,0:T(8,128)(2,1)}, bf16[128,1024]{1,0:T(8,128)(2,1)S(1)}, u32[]{:S(2)}, u32[]{:S(2)}) collective-permute-start(bf16[128,1024]{1,0:T(8,128)(2,1)} %param.5), channel_id=1, source_target_pairs={{0,4},{4,8},{8,12},{12,0},{1,5},{5,9},{9,13},{13,1},{2,6},{6,10},{... | collective-permute-start | bytes 786440 | tf_op jit(solution)/shard_map/ppermute | solution.py:13
  13.9 0.7 copy-start.3
  14.6 59.2 %all-gather.3.cloned.1.call-start = ((), (), s32[]{:S(2)}) async-start(), calls=%async_computation.2 | async-start | bytes 1310720 | tf_op jit(solution)/shard_map/all_gather | solution.py:31
  15.4 88.0 %reduce-scatter.5.cloned.1.call-start = ((), (), s32[]{:S(2)}) async-start(), calls=%async_computation.5 | async-start | bytes 1310720 | tf_op jit(solution)/shard_map/reduce_scatter | solution.py:44
  47.2 0.9 copy-start.2
  50.2 81.2 %reduce-scatter.3.cloned.1.call-start = ((), (), s32[]{:S(2)}) async-start(), calls=%async_computation.3 | async-start | bytes 1310720 | tf_op jit(solution)/shard_map/reduce_scatter | solution.py:44
  78.3 25.8 %copy-start.1 = (bf16[512,1024]{1,0:T(8,128)(2,1)S(1)}, bf16[512,1024]{1,0:T(8,128)(2,1)}, u32[]{:S(2)}) copy-start(bf16[512,1024]{1,0:T(8,128)(2,1)} %all-gather.5.cloned.1.call-done) | copy-start | bytes 3145732
  103.4 28.1 %collective-permute-start.1 = (bf16[128,1024]{1,0:T(8,128)(2,1)}, bf16[128,1024]{1,0:T(8,128)(2,1)S(1)}, u32[]{:S(2)}, u32[]{:S(2)}) collective-permute-start(bf16[128,1024]{1,0:T(8,128)(2,1)} %reduce-scatter.5.cloned.1.call-done), channel_id=1, source_target_pairs={{0,12},{4,0},{8,4},{12,8},{1,13},{5,1},{9,5},{13,9},{2,14},{6,2},{... | collective-permute-start | bytes 786440 | tf_op jit(solution)/shard_map/ppermute | solution.py:13
Sparse Core Ops, SparseCore 0:
  14.8 29.9 all-gather.4
  46.4 27.4 all-gather.2
  76.7 26.6 reduce-scatter.4
  105.6 25.7 reduce-scatter.2
where the time goes:
time: 140 us
  waiting for transfers between devices  92.5 us (66%)
  matrix products  17 us (12%)
  between operations  13.9 us (10%)
  other arithmetic  12.4 us (9%)
  local copies, waits for them, and re-layouts  2.5 us (2%)
  starting transfers between devices  1.41 us (1%)
    reduce_scatter x2, waiting for transfers between devices, local(): lax.psum_scatter((product * scale).astype(jnp.bfloat16), 'dp', scatter_di...  44.2 us
    all_gather x2, waiting for transfers between devices, local(): current = lax.all_gather(shard, 'dp', axis=0, tiled=True)  41.3 us
    reduce_or x1, other arithmetic, local(): target = jnp.any(hits, axis=1).astype(jnp.float32)  9.79 us
    dot_general x2, matrix products, local(): jnp.dot(delta, current, preferred_element_type=jnp.float32)  8.19 us
    ppermute x2, waiting for transfers between devices, passed_along(): lax.ppermute(shard, axis, [(i, (i + by) % devices) for i in range(devices)])  6.19 us
    dot_general x2, matrix products, local(): lax.dot_general(embeds, current, (((1,), (1,)), ((), ())), preferred_elem...  4.89 us
    dot_general x2, matrix products, local(): lax.dot_general(delta, embeds, (((0,), (0,)), ((), ())), preferred_elemen...  3.96 us
  transfers between devices with their start and end apart: 6, of which 5 were waited for; matrix products, arithmetic and copies ran while one was open for 20% of the time, Pallas kernels for 0%

commit v1 on v0

v1 whole, which is shorter than its diff:
```python
import math

import jax
import jax.numpy as jnp
from jax import lax
from jax.sharding import PartitionSpec as P


def local(embeds, weights, pos_ids, pos_count):
    n_label = lax.axis_size("label")
    n_dp = lax.axis_size("dp")
    me_label = lax.axis_index("label")
    me_dp = lax.axis_index("dp")
    rows_dev, width = embeds.shape
    ch_dev = weights.shape[0]
    stretch = ch_dev * n_dp
    slots = pos_ids.shape[1]
    span = stretch * n_label // slots
    scale = 1.0 / math.sqrt(rows_dev * n_dp)
    valid = jnp.arange(slots, dtype=jnp.int32)[None, :] < pos_count[:, None]
    ids = jnp.where(valid, pos_ids, -1)

    def to_dp(x, k):
        return lax.ppermute(x, "dp", [(i, i ^ k) for i in range(n_dp)])

    def to_label(x, by):
        return lax.ppermute(x, "label", [(i, (i + by) % n_label) for i in range(n_label)])

    def delta_of(piece, owner, k):
        start = owner * stretch + (me_dp ^ k) * ch_dev
        column = lax.dynamic_slice_in_dim(ids, start // span, 1, axis=1)
        labels = start + jnp.arange(ch_dev, dtype=jnp.int32)
        target = (column == labels[None, :]).astype(jnp.float32)
        logits = lax.dot_general(
            embeds, piece, (((1,), (1,)), ((), ())), preferred_element_type=jnp.float32
        )
        return (jax.nn.sigmoid(logits) - target).astype(jnp.bfloat16)

    def grad_w_of(delta):
        return lax.dot_general(
            delta, embeds, (((0,), (0,)), ((), ())), preferred_element_type=jnp.float32
        ) * scale

    order = list(range(n_dp))
    prev_owner = (me_label - 1) % n_label
    own = [weights if k == 0 else to_dp(weights, k) for k in order]
    prev = [to_label(own[k], 1) for k in order]
    d_own = [delta_of(own[k], me_label, k) for k in order]
    d_prev = [delta_of(prev[k], prev_owner, k) for k in order]
    back = [to_label(grad_w_of(d_prev[k]).astype(jnp.bfloat16), -1) for k in order]
    total = [grad_w_of(d_own[k]) + back[k].astype(jnp.float32) for k in order]
    grad_w = total[0]
    for k in order[1:]:
        grad_w = grad_w + to_dp(total[k].astype(jnp.bfloat16), k).astype(jnp.float32)
    grad_x = jnp.dot(
        jnp.concatenate(d_own + d_prev, axis=1),
        jnp.concatenate(own + prev, axis=0),
        preferred_element_type=jnp.float32,
    )
    return (grad_w.astype(jnp.bfloat16), grad_x.astype(jnp.bfloat16))


def solution(mesh):
    return jax.shard_map(
        local,
        mesh=mesh,
        in_specs=(
            P(("groups", "label", "dp"), None),
            P(("label", "dp"), None),
            P(("groups", "label", "dp"), None),
            P(("groups", "label", "dp")),
        ),
        out_specs=(P(("groups", "label", "dp"), None), P(("groups", "label", "dp"), None)),
        check_vma=False,
    )
```

time: 140 us -> 74.1 us (0.53)
  waiting for transfers between devices: 92.5 us -> 38.7 us
  starting transfers between devices: 1.41 us -> 18.1 us
  between operations: 13.9 us -> 0.92 us
  other arithmetic: 12.4 us -> 1.68 us
  matrix products: 17 us -> 12.6 us
    reduce_scatter x2 -> x0, waiting for transfers between devices: 44.2 us -> none  [local(): lax.psum_scatter((product * scale).astype(jnp.bfloat16), 'dp', scatter_di...]
    all_gather x2 -> x0, waiting for transfers between devices: 41.3 us -> none  [local(): current = lax.all_gather(shard, 'dp', axis=0, tiled=True)]
    ppermute x2 -> x14, waiting for transfers between devices: 6.19 us -> 38.7 us  [the longest x6 25 us: to_dp(): return lax.ppermute(x, 'dp', [(i, i ^ k) for i in range(n_dp)])]
    ppermute x2 -> x14, starting transfers between devices: 1.25 us -> 18.1 us  [the longest x6 15 us: to_dp(): return lax.ppermute(x, 'dp', [(i, i ^ k) for i in range(n_dp)])]
    reduce_or x1 -> x0, other arithmetic: 9.79 us -> none  [local(): target = jnp.any(hits, axis=1).astype(jnp.float32)]
    dot_general x6 -> x17, matrix products: 17 us -> 12.6 us  [the longest x8 6.56 us: delta_of(): lax.dot_general(embeds, piece, (((1,), (1,)), ((), ())), preferred_elemen...]
  transfers between devices with their start and end apart: 6 -> 14, of which waited for: 5 -> 8; matrix products, arithmetic and copies ran while one was open for 20% -> 19% of each run, Pallas kernels for 0% -> 0%
where the time goes in v1:
time: 74.1 us; the launch traced here: 73.9 us
  waiting for transfers between devices  38.7 us (52%)
  starting transfers between devices  18.1 us (24%)
  matrix products  12.6 us (17%)
  local copies, waits for them, and re-layouts  1.89 us (3%)
  other arithmetic  1.68 us (2%)
  between operations  0.92 us (1%)
    ppermute x6, waiting for transfers between devices, to_dp(): return lax.ppermute(x, 'dp', [(i, i ^ k) for i in range(n_dp)])  25 us
    ppermute x6, starting transfers between devices, to_dp(): return lax.ppermute(x, 'dp', [(i, i ^ k) for i in range(n_dp)])  15 us
    ppermute x8, waiting for transfers between devices, to_label(): lax.ppermute(x, 'label', [(i, (i + by) % n_label) for i in range(n_label)])  13.7 us
    dot_general x8, matrix products, delta_of(): lax.dot_general(embeds, piece, (((1,), (1,)), ((), ())), preferred_elemen...  6.56 us
    ppermute x8, starting transfers between devices, to_label(): lax.ppermute(x, 'label', [(i, (i + by) % n_label) for i in range(n_label)])  3.14 us
    dot_general x8, matrix products, grad_w_of(): lax.dot_general(delta, embeds, (((0,), (0,)), ((), ())), preferred_elemen...  3.06 us
    dot_general x1, matrix products, local(): jnp.dot(jnp.concatenate(d_own + d_prev, axis=1), jnp.concatenate(own + pr...  2.99 us
    unnamed x11, local copies, waits for them, and re-layouts  1.8 us
  transfers between devices with their start and end apart: 14, of which 8 were waited for; matrix products, arithmetic and copies ran while one was open for 19% of the time, Pallas kernels for 0%

profile of v1, /device:TPU:0, one launch (start us, length us, event | category | flops | bytes accessed | tf_op | source)
XLA Modules:
  0.0 73.9 jit_solution(13025308893463347724)
XLA Ops:
  0.6 0.0 copy-start
  0.6 4.1 %collective-permute-start.6 = (bf16[128,1024]{1,0:T(8,128)(2,1)}, bf16[128,1024]{1,0:T(8,128)(2,1)S(1)}, u32[]{:S(2)}, u32[]{:S(2)}) collective-permute-start(bf16[128,1024]{1,0:T(8,128)(2,1)} %param.5), channel_id=1, source_target_pairs={{0,2},{1,3},{2,0},{3,1},{4,6},{5,7},{6,4},{7,5},{8,10},{9,11},{10,... | collective-permute-start | bytes 786440 | tf_op jit(solution)/shard_map/ppermute | solution.py:24
  4.7 1.6 %collective-permute-start.2 = (bf16[128,1024]{1,0:T(8,128)(2,1)}, bf16[128,1024]{1,0:T(8,128)(2,1)S(1)}, u32[]{:S(2)}, u32[]{:S(2)}) collective-permute-start(bf16[128,1024]{1,0:T(8,128)(2,1)} %param.5), channel_id=1, source_target_pairs={{0,1},{1,0},{2,3},{3,2},{4,5},{5,4},{6,7},{7,6},{8,9},{9,8},{10,11... | collective-permute-start | bytes 786440 | tf_op jit(solution)/shard_map/ppermute | solution.py:24
  6.3 0.0 collective-permute-start
  6.3 0.0 collective-permute-start.10
  6.4 1.7 %constant_dynamic-update-slice_fusion.15 = bf16[1024,1024]{1,0:T(8,128)(2,1)} fusion(bf16[128,1024]{1,0:T(8,128)(2,1)} %param.5), kind=kLoop, calls=%fused_computation.80 | loop fusion | bytes 524288
  8.1 0.7 %fusion.44 = s32[768,8]{0,1:T(8,128)S(1)} fusion(s32[768,8]{0,1:T(8,128)} %param.6, s32[768]{0:T(1024)} %param.7), kind=kLoop, calls=%fused_computation.82 | loop fusion | flops 12288 | bytes 52224 | tf_op jit(solution)/shard_map/jit(_where)/select_n | solution.py:21
  8.8 0.1 dynamic-slice_reduce_fusion.6
  8.9 0.0 copy-done
  8.9 1.7 %constant_dynamic-update-slice_fusion.7 = (bf16[768,1024]{0,1:T(8,128)(2,1)S(1)}, bf16[768,128]{0,1:T(8,128)(2,1)S(1)}) fusion(s32[128]{0:T(128)S(1)} %iota_add_fusion.7, s32[768]{0:T(1024)S(1)} %get-tuple-element.9, bf16[768,1024]{1,0:T(8,128)(2,1)S(1)} %copy-done, bf16[128,1024]{1,0:T(8,128)(2,1)} %param.5), kind=kOutput, calls=%fused_computation.72 | convolution fusion | flops 202014720 | bytes 2231808 | tf_op jit(solution)/shard_map/dot_general | solution.py:34
  10.6 0.4 convolution_multiply_fusion.7
  11.0 6.5 %collective-permute-done.2 = bf16[128,1024]{1,0:T(8,128)(2,1)S(1)} collective-permute-done((bf16[128,1024]{1,0:T(8,128)(2,1)}, bf16[128,1024]{1,0:T(8,128)(2,1)S(1)}, u32[]{:S(2)}, u32[]{:S(2)}) %collective-permute-start.2) | collective-permute-done | bytes 262176 | tf_op jit(solution)/shard_map/ppermute | solution.py:24
  17.4 0.7 constant_dynamic-update-slice_fusion.6
  18.1 0.5 collective-permute-done.6
  18.6 0.7 constant_dynamic-update-slice_fusion.5
  19.3 4.4 %collective-permute-done.10 = bf16[128,1024]{1,0:T(8,128)(2,1)S(1)} collective-permute-done((bf16[128,1024]{1,0:T(8,128)(2,1)}, bf16[128,1024]{1,0:T(8,128)(2,1)S(1)}, u32[]{:S(2)}, u32[]{:S(2)}) %collective-permute-start.10) | collective-permute-done | bytes 262176 | tf_op jit(solution)/shard_map/ppermute | solution.py:24
  23.7 0.7 constant_dynamic-update-slice_fusion.4
  24.4 0.0 collective-permute-done
  24.4 0.0 copy-start.1
  24.4 0.7 constant_dynamic-update-slice_fusion.3
  25.2 0.4 fusion
  25.6 0.1 collective-permute-start.1
  25.6 0.5 collective-permute-start.7
  26.1 1.9 %collective-permute-start.3 = (bf16[128,1024]{1,0:T(8,128)(2,1)S(1)}, bf16[128,1024]{1,0:T(8,128)(2,1)S(1)}, u32[]{:S(2)}, u32[]{:S(2)}) collective-permute-start(bf16[128,1024]{1,0:T(8,128)(2,1)S(1)} %collective-permute-done.2), channel_id=1, source_target_pairs={{0,4},{4,8},{8,12},{12,0},{1,5},{5,9},{9,13},{13,1},{2,6},{6,10},{... | collective-permute-start | bytes 786440 | tf_op jit(solution)/shard_map/ppermute | solution.py:27
  28.0 0.4 collective-permute-start.11
  28.4 0.0 copy-done.1
  28.5 9.1 %collective-permute-done.3 = bf16[128,1024]{1,0:T(8,128)(2,1)S(1)} collective-permute-done((bf16[128,1024]{1,0:T(8,128)(2,1)S(1)}, bf16[128,1024]{1,0:T(8,128)(2,1)S(1)}, u32[]{:S(2)}, u32[]{:S(2)}) %collective-permute-start.3) | collective-permute-done | bytes 262176 | tf_op jit(solution)/shard_map/ppermute | solution.py:27
  37.6 0.7 constant_dynamic-update-slice_fusion.2
  38.3 0.4 fusion.1
  38.7 0.0 collective-permute-done.7
  38.7 0.7 constant_dynamic-update-slice_fusion.1
  39.4 0.4 fusion.2
  39.8 0.6 collective-permute-done.11
  40.4 0.7 constant_dynamic-update-slice_fusion
  41.1 0.4 fusion.3
  41.5 0.1 collective-permute-start.12
  41.6 0.1 collective-permute-start.8
  41.7 0.1 collective-permute-start.4
  41.8 3.6 %collective-permute-done.12 = bf16[128,1024]{1,0:T(8,128)(2,1)S(1)} collective-permute-done((bf16[128,1024]{1,0:T(8,128)(2,1)S(1)}, bf16[128,1024]{1,0:T(8,128)(2,1)S(1)}, u32[]{:S(2)}, u32[]{:S(2)}) %collective-permute-start.12) | collective-permute-done | bytes 262176 | tf_op jit(solution)/shard_map/ppermute | solution.py:27
  45.5 0.4 add_convert_fusion.1
  45.8 2.0 %collective-permute-start.13 = (bf16[128,1024]{1,0:T(8,128)(2,1)S(1)}, bf16[128,1024]{1,0:T(8,128)(2,1)S(1)}, u32[]{:S(2)}, u32[]{:S(2)}) collective-permute-start(bf16[128,1024]{1,0:T(8,128)(2,1)S(1)} %add_convert_fusion.1), channel_id=1, source_target_pairs={{0,3},{1,2},{2,1},{3,0},{4,7},{5,6},{6,5},{7,4},{8,11},{9,10},{10,... | collective-permute-start | bytes 786440 | tf_op jit(solution)/shard_map/ppermute | solution.py:24
  47.8 0.4 collective-permute-done.8
  48.3 0.4 add_convert_fusion.2
  48.7 6.7 %collective-permute-start.9 = (bf16[128,1024]{1,0:T(8,128)(2,1)S(1)}, bf16[128,1024]{1,0:T(8,128)(2,1)S(1)}, u32[]{:S(2)}, u32[]{:S(2)}) collective-permute-start(bf16[128,1024]{1,0:T(8,128)(2,1)S(1)} %add_convert_fusion.2), channel_id=1, source_target_pairs={{0,2},{1,3},{2,0},{3,1},{4,6},{5,7},{6,4},{7,5},{8,10},{9,11},{10,... | collective-permute-start | bytes 786440 | tf_op jit(solution)/shard_map/ppermute | solution.py:24
  55.4 0.0 collective-permute-done.4
  55.4 0.4 add_convert_fusion.3
  55.8 0.6 collective-permute-start.5
  56.4 3.0 %convolution_convert_fusion = bf16[768,1024]{1,0:T(8,128)(2,1)} fusion(bf16[768,1024]{0,1:T(8,128)(2,1)S(1)} %get-tuple-element.24, bf16[1024,1024]{1,0:T(8,128)(2,1)S(1)} %constant_dynamic-update-slice_fusion.8), kind=kOutput, calls=%fused_computation | convolution fusion | flops 1611399168 | bytes 5242880 | tf_op jit(solution)/shard_map/dot_general | solution.py:55
  59.3 0.0 collective-permute-done.1
  59.4 0.0 collective-permute-done.13
  59.4 13.6 %collective-permute-done.9 = bf16[128,1024]{1,0:T(8,128)(2,1)S(1)} collective-permute-done((bf16[128,1024]{1,0:T(8,128)(2,1)S(1)}, bf16[128,1024]{1,0:T(8,128)(2,1)S(1)}, u32[]{:S(2)}, u32[]{:S(2)}) %collective-permute-start.9) | collective-permute-done | bytes 262176 | tf_op jit(solution)/shard_map/ppermute | solution.py:24
  73.0 0.0 collective-permute-done.5
  73.0 0.9 %add_convert_fusion = bf16[128,1024]{1,0:T(8,128)(2,1)} fusion(bf16[128,1024]{1,0:T(8,128)(2,1)S(1)} %collective-permute-done.13, bf16[128,1024]{1,0:T(8,128)(2,1)S(1)} %collective-permute-done.9, bf16[128,1024]{1,0:T(8,128)(2,1)S(1)} %collective-permute-done.5, f32[128,1024]{1,0:T(8,128)S(1)} %convolution_multiply_fusion.7, ...), kind=kLoop, calls=%fused_computation.61 | loop fusion | flops 1179648 | bytes 1835008 | tf_op jit(solution)/shard_map/convert_element_type | solution.py:60
  (15 shorter events, 0.2 us)
Async XLA Ops:
  0.6 8.3 %copy-start = (bf16[768,1024]{1,0:T(8,128)(2,1)S(1)}, bf16[768,1024]{1,0:T(8,128)(2,1)}, u32[]{:S(2)}) copy-start(bf16[768,1024]{1,0:T(8,128)(2,1)} %param.4) | copy-start | bytes 4718596
  0.6 18.0 %collective-permute-start.6 = (bf16[128,1024]{1,0:T(8,128)(2,1)}, bf16[128,1024]{1,0:T(8,128)(2,1)S(1)}, u32[]{:S(2)}, u32[]{:S(2)}) collective-permute-start(bf16[128,1024]{1,0:T(8,128)(2,1)} %param.5), channel_id=1, source_target_pairs={{0,2},{1,3},{2,0},{3,1},{4,6},{5,7},{6,4},{7,5},{8,10},{9,11},{10,... | collective-permute-start | bytes 786440 | tf_op jit(solution)/shard_map/ppermute | solution.py:24
  4.7 12.7 %collective-permute-start.2 = (bf16[128,1024]{1,0:T(8,128)(2,1)}, bf16[128,1024]{1,0:T(8,128)(2,1)S(1)}, u32[]{:S(2)}, u32[]{:S(2)}) collective-permute-start(bf16[128,1024]{1,0:T(8,128)(2,1)} %param.5), channel_id=1, source_target_pairs={{0,1},{1,0},{2,3},{3,2},{4,5},{5,4},{6,7},{7,6},{8,9},{9,8},{10,11... | collective-permute-start | bytes 786440 | tf_op jit(solution)/shard_map/ppermute | solution.py:24
  6.3 18.1 %collective-permute-start = (bf16[128,1024]{1,0:T(8,128)(2,1)}, bf16[128,1024]{1,0:T(8,128)(2,1)S(1)}, u32[]{:S(2)}, u32[]{:S(2)}) collective-permute-start(bf16[128,1024]{1,0:T(8,128)(2,1)} %param.5), channel_id=1, source_target_pairs={{0,4},{4,8},{8,12},{12,0},{1,5},{5,9},{9,13},{13,1},{2,6},{6,10},{... | collective-permute-start | bytes 786440 | tf_op jit(solution)/shard_map/ppermute | solution.py:27
  6.3 17.4 %collective-permute-start.10 = (bf16[128,1024]{1,0:T(8,128)(2,1)}, bf16[128,1024]{1,0:T(8,128)(2,1)S(1)}, u32[]{:S(2)}, u32[]{:S(2)}) collective-permute-start(bf16[128,1024]{1,0:T(8,128)(2,1)} %param.5), channel_id=1, source_target_pairs={{0,3},{1,2},{2,1},{3,0},{4,7},{5,6},{6,5},{7,4},{8,11},{9,10},{10,... | collective-permute-start | bytes 786440 | tf_op jit(solution)/shard_map/ppermute | solution.py:24
  24.4 4.0 %copy-start.1 = (bf16[1024,1024]{1,0:T(8,128)(2,1)S(1)}, bf16[1024,1024]{1,0:T(8,128)(2,1)}, u32[]{:S(2)}) copy-start(bf16[1024,1024]{1,0:T(8,128)(2,1)} %constant_dynamic-update-slice_fusion.15) | copy-start | bytes 6291460
  25.6 33.8 %collective-permute-start.1 = (bf16[128,1024]{1,0:T(8,128)(2,1)S(1)}, bf16[128,1024]{1,0:T(8,128)(2,1)S(1)}, u32[]{:S(2)}, u32[]{:S(2)}) collective-permute-start(bf16[128,1024]{1,0:T(8,128)(2,1)S(1)} %fusion), channel_id=1, source_target_pairs={{0,12},{4,0},{8,4},{12,8},{1,13},{5,1},{9,5},{13,9},{2,14},{6,2},{... | collective-permute-start | bytes 786440 | tf_op jit(solution)/shard_map/ppermute | solution.py:27
  25.6 13.1 %collective-permute-start.7 = (bf16[128,1024]{1,0:T(8,128)(2,1)S(1)}, bf16[128,1024]{1,0:T(8,128)(2,1)S(1)}, u32[]{:S(2)}, u32[]{:S(2)}) collective-permute-start(bf16[128,1024]{1,0:T(8,128)(2,1)S(1)} %collective-permute-done.6), channel_id=1, source_target_pairs={{0,4},{4,8},{8,12},{12,0},{1,5},{5,9},{9,13},{13,1},{2,6},{6,10},{... | collective-permute-start | bytes 786440 | tf_op jit(solution)/shard_map/ppermute | solution.py:27
  26.1 11.5 %collective-permute-start.3 = (bf16[128,1024]{1,0:T(8,128)(2,1)S(1)}, bf16[128,1024]{1,0:T(8,128)(2,1)S(1)}, u32[]{:S(2)}, u32[]{:S(2)}) collective-permute-start(bf16[128,1024]{1,0:T(8,128)(2,1)S(1)} %collective-permute-done.2), channel_id=1, source_target_pairs={{0,4},{4,8},{8,12},{12,0},{1,5},{5,9},{9,13},{13,1},{2,6},{6,10},{... | collective-permute-start | bytes 786440 | tf_op jit(solution)/shard_map/ppermute | solution.py:27
  28.0 12.4 %collective-permute-start.11 = (bf16[128,1024]{1,0:T(8,128)(2,1)S(1)}, bf16[128,1024]{1,0:T(8,128)(2,1)S(1)}, u32[]{:S(2)}, u32[]{:S(2)}) collective-permute-start(bf16[128,1024]{1,0:T(8,128)(2,1)S(1)} %collective-permute-done.10), channel_id=1, source_target_pairs={{0,4},{4,8},{8,12},{12,0},{1,5},{5,9},{9,13},{13,1},{2,6},{6,10},{... | collective-permute-start | bytes 786440 | tf_op jit(solution)/shard_map/ppermute | solution.py:27
  41.5 3.9 %collective-permute-start.12 = (bf16[128,1024]{1,0:T(8,128)(2,1)S(1)}, bf16[128,1024]{1,0:T(8,128)(2,1)S(1)}, u32[]{:S(2)}, u32[]{:S(2)}) collective-permute-start(bf16[128,1024]{1,0:T(8,128)(2,1)S(1)} %fusion.3), channel_id=1, source_target_pairs={{0,12},{4,0},{8,4},{12,8},{1,13},{5,1},{9,5},{13,9},{2,14},{6,2},{... | collective-permute-start | bytes 786440 | tf_op jit(solution)/shard_map/ppermute | solution.py:27
  41.6 6.7 %collective-permute-start.8 = (bf16[128,1024]{1,0:T(8,128)(2,1)S(1)}, bf16[128,1024]{1,0:T(8,128)(2,1)S(1)}, u32[]{:S(2)}, u32[]{:S(2)}) collective-permute-start(bf16[128,1024]{1,0:T(8,128)(2,1)S(1)} %fusion.2), channel_id=1, source_target_pairs={{0,12},{4,0},{8,4},{12,8},{1,13},{5,1},{9,5},{13,9},{2,14},{6,2},{... | collective-permute-start | bytes 786440 | tf_op jit(solution)/shard_map/ppermute | solution.py:27
  41.7 13.7 %collective-permute-start.4 = (bf16[128,1024]{1,0:T(8,128)(2,1)S(1)}, bf16[128,1024]{1,0:T(8,128)(2,1)S(1)}, u32[]{:S(2)}, u32[]{:S(2)}) collective-permute-start(bf16[128,1024]{1,0:T(8,128)(2,1)S(1)} %fusion.1), channel_id=1, source_target_pairs={{0,12},{4,0},{8,4},{12,8},{1,13},{5,1},{9,5},{13,9},{2,14},{6,2},{... | collective-permute-start | bytes 786440 | tf_op jit(solution)/shard_map/ppermute | solution.py:27
  45.8 13.5 %collective-permute-start.13 = (bf16[128,1024]{1,0:T(8,128)(2,1)S(1)}, bf16[128,1024]{1,0:T(8,128)(2,1)S(1)}, u32[]{:S(2)}, u32[]{:S(2)}) collective-permute-start(bf16[128,1024]{1,0:T(8,128)(2,1)S(1)} %add_convert_fusion.1), channel_id=1, source_target_pairs={{0,3},{1,2},{2,1},{3,0},{4,7},{5,6},{6,5},{7,4},{8,11},{9,10},{10,... | collective-permute-start | bytes 786440 | tf_op jit(solution)/shard_map/ppermute | solution.py:24
  48.7 24.3 %collective-permute-start.9 = (bf16[128,1024]{1,0:T(8,128)(2,1)S(1)}, bf16[128,1024]{1,0:T(8,128)(2,1)S(1)}, u32[]{:S(2)}, u32[]{:S(2)}) collective-permute-start(bf16[128,1024]{1,0:T(8,128)(2,1)S(1)} %add_convert_fusion.2), channel_id=1, source_target_pairs={{0,2},{1,3},{2,0},{3,1},{4,6},{5,7},{6,4},{7,5},{8,10},{9,11},{10,... | collective-permute-start | bytes 786440 | tf_op jit(solution)/shard_map/ppermute | solution.py:24
  55.8 17.2 %collective-permute-start.5 = (bf16[128,1024]{1,0:T(8,128)(2,1)S(1)}, bf16[128,1024]{1,0:T(8,128)(2,1)S(1)}, u32[]{:S(2)}, u32[]{:S(2)}) collective-permute-start(bf16[128,1024]{1,0:T(8,128)(2,1)S(1)} %add_convert_fusion.3), channel_id=1, source_target_pairs={{0,1},{1,0},{2,3},{3,2},{4,5},{5,4},{6,7},{7,6},{8,9},{9,8},{10,11... | collective-permute-start | bytes 786440 | tf_op jit(solution)/shard_map/ppermute | solution.py:24

commit v2 on v1

--- a/solution.py
+++ b/solution.py
@@ -41,23 +41,45 @@
             delta, embeds, (((0,), (0,)), ((), ())), preferred_element_type=jnp.float32
         ) * scale
 
-    order = list(range(n_dp))
     prev_owner = (me_label - 1) % n_label
-    own = [weights if k == 0 else to_dp(weights, k) for k in order]
-    prev = [to_label(own[k], 1) for k in order]
-    d_own = [delta_of(own[k], me_label, k) for k in order]
-    d_prev = [delta_of(prev[k], prev_owner, k) for k in order]
-    back = [to_label(grad_w_of(d_prev[k]).astype(jnp.bfloat16), -1) for k in order]
-    total = [grad_w_of(d_own[k]) + back[k].astype(jnp.float32) for k in order]
-    grad_w = total[0]
-    for k in order[1:]:
-        grad_w = grad_w + to_dp(total[k].astype(jnp.bfloat16), k).astype(jnp.float32)
+    last = [embeds]
+
+    def in_turn(x):
+        x, _ = lax.optimization_barrier((x, last[0]))
+        return x
+
+    def score(piece, owner, k):
+        delta = delta_of(in_turn(piece), owner, k)
+        last[0] = grad_w_of(delta).astype(jnp.bfloat16)
+        return delta, last[0]
+
+    def join(k):
+        last[0] = (in_turn(w_own[k]).astype(jnp.float32) + in_turn(back[k]).astype(jnp.float32)).astype(jnp.bfloat16)
+        return last[0]
+
+    d_own, w_own, d_prev, w_prev, prev, back, moved = {}, {}, {}, {}, {}, {}, {}
+    own = [weights if k == 0 else to_dp(weights, k) for k in range(n_dp)]
+    for k in range(n_dp):
+        own[k] = in_turn(own[k])
+        prev[k] = to_label(own[k], 1)
+        d_own[k], w_own[k] = score(own[k], me_label, k)
+        if k > 1:
+            moved[k - 1] = to_dp(join(k - 1), k - 1)
+        d_prev[k], w_prev[k] = score(prev[k], prev_owner, k)
+        if k > 0:
+            back[k] = to_label(w_prev[k], -1)
+    stacked = jnp.concatenate(list(d_own.values()) + list(d_prev.values()), axis=1)
     grad_x = jnp.dot(
-        jnp.concatenate(d_own + d_prev, axis=1),
-        jnp.concatenate(own + prev, axis=0),
-        preferred_element_type=jnp.float32,
-    )
-    return (grad_w.astype(jnp.bfloat16), grad_x.astype(jnp.bfloat16))
+        in_turn(stacked), jnp.concatenate(own + list(prev.values()), axis=0), preferred_element_type=jnp.float32
+    ).astype(jnp.bfloat16)
+    last[0] = grad_x
+    back[0] = to_label(in_turn(w_prev[0]), -1)
+    if n_dp > 1:
+        moved[n_dp - 1] = to_dp(join(n_dp - 1), n_dp - 1)
+    grad_w = w_own[0].astype(jnp.float32) + in_turn(back[0]).astype(jnp.float32)
+    for k in range(1, n_dp):
+        grad_w = grad_w + in_turn(moved[k]).astype(jnp.float32)
+    return (grad_w.astype(jnp.bfloat16), grad_x)
 
 
 def solution(mesh):

time: 74.1 us -> 69.9 us (0.943)
  the two profiles are of different devices: /device:TPU:0 before, /device:TPU:13 now
where the time goes in v2:
time: 69.9 us; the launch traced here: 69.7 us
  waiting for transfers between devices  29.6 us (42%)
  starting transfers between devices  22.6 us (32%)
  matrix products  12.6 us (18%)
  local copies, waits for them, and re-layouts  1.95 us (3%)
  other arithmetic  1.89 us (3%)
  between operations  0.99 us (1%)
    ppermute x6, waiting for transfers between devices, to_dp(): return lax.ppermute(x, 'dp', [(i, i ^ k) for i in range(n_dp)])  17 us
    ppermute x8, starting transfers between devices, to_label(): lax.ppermute(x, 'label', [(i, (i + by) % n_label) for i in range(n_label)])  14.4 us
    ppermute x8, waiting for transfers between devices, to_label(): lax.ppermute(x, 'label', [(i, (i + by) % n_label) for i in range(n_label)])  12.7 us
    ppermute x6, starting transfers between devices, to_dp(): return lax.ppermute(x, 'dp', [(i, i ^ k) for i in range(n_dp)])  8.25 us
    dot_general x8, matrix products, delta_of(): lax.dot_general(embeds, piece, (((1,), (1,)), ((), ())), preferred_elemen...  6.55 us
    dot_general x8, matrix products, grad_w_of(): lax.dot_general(delta, embeds, (((0,), (0,)), ((), ())), preferred_elemen...  3.06 us
    dot_general x1, matrix products, local(): jnp.dot(in_turn(stacked), jnp.concatenate(own + list(prev.values()), axis...  2.99 us
    unnamed x14, local copies, waits for them, and re-layouts  1.86 us
  transfers between devices with their start and end apart: 14, of which 6 were waited for; matrix products, arithmetic and copies ran while one was open for 22% of the time, Pallas kernels for 0%

profile of v2, /device:TPU:13, one launch (start us, length us, event | category | flops | bytes accessed | tf_op | source)
XLA Modules:
  0.0 69.7 jit_solution(7762137173151749387)
XLA Ops:
  0.6 0.0 copy-start
  0.6 0.2 collective-permute-start.1
  0.9 2.3 %collective-permute-start.2 = (bf16[128,1024]{1,0:T(8,128)(2,1)}, bf16[128,1024]{1,0:T(8,128)(2,1)S(1)}, u32[]{:S(2)}, u32[]{:S(2)}) collective-permute-start(bf16[128,1024]{1,0:T(8,128)(2,1)} %param.5), channel_id=1, source_target_pairs={{0,2},{1,3},{2,0},{3,1},{4,6},{5,7},{6,4},{7,5},{8,10},{9,11},{10,... | collective-permute-start | bytes 786440 | tf_op jit(solution)/shard_map/ppermute | solution.py:24
  3.2 0.2 collective-permute-start.4
  3.4 2.6 %collective-permute-start = (bf16[128,1024]{1,0:T(8,128)(2,1)}, bf16[128,1024]{1,0:T(8,128)(2,1)S(1)}, u32[]{:S(2)}, u32[]{:S(2)}) collective-permute-start(bf16[128,1024]{1,0:T(8,128)(2,1)} %param.5), channel_id=1, source_target_pairs={{0,4},{4,8},{8,12},{12,0},{1,5},{5,9},{9,13},{13,1},{2,6},{6,10},{... | collective-permute-start | bytes 786440 | tf_op jit(solution)/shard_map/ppermute | solution.py:27
  6.0 1.7 %constant_dynamic-update-slice_fusion.15 = bf16[1024,1024]{1,0:T(8,128)(2,1)} fusion(bf16[128,1024]{1,0:T(8,128)(2,1)} %param.5), kind=kLoop, calls=%fused_computation.92 | loop fusion | bytes 524288
  7.8 0.7 %fusion.56 = s32[768,8]{0,1:T(8,128)S(1)} fusion(s32[768,8]{0,1:T(8,128)} %param.6, s32[768]{0:T(1024)} %param.7), kind=kLoop, calls=%fused_computation.94 | loop fusion | flops 12288 | bytes 52224 | tf_op jit(solution)/shard_map/jit(_where)/select_n | solution.py:21
  8.5 0.1 dynamic-slice_reduce_fusion
  8.6 0.0 copy-done
  8.6 1.7 %constant_dynamic-update-slice_fusion.7 = (bf16[768,1024]{0,1:T(8,128)(2,1)S(1)}, bf16[768,128]{0,1:T(8,128)(2,1)S(1)}) fusion(s32[128]{0:T(128)S(1)} %iota_add_fusion.7, s32[768]{0:T(1024)S(1)} %get-tuple-element.57, bf16[128,1024]{1,0:T(8,128)(2,1)} %param.5, bf16[768,1024]{1,0:T(8,128)(2,1)S(1)} %copy-done), kind=kOutput, calls=%fused_computation.84 | convolution fusion | flops 202014720 | bytes 2231808 | tf_op jit(solution)/shard_map/dot_general | solution.py:34
  10.2 0.4 fusion
  10.6 0.0 collective-permute-done
  10.6 0.0 copy-start.1
  10.7 0.7 %fusion.54 = bf16[768,128]{0,1:T(8,128)(2,1)S(1)} fusion(bf16[128,1024]{1,0:T(8,128)(2,1)S(1)} %collective-permute-done, bf16[768,1024]{1,0:T(8,128)(2,1)S(1)} %copy-done, s32[768]{0:T(1024)S(1)} %get-tuple-element.56, s32[128]{0:T(128)S(1)} %iota_add_fusion.6), kind=kOutput, calls=%fused_computation.71 | convolution fusion | flops 202014720 | bytes 2035200 | tf_op jit(solution)/shard_map/dot_general | solution.py:34
  11.4 0.4 fusion.1
  11.8 0.0 collective-permute-done.1
  11.8 1.9 %collective-permute-start.3 = (bf16[128,1024]{1,0:T(8,128)(2,1)S(1)}, bf16[128,1024]{1,0:T(8,128)(2,1)S(1)}, u32[]{:S(2)}, u32[]{:S(2)}) collective-permute-start(bf16[128,1024]{1,0:T(8,128)(2,1)S(1)} %collective-permute-done.1), channel_id=1, source_target_pairs={{0,4},{4,8},{8,12},{12,0},{1,5},{5,9},{9,13},{13,1},{2,6},{6,10},{... | collective-permute-start | bytes 786440 | tf_op jit(solution)/shard_map/ppermute | solution.py:27
  13.7 0.0 copy-done.1
  13.7 0.7 %constant_dynamic-update-slice_fusion.6 = (bf16[768,1024]{0,1:T(8,128)(2,1)S(1)}, bf16[768,128]{0,1:T(8,128)(2,1)S(1)}) fusion(bf16[768,1024]{0,1:T(8,128)(2,1)S(1)} %get-tuple-element.58, s32[128]{0:T(128)S(1)} %iota_add_fusion.5, s32[768]{0:T(1024)S(1)} %get-tuple-element.55, bf16[128,1024]{1,0:T(8,128)(2,1)S(1)} %collective-permute-done.1, ...), kind=kOutput, calls=%fused_computation.83 | convolution fusion | flops 202014720 | bytes 2232832 | tf_op jit(solution)/shard_map/dot_general | solution.py:34
  14.4 0.4 fusion.2
  14.8 2.2 %collective-permute-done.3 = bf16[128,1024]{1,0:T(8,128)(2,1)S(1)} collective-permute-done((bf16[128,1024]{1,0:T(8,128)(2,1)S(1)}, bf16[128,1024]{1,0:T(8,128)(2,1)S(1)}, u32[]{:S(2)}, u32[]{:S(2)}) %collective-permute-start.3) | collective-permute-done | bytes 262176 | tf_op jit(solution)/shard_map/ppermute | solution.py:27
  17.0 0.7 %fusion.52 = bf16[768,128]{0,1:T(8,128)(2,1)S(1)} fusion(bf16[128,1024]{1,0:T(8,128)(2,1)S(1)} %collective-permute-done.3, bf16[768,1024]{1,0:T(8,128)(2,1)S(1)} %copy-done, s32[768]{0:T(1024)S(1)} %get-tuple-element.54, s32[128]{0:T(128)S(1)} %iota_add_fusion.4), kind=kOutput, calls=%fused_computation.69 | convolution fusion | flops 202014720 | bytes 2035200 | tf_op jit(solution)/shard_map/dot_general | solution.py:34
  17.7 0.4 fusion.3
  18.1 1.4 %collective-permute-start.6 = (bf16[128,1024]{1,0:T(8,128)(2,1)S(1)}, bf16[128,1024]{1,0:T(8,128)(2,1)S(1)}, u32[]{:S(2)}, u32[]{:S(2)}) collective-permute-start(bf16[128,1024]{1,0:T(8,128)(2,1)S(1)} %fusion.3), channel_id=1, source_target_pairs={{0,12},{4,0},{8,4},{12,8},{1,13},{5,1},{9,5},{13,9},{2,14},{6,2},{... | collective-permute-start | bytes 786440 | tf_op jit(solution)/shard_map/ppermute | solution.py:27
  19.5 0.0 collective-permute-done.2
  19.5 4.3 %collective-permute-start.5 = (bf16[128,1024]{1,0:T(8,128)(2,1)S(1)}, bf16[128,1024]{1,0:T(8,128)(2,1)S(1)}, u32[]{:S(2)}, u32[]{:S(2)}) collective-permute-start(bf16[128,1024]{1,0:T(8,128)(2,1)S(1)} %collective-permute-done.2), channel_id=1, source_target_pairs={{0,4},{4,8},{8,12},{12,0},{1,5},{5,9},{9,13},{13,1},{2,6},{6,10},{... | collective-permute-start | bytes 786440 | tf_op jit(solution)/shard_map/ppermute | solution.py:27
  23.8 0.7 %constant_dynamic-update-slice_fusion.5 = (bf16[768,1024]{0,1:T(8,128)(2,1)S(1)}, bf16[768,128]{0,1:T(8,128)(2,1)S(1)}) fusion(bf16[768,1024]{0,1:T(8,128)(2,1)S(1)} %get-tuple-element.60, s32[128]{0:T(128)S(1)} %iota_add_fusion.3, s32[768]{0:T(1024)S(1)} %get-tuple-element.53, bf16[128,1024]{1,0:T(8,128)(2,1)S(1)} %collective-permute-done.2, ...), kind=kOutput, calls=%fused_computation.82 | convolution fusion | flops 202014720 | bytes 2232832 | tf_op jit(solution)/shard_map/dot_general | solution.py:34
  24.5 0.4 fusion.4
  24.9 0.0 collective-permute-done.6
  25.0 0.1 add_convert_fusion.3
  25.0 2.1 %collective-permute-done.5 = bf16[128,1024]{1,0:T(8,128)(2,1)S(1)} collective-permute-done((bf16[128,1024]{1,0:T(8,128)(2,1)S(1)}, bf16[128,1024]{1,0:T(8,128)(2,1)S(1)}, u32[]{:S(2)}, u32[]{:S(2)}) %collective-permute-start.5) | collective-permute-done | bytes 262176 | tf_op jit(solution)/shard_map/ppermute | solution.py:27
  27.1 0.7 fusion.50
  27.8 0.4 fusion.5
  28.2 0.0 collective-permute-done.4
  28.2 2.5 %collective-permute-start.7 = (bf16[128,1024]{1,0:T(8,128)(2,1)S(1)}, bf16[128,1024]{1,0:T(8,128)(2,1)S(1)}, u32[]{:S(2)}, u32[]{:S(2)}) collective-permute-start(bf16[128,1024]{1,0:T(8,128)(2,1)S(1)} %collective-permute-done.4), channel_id=1, source_target_pairs={{0,4},{4,8},{8,12},{12,0},{1,5},{5,9},{9,13},{13,1},{2,6},{6,10},{... | collective-permute-start | bytes 786440 | tf_op jit(solution)/shard_map/ppermute | solution.py:27
  30.8 0.0 collective-permute-start.8
  30.8 2.0 %collective-permute-start.11 = (bf16[128,1024]{1,0:T(8,128)(2,1)S(1)}, bf16[128,1024]{1,0:T(8,128)(2,1)S(1)}, u32[]{:S(2)}, u32[]{:S(2)}) collective-permute-start(bf16[128,1024]{1,0:T(8,128)(2,1)S(1)} %add_convert_fusion.3), channel_id=1, source_target_pairs={{0,1},{1,0},{2,3},{3,2},{4,5},{5,4},{6,7},{7,6},{8,9},{9,8},{10,11... | collective-permute-start | bytes 786440 | tf_op jit(solution)/shard_map/ppermute | solution.py:24
  32.8 0.7 %constant_dynamic-update-slice_fusion.4 = (bf16[768,1024]{0,1:T(8,128)(2,1)S(1)}, bf16[768,128]{0,1:T(8,128)(2,1)S(1)}) fusion(bf16[768,1024]{0,1:T(8,128)(2,1)S(1)} %get-tuple-element.62, s32[128]{0:T(128)S(1)} %iota_add_fusion.1, s32[768]{0:T(1024)S(1)} %get-tuple-element.51, bf16[128,1024]{1,0:T(8,128)(2,1)S(1)} %collective-permute-done.4, ...), kind=kOutput, calls=%fused_computation.81 | convolution fusion | flops 202014720 | bytes 2232832 | tf_op jit(solution)/shard_map/dot_general | solution.py:34
  33.5 0.4 fusion.6
  34.0 3.9 %collective-permute-done.8 = bf16[128,1024]{1,0:T(8,128)(2,1)S(1)} collective-permute-done((bf16[128,1024]{1,0:T(8,128)(2,1)S(1)}, bf16[128,1024]{1,0:T(8,128)(2,1)S(1)}, u32[]{:S(2)}, u32[]{:S(2)}) %collective-permute-start.8) | collective-permute-done | bytes 262176 | tf_op jit(solution)/shard_map/ppermute | solution.py:27
  37.9 0.1 add_convert_fusion.2
  38.0 0.0 collective-permute-done.7
  38.0 0.7 %constant_dynamic-update-slice_fusion = (bf16[768,1024]{0,1:T(8,128)(2,1)S(1)}, bf16[768,128]{0,1:T(8,128)(2,1)S(1)}) fusion(bf16[768,1024]{0,1:T(8,128)(2,1)S(1)} %constant_dynamic-update-slice_fusion.1, s32[128]{0:T(128)S(1)} %iota_add_fusion, s32[768]{0:T(1024)S(1)} %get-tuple-element.50, bf16[128,1024]{1,0:T(8,128)(2,1)S(1)} %collective-permute-done.7, ...), kind=kOutput, calls=%fused_computation.77 | convolution fusion | flops 202014720 | bytes 2232832 | tf_op jit(solution)/shard_map/dot_general | solution.py:34
  38.7 0.4 fusion.7
  39.1 0.1 collective-permute-start.10
  39.2 3.0 %convolution_convert_fusion = bf16[768,1024]{1,0:T(8,128)(2,1)} fusion(bf16[768,1024]{0,1:T(8,128)(2,1)S(1)} %get-tuple-element.42, bf16[1024,1024]{1,0:T(8,128)(2,1)S(1)} %constant_dynamic-update-slice_fusion.8), kind=kOutput, calls=%fused_computation | convolution fusion | flops 1611399168 | bytes 5242880 | tf_op jit(solution)/shard_map/dot_general | solution.py:72
  42.2 3.3 %collective-permute-start.12 = (bf16[128,1024]{1,0:T(8,128)(2,1)S(1)}, bf16[128,1024]{1,0:T(8,128)(2,1)S(1)}, u32[]{:S(2)}, u32[]{:S(2)}) collective-permute-start(bf16[128,1024]{1,0:T(8,128)(2,1)S(1)} %add_convert_fusion.2), channel_id=1, source_target_pairs={{0,2},{1,3},{2,0},{3,1},{4,6},{5,7},{6,4},{7,5},{8,10},{9,11},{10,... | collective-permute-start | bytes 786440 | tf_op jit(solution)/shard_map/ppermute | solution.py:24
  45.5 1.6 %collective-permute-start.9 = (bf16[128,1024]{1,0:T(8,128)(2,1)S(1)}, bf16[128,1024]{1,0:T(8,128)(2,1)S(1)}, u32[]{:S(2)}, u32[]{:S(2)}) collective-permute-start(bf16[128,1024]{1,0:T(8,128)(2,1)S(1)} %fusion.1), channel_id=1, source_target_pairs={{0,12},{4,0},{8,4},{12,8},{1,13},{5,1},{9,5},{13,9},{2,14},{6,2},{... | collective-permute-start | bytes 786440 | tf_op jit(solution)/shard_map/ppermute | solution.py:27
  47.0 0.0 collective-permute-done.10
  47.0 0.1 add_convert_fusion.1
  47.1 0.2 collective-permute-start.13
  47.3 4.5 %collective-permute-done.9 = bf16[128,1024]{1,0:T(8,128)(2,1)S(1)} collective-permute-done((bf16[128,1024]{1,0:T(8,128)(2,1)S(1)}, bf16[128,1024]{1,0:T(8,128)(2,1)S(1)}, u32[]{:S(2)}, u32[]{:S(2)}) %collective-permute-start.9) | collective-permute-done | bytes 262176 | tf_op jit(solution)/shard_map/ppermute | solution.py:27
  51.8 0.0 collective-permute-done.11
  51.8 10.0 %collective-permute-done.12 = bf16[128,1024]{1,0:T(8,128)(2,1)S(1)} collective-permute-done((bf16[128,1024]{1,0:T(8,128)(2,1)S(1)}, bf16[128,1024]{1,0:T(8,128)(2,1)S(1)}, u32[]{:S(2)}, u32[]{:S(2)}) %collective-permute-start.12) | collective-permute-done | bytes 262176 | tf_op jit(solution)/shard_map/ppermute | solution.py:24
  61.8 7.0 %collective-permute-done.13 = bf16[128,1024]{1,0:T(8,128)(2,1)S(1)} collective-permute-done((bf16[128,1024]{1,0:T(8,128)(2,1)S(1)}, bf16[128,1024]{1,0:T(8,128)(2,1)S(1)}, u32[]{:S(2)}, u32[]{:S(2)}) %collective-permute-start.13) | collective-permute-done | bytes 262176 | tf_op jit(solution)/shard_map/ppermute | solution.py:24
  68.8 0.9 %add_convert_fusion = bf16[128,1024]{1,0:T(8,128)(2,1)} fusion(bf16[128,1024]{1,0:T(8,128)(2,1)S(1)} %collective-permute-done.13, bf16[128,1024]{1,0:T(8,128)(2,1)S(1)} %collective-permute-done.12, bf16[128,1024]{1,0:T(8,128)(2,1)S(1)} %collective-permute-done.11, bf16[128,1024]{1,0:T(8,128)(2,1)S(1)} %collective-permute-done.9, bf16[128,1024]{1,0:T(8,128)(2,1)S(1)} %fusion), kind=kLoop, calls=%fused_computation.73 | loop fusion | flops 1310720 | bytes 1572864 | tf_op jit(solution)/shard_map/convert_element_type | solution.py:82
  (18 shorter events, 0.2 us)
Async XLA Ops:
  0.6 8.0 %copy-start = (bf16[768,1024]{1,0:T(8,128)(2,1)S(1)}, bf16[768,1024]{1,0:T(8,128)(2,1)}, u32[]{:S(2)}) copy-start(bf16[768,1024]{1,0:T(8,128)(2,1)} %param.4) | copy-start | bytes 4718596
  0.6 11.1 %collective-permute-start.1 = (bf16[128,1024]{1,0:T(8,128)(2,1)}, bf16[128,1024]{1,0:T(8,128)(2,1)S(1)}, u32[]{:S(2)}, u32[]{:S(2)}) collective-permute-start(bf16[128,1024]{1,0:T(8,128)(2,1)} %param.5), channel_id=1, source_target_pairs={{0,1},{1,0},{2,3},{3,2},{4,5},{5,4},{6,7},{7,6},{8,9},{9,8},{10,11... | collective-permute-start | bytes 786440 | tf_op jit(solution)/shard_map/ppermute | solution.py:24
  0.9 18.6 %collective-permute-start.2 = (bf16[128,1024]{1,0:T(8,128)(2,1)}, bf16[128,1024]{1,0:T(8,128)(2,1)S(1)}, u32[]{:S(2)}, u32[]{:S(2)}) collective-permute-start(bf16[128,1024]{1,0:T(8,128)(2,1)} %param.5), channel_id=1, source_target_pairs={{0,2},{1,3},{2,0},{3,1},{4,6},{5,7},{6,4},{7,5},{8,10},{9,11},{10,... | collective-permute-start | bytes 786440 | tf_op jit(solution)/shard_map/ppermute | solution.py:24
  3.2 25.0 %collective-permute-start.4 = (bf16[128,1024]{1,0:T(8,128)(2,1)}, bf16[128,1024]{1,0:T(8,128)(2,1)S(1)}, u32[]{:S(2)}, u32[]{:S(2)}) collective-permute-start(bf16[128,1024]{1,0:T(8,128)(2,1)} %param.5), channel_id=1, source_target_pairs={{0,3},{1,2},{2,1},{3,0},{4,7},{5,6},{6,5},{7,4},{8,11},{9,10},{10,... | collective-permute-start | bytes 786440 | tf_op jit(solution)/shard_map/ppermute | solution.py:24
  3.4 7.3 %collective-permute-start = (bf16[128,1024]{1,0:T(8,128)(2,1)}, bf16[128,1024]{1,0:T(8,128)(2,1)S(1)}, u32[]{:S(2)}, u32[]{:S(2)}) collective-permute-start(bf16[128,1024]{1,0:T(8,128)(2,1)} %param.5), channel_id=1, source_target_pairs={{0,4},{4,8},{8,12},{12,0},{1,5},{5,9},{9,13},{13,1},{2,6},{6,10},{... | collective-permute-start | bytes 786440 | tf_op jit(solution)/shard_map/ppermute | solution.py:27
  10.6 3.0 %copy-start.1 = (bf16[1024,1024]{1,0:T(8,128)(2,1)S(1)}, bf16[1024,1024]{1,0:T(8,128)(2,1)}, u32[]{:S(2)}) copy-start(bf16[1024,1024]{1,0:T(8,128)(2,1)} %constant_dynamic-update-slice_fusion.15) | copy-start | bytes 6291460
  11.8 5.2 %collective-permute-start.3 = (bf16[128,1024]{1,0:T(8,128)(2,1)S(1)}, bf16[128,1024]{1,0:T(8,128)(2,1)S(1)}, u32[]{:S(2)}, u32[]{:S(2)}) collective-permute-start(bf16[128,1024]{1,0:T(8,128)(2,1)S(1)} %collective-permute-done.1), channel_id=1, source_target_pairs={{0,4},{4,8},{8,12},{12,0},{1,5},{5,9},{9,13},{13,1},{2,6},{6,10},{... | collective-permute-start | bytes 786440 | tf_op jit(solution)/shard_map/ppermute | solution.py:27
  18.1 6.9 %collective-permute-start.6 = (bf16[128,1024]{1,0:T(8,128)(2,1)S(1)}, bf16[128,1024]{1,0:T(8,128)(2,1)S(1)}, u32[]{:S(2)}, u32[]{:S(2)}) collective-permute-start(bf16[128,1024]{1,0:T(8,128)(2,1)S(1)} %fusion.3), channel_id=1, source_target_pairs={{0,12},{4,0},{8,4},{12,8},{1,13},{5,1},{9,5},{13,9},{2,14},{6,2},{... | collective-permute-start | bytes 786440 | tf_op jit(solution)/shard_map/ppermute | solution.py:27
  19.5 7.6 %collective-permute-start.5 = (bf16[128,1024]{1,0:T(8,128)(2,1)S(1)}, bf16[128,1024]{1,0:T(8,128)(2,1)S(1)}, u32[]{:S(2)}, u32[]{:S(2)}) collective-permute-start(bf16[128,1024]{1,0:T(8,128)(2,1)S(1)} %collective-permute-done.2), channel_id=1, source_target_pairs={{0,4},{4,8},{8,12},{12,0},{1,5},{5,9},{9,13},{13,1},{2,6},{6,10},{... | collective-permute-start | bytes 786440 | tf_op jit(solution)/shard_map/ppermute | solution.py:27
  28.2 9.7 %collective-permute-start.7 = (bf16[128,1024]{1,0:T(8,128)(2,1)S(1)}, bf16[128,1024]{1,0:T(8,128)(2,1)S(1)}, u32[]{:S(2)}, u32[]{:S(2)}) collective-permute-start(bf16[128,1024]{1,0:T(8,128)(2,1)S(1)} %collective-permute-done.4), channel_id=1, source_target_pairs={{0,4},{4,8},{8,12},{12,0},{1,5},{5,9},{9,13},{13,1},{2,6},{6,10},{... | collective-permute-start | bytes 786440 | tf_op jit(solution)/shard_map/ppermute | solution.py:27
  30.8 7.1 %collective-permute-start.8 = (bf16[128,1024]{1,0:T(8,128)(2,1)S(1)}, bf16[128,1024]{1,0:T(8,128)(2,1)S(1)}, u32[]{:S(2)}, u32[]{:S(2)}) collective-permute-start(bf16[128,1024]{1,0:T(8,128)(2,1)S(1)} %fusion.5), channel_id=1, source_target_pairs={{0,12},{4,0},{8,4},{12,8},{1,13},{5,1},{9,5},{13,9},{2,14},{6,2},{... | collective-permute-start | bytes 786440 | tf_op jit(solution)/shard_map/ppermute | solution.py:27
  30.8 21.0 %collective-permute-start.11 = (bf16[128,1024]{1,0:T(8,128)(2,1)S(1)}, bf16[128,1024]{1,0:T(8,128)(2,1)S(1)}, u32[]{:S(2)}, u32[]{:S(2)}) collective-permute-start(bf16[128,1024]{1,0:T(8,128)(2,1)S(1)} %add_convert_fusion.3), channel_id=1, source_target_pairs={{0,1},{1,0},{2,3},{3,2},{4,5},{5,4},{6,7},{7,6},{8,9},{9,8},{10,11... | collective-permute-start | bytes 786440 | tf_op jit(solution)/shard_map/ppermute | solution.py:24
  39.1 8.0 %collective-permute-start.10 = (bf16[128,1024]{1,0:T(8,128)(2,1)S(1)}, bf16[128,1024]{1,0:T(8,128)(2,1)S(1)}, u32[]{:S(2)}, u32[]{:S(2)}) collective-permute-start(bf16[128,1024]{1,0:T(8,128)(2,1)S(1)} %fusion.7), channel_id=1, source_target_pairs={{0,12},{4,0},{8,4},{12,8},{1,13},{5,1},{9,5},{13,9},{2,14},{6,2},{... | collective-permute-start | bytes 786440 | tf_op jit(solution)/shard_map/ppermute | solution.py:27
  42.2 19.7 %collective-permute-start.12 = (bf16[128,1024]{1,0:T(8,128)(2,1)S(1)}, bf16[128,1024]{1,0:T(8,128)(2,1)S(1)}, u32[]{:S(2)}, u32[]{:S(2)}) collective-permute-start(bf16[128,1024]{1,0:T(8,128)(2,1)S(1)} %add_convert_fusion.2), channel_id=1, source_target_pairs={{0,2},{1,3},{2,0},{3,1},{4,6},{5,7},{6,4},{7,5},{8,10},{9,11},{10,... | collective-permute-start | bytes 786440 | tf_op jit(solution)/shard_map/ppermute | solution.py:24
  45.5 6.4 %collective-permute-start.9 = (bf16[128,1024]{1,0:T(8,128)(2,1)S(1)}, bf16[128,1024]{1,0:T(8,128)(2,1)S(1)}, u32[]{:S(2)}, u32[]{:S(2)}) collective-permute-start(bf16[128,1024]{1,0:T(8,128)(2,1)S(1)} %fusion.1), channel_id=1, source_target_pairs={{0,12},{4,0},{8,4},{12,8},{1,13},{5,1},{9,5},{13,9},{2,14},{6,2},{... | collective-permute-start | bytes 786440 | tf_op jit(solution)/shard_map/ppermute | solution.py:27
  47.1 21.7 %collective-permute-start.13 = (bf16[128,1024]{1,0:T(8,128)(2,1)S(1)}, bf16[128,1024]{1,0:T(8,128)(2,1)S(1)}, u32[]{:S(2)}, u32[]{:S(2)}) collective-permute-start(bf16[128,1024]{1,0:T(8,128)(2,1)S(1)} %add_convert_fusion.1), channel_id=1, source_target_pairs={{0,3},{1,2},{2,1},{3,0},{4,7},{5,6},{6,5},{7,4},{8,11},{9,10},{10,... | collective-permute-start | bytes 786440 | tf_op jit(solution)/shard_map/ppermute | solution.py:24

commit v3 on v1

v3 whole, which is shorter than its diff:
```python
import math

import jax
import jax.numpy as jnp
from jax import lax
from jax.sharding import PartitionSpec as P


def local(embeds, weights, pos_ids, pos_count):
    n_groups = lax.axis_size("groups")
    n_label = lax.axis_size("label")
    n_dp = lax.axis_size("dp")
    me_group = lax.axis_index("groups")
    me_label = lax.axis_index("label")
    me_dp = lax.axis_index("dp")
    rows_dev, width = embeds.shape
    ch_dev = weights.shape[0]
    stretch = ch_dev * n_dp
    half = ch_dev // 2
    slots = pos_ids.shape[1]
    span = stretch * n_label // slots
    scale = 1.0 / math.sqrt(rows_dev * n_dp)
    even = me_label % 2 == 0
    valid = jnp.arange(slots, dtype=jnp.int32)[None, :] < pos_count[:, None]
    ids = jnp.where(valid, pos_ids, -1)
    last = [embeds]

    def in_turn(x):
        x, _ = lax.optimization_barrier((x, last[0]))
        return x

    def to_dp(x, k):
        return lax.ppermute(x, "dp", [(i, i ^ k) for i in range(n_dp)])

    def to_dp_of(parity, x, k):
        pairs = [
            (label * n_dp + i, label * n_dp + (i ^ k))
            for label in range(parity, n_label, 2) for i in range(n_dp)
        ]
        return lax.ppermute(x, ("label", "dp"), pairs)

    def to_group(x):
        return lax.ppermute(x, "groups", [(i, i ^ 1) for i in range(n_groups)])

    def to_label(parity, x, by):
        return lax.ppermute(x, "label", [(i, (i + by) % n_label) for i in range(parity, n_label, 2)])

    def delta_of(piece, owner, k):
        start = owner * stretch + (me_dp ^ k) * ch_dev
        column = lax.dynamic_slice_in_dim(ids, start // span, 1, axis=1)
        labels = start + jnp.arange(ch_dev, dtype=jnp.int32)
        target = (column == labels[None, :]).astype(jnp.float32)
        logits = lax.dot_general(
            embeds, piece, (((1,), (1,)), ((), ())), preferred_element_type=jnp.float32
        )
        return (jax.nn.sigmoid(logits) - target).astype(jnp.bfloat16)

    def score(piece, owner, k):
        delta = delta_of(in_turn(piece), owner, k)
        last[0] = (
            lax.dot_general(delta, embeds, (((0,), (0,)), ((), ())), preferred_element_type=jnp.float32) * scale
        ).astype(jnp.bfloat16)
        return delta, last[0]

    def join(mine, theirs):
        last[0] = (in_turn(mine).astype(jnp.float32) + in_turn(theirs).astype(jnp.float32)).astype(jnp.bfloat16)
        return last[0]

    near = jnp.where(even, me_label, me_label - 1)
    far = jnp.where(even, (me_label - 1) % n_label, me_label)
    w_near, w_far, d_near, d_far, g_near, g_far = {}, {}, {}, {}, {}, {}
    back_near, back_far, sum_near, sum_far, moved_near, moved_far = {}, {}, {}, {}, {}, {}
    passed_near, passed_far, pieces = {}, {}, {0: weights}

    def pass_on(k):
        pieces[k] = in_turn(pieces[k])
        passed_near[k] = to_label(0, pieces[k], 1)
        passed_far[k] = to_label(1, pieces[k], 1)

    def near_step(k):
        w_near[k] = jnp.where(even, pieces[k], passed_near[k])
        d_near[k], g_near[k] = score(w_near[k], near, k)
        back_near[k] = to_label(1, g_near[k], -1)

    def far_step(k):
        w_far[k] = jnp.where(even, in_turn(passed_far[k]), pieces[k])
        d_far[k], g_far[k] = score(w_far[k], far, k)
        back_far[k] = to_label(0, g_far[k], -1)

    def near_send(k):
        sum_near[k] = join(g_near[k], back_near[k])
        if k > 0:
            moved_near[k] = to_dp_of(0, sum_near[k], k)

    def far_send(k):
        sum_far[k] = join(g_far[k], back_far[k])
        if k > 0:
            moved_far[k] = to_dp_of(1, sum_far[k], k)

    mine = lax.dynamic_slice_in_dim(weights, me_group * half, half, axis=0)
    halves = {k: to_dp(mine, k) for k in range(2, n_dp)}
    others = {}
    pieces[1] = to_dp(weights, 1)

    def swap(k):
        halves[k] = in_turn(halves[k])
        others[k] = to_group(halves[k])

    def whole(k):
        other = in_turn(others[k])
        pieces[k] = jnp.where(
            me_group == 0,
            jnp.concatenate([halves[k], other], axis=0),
            jnp.concatenate([other, halves[k]], axis=0),
        )

    pass_on(0)
    near_step(0)
    far_step(0)
    pass_on(1)
    near_step(1)
    swap(2)
    near_send(1)
    far_step(1)
    for k in range(2, n_dp):
        if k + 1 < n_dp:
            swap(k + 1)
        whole(k)
        pass_on(k)
        near_step(k)
        near_send(k)
        if k == 2:
            far_send(1)
        if k > 2:
            far_step(k - 1)
    far_step(n_dp - 1)
    order = range(n_dp)
    grad_x = jnp.dot(
        in_turn(jnp.concatenate([d_near[k] for k in order] + [d_far[k] for k in order], axis=1)),
        jnp.concatenate([w_near[k] for k in order] + [w_far[k] for k in order], axis=0),
        preferred_element_type=jnp.float32,
    ).astype(jnp.bfloat16)
    last[0] = grad_x
    for k in range(2, n_dp):
        far_send(k)
    near_send(0)
    far_send(0)
    grad_w = jnp.where(even, sum_near[0], sum_far[0]).astype(jnp.float32)
    for k in range(1, n_dp):
        grad_w = grad_w + jnp.where(even, in_turn(moved_near[k]), in_turn(moved_far[k])).astype(jnp.float32)
    return (grad_w.astype(jnp.bfloat16), grad_x)


def solution(mesh):
    return jax.shard_map(
        local,
        mesh=mesh,
        in_specs=(
            P(("groups", "label", "dp"), None),
            P(("label", "dp"), None),
            P(("groups", "label", "dp"), None),
            P(("groups", "label", "dp")),
        ),
        out_specs=(P(("groups", "label", "dp"), None), P(("groups", "label", "dp"), None)),
        check_vma=False,
    )
```

time: 74.1 us -> 116 us (1.57)
  the two profiles are of different devices: /device:TPU:0 before, /device:TPU:9 now
where the time goes in v3:
time: 116 us; the launch traced here: 115 us
  starting transfers between devices  51.4 us (44%)
  waiting for transfers between devices  42.5 us (37%)
  matrix products  13 us (11%)
  other arithmetic  5.33 us (5%)
  local copies, waits for them, and re-layouts  1.38 us (1%)
  between operations  1.23 us (1%)
    ppermute x16, starting transfers between devices, to_label(): lax.ppermute(x, 'label', [(i, (i + by) % n_label) for i in range(parity,...  34.7 us
    ppermute x6, waiting for transfers between devices, to_dp_of(): return lax.ppermute(x, ('label', 'dp'), pairs)  20.2 us
    ppermute x6, starting transfers between devices, to_dp_of(): return lax.ppermute(x, ('label', 'dp'), pairs)  11.6 us
    ppermute x3, waiting for transfers between devices, to_dp(): return lax.ppermute(x, 'dp', [(i, i ^ k) for i in range(n_dp)])  11.4 us
    dot_general x8, matrix products, delta_of(): lax.dot_general(embeds, piece, (((1,), (1,)), ((), ())), preferred_elemen...  6.97 us
    ppermute x16, waiting for transfers between devices, to_label(): lax.ppermute(x, 'label', [(i, (i + by) % n_label) for i in range(parity,...  6.23 us
    ppermute x2, waiting for transfers between devices, to_group(): return lax.ppermute(x, 'groups', [(i, i ^ 1) for i in range(n_groups)])  4.66 us
    dot_general x8, matrix products, score(): lax.dot_general(delta, embeds, (((0,), (0,)), ((), ())), preferred_elemen...  3.04 us
  transfers between devices with their start and end apart: 27, of which 12 were waited for; matrix products, arithmetic and copies ran while one was open for 12% of the time, Pallas kernels for 0%

profile of v3, /device:TPU:9, one launch (start us, length us, event | category | flops | bytes accessed | tf_op | source)
XLA Modules:
  0.0 114.8 jit_solution(6395215961244438526)
XLA Ops:
  0.6 1.4 %collective-permute-start = (bf16[128,1024]{1,0:T(8,128)(2,1)}, bf16[128,1024]{1,0:T(8,128)(2,1)S(1)}, u32[]{:S(2)}, u32[]{:S(2)}) collective-permute-start(bf16[128,1024]{1,0:T(8,128)(2,1)} %param.5), channel_id=1, source_target_pairs={{0,4},{8,12},{1,5},{9,13},{2,6},{10,14},{3,7},{11,15},{16,20},{24,... | collective-permute-start | bytes 786440 | tf_op jit(solution)/shard_map/ppermute | solution.py:46
  2.1 4.2 %collective-permute-start.3 = (bf16[128,1024]{1,0:T(8,128)(2,1)}, bf16[128,1024]{1,0:T(8,128)(2,1)S(1)}, u32[]{:S(2)}, u32[]{:S(2)}) collective-permute-start(bf16[128,1024]{1,0:T(8,128)(2,1)} %param.5), channel_id=1, source_target_pairs={{4,8},{12,0},{5,9},{13,1},{6,10},{14,2},{7,11},{15,3},{20,24},{28,... | collective-permute-start | bytes 786440 | tf_op jit(solution)/shard_map/ppermute | solution.py:46
  6.2 0.2 collective-permute-start.2
  6.5 0.7 fusion.56
  7.2 0.1 dynamic-slice_reduce_fusion
  7.3 0.8 constant_dynamic-update-slice_fusion.15
  8.1 1.4 %constant_dynamic-update-slice_fusion.7 = (bf16[768,1024]{0,1:T(8,128)(2,1)}, bf16[768,128]{0,1:T(8,128)(2,1)S(1)}) fusion(s32[128]{0:T(128)S(1)} %iota_add_fusion.7, s32[768]{0:T(1024)S(1)} %get-tuple-element.95, bf16[128,1024]{1,0:T(8,128)(2,1)S(1)} %get-tuple-element.46, bf16[768,1024]{1,0:T(8,128)(2,1)S(1)} %copy-done), kind=kOutput, calls=%fused_computation.99 | convolution fusion | flops 202014720 | bytes 2231808 | tf_op jit(solution)/shard_map/dot_general | solution.py:53
  9.5 0.4 fusion
  9.9 0.6 copy-done.1
  10.5 0.7 fusion.54
  11.2 0.4 fusion.1
  11.6 1.7 %collective-permute-done.2 = bf16[128,1024]{1,0:T(8,128)(2,1)S(1)} collective-permute-done((bf16[128,1024]{1,0:T(8,128)(2,1)}, bf16[128,1024]{1,0:T(8,128)(2,1)S(1)}, u32[]{:S(2)}, u32[]{:S(2)}) %collective-permute-start.2) | collective-permute-done | bytes 262176 | tf_op jit(solution)/shard_map/ppermute | solution.py:33
  13.3 1.3 %collective-permute-start.5 = (bf16[128,1024]{1,0:T(8,128)(2,1)S(1)}, bf16[128,1024]{1,0:T(8,128)(2,1)S(1)}, u32[]{:S(2)}, u32[]{:S(2)}) collective-permute-start(bf16[128,1024]{1,0:T(8,128)(2,1)S(1)} %collective-permute-done.2), channel_id=1, source_target_pairs={{0,4},{8,12},{1,5},{9,13},{2,6},{10,14},{3,7},{11,15},{16,20},{24,... | collective-permute-start | bytes 786440 | tf_op jit(solution)/shard_map/ppermute | solution.py:46
  14.6 2.1 %collective-permute-done.5 = bf16[128,1024]{1,0:T(8,128)(2,1)S(1)} collective-permute-done((bf16[128,1024]{1,0:T(8,128)(2,1)S(1)}, bf16[128,1024]{1,0:T(8,128)(2,1)S(1)}, u32[]{:S(2)}, u32[]{:S(2)}) %collective-permute-start.5) | collective-permute-done | bytes 262176 | tf_op jit(solution)/shard_map/ppermute | solution.py:46
  16.7 0.8 constant_dynamic-update-slice_fusion.14
  17.5 1.4 %constant_dynamic-update-slice_fusion.6 = (bf16[768,1024]{0,1:T(8,128)(2,1)}, bf16[768,128]{0,1:T(8,128)(2,1)S(1)}) fusion(bf16[768,1024]{0,1:T(8,128)(2,1)} %get-tuple-element.108, s32[128]{0:T(128)S(1)} %iota_add_fusion.5, s32[768]{0:T(1024)S(1)} %get-tuple-element.93, bf16[128,1024]{1,0:T(8,128)(2,1)S(1)} %get-tuple-element.50, ...), kind=kOutput, calls=%fused_computation.98 | convolution fusion | flops 202014720 | bytes 2231808 | tf_op jit(solution)/shard_map/dot_general | solution.py:53
  18.9 0.4 fusion.2
  19.2 2.7 %collective-permute-start.6 = (bf16[128,1024]{1,0:T(8,128)(2,1)S(1)}, bf16[128,1024]{1,0:T(8,128)(2,1)}, u32[]{:S(2)}, u32[]{:S(2)}) collective-permute-start(bf16[128,1024]{1,0:T(8,128)(2,1)S(1)} %fusion.2), channel_id=1, source_target_pairs={{4,0},{12,8},{5,1},{13,9},{6,2},{14,10},{7,3},{15,11},{20,16},{28,... | collective-permute-start | bytes 786440 | tf_op jit(solution)/shard_map/ppermute | solution.py:46
  22.0 0.7 constant_dynamic-slice_fusion
  22.7 2.3 %collective-permute-start.8 = (bf16[64,1024]{1,0:T(8,128)(2,1)}, bf16[64,1024]{1,0:T(8,128)(2,1)S(1)}, u32[]{:S(2)}, u32[]{:S(2)}) collective-permute-start(bf16[64,1024]{1,0:T(8,128)(2,1)} %constant_dynamic-slice_fusion), channel_id=1, source_target_pairs={{0,2},{1,3},{2,0},{3,1},{4,6},{5,7},{6,4},{7,5},{8,10},{9,11},{10,... | collective-permute-start | bytes 393224 | tf_op jit(solution)/shard_map/ppermute | solution.py:33
  25.0 2.7 %collective-permute-start.4 = (bf16[128,1024]{1,0:T(8,128)(2,1)S(1)}, bf16[128,1024]{1,0:T(8,128)(2,1)}, u32[]{:S(2)}, u32[]{:S(2)}) collective-permute-start(bf16[128,1024]{1,0:T(8,128)(2,1)S(1)} %collective-permute-done.2), channel_id=1, source_target_pairs={{4,8},{12,0},{5,9},{13,1},{6,10},{14,2},{7,11},{15,3},{20,24},{28,... | collective-permute-start | bytes 786440 | tf_op jit(solution)/shard_map/ppermute | solution.py:46
  27.6 2.8 %collective-permute-done.8 = bf16[64,1024]{1,0:T(8,128)(2,1)S(1)} collective-permute-done((bf16[64,1024]{1,0:T(8,128)(2,1)}, bf16[64,1024]{1,0:T(8,128)(2,1)S(1)}, u32[]{:S(2)}, u32[]{:S(2)}) %collective-permute-start.8) | collective-permute-done | bytes 131104 | tf_op jit(solution)/shard_map/ppermute | solution.py:33
  30.5 1.2 %collective-permute-start.9 = (bf16[64,1024]{1,0:T(8,128)(2,1)S(1)}, bf16[64,1024]{1,0:T(8,128)(2,1)S(1)}, u32[]{:S(2)}, u32[]{:S(2)}) collective-permute-start(bf16[64,1024]{1,0:T(8,128)(2,1)S(1)} %collective-permute-done.8), channel_id=1, source_target_pairs={{0,16},{16,0},{1,17},{17,1},{2,18},{18,2},{3,19},{19,3},{4,20},{20... | collective-permute-start | bytes 393224 | tf_op jit(solution)/shard_map/ppermute | solution.py:43
  31.7 1.0 add_convert_fusion.8
  32.8 0.7 fusion.52
  33.5 0.4 fusion.3
  33.9 1.4 %collective-permute-done.9 = bf16[64,1024]{1,0:T(8,128)(2,1)S(1)} collective-permute-done((bf16[64,1024]{1,0:T(8,128)(2,1)S(1)}, bf16[64,1024]{1,0:T(8,128)(2,1)S(1)}, u32[]{:S(2)}, u32[]{:S(2)}) %collective-permute-start.9) | collective-permute-done | bytes 131104 | tf_op jit(solution)/shard_map/ppermute | solution.py:43
  35.4 1.3 %collective-permute-start.10 = (bf16[128,1024]{1,0:T(8,128)(2,1)S(1)}, bf16[128,1024]{1,0:T(8,128)(2,1)S(1)}, u32[]{:S(2)}, u32[]{:S(2)}) collective-permute-start(bf16[128,1024]{1,0:T(8,128)(2,1)S(1)} %maximum_select_fusion), channel_id=1, source_target_pairs={{0,4},{8,12},{1,5},{9,13},{2,6},{10,14},{3,7},{11,15},{16,20},{24,... | collective-permute-start | bytes 786440 | tf_op jit(solution)/shard_map/ppermute | solution.py:46
  36.7 2.1 %collective-permute-done.10 = bf16[128,1024]{1,0:T(8,128)(2,1)S(1)} collective-permute-done((bf16[128,1024]{1,0:T(8,128)(2,1)S(1)}, bf16[128,1024]{1,0:T(8,128)(2,1)S(1)}, u32[]{:S(2)}, u32[]{:S(2)}) %collective-permute-start.10) | collective-permute-done | bytes 262176 | tf_op jit(solution)/shard_map/ppermute | solution.py:46
  38.9 0.7 constant_dynamic-update-slice_fusion.5
  39.6 0.4 fusion.4
  40.0 2.1 %collective-permute-start.11 = (bf16[128,1024]{1,0:T(8,128)(2,1)S(1)}, bf16[128,1024]{1,0:T(8,128)(2,1)S(1)}, u32[]{:S(2)}, u32[]{:S(2)}) collective-permute-start(bf16[128,1024]{1,0:T(8,128)(2,1)S(1)} %fusion.4), channel_id=1, source_target_pairs={{4,0},{12,8},{5,1},{13,9},{6,2},{14,10},{7,3},{15,11},{20,16},{28,... | collective-permute-start | bytes 786440 | tf_op jit(solution)/shard_map/ppermute | solution.py:46
  42.0 0.1 collective-permute-start.1
  42.1 1.3 %collective-permute-start.12 = (bf16[128,1024]{1,0:T(8,128)(2,1)S(1)}, bf16[128,1024]{1,0:T(8,128)(2,1)S(1)}, u32[]{:S(2)}, u32[]{:S(2)}) collective-permute-start(bf16[128,1024]{1,0:T(8,128)(2,1)S(1)} %fusion.3), channel_id=1, source_target_pairs={{0,12},{8,4},{1,13},{9,5},{2,14},{10,6},{3,15},{11,7},{16,28},{24,... | collective-permute-start | bytes 786440 | tf_op jit(solution)/shard_map/ppermute | solution.py:46
  43.4 6.9 %collective-permute-done.1 = bf16[64,1024]{1,0:T(8,128)(2,1)S(1)} collective-permute-done((bf16[64,1024]{1,0:T(8,128)(2,1)}, bf16[64,1024]{1,0:T(8,128)(2,1)S(1)}, u32[]{:S(2)}, u32[]{:S(2)}) %collective-permute-start.1) | collective-permute-done | bytes 131104 | tf_op jit(solution)/shard_map/ppermute | solution.py:33
  50.3 1.2 %collective-permute-start.7 = (bf16[64,1024]{1,0:T(8,128)(2,1)S(1)}, bf16[64,1024]{1,0:T(8,128)(2,1)S(1)}, u32[]{:S(2)}, u32[]{:S(2)}) collective-permute-start(bf16[64,1024]{1,0:T(8,128)(2,1)S(1)} %collective-permute-done.1), channel_id=1, source_target_pairs={{0,16},{16,0},{1,17},{17,1},{2,18},{18,2},{3,19},{19,3},{4,20},{20... | collective-permute-start | bytes 393224 | tf_op jit(solution)/shard_map/ppermute | solution.py:43
  51.7 3.3 %collective-permute-done.7 = bf16[64,1024]{1,0:T(8,128)(2,1)S(1)} collective-permute-done((bf16[64,1024]{1,0:T(8,128)(2,1)S(1)}, bf16[64,1024]{1,0:T(8,128)(2,1)S(1)}, u32[]{:S(2)}, u32[]{:S(2)}) %collective-permute-start.7) | collective-permute-done | bytes 131104 | tf_op jit(solution)/shard_map/ppermute | solution.py:43
  55.0 1.3 %collective-permute-start.15 = (bf16[128,1024]{1,0:T(8,128)(2,1)S(1)}, bf16[128,1024]{1,0:T(8,128)(2,1)S(1)}, u32[]{:S(2)}, u32[]{:S(2)}) collective-permute-start(bf16[128,1024]{1,0:T(8,128)(2,1)S(1)} %maximum_select_fusion.1), channel_id=1, source_target_pairs={{0,4},{8,12},{1,5},{9,13},{2,6},{10,14},{3,7},{11,15},{16,20},{24,... | collective-permute-start | bytes 786440 | tf_op jit(solution)/shard_map/ppermute | solution.py:46
  56.4 3.2 %collective-permute-start.19 = (bf16[128,1024]{1,0:T(8,128)(2,1)S(1)}, bf16[128,1024]{1,0:T(8,128)(2,1)S(1)}, u32[]{:S(2)}, u32[]{:S(2)}) collective-permute-start(bf16[128,1024]{1,0:T(8,128)(2,1)S(1)} %fusion), channel_id=1, source_target_pairs={{4,0},{12,8},{5,1},{13,9},{6,2},{14,10},{7,3},{15,11},{20,16},{28,... | collective-permute-start | bytes 786440 | tf_op jit(solution)/shard_map/ppermute | solution.py:46
  59.5 1.3 %collective-permute-start.20 = (bf16[128,1024]{1,0:T(8,128)(2,1)S(1)}, bf16[128,1024]{1,0:T(8,128)(2,1)S(1)}, u32[]{:S(2)}, u32[]{:S(2)}) collective-permute-start(bf16[128,1024]{1,0:T(8,128)(2,1)S(1)} %fusion.1), channel_id=1, source_target_pairs={{0,12},{8,4},{1,13},{9,5},{2,14},{10,6},{3,15},{11,7},{16,28},{24,... | collective-permute-start | bytes 786440 | tf_op jit(solution)/shard_map/ppermute | solution.py:46
  60.8 4.3 %collective-permute-start.14 = (bf16[128,1024]{1,0:T(8,128)(2,1)S(1)}, bf16[128,1024]{1,0:T(8,128)(2,1)S(1)}, u32[]{:S(2)}, u32[]{:S(2)}) collective-permute-start(bf16[128,1024]{1,0:T(8,128)(2,1)S(1)} %maximum_select_fusion), channel_id=1, source_target_pairs={{4,8},{12,0},{5,9},{13,1},{6,10},{14,2},{7,11},{15,3},{20,24},{28,... | collective-permute-start | bytes 786440 | tf_op jit(solution)/shard_map/ppermute | solution.py:46
  65.1 0.7 collective-permute-start.21
  65.9 0.7 constant_dynamic-update-slice_fusion.4
  66.6 0.4 fusion.5
  67.0 2.8 %collective-permute-start.16 = (bf16[128,1024]{1,0:T(8,128)(2,1)S(1)}, bf16[128,1024]{1,0:T(8,128)(2,1)S(1)}, u32[]{:S(2)}, u32[]{:S(2)}) collective-permute-start(bf16[128,1024]{1,0:T(8,128)(2,1)S(1)} %fusion.5), channel_id=1, source_target_pairs={{4,0},{12,8},{5,1},{13,9},{6,2},{14,10},{7,3},{15,11},{20,16},{28,... | collective-permute-start | bytes 786440 | tf_op jit(solution)/shard_map/ppermute | solution.py:46
  70.0 1.0 collective-permute-done.16
  71.0 2.3 %collective-permute-start.13 = (bf16[128,1024]{1,0:T(8,128)(2,1)S(1)}, bf16[128,1024]{1,0:T(8,128)(2,1)S(1)}, u32[]{:S(2)}, u32[]{:S(2)}) collective-permute-start(bf16[128,1024]{1,0:T(8,128)(2,1)S(1)} %maximum_select_fusion.1), channel_id=1, source_target_pairs={{4,8},{12,0},{5,9},{13,1},{6,10},{14,2},{7,11},{15,3},{20,24},{28,... | collective-permute-start | bytes 786440 | tf_op jit(solution)/shard_map/ppermute | solution.py:46
  73.5 0.7 constant_dynamic-update-slice_fusion.1
  74.2 0.4 fusion.6
  74.6 1.3 %collective-permute-start.17 = (bf16[128,1024]{1,0:T(8,128)(2,1)S(1)}, bf16[128,1024]{1,0:T(8,128)(2,1)S(1)}, u32[]{:S(2)}, u32[]{:S(2)}) collective-permute-start(bf16[128,1024]{1,0:T(8,128)(2,1)S(1)} %fusion.6), channel_id=1, source_target_pairs={{0,12},{8,4},{1,13},{9,5},{2,14},{10,6},{3,15},{11,7},{16,28},{24,... | collective-permute-start | bytes 786440 | tf_op jit(solution)/shard_map/ppermute | solution.py:46
  75.9 0.7 collective-permute-done.13
  76.7 0.7 constant_dynamic-update-slice_fusion
  77.4 0.4 fusion.7
  77.8 1.3 %collective-permute-start.18 = (bf16[128,1024]{1,0:T(8,128)(2,1)S(1)}, bf16[128,1024]{1,0:T(8,128)(2,1)S(1)}, u32[]{:S(2)}, u32[]{:S(2)}) collective-permute-start(bf16[128,1024]{1,0:T(8,128)(2,1)S(1)} %fusion.7), channel_id=1, source_target_pairs={{0,12},{8,4},{1,13},{9,5},{2,14},{10,6},{3,15},{11,7},{16,28},{24,... | collective-permute-start | bytes 786440 | tf_op jit(solution)/shard_map/ppermute | solution.py:46
  79.1 3.0 %convolution_convert_fusion = bf16[768,1024]{1,0:T(8,128)(2,1)} fusion(bf16[768,1024]{0,1:T(8,128)(2,1)S(1)} %get-tuple-element.73, bf16[1024,1024]{1,0:T(8,128)(2,1)S(1)} %get-tuple-element.96), kind=kOutput, calls=%fused_computation | convolution fusion | flops 1611399168 | bytes 5242880 | tf_op jit(solution)/shard_map/dot_general | solution.py:138
  82.1 0.2 collective-permute-done.17
  82.3 3.3 %collective-permute-start.22 = (bf16[128,1024]{1,0:T(8,128)(2,1)S(1)}, bf16[128,1024]{1,0:T(8,128)(2,1)S(1)}, u32[]{:S(2)}, u32[]{:S(2)}) collective-permute-start(bf16[128,1024]{1,0:T(8,128)(2,1)S(1)} %add_convert_fusion.6), channel_id=1, source_target_pairs={{4,5},{5,4},{6,7},{7,6},{12,13},{13,12},{14,15},{15,14},{20,21},{2... | collective-permute-start | bytes 786440 | tf_op jit(solution)/shard_map/ppermute | solution.py:40
  85.6 0.7 collective-permute-start.23
  86.4 0.7 collective-permute-start.25
  87.1 3.7 %collective-permute-start.24 = (bf16[128,1024]{1,0:T(8,128)(2,1)S(1)}, bf16[128,1024]{1,0:T(8,128)(2,1)S(1)}, u32[]{:S(2)}, u32[]{:S(2)}) collective-permute-start(bf16[128,1024]{1,0:T(8,128)(2,1)S(1)} %add_convert_fusion.4), channel_id=1, source_target_pairs={{4,6},{5,7},{6,4},{7,5},{12,14},{13,15},{14,12},{15,13},{20,22},{2... | collective-permute-start | bytes 786440 | tf_op jit(solution)/shard_map/ppermute | solution.py:40
  90.9 2.6 %collective-permute-start.26 = (bf16[128,1024]{1,0:T(8,128)(2,1)S(1)}, bf16[128,1024]{1,0:T(8,128)(2,1)S(1)}, u32[]{:S(2)}, u32[]{:S(2)}) collective-permute-start(bf16[128,1024]{1,0:T(8,128)(2,1)S(1)} %add_convert_fusion.3), channel_id=1, source_target_pairs={{4,7},{5,6},{6,5},{7,4},{12,15},{13,14},{14,13},{15,12},{20,23},{2... | collective-permute-start | bytes 786440 | tf_op jit(solution)/shard_map/ppermute | solution.py:40
  93.6 14.5 %collective-permute-done.24 = bf16[128,1024]{1,0:T(8,128)(2,1)S(1)} collective-permute-done((bf16[128,1024]{1,0:T(8,128)(2,1)S(1)}, bf16[128,1024]{1,0:T(8,128)(2,1)S(1)}, u32[]{:S(2)}, u32[]{:S(2)}) %collective-permute-start.24) | collective-permute-done | bytes 262176 | tf_op jit(solution)/shard_map/ppermute | solution.py:40
  108.1 5.7 %collective-permute-done.26 = bf16[128,1024]{1,0:T(8,128)(2,1)S(1)} collective-permute-done((bf16[128,1024]{1,0:T(8,128)(2,1)S(1)}, bf16[128,1024]{1,0:T(8,128)(2,1)S(1)}, u32[]{:S(2)}, u32[]{:S(2)}) %collective-permute-start.26) | collective-permute-done | bytes 262176 | tf_op jit(solution)/shard_map/ppermute | solution.py:40
  113.8 1.0 add_convert_fusion
  (49 shorter events, 1.1 us)
Async XLA Ops:
  0.6 7.5 %copy-start = (bf16[768,1024]{1,0:T(8,128)(2,1)S(1)}, bf16[768,1024]{1,0:T(8,128)(2,1)}, u32[]{:S(2)}) copy-start(bf16[768,1024]{1,0:T(8,128)(2,1)} %param.4) | copy-start | bytes 4718596
  0.6 6.7 %collective-permute-start = (bf16[128,1024]{1,0:T(8,128)(2,1)}, bf16[128,1024]{1,0:T(8,128)(2,1)S(1)}, u32[]{:S(2)}, u32[]{:S(2)}) collective-permute-start(bf16[128,1024]{1,0:T(8,128)(2,1)} %param.5), channel_id=1, source_target_pairs={{0,4},{8,12},{1,5},{9,13},{2,6},{10,14},{3,7},{11,15},{16,20},{24,... | collective-permute-start | bytes 786440 | tf_op jit(solution)/shard_map/ppermute | solution.py:46
  2.1 7.8 %collective-permute-start.3 = (bf16[128,1024]{1,0:T(8,128)(2,1)}, bf16[128,1024]{1,0:T(8,128)(2,1)S(1)}, u32[]{:S(2)}, u32[]{:S(2)}) collective-permute-start(bf16[128,1024]{1,0:T(8,128)(2,1)} %param.5), channel_id=1, source_target_pairs={{4,8},{12,0},{5,9},{13,1},{6,10},{14,2},{7,11},{15,3},{20,24},{28,... | collective-permute-start | bytes 786440 | tf_op jit(solution)/shard_map/ppermute | solution.py:46
  6.2 7.0 %collective-permute-start.2 = (bf16[128,1024]{1,0:T(8,128)(2,1)}, bf16[128,1024]{1,0:T(8,128)(2,1)S(1)}, u32[]{:S(2)}, u32[]{:S(2)}) collective-permute-start(bf16[128,1024]{1,0:T(8,128)(2,1)} %param.5), channel_id=1, source_target_pairs={{0,1},{1,0},{2,3},{3,2},{4,5},{5,4},{6,7},{7,6},{8,9},{9,8},{10,11... | collective-permute-start | bytes 786440 | tf_op jit(solution)/shard_map/ppermute | solution.py:33
  9.5 0.9 copy-start.1
  13.3 3.4 %collective-permute-start.5 = (bf16[128,1024]{1,0:T(8,128)(2,1)S(1)}, bf16[128,1024]{1,0:T(8,128)(2,1)S(1)}, u32[]{:S(2)}, u32[]{:S(2)}) collective-permute-start(bf16[128,1024]{1,0:T(8,128)(2,1)S(1)} %collective-permute-done.2), channel_id=1, source_target_pairs={{0,4},{8,12},{1,5},{9,13},{2,6},{10,14},{3,7},{11,15},{16,20},{24,... | collective-permute-start | bytes 786440 | tf_op jit(solution)/shard_map/ppermute | solution.py:46
  19.2 12.5 %collective-permute-start.6 = (bf16[128,1024]{1,0:T(8,128)(2,1)S(1)}, bf16[128,1024]{1,0:T(8,128)(2,1)}, u32[]{:S(2)}, u32[]{:S(2)}) collective-permute-start(bf16[128,1024]{1,0:T(8,128)(2,1)S(1)} %fusion.2), channel_id=1, source_target_pairs={{4,0},{12,8},{5,1},{13,9},{6,2},{14,10},{7,3},{15,11},{20,16},{28,... | collective-permute-start | bytes 786440 | tf_op jit(solution)/shard_map/ppermute | solution.py:46
  22.7 7.8 %collective-permute-start.8 = (bf16[64,1024]{1,0:T(8,128)(2,1)}, bf16[64,1024]{1,0:T(8,128)(2,1)S(1)}, u32[]{:S(2)}, u32[]{:S(2)}) collective-permute-start(bf16[64,1024]{1,0:T(8,128)(2,1)} %constant_dynamic-slice_fusion), channel_id=1, source_target_pairs={{0,2},{1,3},{2,0},{3,1},{4,6},{5,7},{6,4},{7,5},{8,10},{9,11},{10,... | collective-permute-start | bytes 393224 | tf_op jit(solution)/shard_map/ppermute | solution.py:33
  25.0 7.8 %collective-permute-start.4 = (bf16[128,1024]{1,0:T(8,128)(2,1)S(1)}, bf16[128,1024]{1,0:T(8,128)(2,1)}, u32[]{:S(2)}, u32[]{:S(2)}) collective-permute-start(bf16[128,1024]{1,0:T(8,128)(2,1)S(1)} %collective-permute-done.2), channel_id=1, source_target_pairs={{4,8},{12,0},{5,9},{13,1},{6,10},{14,2},{7,11},{15,3},{20,24},{28,... | collective-permute-start | bytes 786440 | tf_op jit(solution)/shard_map/ppermute | solution.py:46
  30.5 4.8 %collective-permute-start.9 = (bf16[64,1024]{1,0:T(8,128)(2,1)S(1)}, bf16[64,1024]{1,0:T(8,128)(2,1)S(1)}, u32[]{:S(2)}, u32[]{:S(2)}) collective-permute-start(bf16[64,1024]{1,0:T(8,128)(2,1)S(1)} %collective-permute-done.8), channel_id=1, source_target_pairs={{0,16},{16,0},{1,17},{17,1},{2,18},{18,2},{3,19},{19,3},{4,20},{20... | collective-permute-start | bytes 393224 | tf_op jit(solution)/shard_map/ppermute | solution.py:43
  32.8 6.1 %copy-start.3 = (bf16[768,1024]{0,1:T(8,128)(2,1)S(1)}, bf16[768,1024]{0,1:T(8,128)(2,1)}, u32[]{:S(2)}) copy-start(bf16[768,1024]{0,1:T(8,128)(2,1)} %get-tuple-element.110) | copy-start | bytes 4718596
  33.5 5.3 %copy-start.2 = (bf16[1024,1024]{1,0:T(8,128)(2,1)S(1)}, bf16[1024,1024]{1,0:T(8,128)(2,1)}, u32[]{:S(2)}) copy-start(bf16[1024,1024]{1,0:T(8,128)(2,1)} %get-tuple-element.104) | copy-start | bytes 6291460
  35.4 3.4 %collective-permute-start.10 = (bf16[128,1024]{1,0:T(8,128)(2,1)S(1)}, bf16[128,1024]{1,0:T(8,128)(2,1)S(1)}, u32[]{:S(2)}, u32[]{:S(2)}) collective-permute-start(bf16[128,1024]{1,0:T(8,128)(2,1)S(1)} %maximum_select_fusion), channel_id=1, source_target_pairs={{0,4},{8,12},{1,5},{9,13},{2,6},{10,14},{3,7},{11,15},{16,20},{24,... | collective-permute-start | bytes 786440 | tf_op jit(solution)/shard_map/ppermute | solution.py:46
  40.0 11.6 %collective-permute-start.11 = (bf16[128,1024]{1,0:T(8,128)(2,1)S(1)}, bf16[128,1024]{1,0:T(8,128)(2,1)S(1)}, u32[]{:S(2)}, u32[]{:S(2)}) collective-permute-start(bf16[128,1024]{1,0:T(8,128)(2,1)S(1)} %fusion.4), channel_id=1, source_target_pairs={{4,0},{12,8},{5,1},{13,9},{6,2},{14,10},{7,3},{15,11},{20,16},{28,... | collective-permute-start | bytes 786440 | tf_op jit(solution)/shard_map/ppermute | solution.py:46
  42.0 8.3 %collective-permute-start.1 = (bf16[64,1024]{1,0:T(8,128)(2,1)}, bf16[64,1024]{1,0:T(8,128)(2,1)S(1)}, u32[]{:S(2)}, u32[]{:S(2)}) collective-permute-start(bf16[64,1024]{1,0:T(8,128)(2,1)} %constant_dynamic-slice_fusion), channel_id=1, source_target_pairs={{0,3},{1,2},{2,1},{3,0},{4,7},{5,6},{6,5},{7,4},{8,11},{9,10},{10,... | collective-permute-start | bytes 393224 | tf_op jit(solution)/shard_map/ppermute | solution.py:33
  42.1 9.5 %collective-permute-start.12 = (bf16[128,1024]{1,0:T(8,128)(2,1)S(1)}, bf16[128,1024]{1,0:T(8,128)(2,1)S(1)}, u32[]{:S(2)}, u32[]{:S(2)}) collective-permute-start(bf16[128,1024]{1,0:T(8,128)(2,1)S(1)} %fusion.3), channel_id=1, source_target_pairs={{0,12},{8,4},{1,13},{9,5},{2,14},{10,6},{3,15},{11,7},{16,28},{24,... | collective-permute-start | bytes 786440 | tf_op jit(solution)/shard_map/ppermute | solution.py:46
  50.3 4.7 %collective-permute-start.7 = (bf16[64,1024]{1,0:T(8,128)(2,1)S(1)}, bf16[64,1024]{1,0:T(8,128)(2,1)S(1)}, u32[]{:S(2)}, u32[]{:S(2)}) collective-permute-start(bf16[64,1024]{1,0:T(8,128)(2,1)S(1)} %collective-permute-done.1), channel_id=1, source_target_pairs={{0,16},{16,0},{1,17},{17,1},{2,18},{18,2},{3,19},{19,3},{4,20},{20... | collective-permute-start | bytes 393224 | tf_op jit(solution)/shard_map/ppermute | solution.py:43
  55.0 10.8 %collective-permute-start.15 = (bf16[128,1024]{1,0:T(8,128)(2,1)S(1)}, bf16[128,1024]{1,0:T(8,128)(2,1)S(1)}, u32[]{:S(2)}, u32[]{:S(2)}) collective-permute-start(bf16[128,1024]{1,0:T(8,128)(2,1)S(1)} %maximum_select_fusion.1), channel_id=1, source_target_pairs={{0,4},{8,12},{1,5},{9,13},{2,6},{10,14},{3,7},{11,15},{16,20},{24,... | collective-permute-start | bytes 786440 | tf_op jit(solution)/shard_map/ppermute | solution.py:46
  56.4 30.0 %collective-permute-start.19 = (bf16[128,1024]{1,0:T(8,128)(2,1)S(1)}, bf16[128,1024]{1,0:T(8,128)(2,1)S(1)}, u32[]{:S(2)}, u32[]{:S(2)}) collective-permute-start(bf16[128,1024]{1,0:T(8,128)(2,1)S(1)} %fusion), channel_id=1, source_target_pairs={{4,0},{12,8},{5,1},{13,9},{6,2},{14,10},{7,3},{15,11},{20,16},{28,... | collective-permute-start | bytes 786440 | tf_op jit(solution)/shard_map/ppermute | solution.py:46
  59.5 27.6 %collective-permute-start.20 = (bf16[128,1024]{1,0:T(8,128)(2,1)S(1)}, bf16[128,1024]{1,0:T(8,128)(2,1)S(1)}, u32[]{:S(2)}, u32[]{:S(2)}) collective-permute-start(bf16[128,1024]{1,0:T(8,128)(2,1)S(1)} %fusion.1), channel_id=1, source_target_pairs={{0,12},{8,4},{1,13},{9,5},{2,14},{10,6},{3,15},{11,7},{16,28},{24,... | collective-permute-start | bytes 786440 | tf_op jit(solution)/shard_map/ppermute | solution.py:46
  60.8 12.6 %collective-permute-start.14 = (bf16[128,1024]{1,0:T(8,128)(2,1)S(1)}, bf16[128,1024]{1,0:T(8,128)(2,1)S(1)}, u32[]{:S(2)}, u32[]{:S(2)}) collective-permute-start(bf16[128,1024]{1,0:T(8,128)(2,1)S(1)} %maximum_select_fusion), channel_id=1, source_target_pairs={{4,8},{12,0},{5,9},{13,1},{6,10},{14,2},{7,11},{15,3},{20,24},{28,... | collective-permute-start | bytes 786440 | tf_op jit(solution)/shard_map/ppermute | solution.py:46
  65.1 28.5 %collective-permute-start.21 = (bf16[128,1024]{1,0:T(8,128)(2,1)S(1)}, bf16[128,1024]{1,0:T(8,128)(2,1)S(1)}, u32[]{:S(2)}, u32[]{:S(2)}) collective-permute-start(bf16[128,1024]{1,0:T(8,128)(2,1)S(1)} %add_convert_fusion.8), channel_id=1, source_target_pairs={{0,1},{1,0},{2,3},{3,2},{8,9},{9,8},{10,11},{11,10},{16,17},{17,16... | collective-permute-start | bytes 786440 | tf_op jit(solution)/shard_map/ppermute | solution.py:40
  67.0 4.0 %collective-permute-start.16 = (bf16[128,1024]{1,0:T(8,128)(2,1)S(1)}, bf16[128,1024]{1,0:T(8,128)(2,1)S(1)}, u32[]{:S(2)}, u32[]{:S(2)}) collective-permute-start(bf16[128,1024]{1,0:T(8,128)(2,1)S(1)} %fusion.5), channel_id=1, source_target_pairs={{4,0},{12,8},{5,1},{13,9},{6,2},{14,10},{7,3},{15,11},{20,16},{28,... | collective-permute-start | bytes 786440 | tf_op jit(solution)/shard_map/ppermute | solution.py:46
  71.0 5.6 %collective-permute-start.13 = (bf16[128,1024]{1,0:T(8,128)(2,1)S(1)}, bf16[128,1024]{1,0:T(8,128)(2,1)S(1)}, u32[]{:S(2)}, u32[]{:S(2)}) collective-permute-start(bf16[128,1024]{1,0:T(8,128)(2,1)S(1)} %maximum_select_fusion.1), channel_id=1, source_target_pairs={{4,8},{12,0},{5,9},{13,1},{6,10},{14,2},{7,11},{15,3},{20,24},{28,... | collective-permute-start | bytes 786440 | tf_op jit(solution)/shard_map/ppermute | solution.py:46
  74.6 7.7 %collective-permute-start.17 = (bf16[128,1024]{1,0:T(8,128)(2,1)S(1)}, bf16[128,1024]{1,0:T(8,128)(2,1)S(1)}, u32[]{:S(2)}, u32[]{:S(2)}) collective-permute-start(bf16[128,1024]{1,0:T(8,128)(2,1)S(1)} %fusion.6), channel_id=1, source_target_pairs={{0,12},{8,4},{1,13},{9,5},{2,14},{10,6},{3,15},{11,7},{16,28},{24,... | collective-permute-start | bytes 786440 | tf_op jit(solution)/shard_map/ppermute | solution.py:46
  77.8 7.8 %collective-permute-start.18 = (bf16[128,1024]{1,0:T(8,128)(2,1)S(1)}, bf16[128,1024]{1,0:T(8,128)(2,1)S(1)}, u32[]{:S(2)}, u32[]{:S(2)}) collective-permute-start(bf16[128,1024]{1,0:T(8,128)(2,1)S(1)} %fusion.7), channel_id=1, source_target_pairs={{0,12},{8,4},{1,13},{9,5},{2,14},{10,6},{3,15},{11,7},{16,28},{24,... | collective-permute-start | bytes 786440 | tf_op jit(solution)/shard_map/ppermute | solution.py:46
  82.3 8.6 %collective-permute-start.22 = (bf16[128,1024]{1,0:T(8,128)(2,1)S(1)}, bf16[128,1024]{1,0:T(8,128)(2,1)S(1)}, u32[]{:S(2)}, u32[]{:S(2)}) collective-permute-start(bf16[128,1024]{1,0:T(8,128)(2,1)S(1)} %add_convert_fusion.6), channel_id=1, source_target_pairs={{4,5},{5,4},{6,7},{7,6},{12,13},{13,12},{14,15},{15,14},{20,21},{2... | collective-permute-start | bytes 786440 | tf_op jit(solution)/shard_map/ppermute | solution.py:40
  85.6 8.0 %collective-permute-start.23 = (bf16[128,1024]{1,0:T(8,128)(2,1)S(1)}, bf16[128,1024]{1,0:T(8,128)(2,1)S(1)}, u32[]{:S(2)}, u32[]{:S(2)}) collective-permute-start(bf16[128,1024]{1,0:T(8,128)(2,1)S(1)} %add_convert_fusion.7), channel_id=1, source_target_pairs={{0,2},{1,3},{2,0},{3,1},{8,10},{9,11},{10,8},{11,9},{16,18},{17,19... | collective-permute-start | bytes 786440 | tf_op jit(solution)/shard_map/ppermute | solution.py:40
  86.4 7.2 %collective-permute-start.25 = (bf16[128,1024]{1,0:T(8,128)(2,1)S(1)}, bf16[128,1024]{1,0:T(8,128)(2,1)S(1)}, u32[]{:S(2)}, u32[]{:S(2)}) collective-permute-start(bf16[128,1024]{1,0:T(8,128)(2,1)S(1)} %add_convert_fusion.5), channel_id=1, source_target_pairs={{0,3},{1,2},{2,1},{3,0},{8,11},{9,10},{10,9},{11,8},{16,19},{17,18... | collective-permute-start | bytes 786440 | tf_op jit(solution)/shard_map/ppermute | solution.py:40
  87.1 21.0 %collective-permute-start.24 = (bf16[128,1024]{1,0:T(8,128)(2,1)S(1)}, bf16[128,1024]{1,0:T(8,128)(2,1)S(1)}, u32[]{:S(2)}, u32[]{:S(2)}) collective-permute-start(bf16[128,1024]{1,0:T(8,128)(2,1)S(1)} %add_convert_fusion.4), channel_id=1, source_target_pairs={{4,6},{5,7},{6,4},{7,5},{12,14},{13,15},{14,12},{15,13},{20,22},{2... | collective-permute-start | bytes 786440 | tf_op jit(solution)/shard_map/ppermute | solution.py:40
  90.9 22.9 %collective-permute-start.26 = (bf16[128,1024]{1,0:T(8,128)(2,1)S(1)}, bf16[128,1024]{1,0:T(8,128)(2,1)S(1)}, u32[]{:S(2)}, u32[]{:S(2)}) collective-permute-start(bf16[128,1024]{1,0:T(8,128)(2,1)S(1)} %add_convert_fusion.3), channel_id=1, source_target_pairs={{4,7},{5,6},{6,5},{7,4},{12,15},{13,14},{14,13},{15,12},{20,23},{2... | collective-permute-start | bytes 786440 | tf_op jit(solution)/shard_map/ppermute | solution.py:40

commit v4 on v1

v4 whole, which is shorter than its diff:
```python
import math

import jax
import jax.numpy as jnp
from jax import lax
from jax.sharding import PartitionSpec as P


def local(embeds, weights, pos_ids, pos_count):
    n_label = lax.axis_size("label")
    n_dp = lax.axis_size("dp")
    me_label = lax.axis_index("label")
    me_dp = lax.axis_index("dp")
    rows_dev, width = embeds.shape
    ch_dev = weights.shape[0]
    stretch = ch_dev * n_dp
    slots = pos_ids.shape[1]
    span = stretch * n_label // slots
    scale = 1.0 / math.sqrt(rows_dev * n_dp)
    valid = jnp.arange(slots, dtype=jnp.int32)[None, :] < pos_count[:, None]
    ids = jnp.where(valid, pos_ids, -1)
    last = [embeds]

    def in_turn(x):
        x, _ = lax.optimization_barrier((x, last[0]))
        return x

    def to_dp(x, k):
        return lax.ppermute(x, "dp", [(i, i ^ k) for i in range(n_dp)])

    def to_label(x, by):
        return lax.ppermute(x, "label", [(i, (i + by) % n_label) for i in range(n_label)])

    def delta_of(rows, row_ids, piece, k):
        start = me_label * stretch + (me_dp ^ k) * ch_dev
        column = lax.dynamic_slice_in_dim(row_ids, start // span, 1, axis=1)
        labels = start + jnp.arange(ch_dev, dtype=jnp.int32)
        target = (column == labels[None, :]).astype(jnp.float32)
        logits = lax.dot_general(
            rows, piece, (((1,), (1,)), ((), ())), preferred_element_type=jnp.float32
        )
        return (jax.nn.sigmoid(logits) - target).astype(jnp.bfloat16)

    def grad_w_of(delta, rows):
        return lax.dot_general(
            delta, rows, (((0,), (0,)), ((), ())), preferred_element_type=jnp.float32
        )

    def grad_x_of(deltas):
        return jnp.dot(
            in_turn(jnp.concatenate([deltas[k] for k in range(n_dp)], axis=1)),
            jnp.concatenate([pieces[k] for k in range(n_dp)], axis=0),
            preferred_element_type=jnp.float32,
        )

    d_own, d_next, g_own, total, moved = {}, {}, {}, {}, {}
    pieces = {k: weights if k == 0 else to_dp(weights, k) for k in range(n_dp)}
    next_rows = to_label(embeds, -1)
    next_ids = to_label(ids, -1)

    def own_step(k):
        pieces[k] = in_turn(pieces[k])
        d_own[k] = delta_of(embeds, ids, pieces[k], k)
        g_own[k] = grad_w_of(d_own[k], embeds)
        last[0] = g_own[k]

    def next_step(k):
        d_next[k] = delta_of(next_rows, next_ids, in_turn(pieces[k]), k)
        total[k] = (g_own[k] + grad_w_of(d_next[k], next_rows)) * scale
        if k > 0:
            total[k] = total[k].astype(jnp.bfloat16)
            moved[k] = to_dp(total[k], k)
        last[0] = total[k]

    own_step(0)
    for k in range(1, n_dp - 1):
        own_step(k)
    for k in range(n_dp - 2, 0, -1):
        next_step(k)
    next_step(0)
    if n_dp > 1:
        own_step(n_dp - 1)
        next_step(n_dp - 1)
    theirs = grad_x_of(d_next).astype(jnp.bfloat16)
    last[0] = theirs
    back = to_label(theirs, 1)
    grad_x = grad_x_of(d_own)
    last[0] = grad_x
    grad_x = (grad_x + in_turn(back).astype(jnp.float32)).astype(jnp.bfloat16)
    last[0] = grad_x
    grad_w = total[0]
    for k in range(1, n_dp):
        grad_w = grad_w + in_turn(moved[k]).astype(jnp.float32)
    return (grad_w.astype(jnp.bfloat16), grad_x)


def solution(mesh):
    return jax.shard_map(
        local,
        mesh=mesh,
        in_specs=(
            P(("groups", "label", "dp"), None),
            P(("label", "dp"), None),
            P(("groups", "label", "dp"), None),
            P(("groups", "label", "dp")),
        ),
        out_specs=(P(("groups", "label", "dp"), None), P(("groups", "label", "dp"), None)),
        check_vma=False,
    )
```

time: 74.1 us -> 63.7 us (0.86)
  the two profiles are of different devices: /device:TPU:0 before, /device:TPU:9 now
where the time goes in v4:
time: 63.7 us; the launch traced here: 63.5 us
  waiting for transfers between devices  33.9 us (53%)
  matrix products  12.3 us (19%)
  starting transfers between devices  11.2 us (18%)
  other arithmetic  3.47 us (5%)
  local copies, waits for them, and re-layouts  1.67 us (3%)
  between operations  0.91 us (1%)
    ppermute x6, waiting for transfers between devices, to_dp(): return lax.ppermute(x, 'dp', [(i, i ^ k) for i in range(n_dp)])  20.6 us
    ppermute x3, waiting for transfers between devices, to_label(): lax.ppermute(x, 'label', [(i, (i + by) % n_label) for i in range(n_label)])  13.3 us
    dot_general x8, matrix products, delta_of(): lax.dot_general(rows, piece, (((1,), (1,)), ((), ())), preferred_element_...  7.21 us
    ppermute x6, starting transfers between devices, to_dp(): return lax.ppermute(x, 'dp', [(i, i ^ k) for i in range(n_dp)])  6.89 us
    ppermute x3, starting transfers between devices, to_label(): lax.ppermute(x, 'label', [(i, (i + by) % n_label) for i in range(n_label)])  4.33 us
    dot_general x8, matrix products, grad_w_of(): lax.dot_general(delta, rows, (((0,), (0,)), ((), ())), preferred_element_...  3.05 us
    dot_general x2, matrix products, grad_x_of(): jnp.dot(in_turn(jnp.concatenate([deltas[k] for k in range(n_dp)], axis=1)...  2.03 us
    convert_element_type x1, other arithmetic, local(): grad_x = (grad_x + in_turn(back).astype(jnp.float32)).astype(jnp.bfloat16)  1.75 us
  transfers between devices with their start and end apart: 9, of which 4 were waited for; matrix products, arithmetic and copies ran while one was open for 20% of the time, Pallas kernels for 0%

profile of v4, /device:TPU:9, one launch (start us, length us, event | category | flops | bytes accessed | tf_op | source)
XLA Modules:
  0.0 63.5 jit_solution(16780646129905343374)
XLA Ops:
  0.6 0.1 collective-permute-start
  0.7 2.6 %collective-permute-start.5 = (bf16[128,1024]{1,0:T(8,128)(2,1)}, bf16[128,1024]{1,0:T(8,128)(2,1)S(1)}, u32[]{:S(2)}, u32[]{:S(2)}) collective-permute-start(bf16[128,1024]{1,0:T(8,128)(2,1)} %param.5), channel_id=1, source_target_pairs={{0,3},{1,2},{2,1},{3,0},{4,7},{5,6},{6,5},{7,4},{8,11},{9,10},{10,... | collective-permute-start | bytes 786440 | tf_op jit(solution)/shard_map/ppermute | solution.py:29
  3.3 1.0 %collective-permute-start.1 = (bf16[128,1024]{1,0:T(8,128)(2,1)}, bf16[128,1024]{1,0:T(8,128)(2,1)S(1)}, u32[]{:S(2)}, u32[]{:S(2)}) collective-permute-start(bf16[128,1024]{1,0:T(8,128)(2,1)} %param.5), channel_id=1, source_target_pairs={{0,2},{1,3},{2,0},{3,1},{4,6},{5,7},{6,4},{7,5},{8,10},{9,11},{10,... | collective-permute-start | bytes 786440 | tf_op jit(solution)/shard_map/ppermute | solution.py:29
  4.2 0.7 %fusion.55 = s32[768,8]{0,1:T(8,128)S(1)} fusion(s32[768,8]{0,1:T(8,128)} %param.6, s32[768]{0:T(1024)} %param.7), kind=kLoop, calls=%fused_computation.73 | loop fusion | flops 12288 | bytes 52224 | tf_op jit(solution)/shard_map/jit(_where)/select_n | solution.py:21
  5.0 1.5 %collective-permute-start.3 = (s32[768,8]{0,1:T(8,128)S(1)}, s32[768,8]{0,1:T(8,128)S(1)}, u32[]{:S(2)}, u32[]{:S(2)}) collective-permute-start(s32[768,8]{0,1:T(8,128)S(1)} %fusion.55), channel_id=1, source_target_pairs={{0,12},{4,0},{8,4},{12,8},{1,13},{5,1},{9,5},{13,9},{2,14},{6,2},{... | collective-permute-start | bytes 73736 | tf_op jit(solution)/shard_map/ppermute | solution.py:32
  6.5 0.1 collective-permute-start.2
  6.6 1.0 %constant_dynamic-update-slice_fusion.3 = bf16[512,1024]{1,0:T(8,128)(2,1)S(1)} fusion(bf16[128,1024]{1,0:T(8,128)(2,1)} %param.5), kind=kLoop, calls=%fused_computation.77 | loop fusion | bytes 524288
  7.6 0.0 copy-start
  7.7 2.3 %fusion.54 = bf16[768,128]{0,1:T(8,128)(2,1)S(1)} fusion(bf16[128,1024]{1,0:T(8,128)(2,1)} %param.5, bf16[768,1024]{1,0:T(8,128)(2,1)} %param.4, s32[768]{0:T(1024)S(1)} %get-tuple-element.37, s32[128]{0:T(128)S(1)} %iota_add_fusion.3), kind=kOutput, calls=%fused_computation.68 | convolution fusion | flops 202014720 | bytes 2035200 | tf_op jit(solution)/shard_map/dot_general | solution.py:39
  10.0 0.0 copy-done
  10.0 0.4 fusion.56
  10.4 0.0 collective-permute-done.3
  10.5 0.0 collective-permute-done
  10.5 0.7 %fusion.53 = bf16[768,128]{0,1:T(8,128)(2,1)S(1)} fusion(bf16[128,1024]{1,0:T(8,128)(2,1)S(1)} %collective-permute-done, bf16[768,1024]{1,0:T(8,128)(2,1)S(1)} %copy-done, s32[768]{0:T(1024)S(1)} %get-tuple-element.36, s32[128]{0:T(128)S(1)} %iota_add_fusion.2), kind=kOutput, calls=%fused_computation.67 | convolution fusion | flops 202014720 | bytes 2035200 | tf_op jit(solution)/shard_map/dot_general | solution.py:39
  11.2 0.4 fusion.57
  11.6 13.6 %collective-permute-done.1 = bf16[128,1024]{1,0:T(8,128)(2,1)S(1)} collective-permute-done((bf16[128,1024]{1,0:T(8,128)(2,1)}, bf16[128,1024]{1,0:T(8,128)(2,1)S(1)}, u32[]{:S(2)}, u32[]{:S(2)}) %collective-permute-start.1) | collective-permute-done | bytes 262176 | tf_op jit(solution)/shard_map/ppermute | solution.py:29
  25.1 0.7 %fusion.52 = bf16[768,128]{0,1:T(8,128)(2,1)S(1)} fusion(bf16[128,1024]{1,0:T(8,128)(2,1)S(1)} %collective-permute-done.1, bf16[768,1024]{1,0:T(8,128)(2,1)S(1)} %copy-done, s32[768]{0:T(1024)S(1)} %get-tuple-element.35, s32[128]{0:T(128)S(1)} %iota_add_fusion.1), kind=kOutput, calls=%fused_computation.66 | convolution fusion | flops 202014720 | bytes 2035200 | tf_op jit(solution)/shard_map/dot_general | solution.py:39
  25.8 0.4 fusion.58
  26.3 0.3 collective-permute-done.2
  26.6 0.7 %fusion.51 = bf16[768,128]{0,1:T(8,128)(2,1)S(1)} fusion(bf16[128,1024]{1,0:T(8,128)(2,1)S(1)} %collective-permute-done.1, bf16[768,1024]{1,0:T(8,128)(2,1)S(1)} %collective-permute-done.2, s32[768]{0:T(1024)S(1)} %get-tuple-element.33, s32[128]{0:T(128)S(1)} %iota_add_fusion.1), kind=kOutput, calls=%fused_computation.65 | convolution fusion | flops 202014720 | bytes 2035200 | tf_op jit(solution)/shard_map/dot_general | solution.py:39
  27.3 0.4 fusion.4
  27.6 0.7 %fusion.50 = bf16[768,128]{0,1:T(8,128)(2,1)S(1)} fusion(bf16[128,1024]{1,0:T(8,128)(2,1)S(1)} %collective-permute-done, bf16[768,1024]{1,0:T(8,128)(2,1)S(1)} %collective-permute-done.2, s32[768]{0:T(1024)S(1)} %get-tuple-element.32, s32[128]{0:T(128)S(1)} %iota_add_fusion.2), kind=kOutput, calls=%fused_computation.64 | convolution fusion | flops 202014720 | bytes 2035200 | tf_op jit(solution)/shard_map/dot_general | solution.py:39
  28.4 0.0 copy-start.1
  28.4 0.4 fusion.5
  28.8 0.5 copy-done.1
  29.3 0.7 %fusion.49 = bf16[768,128]{0,1:T(8,128)(2,1)S(1)} fusion(bf16[128,1024]{1,0:T(8,128)(2,1)S(1)} %copy-done.1, bf16[768,1024]{1,0:T(8,128)(2,1)S(1)} %collective-permute-done.2, s32[768]{0:T(1024)S(1)} %get-tuple-element.31, s32[128]{0:T(128)S(1)} %iota_add_fusion.3), kind=kOutput, calls=%fused_computation.63 | convolution fusion | flops 202014720 | bytes 2035200 | tf_op jit(solution)/shard_map/dot_general | solution.py:39
  30.0 0.4 fusion.1
  30.4 0.0 collective-permute-done.5
  30.4 0.7 %fusion.48 = bf16[768,128]{0,1:T(8,128)(2,1)S(1)} fusion(bf16[128,1024]{1,0:T(8,128)(2,1)S(1)} %collective-permute-done.5, bf16[768,1024]{1,0:T(8,128)(2,1)S(1)} %copy-done, s32[768]{0:T(1024)S(1)} %get-tuple-element.34, s32[128]{0:T(128)S(1)} %iota_add_fusion), kind=kOutput, calls=%fused_computation.62 | convolution fusion | flops 202014720 | bytes 2035200 | tf_op jit(solution)/shard_map/dot_general | solution.py:39
  31.2 0.4 fusion.59
  31.5 0.7 %fusion.47 = bf16[768,128]{0,1:T(8,128)(2,1)S(1)} fusion(bf16[128,1024]{1,0:T(8,128)(2,1)S(1)} %collective-permute-done.5, bf16[768,1024]{1,0:T(8,128)(2,1)S(1)} %collective-permute-done.2, s32[768]{0:T(1024)S(1)} %get-tuple-element.30, s32[128]{0:T(128)S(1)} %iota_add_fusion), kind=kOutput, calls=%fused_computation.61 | convolution fusion | flops 202014720 | bytes 2035200 | tf_op jit(solution)/shard_map/dot_general | solution.py:39
  32.3 0.1 pad_maximum_fusion.1
  32.3 0.4 fusion.6
  32.7 1.0 %convolution_convert_fusion = bf16[768,1024]{1,0:T(8,128)(2,1)S(1)} fusion(bf16[768,512]{0,1:T(8,128)(2,1)S(1)} %pad_maximum_fusion.1, bf16[512,1024]{1,0:T(8,128)(2,1)S(1)} %constant_dynamic-update-slice_fusion), kind=kOutput, calls=%fused_computation.1 | convolution fusion | flops 806092800 | bytes 3407872 | tf_op jit(solution)/shard_map/dot_general | solution.py:50
  33.7 2.7 %collective-permute-start.6 = (bf16[768,1024]{1,0:T(8,128)(2,1)S(1)}, bf16[768,1024]{1,0:T(8,128)(2,1)S(1)}, u32[]{:S(2)}, u32[]{:S(2)}) collective-permute-start(bf16[768,1024]{1,0:T(8,128)(2,1)S(1)} %convolution_convert_fusion), channel_id=1, source_target_pairs={{0,4},{4,8},{8,12},{12,0},{1,5},{5,9},{9,13},{13,1},{2,6},{6,10},{... | collective-permute-start | bytes 4718600 | tf_op jit(solution)/shard_map/ppermute | solution.py:32
  36.5 1.9 %collective-permute-start.4 = (bf16[128,1024]{1,0:T(8,128)(2,1)S(1)}, bf16[128,1024]{1,0:T(8,128)(2,1)S(1)}, u32[]{:S(2)}, u32[]{:S(2)}) collective-permute-start(bf16[128,1024]{1,0:T(8,128)(2,1)S(1)} %fusion.5), channel_id=1, source_target_pairs={{0,1},{1,0},{2,3},{3,2},{4,5},{5,4},{6,7},{7,6},{8,9},{9,8},{10,11... | collective-permute-start | bytes 786440 | tf_op jit(solution)/shard_map/ppermute | solution.py:29
  38.3 1.2 %collective-permute-start.7 = (bf16[128,1024]{1,0:T(8,128)(2,1)S(1)}, bf16[128,1024]{1,0:T(8,128)(2,1)S(1)}, u32[]{:S(2)}, u32[]{:S(2)}) collective-permute-start(bf16[128,1024]{1,0:T(8,128)(2,1)S(1)} %fusion.4), channel_id=1, source_target_pairs={{0,2},{1,3},{2,0},{3,1},{4,6},{5,7},{6,4},{7,5},{8,10},{9,11},{10,... | collective-permute-start | bytes 786440 | tf_op jit(solution)/shard_map/ppermute | solution.py:29
  39.5 0.3 collective-permute-start.8
  39.7 0.1 pad_maximum_fusion
  39.8 1.0 %fusion.60 = f32[768,1024]{1,0:T(8,128)S(1)} fusion(bf16[768,512]{0,1:T(8,128)(2,1)S(1)} %pad_maximum_fusion, bf16[512,1024]{1,0:T(8,128)(2,1)S(1)} %constant_dynamic-update-slice_fusion), kind=kOutput, calls=%fused_computation.94 | convolution fusion | flops 805306368 | bytes 4980736 | tf_op jit(solution)/shard_map/dot_general | solution.py:50
  40.8 13.0 %collective-permute-done.6 = bf16[768,1024]{1,0:T(8,128)(2,1)S(1)} collective-permute-done((bf16[768,1024]{1,0:T(8,128)(2,1)S(1)}, bf16[768,1024]{1,0:T(8,128)(2,1)S(1)}, u32[]{:S(2)}, u32[]{:S(2)}) %collective-permute-start.6) | collective-permute-done | bytes 1572896 | tf_op jit(solution)/shard_map/ppermute | solution.py:32
  53.8 1.8 %add_convert_fusion = bf16[768,1024]{1,0:T(8,128)(2,1)} fusion(f32[768,1024]{1,0:T(8,128)S(1)} %fusion.60, bf16[768,1024]{1,0:T(8,128)(2,1)S(1)} %collective-permute-done.6), kind=kLoop, calls=%fused_computation | loop fusion | flops 2359296 | bytes 6291456 | tf_op jit(solution)/shard_map/convert_element_type | solution.py:89
  55.6 7.1 %collective-permute-done.8 = bf16[128,1024]{1,0:T(8,128)(2,1)S(1)} collective-permute-done((bf16[128,1024]{1,0:T(8,128)(2,1)S(1)}, bf16[128,1024]{1,0:T(8,128)(2,1)S(1)}, u32[]{:S(2)}, u32[]{:S(2)}) %collective-permute-start.8) | collective-permute-done | bytes 262176 | tf_op jit(solution)/shard_map/ppermute | solution.py:29
  62.6 0.0 collective-permute-done.7
  62.6 0.0 collective-permute-done.4
  62.6 0.9 %add_convert_fusion.1 = bf16[128,1024]{1,0:T(8,128)(2,1)} fusion(bf16[128,1024]{1,0:T(8,128)(2,1)S(1)} %collective-permute-done.8, bf16[128,1024]{1,0:T(8,128)(2,1)S(1)} %collective-permute-done.7, f32[128,1024]{1,0:T(8,128)S(1)} %fusion.1, bf16[128,1024]{1,0:T(8,128)(2,1)S(1)} %collective-permute-done.4), kind=kLoop, calls=%fused_computation.71 | loop fusion | flops 917504 | bytes 1572864 | tf_op jit(solution)/shard_map/convert_element_type | solution.py:94
  (9 shorter events, 0.2 us)
Async XLA Ops:
  0.6 9.8 %collective-permute-start = (bf16[128,1024]{1,0:T(8,128)(2,1)}, bf16[128,1024]{1,0:T(8,128)(2,1)S(1)}, u32[]{:S(2)}, u32[]{:S(2)}) collective-permute-start(bf16[128,1024]{1,0:T(8,128)(2,1)} %param.5), channel_id=1, source_target_pairs={{0,1},{1,0},{2,3},{3,2},{4,5},{5,4},{6,7},{7,6},{8,9},{9,8},{10,11... | collective-permute-start | bytes 786440 | tf_op jit(solution)/shard_map/ppermute | solution.py:29
  0.7 29.7 %collective-permute-start.5 = (bf16[128,1024]{1,0:T(8,128)(2,1)}, bf16[128,1024]{1,0:T(8,128)(2,1)S(1)}, u32[]{:S(2)}, u32[]{:S(2)}) collective-permute-start(bf16[128,1024]{1,0:T(8,128)(2,1)} %param.5), channel_id=1, source_target_pairs={{0,3},{1,2},{2,1},{3,0},{4,7},{5,6},{6,5},{7,4},{8,11},{9,10},{10,... | collective-permute-start | bytes 786440 | tf_op jit(solution)/shard_map/ppermute | solution.py:29
  3.3 21.8 %collective-permute-start.1 = (bf16[128,1024]{1,0:T(8,128)(2,1)}, bf16[128,1024]{1,0:T(8,128)(2,1)S(1)}, u32[]{:S(2)}, u32[]{:S(2)}) collective-permute-start(bf16[128,1024]{1,0:T(8,128)(2,1)} %param.5), channel_id=1, source_target_pairs={{0,2},{1,3},{2,0},{3,1},{4,6},{5,7},{6,4},{7,5},{8,10},{9,11},{10,... | collective-permute-start | bytes 786440 | tf_op jit(solution)/shard_map/ppermute | solution.py:29
  5.0 5.4 %collective-permute-start.3 = (s32[768,8]{0,1:T(8,128)S(1)}, s32[768,8]{0,1:T(8,128)S(1)}, u32[]{:S(2)}, u32[]{:S(2)}) collective-permute-start(s32[768,8]{0,1:T(8,128)S(1)} %fusion.55), channel_id=1, source_target_pairs={{0,12},{4,0},{8,4},{12,8},{1,13},{5,1},{9,5},{13,9},{2,14},{6,2},{... | collective-permute-start | bytes 73736 | tf_op jit(solution)/shard_map/ppermute | solution.py:32
  6.5 20.1 %collective-permute-start.2 = (bf16[768,1024]{1,0:T(8,128)(2,1)}, bf16[768,1024]{1,0:T(8,128)(2,1)S(1)}, u32[]{:S(2)}, u32[]{:S(2)}) collective-permute-start(bf16[768,1024]{1,0:T(8,128)(2,1)} %param.4), channel_id=1, source_target_pairs={{0,12},{4,0},{8,4},{12,8},{1,13},{5,1},{9,5},{13,9},{2,14},{6,2},{... | collective-permute-start | bytes 4718600 | tf_op jit(solution)/shard_map/ppermute | solution.py:32
  7.6 2.3 %copy-start = (bf16[768,1024]{1,0:T(8,128)(2,1)S(1)}, bf16[768,1024]{1,0:T(8,128)(2,1)}, u32[]{:S(2)}) copy-start(bf16[768,1024]{1,0:T(8,128)(2,1)} %param.4) | copy-start | bytes 4718596
  28.4 1.0 %copy-start.1 = (bf16[128,1024]{1,0:T(8,128)(2,1)S(1)}, bf16[128,1024]{1,0:T(8,128)(2,1)}, u32[]{:S(2)}) copy-start(bf16[128,1024]{1,0:T(8,128)(2,1)} %param.5) | copy-start | bytes 786436
  33.7 20.1 %collective-permute-start.6 = (bf16[768,1024]{1,0:T(8,128)(2,1)S(1)}, bf16[768,1024]{1,0:T(8,128)(2,1)S(1)}, u32[]{:S(2)}, u32[]{:S(2)}) collective-permute-start(bf16[768,1024]{1,0:T(8,128)(2,1)S(1)} %convolution_convert_fusion), channel_id=1, source_target_pairs={{0,4},{4,8},{8,12},{12,0},{1,5},{5,9},{9,13},{13,1},{2,6},{6,10},{... | collective-permute-start | bytes 4718600 | tf_op jit(solution)/shard_map/ppermute | solution.py:32
  36.5 26.2 %collective-permute-start.4 = (bf16[128,1024]{1,0:T(8,128)(2,1)S(1)}, bf16[128,1024]{1,0:T(8,128)(2,1)S(1)}, u32[]{:S(2)}, u32[]{:S(2)}) collective-permute-start(bf16[128,1024]{1,0:T(8,128)(2,1)S(1)} %fusion.5), channel_id=1, source_target_pairs={{0,1},{1,0},{2,3},{3,2},{4,5},{5,4},{6,7},{7,6},{8,9},{9,8},{10,11... | collective-permute-start | bytes 786440 | tf_op jit(solution)/shard_map/ppermute | solution.py:29
  38.3 24.3 %collective-permute-start.7 = (bf16[128,1024]{1,0:T(8,128)(2,1)S(1)}, bf16[128,1024]{1,0:T(8,128)(2,1)S(1)}, u32[]{:S(2)}, u32[]{:S(2)}) collective-permute-start(bf16[128,1024]{1,0:T(8,128)(2,1)S(1)} %fusion.4), channel_id=1, source_target_pairs={{0,2},{1,3},{2,0},{3,1},{4,6},{5,7},{6,4},{7,5},{8,10},{9,11},{10,... | collective-permute-start | bytes 786440 | tf_op jit(solution)/shard_map/ppermute | solution.py:29
  39.5 23.2 %collective-permute-start.8 = (bf16[128,1024]{1,0:T(8,128)(2,1)S(1)}, bf16[128,1024]{1,0:T(8,128)(2,1)S(1)}, u32[]{:S(2)}, u32[]{:S(2)}) collective-permute-start(bf16[128,1024]{1,0:T(8,128)(2,1)S(1)} %fusion.6), channel_id=1, source_target_pairs={{0,3},{1,2},{2,1},{3,0},{4,7},{5,6},{6,5},{7,4},{8,11},{9,10},{10,... | collective-permute-start | bytes 786440 | tf_op jit(solution)/shard_map/ppermute | solution.py:29

commit v5 on v4

--- a/solution.py
+++ b/solution.py
@@ -54,9 +54,11 @@
         )
 
     d_own, d_next, g_own, total, moved = {}, {}, {}, {}, {}
-    pieces = {k: weights if k == 0 else to_dp(weights, k) for k in range(n_dp)}
+    pieces = {0: weights}
+    for k in range(1, n_dp):
+        step = k & -k
+        pieces[k] = to_dp(pieces[k ^ step], step)
     next_rows = to_label(embeds, -1)
-    next_ids = to_label(ids, -1)
 
     def own_step(k):
         pieces[k] = in_turn(pieces[k])
@@ -73,11 +75,11 @@
         last[0] = total[k]
 
     own_step(0)
+    next_ids = to_label(in_turn(ids), -1)
     for k in range(1, n_dp - 1):
         own_step(k)
-    for k in range(n_dp - 2, 0, -1):
+    for k in range(n_dp - 1):
         next_step(k)
-    next_step(0)
     if n_dp > 1:
         own_step(n_dp - 1)
         next_step(n_dp - 1)

time: 63.7 us -> 65.4 us (1.027)
  waiting for transfers between devices: 33.9 us -> 38.9 us
  starting transfers between devices: 11.2 us -> 9.45 us
  local copies, waits for them, and re-layouts: 1.67 us -> 0.3 us
    ppermute x3, waiting for transfers between devices: 13.3 us -> 29.2 us  [to_label(): lax.ppermute(x, 'label', [(i, (i + by) % n_label) for i in range(n_label)])]
    ppermute x6, waiting for transfers between devices: 20.6 us -> 9.69 us  [to_dp(): return lax.ppermute(x, 'dp', [(i, i ^ k) for i in range(n_dp)])]
    ppermute x3, starting transfers between devices: 4.33 us -> 2.9 us  [to_label(): lax.ppermute(x, 'label', [(i, (i + by) % n_label) for i in range(n_label)])]
    unnamed x7, local copies, waits for them, and re-layouts: 1.56 us -> 0.21 us
  transfers between devices with their start and end apart: 9 -> 9, of which waited for: 4 -> 4; matrix products, arithmetic and copies ran while one was open for 20% -> 18% of each run, Pallas kernels for 0% -> 0%
where the time goes in v5:
time: 65.4 us; the launch traced here: 65.2 us
  waiting for transfers between devices  38.9 us (59%)
  matrix products  12.3 us (19%)
  starting transfers between devices  9.45 us (14%)
  other arithmetic  3.47 us (5%)
  between operations  0.86 us (1%)
    ppermute x3, waiting for transfers between devices, to_label(): lax.ppermute(x, 'label', [(i, (i + by) % n_label) for i in range(n_label)])  29.2 us
    ppermute x6, waiting for transfers between devices, to_dp(): return lax.ppermute(x, 'dp', [(i, i ^ k) for i in range(n_dp)])  9.69 us
    dot_general x8, matrix products, delta_of(): lax.dot_general(rows, piece, (((1,), (1,)), ((), ())), preferred_element_...  7.21 us
    ppermute x6, starting transfers between devices, to_dp(): return lax.ppermute(x, 'dp', [(i, i ^ k) for i in range(n_dp)])  6.55 us
    dot_general x8, matrix products, grad_w_of(): lax.dot_general(delta, rows, (((0,), (0,)), ((), ())), preferred_element_...  3.04 us
    ppermute x3, starting transfers between devices, to_label(): lax.ppermute(x, 'label', [(i, (i + by) % n_label) for i in range(n_label)])  2.9 us
    dot_general x2, matrix products, grad_x_of(): jnp.dot(in_turn(jnp.concatenate([deltas[k] for k in range(n_dp)], axis=1)...  2.03 us
    convert_element_type x1, other arithmetic, local(): grad_x = (grad_x + in_turn(back).astype(jnp.float32)).astype(jnp.bfloat16)  1.75 us
  transfers between devices with their start and end apart: 9, of which 4 were waited for; matrix products, arithmetic and copies ran while one was open for 18% of the time, Pallas kernels for 0%

profile of v5, /device:TPU:9, one launch (start us, length us, event | category | flops | bytes accessed | tf_op | source)
XLA Modules:
  0.0 65.2 jit_solution(14554579563698574315)
XLA Ops:
  0.6 0.1 collective-permute-start.1
  0.7 2.5 %collective-permute-start = (bf16[128,1024]{1,0:T(8,128)(2,1)}, bf16[128,1024]{1,0:T(8,128)(2,1)S(1)}, u32[]{:S(2)}, u32[]{:S(2)}) collective-permute-start(bf16[128,1024]{1,0:T(8,128)(2,1)} %param.5), channel_id=1, source_target_pairs={{0,2},{1,3},{2,0},{3,1},{4,6},{5,7},{6,4},{7,5},{8,10},{9,11},{10,... | collective-permute-start | bytes 786440 | tf_op jit(solution)/shard_map/ppermute | solution.py:29
  3.2 1.2 %collective-permute-start.2 = (bf16[768,1024]{1,0:T(8,128)(2,1)}, bf16[768,1024]{1,0:T(8,128)(2,1)S(1)}, u32[]{:S(2)}, u32[]{:S(2)}) collective-permute-start(bf16[768,1024]{1,0:T(8,128)(2,1)} %param.4), channel_id=1, source_target_pairs={{0,12},{4,0},{8,4},{12,8},{1,13},{5,1},{9,5},{13,9},{2,14},{6,2},{... | collective-permute-start | bytes 4718600 | tf_op jit(solution)/shard_map/ppermute | solution.py:32
  4.4 0.7 %fusion.55 = s32[768,8]{0,1:T(8,128)S(1)} fusion(s32[768,8]{0,1:T(8,128)} %param.6, s32[768]{0:T(1024)} %param.7), kind=kLoop, calls=%fused_computation.73 | loop fusion | flops 12288 | bytes 52224 | tf_op jit(solution)/shard_map/jit(_where)/select_n | solution.py:21
  5.2 0.0 copy-start
  5.2 2.3 %fusion.54 = bf16[768,128]{0,1:T(8,128)(2,1)S(1)} fusion(bf16[128,1024]{1,0:T(8,128)(2,1)} %param.5, bf16[768,1024]{1,0:T(8,128)(2,1)} %param.4, s32[768]{0:T(1024)S(1)} %get-tuple-element.39, s32[128]{0:T(128)S(1)} %iota_add_fusion.3), kind=kOutput, calls=%fused_computation.68 | convolution fusion | flops 202014720 | bytes 2035200 | tf_op jit(solution)/shard_map/dot_general | solution.py:39
  7.5 0.0 copy-done
  7.5 0.0 copy-start.1
  7.6 0.4 fusion.56
  7.9 0.4 collective-permute-start.3
  8.4 0.1 copy-done.1
  8.5 15.5 %collective-permute-done.3 = s32[768,8]{0,1:T(8,128)S(1)} collective-permute-done((s32[768,8]{0,1:T(8,128)S(1)}, s32[768,8]{0,1:T(8,128)S(1)}, u32[]{:S(2)}, u32[]{:S(2)}) %collective-permute-start.3) | collective-permute-done | bytes 24608 | tf_op jit(solution)/shard_map/ppermute | solution.py:32
  24.1 0.0 collective-permute-done.1
  24.1 0.7 %fusion.53 = bf16[768,128]{0,1:T(8,128)(2,1)S(1)} fusion(bf16[128,1024]{1,0:T(8,128)(2,1)S(1)} %collective-permute-done.1, bf16[768,1024]{1,0:T(8,128)(2,1)S(1)} %copy-done, s32[768]{0:T(1024)S(1)} %get-tuple-element.38, s32[128]{0:T(128)S(1)} %iota_add_fusion.2), kind=kOutput, calls=%fused_computation.67 | convolution fusion | flops 202014720 | bytes 2035200 | tf_op jit(solution)/shard_map/dot_general | solution.py:39
  24.8 0.4 fusion.57
  25.2 0.0 collective-permute-done
  25.2 0.7 %fusion.52 = bf16[768,128]{0,1:T(8,128)(2,1)S(1)} fusion(bf16[128,1024]{1,0:T(8,128)(2,1)S(1)} %collective-permute-done, bf16[768,1024]{1,0:T(8,128)(2,1)S(1)} %copy-done, s32[768]{0:T(1024)S(1)} %get-tuple-element.37, s32[128]{0:T(128)S(1)} %iota_add_fusion.1), kind=kOutput, calls=%fused_computation.66 | convolution fusion | flops 202014720 | bytes 2035200 | tf_op jit(solution)/shard_map/dot_general | solution.py:39
  25.9 0.4 fusion.58
  26.3 1.4 %collective-permute-start.5 = (bf16[128,1024]{1,0:T(8,128)(2,1)S(1)}, bf16[128,1024]{1,0:T(8,128)(2,1)S(1)}, u32[]{:S(2)}, u32[]{:S(2)}) collective-permute-start(bf16[128,1024]{1,0:T(8,128)(2,1)S(1)} %collective-permute-done), channel_id=1, source_target_pairs={{0,1},{1,0},{2,3},{3,2},{4,5},{5,4},{6,7},{7,6},{8,9},{9,8},{10,11... | collective-permute-start | bytes 786440 | tf_op jit(solution)/shard_map/ppermute | solution.py:29
  27.7 0.0 collective-permute-done.2
  27.7 0.7 %fusion.51 = bf16[768,128]{0,1:T(8,128)(2,1)S(1)} fusion(bf16[128,1024]{1,0:T(8,128)(2,1)S(1)} %copy-done.1, bf16[768,1024]{1,0:T(8,128)(2,1)S(1)} %collective-permute-done.2, s32[768]{0:T(1024)S(1)} %get-tuple-element.35, s32[128]{0:T(128)S(1)} %iota_add_fusion.3), kind=kOutput, calls=%fused_computation.65 | convolution fusion | flops 202014720 | bytes 2035200 | tf_op jit(solution)/shard_map/dot_general | solution.py:39
  28.4 0.4 fusion.3
  28.8 0.7 %fusion.50 = bf16[768,128]{0,1:T(8,128)(2,1)S(1)} fusion(bf16[128,1024]{1,0:T(8,128)(2,1)S(1)} %collective-permute-done.1, bf16[768,1024]{1,0:T(8,128)(2,1)S(1)} %collective-permute-done.2, s32[768]{0:T(1024)S(1)} %get-tuple-element.34, s32[128]{0:T(128)S(1)} %iota_add_fusion.2), kind=kOutput, calls=%fused_computation.64 | convolution fusion | flops 202014720 | bytes 2035200 | tf_op jit(solution)/shard_map/dot_general | solution.py:39
  29.5 0.4 fusion.4
  29.9 0.7 %fusion.49 = bf16[768,128]{0,1:T(8,128)(2,1)S(1)} fusion(bf16[128,1024]{1,0:T(8,128)(2,1)S(1)} %collective-permute-done, bf16[768,1024]{1,0:T(8,128)(2,1)S(1)} %collective-permute-done.2, s32[768]{0:T(1024)S(1)} %get-tuple-element.33, s32[128]{0:T(128)S(1)} %iota_add_fusion.1), kind=kOutput, calls=%fused_computation.63 | convolution fusion | flops 202014720 | bytes 2035200 | tf_op jit(solution)/shard_map/dot_general | solution.py:39
  30.6 0.4 fusion.5
  31.0 3.0 %collective-permute-done.5 = bf16[128,1024]{1,0:T(8,128)(2,1)S(1)} collective-permute-done((bf16[128,1024]{1,0:T(8,128)(2,1)S(1)}, bf16[128,1024]{1,0:T(8,128)(2,1)S(1)}, u32[]{:S(2)}, u32[]{:S(2)}) %collective-permute-start.5) | collective-permute-done | bytes 262176 | tf_op jit(solution)/shard_map/ppermute | solution.py:29
  34.0 0.7 %fusion.48 = bf16[768,128]{0,1:T(8,128)(2,1)S(1)} fusion(bf16[128,1024]{1,0:T(8,128)(2,1)S(1)} %collective-permute-done.5, bf16[768,1024]{1,0:T(8,128)(2,1)S(1)} %copy-done, s32[768]{0:T(1024)S(1)} %get-tuple-element.36, s32[128]{0:T(128)S(1)} %iota_add_fusion), kind=kOutput, calls=%fused_computation.62 | convolution fusion | flops 202014720 | bytes 2035200 | tf_op jit(solution)/shard_map/dot_general | solution.py:39
  34.7 0.4 fusion.59
  35.1 0.7 %fusion.47 = bf16[768,128]{0,1:T(8,128)(2,1)S(1)} fusion(bf16[128,1024]{1,0:T(8,128)(2,1)S(1)} %collective-permute-done.5, bf16[768,1024]{1,0:T(8,128)(2,1)S(1)} %collective-permute-done.2, s32[768]{0:T(1024)S(1)} %get-tuple-element.32, s32[128]{0:T(128)S(1)} %iota_add_fusion), kind=kOutput, calls=%fused_computation.61 | convolution fusion | flops 202014720 | bytes 2035200 | tf_op jit(solution)/shard_map/dot_general | solution.py:39
  35.8 0.1 pad_maximum_fusion.1
  35.9 0.4 fusion.6
  36.3 1.0 %convolution_convert_fusion = bf16[768,1024]{1,0:T(8,128)(2,1)S(1)} fusion(bf16[768,512]{0,1:T(8,128)(2,1)S(1)} %pad_maximum_fusion.1, bf16[512,1024]{1,0:T(8,128)(2,1)S(1)} %constant_dynamic-update-slice_fusion), kind=kOutput, calls=%fused_computation.1 | convolution fusion | flops 806092800 | bytes 3407872 | tf_op jit(solution)/shard_map/dot_general | solution.py:50
  37.3 1.2 %collective-permute-start.6 = (bf16[768,1024]{1,0:T(8,128)(2,1)S(1)}, bf16[768,1024]{1,0:T(8,128)(2,1)S(1)}, u32[]{:S(2)}, u32[]{:S(2)}) collective-permute-start(bf16[768,1024]{1,0:T(8,128)(2,1)S(1)} %convolution_convert_fusion), channel_id=1, source_target_pairs={{0,4},{4,8},{8,12},{12,0},{1,5},{5,9},{9,13},{13,1},{2,6},{6,10},{... | collective-permute-start | bytes 4718600 | tf_op jit(solution)/shard_map/ppermute | solution.py:32
  38.5 0.1 collective-permute-start.7
  38.6 1.3 %collective-permute-start.4 = (bf16[128,1024]{1,0:T(8,128)(2,1)S(1)}, bf16[128,1024]{1,0:T(8,128)(2,1)S(1)}, u32[]{:S(2)}, u32[]{:S(2)}) collective-permute-start(bf16[128,1024]{1,0:T(8,128)(2,1)S(1)} %fusion.4), channel_id=1, source_target_pairs={{0,1},{1,0},{2,3},{3,2},{4,5},{5,4},{6,7},{7,6},{8,9},{9,8},{10,11... | collective-permute-start | bytes 786440 | tf_op jit(solution)/shard_map/ppermute | solution.py:29
  39.9 1.3 %collective-permute-start.8 = (bf16[128,1024]{1,0:T(8,128)(2,1)S(1)}, bf16[128,1024]{1,0:T(8,128)(2,1)S(1)}, u32[]{:S(2)}, u32[]{:S(2)}) collective-permute-start(bf16[128,1024]{1,0:T(8,128)(2,1)S(1)} %fusion.6), channel_id=1, source_target_pairs={{0,3},{1,2},{2,1},{3,0},{4,7},{5,6},{6,5},{7,4},{8,11},{9,10},{10,... | collective-permute-start | bytes 786440 | tf_op jit(solution)/shard_map/ppermute | solution.py:29
  41.2 0.1 pad_maximum_fusion
  41.2 1.0 %fusion.60 = f32[768,1024]{1,0:T(8,128)S(1)} fusion(bf16[768,512]{0,1:T(8,128)(2,1)S(1)} %pad_maximum_fusion, bf16[512,1024]{1,0:T(8,128)(2,1)S(1)} %constant_dynamic-update-slice_fusion), kind=kOutput, calls=%fused_computation.94 | convolution fusion | flops 805306368 | bytes 4980736 | tf_op jit(solution)/shard_map/dot_general | solution.py:50
  42.3 13.6 %collective-permute-done.6 = bf16[768,1024]{1,0:T(8,128)(2,1)S(1)} collective-permute-done((bf16[768,1024]{1,0:T(8,128)(2,1)S(1)}, bf16[768,1024]{1,0:T(8,128)(2,1)S(1)}, u32[]{:S(2)}, u32[]{:S(2)}) %collective-permute-start.6) | collective-permute-done | bytes 1572896 | tf_op jit(solution)/shard_map/ppermute | solution.py:32
  55.9 1.8 %add_convert_fusion = bf16[768,1024]{1,0:T(8,128)(2,1)} fusion(f32[768,1024]{1,0:T(8,128)S(1)} %fusion.60, bf16[768,1024]{1,0:T(8,128)(2,1)S(1)} %collective-permute-done.6), kind=kLoop, calls=%fused_computation | loop fusion | flops 2359296 | bytes 6291456 | tf_op jit(solution)/shard_map/convert_element_type | solution.py:91
  57.6 6.7 %collective-permute-done.8 = bf16[128,1024]{1,0:T(8,128)(2,1)S(1)} collective-permute-done((bf16[128,1024]{1,0:T(8,128)(2,1)S(1)}, bf16[128,1024]{1,0:T(8,128)(2,1)S(1)}, u32[]{:S(2)}, u32[]{:S(2)}) %collective-permute-start.8) | collective-permute-done | bytes 262176 | tf_op jit(solution)/shard_map/ppermute | solution.py:29
  64.4 0.0 collective-permute-done.7
  64.4 0.0 collective-permute-done.4
  64.4 0.9 %add_convert_fusion.1 = bf16[128,1024]{1,0:T(8,128)(2,1)} fusion(bf16[128,1024]{1,0:T(8,128)(2,1)S(1)} %collective-permute-done.8, bf16[128,1024]{1,0:T(8,128)(2,1)S(1)} %collective-permute-done.7, f32[128,1024]{1,0:T(8,128)S(1)} %fusion.3, bf16[128,1024]{1,0:T(8,128)(2,1)S(1)} %collective-permute-done.4), kind=kLoop, calls=%fused_computation.71 | loop fusion | flops 917504 | bytes 1572864 | tf_op jit(solution)/shard_map/convert_element_type | solution.py:96
  (10 shorter events, 0.2 us)
Async XLA Ops:
  0.6 23.5 %collective-permute-start.1 = (bf16[128,1024]{1,0:T(8,128)(2,1)}, bf16[128,1024]{1,0:T(8,128)(2,1)S(1)}, u32[]{:S(2)}, u32[]{:S(2)}) collective-permute-start(bf16[128,1024]{1,0:T(8,128)(2,1)} %param.5), channel_id=1, source_target_pairs={{0,1},{1,0},{2,3},{3,2},{4,5},{5,4},{6,7},{7,6},{8,9},{9,8},{10,11... | collective-permute-start | bytes 786440 | tf_op jit(solution)/shard_map/ppermute | solution.py:29
  0.7 24.5 %collective-permute-start = (bf16[128,1024]{1,0:T(8,128)(2,1)}, bf16[128,1024]{1,0:T(8,128)(2,1)S(1)}, u32[]{:S(2)}, u32[]{:S(2)}) collective-permute-start(bf16[128,1024]{1,0:T(8,128)(2,1)} %param.5), channel_id=1, source_target_pairs={{0,2},{1,3},{2,0},{3,1},{4,6},{5,7},{6,4},{7,5},{8,10},{9,11},{10,... | collective-permute-start | bytes 786440 | tf_op jit(solution)/shard_map/ppermute | solution.py:29
  3.2 24.6 %collective-permute-start.2 = (bf16[768,1024]{1,0:T(8,128)(2,1)}, bf16[768,1024]{1,0:T(8,128)(2,1)S(1)}, u32[]{:S(2)}, u32[]{:S(2)}) collective-permute-start(bf16[768,1024]{1,0:T(8,128)(2,1)} %param.4), channel_id=1, source_target_pairs={{0,12},{4,0},{8,4},{12,8},{1,13},{5,1},{9,5},{13,9},{2,14},{6,2},{... | collective-permute-start | bytes 4718600 | tf_op jit(solution)/shard_map/ppermute | solution.py:32
  5.2 2.3 %copy-start = (bf16[768,1024]{1,0:T(8,128)(2,1)S(1)}, bf16[768,1024]{1,0:T(8,128)(2,1)}, u32[]{:S(2)}) copy-start(bf16[768,1024]{1,0:T(8,128)(2,1)} %param.4) | copy-start | bytes 4718596
  7.5 1.0 %copy-start.1 = (bf16[128,1024]{1,0:T(8,128)(2,1)S(1)}, bf16[128,1024]{1,0:T(8,128)(2,1)}, u32[]{:S(2)}) copy-start(bf16[128,1024]{1,0:T(8,128)(2,1)} %param.5) | copy-start | bytes 786436
  7.9 16.1 %collective-permute-start.3 = (s32[768,8]{0,1:T(8,128)S(1)}, s32[768,8]{0,1:T(8,128)S(1)}, u32[]{:S(2)}, u32[]{:S(2)}) collective-permute-start(s32[768,8]{0,1:T(8,128)S(1)} %fusion.55), channel_id=1, source_target_pairs={{0,12},{4,0},{8,4},{12,8},{1,13},{5,1},{9,5},{13,9},{2,14},{6,2},{... | collective-permute-start | bytes 73736 | tf_op jit(solution)/shard_map/ppermute | solution.py:32
  26.3 7.7 %collective-permute-start.5 = (bf16[128,1024]{1,0:T(8,128)(2,1)S(1)}, bf16[128,1024]{1,0:T(8,128)(2,1)S(1)}, u32[]{:S(2)}, u32[]{:S(2)}) collective-permute-start(bf16[128,1024]{1,0:T(8,128)(2,1)S(1)} %collective-permute-done), channel_id=1, source_target_pairs={{0,1},{1,0},{2,3},{3,2},{4,5},{5,4},{6,7},{7,6},{8,9},{9,8},{10,11... | collective-permute-start | bytes 786440 | tf_op jit(solution)/shard_map/ppermute | solution.py:29
  37.3 18.6 %collective-permute-start.6 = (bf16[768,1024]{1,0:T(8,128)(2,1)S(1)}, bf16[768,1024]{1,0:T(8,128)(2,1)S(1)}, u32[]{:S(2)}, u32[]{:S(2)}) collective-permute-start(bf16[768,1024]{1,0:T(8,128)(2,1)S(1)} %convolution_convert_fusion), channel_id=1, source_target_pairs={{0,4},{4,8},{8,12},{12,0},{1,5},{5,9},{9,13},{13,1},{2,6},{6,10},{... | collective-permute-start | bytes 4718600 | tf_op jit(solution)/shard_map/ppermute | solution.py:32
  38.5 25.8 %collective-permute-start.7 = (bf16[128,1024]{1,0:T(8,128)(2,1)S(1)}, bf16[128,1024]{1,0:T(8,128)(2,1)S(1)}, u32[]{:S(2)}, u32[]{:S(2)}) collective-permute-start(bf16[128,1024]{1,0:T(8,128)(2,1)S(1)} %fusion.5), channel_id=1, source_target_pairs={{0,2},{1,3},{2,0},{3,1},{4,6},{5,7},{6,4},{7,5},{8,10},{9,11},{10,... | collective-permute-start | bytes 786440 | tf_op jit(solution)/shard_map/ppermute | solution.py:29
  38.6 25.8 %collective-permute-start.4 = (bf16[128,1024]{1,0:T(8,128)(2,1)S(1)}, bf16[128,1024]{1,0:T(8,128)(2,1)S(1)}, u32[]{:S(2)}, u32[]{:S(2)}) collective-permute-start(bf16[128,1024]{1,0:T(8,128)(2,1)S(1)} %fusion.4), channel_id=1, source_target_pairs={{0,1},{1,0},{2,3},{3,2},{4,5},{5,4},{6,7},{7,6},{8,9},{9,8},{10,11... | collective-permute-start | bytes 786440 | tf_op jit(solution)/shard_map/ppermute | solution.py:29
  39.9 24.5 %collective-permute-start.8 = (bf16[128,1024]{1,0:T(8,128)(2,1)S(1)}, bf16[128,1024]{1,0:T(8,128)(2,1)S(1)}, u32[]{:S(2)}, u32[]{:S(2)}) collective-permute-start(bf16[128,1024]{1,0:T(8,128)(2,1)S(1)} %fusion.6), channel_id=1, source_target_pairs={{0,3},{1,2},{2,1},{3,0},{4,7},{5,6},{6,5},{7,4},{8,11},{9,10},{10,... | collective-permute-start | bytes 786440 | tf_op jit(solution)/shard_map/ppermute | solution.py:29

commit v6 on v5

--- a/solution.py
+++ b/solution.py
@@ -78,6 +78,7 @@
     next_ids = to_label(in_turn(ids), -1)
     for k in range(1, n_dp - 1):
         own_step(k)
+    next_ids = in_turn(next_ids)
     for k in range(n_dp - 1):
         next_step(k)
     if n_dp > 1:

time: 65.4 us -> 63.1 us (0.965)
  waiting for transfers between devices: 38.9 us -> 36.6 us
    ppermute x3, waiting for transfers between devices: 29.2 us -> 21.9 us  [to_label(): lax.ppermute(x, 'label', [(i, (i + by) % n_label) for i in range(n_label)])]
    ppermute x6, waiting for transfers between devices: 9.69 us -> 14.8 us  [to_dp(): return lax.ppermute(x, 'dp', [(i, i ^ k) for i in range(n_dp)])]
  transfers between devices with their start and end apart: 9 -> 9, of which waited for: 4 -> 6; matrix products, arithmetic and copies ran while one was open for 18% -> 19% of each run, Pallas kernels for 0% -> 0%
where the time goes in v6:
time: 63.1 us; the launch traced here: 62.9 us
  waiting for transfers between devices  36.6 us (58%)
  matrix products  12.3 us (19%)
  starting transfers between devices  9.4 us (15%)
  other arithmetic  3.47 us (5%)
  between operations  0.83 us (1%)
    ppermute x3, waiting for transfers between devices, to_label(): lax.ppermute(x, 'label', [(i, (i + by) % n_label) for i in range(n_label)])  21.9 us
    ppermute x6, waiting for transfers between devices, to_dp(): return lax.ppermute(x, 'dp', [(i, i ^ k) for i in range(n_dp)])  14.8 us
    dot_general x8, matrix products, delta_of(): lax.dot_general(rows, piece, (((1,), (1,)), ((), ())), preferred_element_...  7.2 us
    ppermute x6, starting transfers between devices, to_dp(): return lax.ppermute(x, 'dp', [(i, i ^ k) for i in range(n_dp)])  6.48 us
    dot_general x8, matrix products, grad_w_of(): lax.dot_general(delta, rows, (((0,), (0,)), ((), ())), preferred_element_...  3.05 us
    ppermute x3, starting transfers between devices, to_label(): lax.ppermute(x, 'label', [(i, (i + by) % n_label) for i in range(n_label)])  2.92 us
    dot_general x2, matrix products, grad_x_of(): jnp.dot(in_turn(jnp.concatenate([deltas[k] for k in range(n_dp)], axis=1)...  2.03 us
    convert_element_type x1, other arithmetic, local(): grad_x = (grad_x + in_turn(back).astype(jnp.float32)).astype(jnp.bfloat16)  1.75 us
  transfers between devices with their start and end apart: 9, of which 6 were waited for; matrix products, arithmetic and copies ran while one was open for 19% of the time, Pallas kernels for 0%

profile of v6, /device:TPU:9, one launch (start us, length us, event | category | flops | bytes accessed | tf_op | source)
XLA Modules:
  0.0 62.9 jit_solution(2128080385220128037)
XLA Ops:
  0.6 0.1 collective-permute-start.1
  0.7 2.5 %collective-permute-start = (bf16[128,1024]{1,0:T(8,128)(2,1)}, bf16[128,1024]{1,0:T(8,128)(2,1)S(1)}, u32[]{:S(2)}, u32[]{:S(2)}) collective-permute-start(bf16[128,1024]{1,0:T(8,128)(2,1)} %param.5), channel_id=1, source_target_pairs={{0,2},{1,3},{2,0},{3,1},{4,6},{5,7},{6,4},{7,5},{8,10},{9,11},{10,... | collective-permute-start | bytes 786440 | tf_op jit(solution)/shard_map/ppermute | solution.py:29
  3.2 1.2 %collective-permute-start.2 = (bf16[768,1024]{1,0:T(8,128)(2,1)}, bf16[768,1024]{1,0:T(8,128)(2,1)S(1)}, u32[]{:S(2)}, u32[]{:S(2)}) collective-permute-start(bf16[768,1024]{1,0:T(8,128)(2,1)} %param.4), channel_id=1, source_target_pairs={{0,12},{4,0},{8,4},{12,8},{1,13},{5,1},{9,5},{13,9},{2,14},{6,2},{... | collective-permute-start | bytes 4718600 | tf_op jit(solution)/shard_map/ppermute | solution.py:32
  4.4 0.7 %fusion.55 = s32[768,8]{0,1:T(8,128)S(1)} fusion(s32[768,8]{0,1:T(8,128)} %param.6, s32[768]{0:T(1024)} %param.7), kind=kLoop, calls=%fused_computation.73 | loop fusion | flops 12288 | bytes 52224 | tf_op jit(solution)/shard_map/jit(_where)/select_n | solution.py:21
  5.2 0.0 copy-start
  5.2 2.3 %fusion.54 = bf16[768,128]{0,1:T(8,128)(2,1)S(1)} fusion(bf16[128,1024]{1,0:T(8,128)(2,1)} %param.5, bf16[768,1024]{1,0:T(8,128)(2,1)} %param.4, s32[768]{0:T(1024)S(1)} %get-tuple-element.41, s32[128]{0:T(128)S(1)} %iota_add_fusion.3), kind=kOutput, calls=%fused_computation.68 | convolution fusion | flops 202014720 | bytes 2035200 | tf_op jit(solution)/shard_map/dot_general | solution.py:39
  7.5 0.0 copy-done
  7.5 0.0 copy-start.1
  7.5 0.4 fusion.56
  7.9 0.4 collective-permute-start.3
  8.4 0.1 copy-done.1
  8.5 3.3 %collective-permute-done.1 = bf16[128,1024]{1,0:T(8,128)(2,1)S(1)} collective-permute-done((bf16[128,1024]{1,0:T(8,128)(2,1)}, bf16[128,1024]{1,0:T(8,128)(2,1)S(1)}, u32[]{:S(2)}, u32[]{:S(2)}) %collective-permute-start.1) | collective-permute-done | bytes 262176 | tf_op jit(solution)/shard_map/ppermute | solution.py:29
  11.8 0.7 %fusion.53 = bf16[768,128]{0,1:T(8,128)(2,1)S(1)} fusion(bf16[128,1024]{1,0:T(8,128)(2,1)S(1)} %collective-permute-done.1, bf16[768,1024]{1,0:T(8,128)(2,1)S(1)} %copy-done, s32[768]{0:T(1024)S(1)} %get-tuple-element.40, s32[128]{0:T(128)S(1)} %iota_add_fusion.2), kind=kOutput, calls=%fused_computation.67 | convolution fusion | flops 202014720 | bytes 2035200 | tf_op jit(solution)/shard_map/dot_general | solution.py:39
  12.5 0.4 fusion.57
  12.9 1.9 %collective-permute-done = bf16[128,1024]{1,0:T(8,128)(2,1)S(1)} collective-permute-done((bf16[128,1024]{1,0:T(8,128)(2,1)}, bf16[128,1024]{1,0:T(8,128)(2,1)S(1)}, u32[]{:S(2)}, u32[]{:S(2)}) %collective-permute-start) | collective-permute-done | bytes 262176 | tf_op jit(solution)/shard_map/ppermute | solution.py:29
  14.8 0.7 %fusion.52 = bf16[768,128]{0,1:T(8,128)(2,1)S(1)} fusion(bf16[128,1024]{1,0:T(8,128)(2,1)S(1)} %collective-permute-done, bf16[768,1024]{1,0:T(8,128)(2,1)S(1)} %copy-done, s32[768]{0:T(1024)S(1)} %get-tuple-element.39, s32[128]{0:T(128)S(1)} %iota_add_fusion.1), kind=kOutput, calls=%fused_computation.66 | convolution fusion | flops 202014720 | bytes 2035200 | tf_op jit(solution)/shard_map/dot_general | solution.py:39
  15.5 0.4 fusion.58
  15.8 8.2 %collective-permute-done.3 = s32[768,8]{0,1:T(8,128)S(1)} collective-permute-done((s32[768,8]{0,1:T(8,128)S(1)}, s32[768,8]{0,1:T(8,128)S(1)}, u32[]{:S(2)}, u32[]{:S(2)}) %collective-permute-start.3) | collective-permute-done | bytes 24608 | tf_op jit(solution)/shard_map/ppermute | solution.py:32
  24.1 1.3 %collective-permute-start.5 = (bf16[128,1024]{1,0:T(8,128)(2,1)S(1)}, bf16[128,1024]{1,0:T(8,128)(2,1)S(1)}, u32[]{:S(2)}, u32[]{:S(2)}) collective-permute-start(bf16[128,1024]{1,0:T(8,128)(2,1)S(1)} %collective-permute-done), channel_id=1, source_target_pairs={{0,1},{1,0},{2,3},{3,2},{4,5},{5,4},{6,7},{7,6},{8,9},{9,8},{10,11... | collective-permute-start | bytes 786440 | tf_op jit(solution)/shard_map/ppermute | solution.py:29
  25.5 0.0 collective-permute-done.2
  25.5 0.7 %fusion.51 = bf16[768,128]{0,1:T(8,128)(2,1)S(1)} fusion(bf16[128,1024]{1,0:T(8,128)(2,1)S(1)} %copy-done.1, bf16[768,1024]{1,0:T(8,128)(2,1)S(1)} %collective-permute-done.2, s32[768]{0:T(1024)S(1)} %get-tuple-element.37, s32[128]{0:T(128)S(1)} %iota_add_fusion.3), kind=kOutput, calls=%fused_computation.65 | convolution fusion | flops 202014720 | bytes 2035200 | tf_op jit(solution)/shard_map/dot_general | solution.py:39
  26.2 0.4 fusion.3
  26.6 0.7 %fusion.50 = bf16[768,128]{0,1:T(8,128)(2,1)S(1)} fusion(bf16[128,1024]{1,0:T(8,128)(2,1)S(1)} %collective-permute-done.1, bf16[768,1024]{1,0:T(8,128)(2,1)S(1)} %collective-permute-done.2, s32[768]{0:T(1024)S(1)} %get-tuple-element.36, s32[128]{0:T(128)S(1)} %iota_add_fusion.2), kind=kOutput, calls=%fused_computation.64 | convolution fusion | flops 202014720 | bytes 2035200 | tf_op jit(solution)/shard_map/dot_general | solution.py:39
  27.3 0.4 fusion.4
  27.7 0.7 %fusion.49 = bf16[768,128]{0,1:T(8,128)(2,1)S(1)} fusion(bf16[128,1024]{1,0:T(8,128)(2,1)S(1)} %collective-permute-done, bf16[768,1024]{1,0:T(8,128)(2,1)S(1)} %collective-permute-done.2, s32[768]{0:T(1024)S(1)} %get-tuple-element.35, s32[128]{0:T(128)S(1)} %iota_add_fusion.1), kind=kOutput, calls=%fused_computation.63 | convolution fusion | flops 202014720 | bytes 2035200 | tf_op jit(solution)/shard_map/dot_general | solution.py:39
  28.4 0.4 fusion.5
  28.8 2.9 %collective-permute-done.5 = bf16[128,1024]{1,0:T(8,128)(2,1)S(1)} collective-permute-done((bf16[128,1024]{1,0:T(8,128)(2,1)S(1)}, bf16[128,1024]{1,0:T(8,128)(2,1)S(1)}, u32[]{:S(2)}, u32[]{:S(2)}) %collective-permute-start.5) | collective-permute-done | bytes 262176 | tf_op jit(solution)/shard_map/ppermute | solution.py:29
  31.7 0.7 %fusion.48 = bf16[768,128]{0,1:T(8,128)(2,1)S(1)} fusion(bf16[128,1024]{1,0:T(8,128)(2,1)S(1)} %collective-permute-done.5, bf16[768,1024]{1,0:T(8,128)(2,1)S(1)} %copy-done, s32[768]{0:T(1024)S(1)} %get-tuple-element.38, s32[128]{0:T(128)S(1)} %iota_add_fusion), kind=kOutput, calls=%fused_computation.62 | convolution fusion | flops 202014720 | bytes 2035200 | tf_op jit(solution)/shard_map/dot_general | solution.py:39
  32.4 0.4 fusion.59
  32.8 0.7 %fusion.47 = bf16[768,128]{0,1:T(8,128)(2,1)S(1)} fusion(bf16[128,1024]{1,0:T(8,128)(2,1)S(1)} %collective-permute-done.5, bf16[768,1024]{1,0:T(8,128)(2,1)S(1)} %collective-permute-done.2, s32[768]{0:T(1024)S(1)} %get-tuple-element.34, s32[128]{0:T(128)S(1)} %iota_add_fusion), kind=kOutput, calls=%fused_computation.61 | convolution fusion | flops 202014720 | bytes 2035200 | tf_op jit(solution)/shard_map/dot_general | solution.py:39
  33.5 0.1 pad_maximum_fusion.1
  33.6 0.4 fusion.6
  34.0 1.0 %convolution_convert_fusion = bf16[768,1024]{1,0:T(8,128)(2,1)S(1)} fusion(bf16[768,512]{0,1:T(8,128)(2,1)S(1)} %pad_maximum_fusion.1, bf16[512,1024]{1,0:T(8,128)(2,1)S(1)} %constant_dynamic-update-slice_fusion), kind=kOutput, calls=%fused_computation.1 | convolution fusion | flops 806092800 | bytes 3407872 | tf_op jit(solution)/shard_map/dot_general | solution.py:50
  35.0 1.3 %collective-permute-start.6 = (bf16[768,1024]{1,0:T(8,128)(2,1)S(1)}, bf16[768,1024]{1,0:T(8,128)(2,1)S(1)}, u32[]{:S(2)}, u32[]{:S(2)}) collective-permute-start(bf16[768,1024]{1,0:T(8,128)(2,1)S(1)} %convolution_convert_fusion), channel_id=1, source_target_pairs={{0,4},{4,8},{8,12},{12,0},{1,5},{5,9},{9,13},{13,1},{2,6},{6,10},{... | collective-permute-start | bytes 4718600 | tf_op jit(solution)/shard_map/ppermute | solution.py:32
  36.2 0.1 collective-permute-start.7
  36.3 1.3 %collective-permute-start.4 = (bf16[128,1024]{1,0:T(8,128)(2,1)S(1)}, bf16[128,1024]{1,0:T(8,128)(2,1)S(1)}, u32[]{:S(2)}, u32[]{:S(2)}) collective-permute-start(bf16[128,1024]{1,0:T(8,128)(2,1)S(1)} %fusion.4), channel_id=1, source_target_pairs={{0,1},{1,0},{2,3},{3,2},{4,5},{5,4},{6,7},{7,6},{8,9},{9,8},{10,11... | collective-permute-start | bytes 786440 | tf_op jit(solution)/shard_map/ppermute | solution.py:29
  37.6 1.3 %collective-permute-start.8 = (bf16[128,1024]{1,0:T(8,128)(2,1)S(1)}, bf16[128,1024]{1,0:T(8,128)(2,1)S(1)}, u32[]{:S(2)}, u32[]{:S(2)}) collective-permute-start(bf16[128,1024]{1,0:T(8,128)(2,1)S(1)} %fusion.6), channel_id=1, source_target_pairs={{0,3},{1,2},{2,1},{3,0},{4,7},{5,6},{6,5},{7,4},{8,11},{9,10},{10,... | collective-permute-start | bytes 786440 | tf_op jit(solution)/shard_map/ppermute | solution.py:29
  38.9 0.1 pad_maximum_fusion
  38.9 1.0 %fusion.60 = f32[768,1024]{1,0:T(8,128)S(1)} fusion(bf16[768,512]{0,1:T(8,128)(2,1)S(1)} %pad_maximum_fusion, bf16[512,1024]{1,0:T(8,128)(2,1)S(1)} %constant_dynamic-update-slice_fusion), kind=kOutput, calls=%fused_computation.94 | convolution fusion | flops 805306368 | bytes 4980736 | tf_op jit(solution)/shard_map/dot_general | solution.py:50
  40.0 13.6 %collective-permute-done.6 = bf16[768,1024]{1,0:T(8,128)(2,1)S(1)} collective-permute-done((bf16[768,1024]{1,0:T(8,128)(2,1)S(1)}, bf16[768,1024]{1,0:T(8,128)(2,1)S(1)}, u32[]{:S(2)}, u32[]{:S(2)}) %collective-permute-start.6) | collective-permute-done | bytes 1572896 | tf_op jit(solution)/shard_map/ppermute | solution.py:32
  53.6 1.8 %add_convert_fusion = bf16[768,1024]{1,0:T(8,128)(2,1)} fusion(f32[768,1024]{1,0:T(8,128)S(1)} %fusion.60, bf16[768,1024]{1,0:T(8,128)(2,1)S(1)} %collective-permute-done.6), kind=kLoop, calls=%fused_computation | loop fusion | flops 2359296 | bytes 6291456 | tf_op jit(solution)/shard_map/convert_element_type | solution.py:92
  55.4 6.7 %collective-permute-done.8 = bf16[128,1024]{1,0:T(8,128)(2,1)S(1)} collective-permute-done((bf16[128,1024]{1,0:T(8,128)(2,1)S(1)}, bf16[128,1024]{1,0:T(8,128)(2,1)S(1)}, u32[]{:S(2)}, u32[]{:S(2)}) %collective-permute-start.8) | collective-permute-done | bytes 262176 | tf_op jit(solution)/shard_map/ppermute | solution.py:29
  62.1 0.0 collective-permute-done.7
  62.1 0.0 collective-permute-done.4
  62.1 0.9 %add_convert_fusion.1 = bf16[128,1024]{1,0:T(8,128)(2,1)} fusion(bf16[128,1024]{1,0:T(8,128)(2,1)S(1)} %collective-permute-done.8, bf16[128,1024]{1,0:T(8,128)(2,1)S(1)} %collective-permute-done.7, f32[128,1024]{1,0:T(8,128)S(1)} %fusion.3, bf16[128,1024]{1,0:T(8,128)(2,1)S(1)} %collective-permute-done.4), kind=kLoop, calls=%fused_computation.71 | loop fusion | flops 917504 | bytes 1572864 | tf_op jit(solution)/shard_map/convert_element_type | solution.py:97
  (10 shorter events, 0.2 us)
Async XLA Ops:
  0.6 11.2 %collective-permute-start.1 = (bf16[128,1024]{1,0:T(8,128)(2,1)}, bf16[128,1024]{1,0:T(8,128)(2,1)S(1)}, u32[]{:S(2)}, u32[]{:S(2)}) collective-permute-start(bf16[128,1024]{1,0:T(8,128)(2,1)} %param.5), channel_id=1, source_target_pairs={{0,1},{1,0},{2,3},{3,2},{4,5},{5,4},{6,7},{7,6},{8,9},{9,8},{10,11... | collective-permute-start | bytes 786440 | tf_op jit(solution)/shard_map/ppermute | solution.py:29
  0.7 14.0 %collective-permute-start = (bf16[128,1024]{1,0:T(8,128)(2,1)}, bf16[128,1024]{1,0:T(8,128)(2,1)S(1)}, u32[]{:S(2)}, u32[]{:S(2)}) collective-permute-start(bf16[128,1024]{1,0:T(8,128)(2,1)} %param.5), channel_id=1, source_target_pairs={{0,2},{1,3},{2,0},{3,1},{4,6},{5,7},{6,4},{7,5},{8,10},{9,11},{10,... | collective-permute-start | bytes 786440 | tf_op jit(solution)/shard_map/ppermute | solution.py:29
  3.2 22.3 %collective-permute-start.2 = (bf16[768,1024]{1,0:T(8,128)(2,1)}, bf16[768,1024]{1,0:T(8,128)(2,1)S(1)}, u32[]{:S(2)}, u32[]{:S(2)}) collective-permute-start(bf16[768,1024]{1,0:T(8,128)(2,1)} %param.4), channel_id=1, source_target_pairs={{0,12},{4,0},{8,4},{12,8},{1,13},{5,1},{9,5},{13,9},{2,14},{6,2},{... | collective-permute-start | bytes 4718600 | tf_op jit(solution)/shard_map/ppermute | solution.py:32
  5.2 2.3 %copy-start = (bf16[768,1024]{1,0:T(8,128)(2,1)S(1)}, bf16[768,1024]{1,0:T(8,128)(2,1)}, u32[]{:S(2)}) copy-start(bf16[768,1024]{1,0:T(8,128)(2,1)} %param.4) | copy-start | bytes 4718596
  7.5 1.0 %copy-start.1 = (bf16[128,1024]{1,0:T(8,128)(2,1)S(1)}, bf16[128,1024]{1,0:T(8,128)(2,1)}, u32[]{:S(2)}) copy-start(bf16[128,1024]{1,0:T(8,128)(2,1)} %param.5) | copy-start | bytes 786436
  7.9 16.1 %collective-permute-start.3 = (s32[768,8]{0,1:T(8,128)S(1)}, s32[768,8]{0,1:T(8,128)S(1)}, u32[]{:S(2)}, u32[]{:S(2)}) collective-permute-start(s32[768,8]{0,1:T(8,128)S(1)} %fusion.55), channel_id=1, source_target_pairs={{0,12},{4,0},{8,4},{12,8},{1,13},{5,1},{9,5},{13,9},{2,14},{6,2},{... | collective-permute-start | bytes 73736 | tf_op jit(solution)/shard_map/ppermute | solution.py:32
  24.1 7.6 %collective-permute-start.5 = (bf16[128,1024]{1,0:T(8,128)(2,1)S(1)}, bf16[128,1024]{1,0:T(8,128)(2,1)S(1)}, u32[]{:S(2)}, u32[]{:S(2)}) collective-permute-start(bf16[128,1024]{1,0:T(8,128)(2,1)S(1)} %collective-permute-done), channel_id=1, source_target_pairs={{0,1},{1,0},{2,3},{3,2},{4,5},{5,4},{6,7},{7,6},{8,9},{9,8},{10,11... | collective-permute-start | bytes 786440 | tf_op jit(solution)/shard_map/ppermute | solution.py:29
  35.0 18.6 %collective-permute-start.6 = (bf16[768,1024]{1,0:T(8,128)(2,1)S(1)}, bf16[768,1024]{1,0:T(8,128)(2,1)S(1)}, u32[]{:S(2)}, u32[]{:S(2)}) collective-permute-start(bf16[768,1024]{1,0:T(8,128)(2,1)S(1)} %convolution_convert_fusion), channel_id=1, source_target_pairs={{0,4},{4,8},{8,12},{12,0},{1,5},{5,9},{9,13},{13,1},{2,6},{6,10},{... | collective-permute-start | bytes 4718600 | tf_op jit(solution)/shard_map/ppermute | solution.py:32
  36.2 25.8 %collective-permute-start.7 = (bf16[128,1024]{1,0:T(8,128)(2,1)S(1)}, bf16[128,1024]{1,0:T(8,128)(2,1)S(1)}, u32[]{:S(2)}, u32[]{:S(2)}) collective-permute-start(bf16[128,1024]{1,0:T(8,128)(2,1)S(1)} %fusion.5), channel_id=1, source_target_pairs={{0,2},{1,3},{2,0},{3,1},{4,6},{5,7},{6,4},{7,5},{8,10},{9,11},{10,... | collective-permute-start | bytes 786440 | tf_op jit(solution)/shard_map/ppermute | solution.py:29
  36.3 25.8 %collective-permute-start.4 = (bf16[128,1024]{1,0:T(8,128)(2,1)S(1)}, bf16[128,1024]{1,0:T(8,128)(2,1)S(1)}, u32[]{:S(2)}, u32[]{:S(2)}) collective-permute-start(bf16[128,1024]{1,0:T(8,128)(2,1)S(1)} %fusion.4), channel_id=1, source_target_pairs={{0,1},{1,0},{2,3},{3,2},{4,5},{5,4},{6,7},{7,6},{8,9},{9,8},{10,11... | collective-permute-start | bytes 786440 | tf_op jit(solution)/shard_map/ppermute | solution.py:29
  37.6 24.5 %collective-permute-start.8 = (bf16[128,1024]{1,0:T(8,128)(2,1)S(1)}, bf16[128,1024]{1,0:T(8,128)(2,1)S(1)}, u32[]{:S(2)}, u32[]{:S(2)}) collective-permute-start(bf16[128,1024]{1,0:T(8,128)(2,1)S(1)} %fusion.6), channel_id=1, source_target_pairs={{0,3},{1,2},{2,1},{3,0},{4,7},{5,6},{6,5},{7,4},{8,11},{9,10},{10,... | collective-permute-start | bytes 786440 | tf_op jit(solution)/shard_map/ppermute | solution.py:29

commit v7 on v6

--- a/solution.py
+++ b/solution.py
@@ -4,6 +4,9 @@
 import jax.numpy as jnp
 from jax import lax
 from jax.sharding import PartitionSpec as P
+
+CHUNKS = 1
+DIRECT_EIGHTHS = 2
 
 
 def local(embeds, weights, pos_ids, pos_count):
@@ -17,6 +20,8 @@
     slots = pos_ids.shape[1]
     span = stretch * n_label // slots
     scale = 1.0 / math.sqrt(rows_dev * n_dp)
+    run = rows_dev // CHUNKS
+    direct = ch_dev * DIRECT_EIGHTHS // 8
     valid = jnp.arange(slots, dtype=jnp.int32)[None, :] < pos_count[:, None]
     ids = jnp.where(valid, pos_ids, -1)
     last = [embeds]
@@ -48,17 +53,18 @@
 
     def grad_x_of(deltas):
         return jnp.dot(
-            in_turn(jnp.concatenate([deltas[k] for k in range(n_dp)], axis=1)),
+            in_turn(jnp.concatenate(deltas, axis=1)),
             jnp.concatenate([pieces[k] for k in range(n_dp)], axis=0),
             preferred_element_type=jnp.float32,
         )
 
-    d_own, d_next, g_own, total, moved = {}, {}, {}, {}, {}
     pieces = {0: weights}
     for k in range(1, n_dp):
         step = k & -k
         pieces[k] = to_dp(pieces[k ^ step], step)
-    next_rows = to_label(embeds, -1)
+    next_rows = [to_label(embeds[c * run:(c + 1) * run], -1) for c in range(CHUNKS)]
+    d_own, g_own = {}, {}
+    d_next = [{} for _ in range(CHUNKS)]
 
     def own_step(k):
         pieces[k] = in_turn(pieces[k])
@@ -66,35 +72,56 @@
         g_own[k] = grad_w_of(d_own[k], embeds)
         last[0] = g_own[k]
 
-    def next_step(k):
-        d_next[k] = delta_of(next_rows, next_ids, in_turn(pieces[k]), k)
-        total[k] = (g_own[k] + grad_w_of(d_next[k], next_rows)) * scale
-        if k > 0:
-            total[k] = total[k].astype(jnp.bfloat16)
-            moved[k] = to_dp(total[k], k)
-        last[0] = total[k]
+    def next_step(c, k):
+        d_next[c][k] = delta_of(next_rows[c], next_ids[c * run:(c + 1) * run], in_turn(pieces[k]), k)
+        g_own[k] = g_own[k] + grad_w_of(d_next[c][k], next_rows[c])
+        last[0] = g_own[k]
 
     own_step(0)
     next_ids = to_label(in_turn(ids), -1)
-    for k in range(1, n_dp - 1):
+    for k in range(1, n_dp):
         own_step(k)
     next_ids = in_turn(next_ids)
-    for k in range(n_dp - 1):
-        next_step(k)
-    if n_dp > 1:
-        own_step(n_dp - 1)
-        next_step(n_dp - 1)
-    theirs = grad_x_of(d_next).astype(jnp.bfloat16)
-    last[0] = theirs
-    back = to_label(theirs, 1)
-    grad_x = grad_x_of(d_own)
+    for c in range(CHUNKS):
+        for k in range(n_dp - 1, -1, -1):
+            next_step(c, k)
+    theirs = [grad_x_of([d_next[c][k] for k in range(n_dp)]).astype(jnp.bfloat16) for c in range(CHUNKS)]
+    last[0] = theirs[-1]
+    back = [to_label(t, 1) for t in theirs]
+
+    relayed, moved, low, high = {}, [], [], []
+    for k in range(n_dp - 1, 0, -1):
+        step = k & -k
+        whole = g_own[k] * scale
+        if step == k and k not in relayed:
+            moved.append(to_dp(whole.astype(jnp.bfloat16), k))
+            continue
+        part = whole[direct:]
+        for term in relayed.get(k, ()):
+            part = part + term.astype(jnp.float32)
+        part = part.astype(jnp.bfloat16)
+        last[0] = part
+        if step == k:
+            high.append(to_dp(part, k))
+        else:
+            relayed.setdefault(k ^ step, []).append(in_turn(to_dp(part, step)))
+        low.append(to_dp(whole[:direct].astype(jnp.bfloat16), k))
+    grad_x = grad_x_of([d_own[k] for k in range(n_dp)])
     last[0] = grad_x
-    grad_x = (grad_x + in_turn(back).astype(jnp.float32)).astype(jnp.bfloat16)
-    last[0] = grad_x
-    grad_w = total[0]
-    for k in range(1, n_dp):
-        grad_w = grad_w + in_turn(moved[k]).astype(jnp.float32)
-    return (grad_w.astype(jnp.bfloat16), grad_x)
+    grad_w = g_own[0] * scale
+    for term in moved:
+        grad_w = grad_w + in_turn(term).astype(jnp.float32)
+    if high:
+        rest, grad_w = grad_w[:direct], grad_w[direct:]
+        for term in low:
+            rest = rest + in_turn(term).astype(jnp.float32)
+        for term in high:
+            grad_w = grad_w + in_turn(term).astype(jnp.float32)
+        grad_w = jnp.concatenate([rest, grad_w], axis=0)
+    grad_w = grad_w.astype(jnp.bfloat16)
+    last[0] = grad_w
+    grad_x = (grad_x + jnp.concatenate([in_turn(b) for b in back], axis=0).astype(jnp.float32)).astype(jnp.bfloat16)
+    return (grad_w, grad_x)
 
 
 def solution(mesh):

time: 63.1 us -> 55.6 us (0.88)
  the two profiles are of different devices: /device:TPU:9 before, /device:TPU:0 now
where the time goes in v7:
time: 55.6 us; the launch traced here: 55.4 us
  waiting for transfers between devices  21.8 us (39%)
  starting transfers between devices  16.6 us (30%)
  matrix products  12.3 us (22%)
  other arithmetic  3.52 us (6%)
  between operations  0.93 us (2%)
    ppermute x8, waiting for transfers between devices, to_dp(): return lax.ppermute(x, 'dp', [(i, i ^ k) for i in range(n_dp)])  21 us
    ppermute x8, starting transfers between devices, to_dp(): return lax.ppermute(x, 'dp', [(i, i ^ k) for i in range(n_dp)])  14.9 us
    dot_general x8, matrix products, delta_of(): lax.dot_general(rows, piece, (((1,), (1,)), ((), ())), preferred_element_...  7.22 us
    dot_general x8, matrix products, grad_w_of(): lax.dot_general(delta, rows, (((0,), (0,)), ((), ())), preferred_element_...  3.06 us
    dot_general x2, matrix products, grad_x_of(): jnp.dot(in_turn(jnp.concatenate(deltas, axis=1)), jnp.concatenate([pieces...  2.02 us
    convert_element_type x1, other arithmetic, local(): (grad_x + jnp.concatenate([in_turn(b) for b in back], axis=0).astype(jnp....  1.75 us
    ppermute x3, starting transfers between devices, to_label(): lax.ppermute(x, 'label', [(i, (i + by) % n_label) for i in range(n_label)])  1.72 us
  transfers between devices with their start and end apart: 11, of which 5 were waited for; matrix products, arithmetic and copies ran while one was open for 24% of the time, Pallas kernels for 0%

profile of v7, /device:TPU:0, one launch (start us, length us, event | category | flops | bytes accessed | tf_op | source)
XLA Modules:
  0.0 55.4 jit_solution(8287648586503622135)
XLA Ops:
  0.6 4.1 %collective-permute-start.1 = (bf16[128,1024]{1,0:T(8,128)(2,1)}, bf16[128,1024]{1,0:T(8,128)(2,1)S(1)}, u32[]{:S(2)}, u32[]{:S(2)}) collective-permute-start(bf16[128,1024]{1,0:T(8,128)(2,1)} %param.5), channel_id=1, source_target_pairs={{0,2},{1,3},{2,0},{3,1},{4,6},{5,7},{6,4},{7,5},{8,10},{9,11},{10,... | collective-permute-start | bytes 786440 | tf_op jit(solution)/shard_map/ppermute | solution.py:34
  4.7 1.6 %collective-permute-start = (bf16[128,1024]{1,0:T(8,128)(2,1)}, bf16[128,1024]{1,0:T(8,128)(2,1)S(1)}, u32[]{:S(2)}, u32[]{:S(2)}) collective-permute-start(bf16[128,1024]{1,0:T(8,128)(2,1)} %param.5), channel_id=1, source_target_pairs={{0,1},{1,0},{2,3},{3,2},{4,5},{5,4},{6,7},{7,6},{8,9},{9,8},{10,11... | collective-permute-start | bytes 786440 | tf_op jit(solution)/shard_map/ppermute | solution.py:34
  6.3 0.4 collective-permute-start.3
  6.7 0.7 %fusion.52 = s32[768,8]{0,1:T(8,128)S(1)} fusion(s32[768,8]{0,1:T(8,128)} %param.6, s32[768]{0:T(1024)} %param.7), kind=kLoop, calls=%fused_computation.78 | loop fusion | flops 12288 | bytes 52224 | tf_op jit(solution)/shard_map/jit(_where)/select_n | solution.py:26
  7.5 0.0 copy-start
  7.5 2.3 %fusion.47 = bf16[768,128]{0,1:T(8,128)(2,1)S(1)} fusion(bf16[128,1024]{1,0:T(8,128)(2,1)} %param.5, bf16[768,1024]{1,0:T(8,128)(2,1)} %param.4, s32[768]{0:T(1024)S(1)} %get-tuple-element.45, s32[128]{0:T(128)S(1)} %iota_add_fusion.3), kind=kOutput, calls=%fused_computation.61 | convolution fusion | flops 202014720 | bytes 2035200 | tf_op jit(solution)/shard_map/dot_general | solution.py:44
  9.8 0.0 copy-done
  9.8 0.0 copy-start.1
  9.8 0.4 fusion.53
  10.2 1.3 %collective-permute-start.4 = (s32[768,8]{0,1:T(8,128)S(1)}, s32[768,8]{0,1:T(8,128)S(1)}, u32[]{:S(2)}, u32[]{:S(2)}) collective-permute-start(s32[768,8]{0,1:T(8,128)S(1)} %fusion.52), channel_id=1, source_target_pairs={{0,12},{4,0},{8,4},{12,8},{1,13},{5,1},{9,5},{13,9},{2,14},{6,2},{... | collective-permute-start | bytes 73736 | tf_op jit(solution)/shard_map/ppermute | solution.py:37
  11.5 0.0 copy-done.1
  11.5 5.6 %collective-permute-done = bf16[128,1024]{1,0:T(8,128)(2,1)S(1)} collective-permute-done((bf16[128,1024]{1,0:T(8,128)(2,1)}, bf16[128,1024]{1,0:T(8,128)(2,1)S(1)}, u32[]{:S(2)}, u32[]{:S(2)}) %collective-permute-start) | collective-permute-done | bytes 262176 | tf_op jit(solution)/shard_map/ppermute | solution.py:34
  17.2 0.7 %fusion.46 = bf16[768,128]{0,1:T(8,128)(2,1)S(1)} fusion(bf16[128,1024]{1,0:T(8,128)(2,1)S(1)} %collective-permute-done, bf16[768,1024]{1,0:T(8,128)(2,1)S(1)} %copy-done, s32[768]{0:T(1024)S(1)} %get-tuple-element.44, s32[128]{0:T(128)S(1)} %iota_add_fusion.2), kind=kOutput, calls=%fused_computation.60 | convolution fusion | flops 202014720 | bytes 2035200 | tf_op jit(solution)/shard_map/dot_general | solution.py:44
  17.9 0.4 fusion.54
  18.3 0.0 collective-permute-done.1
  18.3 1.6 %collective-permute-start.2 = (bf16[128,1024]{1,0:T(8,128)(2,1)S(1)}, bf16[128,1024]{1,0:T(8,128)(2,1)S(1)}, u32[]{:S(2)}, u32[]{:S(2)}) collective-permute-start(bf16[128,1024]{1,0:T(8,128)(2,1)S(1)} %collective-permute-done.1), channel_id=1, source_target_pairs={{0,1},{1,0},{2,3},{3,2},{4,5},{5,4},{6,7},{7,6},{8,9},{9,8},{10,11... | collective-permute-start | bytes 786440 | tf_op jit(solution)/shard_map/ppermute | solution.py:34
  19.9 0.7 %fusion.45 = bf16[768,128]{0,1:T(8,128)(2,1)S(1)} fusion(bf16[128,1024]{1,0:T(8,128)(2,1)S(1)} %collective-permute-done.1, bf16[768,1024]{1,0:T(8,128)(2,1)S(1)} %copy-done, s32[768]{0:T(1024)S(1)} %get-tuple-element.43, s32[128]{0:T(128)S(1)} %iota_add_fusion.1), kind=kOutput, calls=%fused_computation.59 | convolution fusion | flops 202014720 | bytes 2035200 | tf_op jit(solution)/shard_map/dot_general | solution.py:44
  20.6 0.4 fusion.55
  21.0 4.3 %collective-permute-done.2 = bf16[128,1024]{1,0:T(8,128)(2,1)S(1)} collective-permute-done((bf16[128,1024]{1,0:T(8,128)(2,1)S(1)}, bf16[128,1024]{1,0:T(8,128)(2,1)S(1)}, u32[]{:S(2)}, u32[]{:S(2)}) %collective-permute-start.2) | collective-permute-done | bytes 262176 | tf_op jit(solution)/shard_map/ppermute | solution.py:34
  25.2 0.7 %fusion.44 = bf16[768,128]{0,1:T(8,128)(2,1)S(1)} fusion(bf16[128,1024]{1,0:T(8,128)(2,1)S(1)} %collective-permute-done.2, bf16[768,1024]{1,0:T(8,128)(2,1)S(1)} %copy-done, s32[768]{0:T(1024)S(1)} %get-tuple-element.42, s32[128]{0:T(128)S(1)} %iota_add_fusion), kind=kOutput, calls=%fused_computation.58 | convolution fusion | flops 202014720 | bytes 2035200 | tf_op jit(solution)/shard_map/dot_general | solution.py:44
  26.0 0.4 fusion.56
  26.3 0.0 collective-permute-done.4
  26.4 0.0 collective-permute-done.3
  26.4 0.7 %fusion.43 = bf16[768,128]{0,1:T(8,128)(2,1)S(1)} fusion(bf16[128,1024]{1,0:T(8,128)(2,1)S(1)} %collective-permute-done.2, bf16[768,1024]{1,0:T(8,128)(2,1)S(1)} %collective-permute-done.3, s32[768]{0:T(1024)S(1)} %get-tuple-element.41, s32[128]{0:T(128)S(1)} %iota_add_fusion), kind=kOutput, calls=%fused_computation.57 | convolution fusion | flops 202014720 | bytes 2035200 | tf_op jit(solution)/shard_map/dot_general | solution.py:44
  27.2 0.4 multiply_convert_fusion
  27.6 1.8 %collective-permute-start.6 = (bf16[96,1024]{1,0:T(8,128)(2,1)S(1)}, bf16[96,1024]{1,0:T(8,128)(2,1)S(1)}, u32[]{:S(2)}, u32[]{:S(2)}) collective-permute-start(bf16[96,1024]{1,0:T(8,128)(2,1)S(1)} %slice.28), channel_id=1, source_target_pairs={{0,1},{1,0},{2,3},{3,2},{4,5},{5,4},{6,7},{7,6},{8,9},{9,8},{10,11... | collective-permute-start | bytes 589832 | tf_op jit(solution)/shard_map/ppermute | solution.py:34
  29.4 0.7 %fusion.42 = bf16[768,128]{0,1:T(8,128)(2,1)S(1)} fusion(bf16[128,1024]{1,0:T(8,128)(2,1)S(1)} %collective-permute-done.1, bf16[768,1024]{1,0:T(8,128)(2,1)S(1)} %collective-permute-done.3, s32[768]{0:T(1024)S(1)} %get-tuple-element.40, s32[128]{0:T(128)S(1)} %iota_add_fusion.1), kind=kOutput, calls=%fused_computation.56 | convolution fusion | flops 202014720 | bytes 2035200 | tf_op jit(solution)/shard_map/dot_general | solution.py:44
  30.1 0.4 broadcast_multiply_fusion
  30.5 0.7 %fusion.41 = bf16[768,128]{0,1:T(8,128)(2,1)S(1)} fusion(bf16[128,1024]{1,0:T(8,128)(2,1)S(1)} %collective-permute-done, bf16[768,1024]{1,0:T(8,128)(2,1)S(1)} %collective-permute-done.3, s32[768]{0:T(1024)S(1)} %get-tuple-element.39, s32[128]{0:T(128)S(1)} %iota_add_fusion.2), kind=kOutput, calls=%fused_computation.55 | convolution fusion | flops 202014720 | bytes 2035200 | tf_op jit(solution)/shard_map/dot_general | solution.py:44
  31.2 0.4 multiply_convert_fusion.1
  31.6 0.7 %fusion.40 = bf16[768,128]{0,1:T(8,128)(2,1)S(1)} fusion(bf16[128,1024]{1,0:T(8,128)(2,1)S(1)} %copy-done.1, bf16[768,1024]{1,0:T(8,128)(2,1)S(1)} %collective-permute-done.3, s32[768]{0:T(1024)S(1)} %get-tuple-element.38, s32[128]{0:T(128)S(1)} %iota_add_fusion.3), kind=kOutput, calls=%fused_computation.54 | convolution fusion | flops 202014720 | bytes 2035200 | tf_op jit(solution)/shard_map/dot_general | solution.py:44
  32.3 0.1 pad_maximum_fusion.1
  32.4 0.4 convolution_add_fusion
  32.8 1.0 %convolution_convert_fusion = bf16[768,1024]{1,0:T(8,128)(2,1)S(1)} fusion(bf16[768,512]{0,1:T(8,128)(2,1)S(1)} %pad_maximum_fusion.1, bf16[512,1024]{1,0:T(8,128)(2,1)S(1)} %constant_dynamic-update-slice_fusion), kind=kOutput, calls=%fused_computation.1 | convolution fusion | flops 806092800 | bytes 3407872 | tf_op jit(solution)/shard_map/dot_general | solution.py:55
  33.8 0.1 collective-permute-start.10
  33.8 0.1 pad_maximum_fusion
  33.9 2.0 %collective-permute-start.7 = (bf16[32,1024]{1,0:T(8,128)(2,1)S(1)}, bf16[32,1024]{1,0:T(8,128)(2,1)S(1)}, u32[]{:S(2)}, u32[]{:S(2)}) collective-permute-start(bf16[32,1024]{1,0:T(8,128)(2,1)S(1)} %slice.30), channel_id=1, source_target_pairs={{0,3},{1,2},{2,1},{3,0},{4,7},{5,6},{6,5},{7,4},{8,11},{9,10},{10,... | collective-permute-start | bytes 196616 | tf_op jit(solution)/shard_map/ppermute | solution.py:34
  35.9 0.4 collective-permute-start.8
  36.3 2.2 %collective-permute-start.5 = (bf16[128,1024]{1,0:T(8,128)(2,1)S(1)}, bf16[128,1024]{1,0:T(8,128)(2,1)S(1)}, u32[]{:S(2)}, u32[]{:S(2)}) collective-permute-start(bf16[128,1024]{1,0:T(8,128)(2,1)S(1)} %multiply_convert_fusion.1), channel_id=1, source_target_pairs={{0,1},{1,0},{2,3},{3,2},{4,5},{5,4},{6,7},{7,6},{8,9},{9,8},{10,11... | collective-permute-start | bytes 786440 | tf_op jit(solution)/shard_map/ppermute | solution.py:34
  38.4 0.0 collective-permute-done.6
  38.5 1.4 %collective-permute-start.9 = (bf16[96,1024]{1,0:T(8,128)(2,1)S(1)}, bf16[96,1024]{1,0:T(8,128)(2,1)S(1)}, u32[]{:S(2)}, u32[]{:S(2)}) collective-permute-start(bf16[96,1024]{1,0:T(8,128)(2,1)S(1)} %fusion.49), channel_id=1, source_target_pairs={{0,2},{1,3},{2,0},{3,1},{4,6},{5,7},{6,4},{7,5},{8,10},{9,11},{10,... | collective-permute-start | bytes 589832 | tf_op jit(solution)/shard_map/ppermute | solution.py:34
  39.9 1.0 %fusion.57 = f32[768,1024]{1,0:T(8,128)S(1)} fusion(bf16[768,512]{0,1:T(8,128)(2,1)S(1)} %pad_maximum_fusion, bf16[512,1024]{1,0:T(8,128)(2,1)S(1)} %constant_dynamic-update-slice_fusion), kind=kOutput, calls=%fused_computation.99 | convolution fusion | flops 805306368 | bytes 4980736 | tf_op jit(solution)/shard_map/dot_general | solution.py:55
  40.9 2.7 %collective-permute-done.8 = bf16[32,1024]{1,0:T(8,128)(2,1)S(1)} collective-permute-done((bf16[32,1024]{1,0:T(8,128)(2,1)S(1)}, bf16[32,1024]{1,0:T(8,128)(2,1)S(1)}, u32[]{:S(2)}, u32[]{:S(2)}) %collective-permute-start.8) | collective-permute-done | bytes 65568 | tf_op jit(solution)/shard_map/ppermute | solution.py:34
  43.6 0.0 collective-permute-done.7
  43.6 8.3 %collective-permute-done.5 = bf16[128,1024]{1,0:T(8,128)(2,1)S(1)} collective-permute-done((bf16[128,1024]{1,0:T(8,128)(2,1)S(1)}, bf16[128,1024]{1,0:T(8,128)(2,1)S(1)}, u32[]{:S(2)}, u32[]{:S(2)}) %collective-permute-start.5) | collective-permute-done | bytes 262176 | tf_op jit(solution)/shard_map/ppermute | solution.py:34
  51.9 0.1 convert_add_fusion
  52.1 0.0 collective-permute-done.9
  52.1 0.1 fusion.48
  52.1 0.7 %pad_maximum_fusion.2 = bf16[128,1024]{1,0:T(8,128)(2,1)} fusion(bf16[96,1024]{1,0:T(8,128)(2,1)S(1)} %fusion.48, bf16[32,1024]{1,0:T(8,128)(2,1)S(1)} %fusion.51), kind=kLoop, calls=%fused_computation.71 | loop fusion | flops 524288 | bytes 524288 | tf_op jit(solution)/shard_map/concatenate | solution.py:120
  52.8 0.8 %collective-permute-done.10 = bf16[768,1024]{1,0:T(8,128)(2,1)S(1)} collective-permute-done((bf16[768,1024]{1,0:T(8,128)(2,1)S(1)}, bf16[768,1024]{1,0:T(8,128)(2,1)S(1)}, u32[]{:S(2)}, u32[]{:S(2)}) %collective-permute-start.10) | collective-permute-done | bytes 1572896 | tf_op jit(solution)/shard_map/ppermute | solution.py:37
  53.7 1.8 %add_convert_fusion = bf16[768,1024]{1,0:T(8,128)(2,1)} fusion(f32[768,1024]{1,0:T(8,128)S(1)} %fusion.57, bf16[768,1024]{1,0:T(8,128)(2,1)S(1)} %collective-permute-done.10), kind=kLoop, calls=%fused_computation | loop fusion | flops 2359296 | bytes 6291456 | tf_op jit(solution)/shard_map/convert_element_type | solution.py:123
  (15 shorter events, 0.3 us)
Async XLA Ops:
  0.6 17.6 %collective-permute-start.1 = (bf16[128,1024]{1,0:T(8,128)(2,1)}, bf16[128,1024]{1,0:T(8,128)(2,1)S(1)}, u32[]{:S(2)}, u32[]{:S(2)}) collective-permute-start(bf16[128,1024]{1,0:T(8,128)(2,1)} %param.5), channel_id=1, source_target_pairs={{0,2},{1,3},{2,0},{3,1},{4,6},{5,7},{6,4},{7,5},{8,10},{9,11},{10,... | collective-permute-start | bytes 786440 | tf_op jit(solution)/shard_map/ppermute | solution.py:34
  4.7 12.4 %collective-permute-start = (bf16[128,1024]{1,0:T(8,128)(2,1)}, bf16[128,1024]{1,0:T(8,128)(2,1)S(1)}, u32[]{:S(2)}, u32[]{:S(2)}) collective-permute-start(bf16[128,1024]{1,0:T(8,128)(2,1)} %param.5), channel_id=1, source_target_pairs={{0,1},{1,0},{2,3},{3,2},{4,5},{5,4},{6,7},{7,6},{8,9},{9,8},{10,11... | collective-permute-start | bytes 786440 | tf_op jit(solution)/shard_map/ppermute | solution.py:34
  6.3 20.1 %collective-permute-start.3 = (bf16[768,1024]{1,0:T(8,128)(2,1)}, bf16[768,1024]{1,0:T(8,128)(2,1)S(1)}, u32[]{:S(2)}, u32[]{:S(2)}) collective-permute-start(bf16[768,1024]{1,0:T(8,128)(2,1)} %param.4), channel_id=1, source_target_pairs={{0,12},{4,0},{8,4},{12,8},{1,13},{5,1},{9,5},{13,9},{2,14},{6,2},{... | collective-permute-start | bytes 4718600 | tf_op jit(solution)/shard_map/ppermute | solution.py:37
  7.5 2.3 %copy-start = (bf16[768,1024]{1,0:T(8,128)(2,1)S(1)}, bf16[768,1024]{1,0:T(8,128)(2,1)}, u32[]{:S(2)}) copy-start(bf16[768,1024]{1,0:T(8,128)(2,1)} %param.4) | copy-start | bytes 4718596
  9.8 1.7 %copy-start.1 = (bf16[128,1024]{1,0:T(8,128)(2,1)S(1)}, bf16[128,1024]{1,0:T(8,128)(2,1)}, u32[]{:S(2)}) copy-start(bf16[128,1024]{1,0:T(8,128)(2,1)} %param.5) | copy-start | bytes 786436
  10.2 16.1 %collective-permute-start.4 = (s32[768,8]{0,1:T(8,128)S(1)}, s32[768,8]{0,1:T(8,128)S(1)}, u32[]{:S(2)}, u32[]{:S(2)}) collective-permute-start(s32[768,8]{0,1:T(8,128)S(1)} %fusion.52), channel_id=1, source_target_pairs={{0,12},{4,0},{8,4},{12,8},{1,13},{5,1},{9,5},{13,9},{2,14},{6,2},{... | collective-permute-start | bytes 73736 | tf_op jit(solution)/shard_map/ppermute | solution.py:37
  18.3 7.0 %collective-permute-start.2 = (bf16[128,1024]{1,0:T(8,128)(2,1)S(1)}, bf16[128,1024]{1,0:T(8,128)(2,1)S(1)}, u32[]{:S(2)}, u32[]{:S(2)}) collective-permute-start(bf16[128,1024]{1,0:T(8,128)(2,1)S(1)} %collective-permute-done.1), channel_id=1, source_target_pairs={{0,1},{1,0},{2,3},{3,2},{4,5},{5,4},{6,7},{7,6},{8,9},{9,8},{10,11... | collective-permute-start | bytes 786440 | tf_op jit(solution)/shard_map/ppermute | solution.py:34
  27.6 10.9 %collective-permute-start.6 = (bf16[96,1024]{1,0:T(8,128)(2,1)S(1)}, bf16[96,1024]{1,0:T(8,128)(2,1)S(1)}, u32[]{:S(2)}, u32[]{:S(2)}) collective-permute-start(bf16[96,1024]{1,0:T(8,128)(2,1)S(1)} %slice.28), channel_id=1, source_target_pairs={{0,1},{1,0},{2,3},{3,2},{4,5},{5,4},{6,7},{7,6},{8,9},{9,8},{10,11... | collective-permute-start | bytes 589832 | tf_op jit(solution)/shard_map/ppermute | solution.py:34
  33.8 19.9 %collective-permute-start.10 = (bf16[768,1024]{1,0:T(8,128)(2,1)S(1)}, bf16[768,1024]{1,0:T(8,128)(2,1)S(1)}, u32[]{:S(2)}, u32[]{:S(2)}) collective-permute-start(bf16[768,1024]{1,0:T(8,128)(2,1)S(1)} %convolution_convert_fusion), channel_id=1, source_target_pairs={{0,4},{4,8},{8,12},{12,0},{1,5},{5,9},{9,13},{13,1},{2,6},{6,10},{... | collective-permute-start | bytes 4718600 | tf_op jit(solution)/shard_map/ppermute | solution.py:37
  33.9 9.7 %collective-permute-start.7 = (bf16[32,1024]{1,0:T(8,128)(2,1)S(1)}, bf16[32,1024]{1,0:T(8,128)(2,1)S(1)}, u32[]{:S(2)}, u32[]{:S(2)}) collective-permute-start(bf16[32,1024]{1,0:T(8,128)(2,1)S(1)} %slice.30), channel_id=1, source_target_pairs={{0,3},{1,2},{2,1},{3,0},{4,7},{5,6},{6,5},{7,4},{8,11},{9,10},{10,... | collective-permute-start | bytes 196616 | tf_op jit(solution)/shard_map/ppermute | solution.py:34
  35.9 7.7 %collective-permute-start.8 = (bf16[32,1024]{1,0:T(8,128)(2,1)S(1)}, bf16[32,1024]{1,0:T(8,128)(2,1)S(1)}, u32[]{:S(2)}, u32[]{:S(2)}) collective-permute-start(bf16[32,1024]{1,0:T(8,128)(2,1)S(1)} %slice.45), channel_id=1, source_target_pairs={{0,2},{1,3},{2,0},{3,1},{4,6},{5,7},{6,4},{7,5},{8,10},{9,11},{10,... | collective-permute-start | bytes 196616 | tf_op jit(solution)/shard_map/ppermute | solution.py:34
  36.3 15.7 %collective-permute-start.5 = (bf16[128,1024]{1,0:T(8,128)(2,1)S(1)}, bf16[128,1024]{1,0:T(8,128)(2,1)S(1)}, u32[]{:S(2)}, u32[]{:S(2)}) collective-permute-start(bf16[128,1024]{1,0:T(8,128)(2,1)S(1)} %multiply_convert_fusion.1), channel_id=1, source_target_pairs={{0,1},{1,0},{2,3},{3,2},{4,5},{5,4},{6,7},{7,6},{8,9},{9,8},{10,11... | collective-permute-start | bytes 786440 | tf_op jit(solution)/shard_map/ppermute | solution.py:34
  38.5 13.6 %collective-permute-start.9 = (bf16[96,1024]{1,0:T(8,128)(2,1)S(1)}, bf16[96,1024]{1,0:T(8,128)(2,1)S(1)}, u32[]{:S(2)}, u32[]{:S(2)}) collective-permute-start(bf16[96,1024]{1,0:T(8,128)(2,1)S(1)} %fusion.49), channel_id=1, source_target_pairs={{0,2},{1,3},{2,0},{3,1},{4,6},{5,7},{6,4},{7,5},{8,10},{9,11},{10,... | collective-permute-start | bytes 589832 | tf_op jit(solution)/shard_map/ppermute | solution.py:34

commit v8 on v7

--- a/solution.py
+++ b/solution.py
@@ -5,7 +5,7 @@
 from jax import lax
 from jax.sharding import PartitionSpec as P
 
-CHUNKS = 1
+FIRST_RUN_THIRDS = 2
 DIRECT_EIGHTHS = 2
 
 
@@ -20,7 +20,8 @@
     slots = pos_ids.shape[1]
     span = stretch * n_label // slots
     scale = 1.0 / math.sqrt(rows_dev * n_dp)
-    run = rows_dev // CHUNKS
+    cut = rows_dev * FIRST_RUN_THIRDS // 3
+    runs = [slice(0, cut), slice(cut, rows_dev)]
     direct = ch_dev * DIRECT_EIGHTHS // 8
     valid = jnp.arange(slots, dtype=jnp.int32)[None, :] < pos_count[:, None]
     ids = jnp.where(valid, pos_ids, -1)
@@ -62,9 +63,9 @@
     for k in range(1, n_dp):
         step = k & -k
         pieces[k] = to_dp(pieces[k ^ step], step)
-    next_rows = [to_label(embeds[c * run:(c + 1) * run], -1) for c in range(CHUNKS)]
+    next_rows = [to_label(embeds[runs[0]], -1)]
     d_own, g_own = {}, {}
-    d_next = [{} for _ in range(CHUNKS)]
+    d_next = [{} for _ in runs]
 
     def own_step(k):
         pieces[k] = in_turn(pieces[k])
@@ -73,21 +74,30 @@
         last[0] = g_own[k]
 
     def next_step(c, k):
-        d_next[c][k] = delta_of(next_rows[c], next_ids[c * run:(c + 1) * run], in_turn(pieces[k]), k)
+        d_next[c][k] = delta_of(next_rows[c], next_ids[runs[c]], in_turn(pieces[k]), k)
         g_own[k] = g_own[k] + grad_w_of(d_next[c][k], next_rows[c])
         last[0] = g_own[k]
 
-    own_step(0)
-    next_ids = to_label(in_turn(ids), -1)
-    for k in range(1, n_dp):
+    def send_back(c):
+        theirs = grad_x_of([d_next[c][k] for k in range(n_dp)]).astype(jnp.bfloat16)
+        last[0] = theirs
+        return to_label(theirs, 1)
+
+    next_ids = to_label(ids, -1)
+    for k in [*range(1, min(2, n_dp)), 0, *range(2, n_dp - 1)]:
         own_step(k)
+        if len(next_rows) < len(runs):
+            next_rows.append(to_label(in_turn(embeds)[runs[1]], -1))
     next_ids = in_turn(next_ids)
-    for c in range(CHUNKS):
-        for k in range(n_dp - 1, -1, -1):
-            next_step(c, k)
-    theirs = [grad_x_of([d_next[c][k] for k in range(n_dp)]).astype(jnp.bfloat16) for c in range(CHUNKS)]
-    last[0] = theirs[-1]
-    back = [to_label(t, 1) for t in theirs]
+    for k in range(n_dp - 2, -1, -1):
+        next_step(0, k)
+    if n_dp > 1:
+        own_step(n_dp - 1)
+        next_step(0, n_dp - 1)
+    back = [send_back(0)]
+    for k in range(n_dp - 1, -1, -1):
+        next_step(1, k)
+    back.append(send_back(1))
 
     relayed, moved, low, high = {}, [], [], []
     for k in range(n_dp - 1, 0, -1):
@@ -115,12 +125,18 @@
         rest, grad_w = grad_w[:direct], grad_w[direct:]
         for term in low:
             rest = rest + in_turn(term).astype(jnp.float32)
+        last[0] = rest
+    first = jnp.pad(in_turn(back[0]), ((0, rows_dev - cut), (0, 0)))
+    out_x = (grad_x + first.astype(jnp.float32)).astype(jnp.bfloat16)
+    last[0] = out_x
+    if high:
         for term in high:
             grad_w = grad_w + in_turn(term).astype(jnp.float32)
         grad_w = jnp.concatenate([rest, grad_w], axis=0)
     grad_w = grad_w.astype(jnp.bfloat16)
     last[0] = grad_w
-    grad_x = (grad_x + jnp.concatenate([in_turn(b) for b in back], axis=0).astype(jnp.float32)).astype(jnp.bfloat16)
+    second = (grad_x[cut:] + in_turn(back[1]).astype(jnp.float32)).astype(jnp.bfloat16)
+    grad_x = lax.dynamic_update_slice_in_dim(out_x, second, cut, axis=0)
     return (grad_w, grad_x)
 
 

time: 55.6 us -> 60.6 us (1.090)
  waiting for transfers between devices: 21.8 us -> 27.3 us
  local copies, waits for them, and re-layouts: 0.2 us -> 4.18 us
  starting transfers between devices: 16.6 us -> 13.3 us
  other arithmetic: 3.52 us -> 2.35 us
    ppermute x8, starting transfers between devices: 14.9 us -> 11 us  [to_dp(): return lax.ppermute(x, 'dp', [(i, i ^ k) for i in range(n_dp)])]
    ppermute x8, waiting for transfers between devices: 21 us -> 23.8 us  [to_dp(): return lax.ppermute(x, 'dp', [(i, i ^ k) for i in range(n_dp)])]
    ppermute x3 -> x5, waiting for transfers between devices: 0.83 us -> 3.45 us  [to_label(): lax.ppermute(x, 'label', [(i, (i + by) % n_label) for i in range(n_label)])]
    slice x0 -> x4, local copies, waits for them, and re-layouts: none -> 2.3 us  [the longest x1 2.26 us: local(): next_rows = [to_label(embeds[runs[0]], -1)]]
    unnamed x7 -> x9, local copies, waits for them, and re-layouts: 0.07 us -> 1.76 us
    convert_element_type x1, other arithmetic: 1.75 us -> 0.44 us  [local(): out_x = (grad_x + first.astype(jnp.float32)).astype(jnp.bfloat16)]
    dot_general x8 -> x12, matrix products: 7.22 us -> 6.25 us  [delta_of(): lax.dot_general(rows, piece, (((1,), (1,)), ((), ())), preferred_element_...]
    dot_general x8 -> x12, matrix products: 3.06 us -> 3.77 us  [grad_w_of(): lax.dot_general(delta, rows, (((0,), (0,)), ((), ())), preferred_element_...]
  transfers between devices with their start and end apart: 11 -> 13, of which waited for: 5 -> 6; matrix products, arithmetic and copies ran while one was open for 24% -> 27% of each run, Pallas kernels for 0% -> 0%
where the time goes in v8:
time: 60.6 us; the launch traced here: 60.4 us
  waiting for transfers between devices  27.3 us (45%)
  starting transfers between devices  13.3 us (22%)
  matrix products  12.2 us (20%)
  local copies, waits for them, and re-layouts  4.18 us (7%)
  other arithmetic  2.35 us (4%)
  between operations  1.06 us (2%)
    ppermute x8, waiting for transfers between devices, to_dp(): return lax.ppermute(x, 'dp', [(i, i ^ k) for i in range(n_dp)])  23.8 us
    ppermute x8, starting transfers between devices, to_dp(): return lax.ppermute(x, 'dp', [(i, i ^ k) for i in range(n_dp)])  11 us
    dot_general x12, matrix products, delta_of(): lax.dot_general(rows, piece, (((1,), (1,)), ((), ())), preferred_element_...  6.25 us
    dot_general x12, matrix products, grad_w_of(): lax.dot_general(delta, rows, (((0,), (0,)), ((), ())), preferred_element_...  3.77 us
    ppermute x5, waiting for transfers between devices, to_label(): lax.ppermute(x, 'label', [(i, (i + by) % n_label) for i in range(n_label)])  3.45 us
    ppermute x5, starting transfers between devices, to_label(): lax.ppermute(x, 'label', [(i, (i + by) % n_label) for i in range(n_label)])  2.33 us
    slice x1, local copies, waits for them, and re-layouts, local(): next_rows = [to_label(embeds[runs[0]], -1)]  2.26 us
    dot_general x3, matrix products, grad_x_of(): jnp.dot(in_turn(jnp.concatenate(deltas, axis=1)), jnp.concatenate([pieces...  2.2 us
  transfers between devices with their start and end apart: 13, of which 6 were waited for; matrix products, arithmetic and copies ran while one was open for 27% of the time, Pallas kernels for 0%

profile of v8, /device:TPU:0, one launch (start us, length us, event | category | flops | bytes accessed | tf_op | source)
XLA Modules:
  0.0 60.4 jit_solution(6252070066515176395)
XLA Ops:
  0.6 0.0 copy-start
  0.6 3.1 %collective-permute-start = (bf16[128,1024]{1,0:T(8,128)(2,1)}, bf16[128,1024]{1,0:T(8,128)(2,1)S(1)}, u32[]{:S(2)}, u32[]{:S(2)}) collective-permute-start(bf16[128,1024]{1,0:T(8,128)(2,1)} %param.5), channel_id=1, source_target_pairs={{0,1},{1,0},{2,3},{3,2},{4,5},{5,4},{6,7},{7,6},{8,9},{9,8},{10,11... | collective-permute-start | bytes 786440 | tf_op jit(solution)/shard_map/ppermute | solution.py:35
  3.7 2.6 %collective-permute-start.1 = (bf16[128,1024]{1,0:T(8,128)(2,1)}, bf16[128,1024]{1,0:T(8,128)(2,1)S(1)}, u32[]{:S(2)}, u32[]{:S(2)}) collective-permute-start(bf16[128,1024]{1,0:T(8,128)(2,1)} %param.5), channel_id=1, source_target_pairs={{0,2},{1,3},{2,0},{3,1},{4,6},{5,7},{6,4},{7,5},{8,10},{9,11},{10,... | collective-permute-start | bytes 786440 | tf_op jit(solution)/shard_map/ppermute | solution.py:35
  6.3 0.7 %fusion.73 = s32[768,8]{0,1:T(8,128)S(1)} fusion(s32[768,8]{0,1:T(8,128)} %param.6, s32[768]{0:T(1024)} %param.7), kind=kLoop, calls=%fused_computation.110 | loop fusion | flops 12288 | bytes 52224 | tf_op jit(solution)/shard_map/jit(_where)/select_n | solution.py:27
  7.1 0.4 collective-permute-start.3
  7.4 2.3 %slice.42 = bf16[512,1024]{1,0:T(8,128)(2,1)} slice(bf16[768,1024]{1,0:T(8,128)(2,1)} %param.4), slice={[0:512], [0:1024]} | slice | bytes 2097152 | tf_op jit(solution)/shard_map/slice | solution.py:66
  9.7 1.2 %collective-permute-start.2 = (bf16[512,1024]{1,0:T(8,128)(2,1)}, bf16[512,1024]{1,0:T(8,128)(2,1)S(1)}, u32[]{:S(2)}, u32[]{:S(2)}) collective-permute-start(bf16[512,1024]{1,0:T(8,128)(2,1)} %slice.42), channel_id=1, source_target_pairs={{0,12},{4,0},{8,4},{12,8},{1,13},{5,1},{9,5},{13,9},{2,14},{6,2},{... | collective-permute-start | bytes 3145736 | tf_op jit(solution)/shard_map/ppermute | solution.py:38
  11.0 4.7 %collective-permute-done = bf16[128,1024]{1,0:T(8,128)(2,1)S(1)} collective-permute-done((bf16[128,1024]{1,0:T(8,128)(2,1)}, bf16[128,1024]{1,0:T(8,128)(2,1)S(1)}, u32[]{:S(2)}, u32[]{:S(2)}) %collective-permute-start) | collective-permute-done | bytes 262176 | tf_op jit(solution)/shard_map/ppermute | solution.py:35
  15.7 0.7 %fusion.23 = bf16[768,128]{0,1:T(8,128)(2,1)S(1)} fusion(bf16[128,1024]{1,0:T(8,128)(2,1)S(1)} %collective-permute-done, bf16[768,1024]{1,0:T(8,128)(2,1)S(1)} %copy-done, s32[768]{0:T(1024)S(1)} %get-tuple-element.53, s32[128]{0:T(128)S(1)} %iota_add_fusion.3), kind=kOutput, calls=%fused_computation.38 | convolution fusion | flops 202014720 | bytes 2035200 | tf_op jit(solution)/shard_map/dot_general | solution.py:45
  16.4 0.0 copy-start.2
  16.5 0.4 fusion.78
  16.8 0.6 copy-done.2
  17.4 0.7 %fusion.22 = bf16[768,128]{0,1:T(8,128)(2,1)S(1)} fusion(bf16[128,1024]{1,0:T(8,128)(2,1)S(1)} %copy-done.2, bf16[768,1024]{1,0:T(8,128)(2,1)S(1)} %copy-done, s32[768]{0:T(1024)S(1)} %get-tuple-element.52, s32[128]{0:T(128)S(1)} %iota_add_fusion.2), kind=kOutput, calls=%fused_computation.37 | convolution fusion | flops 202014720 | bytes 2035200 | tf_op jit(solution)/shard_map/dot_general | solution.py:45
  18.1 0.4 fusion.79
  18.5 0.0 collective-permute-done.1
  18.5 0.7 %fusion.21 = bf16[768,128]{0,1:T(8,128)(2,1)S(1)} fusion(bf16[128,1024]{1,0:T(8,128)(2,1)S(1)} %collective-permute-done.1, bf16[768,1024]{1,0:T(8,128)(2,1)S(1)} %copy-done, s32[768]{0:T(1024)S(1)} %get-tuple-element.51, s32[128]{0:T(128)S(1)} %iota_add_fusion.1), kind=kOutput, calls=%fused_computation.36 | convolution fusion | flops 202014720 | bytes 2035200 | tf_op jit(solution)/shard_map/dot_general | solution.py:45
  19.2 0.4 fusion.80
  19.6 0.0 collective-permute-done.3
  19.7 0.3 collective-permute-start.4
  20.0 0.1 collective-permute-start.5
  20.1 3.4 %collective-permute-done.2 = bf16[512,1024]{1,0:T(8,128)(2,1)S(1)} collective-permute-done((bf16[512,1024]{1,0:T(8,128)(2,1)}, bf16[512,1024]{1,0:T(8,128)(2,1)S(1)}, u32[]{:S(2)}, u32[]{:S(2)}) %collective-permute-start.2) | collective-permute-done | bytes 1048608 | tf_op jit(solution)/shard_map/ppermute | solution.py:38
  23.6 0.5 fusion.47
  24.1 0.3 convolution_add_fusion.3
  24.4 0.5 fusion.46
  25.0 0.3 convolution_add_fusion.2
  25.3 0.5 fusion.45
  25.8 0.3 convolution_add_fusion.1
  26.2 2.3 %collective-permute-done.5 = bf16[128,1024]{1,0:T(8,128)(2,1)S(1)} collective-permute-done((bf16[128,1024]{1,0:T(8,128)(2,1)S(1)}, bf16[128,1024]{1,0:T(8,128)(2,1)S(1)}, u32[]{:S(2)}, u32[]{:S(2)}) %collective-permute-start.5) | collective-permute-done | bytes 262176 | tf_op jit(solution)/shard_map/ppermute | solution.py:35
  28.5 0.7 %fusion.20 = bf16[768,128]{0,1:T(8,128)(2,1)S(1)} fusion(bf16[128,1024]{1,0:T(8,128)(2,1)S(1)} %collective-permute-done.5, bf16[768,1024]{1,0:T(8,128)(2,1)S(1)} %copy-done, s32[768]{0:T(1024)S(1)} %get-tuple-element.50, s32[128]{0:T(128)S(1)} %iota_add_fusion), kind=kOutput, calls=%fused_computation.35 | convolution fusion | flops 202014720 | bytes 2035200 | tf_op jit(solution)/shard_map/dot_general | solution.py:45
  29.2 0.4 fusion.81
  29.6 0.5 fusion.44
  30.1 0.3 convolution_add_fusion
  30.5 0.7 %convolution_convert_fusion = bf16[512,1024]{1,0:T(8,128)(2,1)S(1)} fusion(bf16[512,512]{0,1:T(8,128)(2,1)S(1)} %pad_maximum_fusion.1, bf16[512,1024]{1,0:T(8,128)(2,1)S(1)} %constant_dynamic-update-slice_fusion), kind=kOutput, calls=%fused_computation.1 | convolution fusion | flops 537395200 | bytes 2621440 | tf_op jit(solution)/shard_map/dot_general | solution.py:56
  31.2 0.0 collective-permute-done.4
  31.2 0.3 fusion.64
  31.6 0.2 multiply_convert_fusion
  31.9 0.1 collective-permute-start.11
  31.9 2.7 %collective-permute-start.8 = (bf16[32,1024]{1,0:T(8,128)(2,1)S(1)}, bf16[32,1024]{1,0:T(8,128)(2,1)S(1)}, u32[]{:S(2)}, u32[]{:S(2)}) collective-permute-start(bf16[32,1024]{1,0:T(8,128)(2,1)S(1)} %slice.56), channel_id=1, source_target_pairs={{0,3},{1,2},{2,1},{3,0},{4,7},{5,6},{6,5},{7,4},{8,11},{9,10},{10,... | collective-permute-start | bytes 196616 | tf_op jit(solution)/shard_map/ppermute | solution.py:35
  34.7 0.0 collective-permute-start.7
  34.7 0.3 fusion.65
  35.0 0.2 broadcast_multiply_fusion
  35.3 0.3 fusion.66
  35.6 0.2 multiply_convert_fusion.1
  35.9 0.3 fusion.67
  36.2 0.2 convolution_add_fusion.4
  36.5 1.8 %collective-permute-start.9 = (bf16[32,1024]{1,0:T(8,128)(2,1)S(1)}, bf16[32,1024]{1,0:T(8,128)(2,1)S(1)}, u32[]{:S(2)}, u32[]{:S(2)}) collective-permute-start(bf16[32,1024]{1,0:T(8,128)(2,1)S(1)} %slice.75), channel_id=1, source_target_pairs={{0,2},{1,3},{2,0},{3,1},{4,6},{5,7},{6,4},{7,5},{8,10},{9,11},{10,... | collective-permute-start | bytes 196616 | tf_op jit(solution)/shard_map/ppermute | solution.py:35
  38.2 0.5 convolution_convert_fusion.1
  38.7 0.4 collective-permute-start.6
  39.1 0.1 pad_maximum_fusion
  39.1 5.2 %collective-permute-done.7 = bf16[96,1024]{1,0:T(8,128)(2,1)S(1)} collective-permute-done((bf16[96,1024]{1,0:T(8,128)(2,1)S(1)}, bf16[96,1024]{1,0:T(8,128)(2,1)S(1)}, u32[]{:S(2)}, u32[]{:S(2)}) %collective-permute-start.7) | collective-permute-done | bytes 196640 | tf_op jit(solution)/shard_map/ppermute | solution.py:35
  44.3 0.4 collective-permute-start.12
  44.8 1.0 %fusion.82 = f32[768,1024]{1,0:T(8,128)S(1)} fusion(bf16[768,512]{0,1:T(8,128)(2,1)S(1)} %pad_maximum_fusion, bf16[512,1024]{1,0:T(8,128)(2,1)S(1)} %constant_dynamic-update-slice_fusion), kind=kOutput, calls=%fused_computation.139 | convolution fusion | flops 805306368 | bytes 4980736 | tf_op jit(solution)/shard_map/dot_general | solution.py:56
  45.8 0.0 collective-permute-done.9
  45.8 0.3 collective-permute-start.10
  46.1 0.0 collective-permute-done.8
  46.1 3.8 %collective-permute-done.6 = bf16[128,1024]{1,0:T(8,128)(2,1)S(1)} collective-permute-done((bf16[128,1024]{1,0:T(8,128)(2,1)S(1)}, bf16[128,1024]{1,0:T(8,128)(2,1)S(1)}, u32[]{:S(2)}, u32[]{:S(2)}) %collective-permute-start.6) | collective-permute-done | bytes 262176 | tf_op jit(solution)/shard_map/ppermute | solution.py:35
  49.9 0.1 convert_add_fusion
  50.1 0.0 collective-permute-done.11
  50.1 0.4 add_convert_fusion
  50.5 7.8 %collective-permute-done.10 = bf16[96,1024]{1,0:T(8,128)(2,1)S(1)} collective-permute-done((bf16[96,1024]{1,0:T(8,128)(2,1)S(1)}, bf16[96,1024]{1,0:T(8,128)(2,1)S(1)}, u32[]{:S(2)}, u32[]{:S(2)}) %collective-permute-start.10) | collective-permute-done | bytes 196640 | tf_op jit(solution)/shard_map/ppermute | solution.py:35
  58.4 0.7 %pad_maximum_fusion.2 = bf16[128,1024]{1,0:T(8,128)(2,1)} fusion(bf16[96,1024]{1,0:T(8,128)(2,1)S(1)} %fusion.70, bf16[32,1024]{1,0:T(8,128)(2,1)S(1)} %fusion.72), kind=kLoop, calls=%fused_computation.103 | loop fusion | flops 524288 | bytes 524288 | tf_op jit(solution)/shard_map/concatenate | solution.py:135
  59.1 0.1 fusion.69
  59.2 0.0 copy-start.1
  59.3 1.1 %copy-done.1 = bf16[768,1024]{1,0:T(8,128)(2,1)} copy-done((bf16[768,1024]{1,0:T(8,128)(2,1)}, bf16[768,1024]{1,0:T(8,128)(2,1)S(1)}, u32[]{:S(2)}) %copy-start.1) | copy-done | bytes 1572888
  (24 shorter events, 0.4 us)
Async XLA Ops:
  0.6 15.1 %copy-start = (bf16[768,1024]{1,0:T(8,128)(2,1)S(1)}, bf16[768,1024]{1,0:T(8,128)(2,1)}, u32[]{:S(2)}) copy-start(bf16[768,1024]{1,0:T(8,128)(2,1)} %param.4) | copy-start | bytes 4718596
  0.6 15.1 %collective-permute-start = (bf16[128,1024]{1,0:T(8,128)(2,1)}, bf16[128,1024]{1,0:T(8,128)(2,1)S(1)}, u32[]{:S(2)}, u32[]{:S(2)}) collective-permute-start(bf16[128,1024]{1,0:T(8,128)(2,1)} %param.5), channel_id=1, source_target_pairs={{0,1},{1,0},{2,3},{3,2},{4,5},{5,4},{6,7},{7,6},{8,9},{9,8},{10,11... | collective-permute-start | bytes 786440 | tf_op jit(solution)/shard_map/ppermute | solution.py:35
  3.7 14.8 %collective-permute-start.1 = (bf16[128,1024]{1,0:T(8,128)(2,1)}, bf16[128,1024]{1,0:T(8,128)(2,1)S(1)}, u32[]{:S(2)}, u32[]{:S(2)}) collective-permute-start(bf16[128,1024]{1,0:T(8,128)(2,1)} %param.5), channel_id=1, source_target_pairs={{0,2},{1,3},{2,0},{3,1},{4,6},{5,7},{6,4},{7,5},{8,10},{9,11},{10,... | collective-permute-start | bytes 786440 | tf_op jit(solution)/shard_map/ppermute | solution.py:35
  7.1 12.5 %collective-permute-start.3 = (s32[768,8]{0,1:T(8,128)S(1)}, s32[768,8]{0,1:T(8,128)S(1)}, u32[]{:S(2)}, u32[]{:S(2)}) collective-permute-start(s32[768,8]{0,1:T(8,128)S(1)} %fusion.73), channel_id=1, source_target_pairs={{0,12},{4,0},{8,4},{12,8},{1,13},{5,1},{9,5},{13,9},{2,14},{6,2},{... | collective-permute-start | bytes 73736 | tf_op jit(solution)/shard_map/ppermute | solution.py:38
  9.7 13.9 %collective-permute-start.2 = (bf16[512,1024]{1,0:T(8,128)(2,1)}, bf16[512,1024]{1,0:T(8,128)(2,1)S(1)}, u32[]{:S(2)}, u32[]{:S(2)}) collective-permute-start(bf16[512,1024]{1,0:T(8,128)(2,1)} %slice.42), channel_id=1, source_target_pairs={{0,12},{4,0},{8,4},{12,8},{1,13},{5,1},{9,5},{13,9},{2,14},{6,2},{... | collective-permute-start | bytes 3145736 | tf_op jit(solution)/shard_map/ppermute | solution.py:38
  16.4 1.0 %copy-start.2 = (bf16[128,1024]{1,0:T(8,128)(2,1)S(1)}, bf16[128,1024]{1,0:T(8,128)(2,1)}, u32[]{:S(2)}) copy-start(bf16[128,1024]{1,0:T(8,128)(2,1)} %param.5) | copy-start | bytes 786436
  19.7 11.5 %collective-permute-start.4 = (bf16[256,1024]{1,0:T(8,128)(2,1)S(1)}, bf16[256,1024]{1,0:T(8,128)(2,1)S(1)}, u32[]{:S(2)}, u32[]{:S(2)}) collective-permute-start(bf16[256,1024]{1,0:T(8,128)(2,1)S(1)} %slice.44), channel_id=1, source_target_pairs={{0,12},{4,0},{8,4},{12,8},{1,13},{5,1},{9,5},{13,9},{2,14},{6,2},{... | collective-permute-start | bytes 1572872 | tf_op jit(solution)/shard_map/ppermute | solution.py:38
  20.0 8.5 %collective-permute-start.5 = (bf16[128,1024]{1,0:T(8,128)(2,1)S(1)}, bf16[128,1024]{1,0:T(8,128)(2,1)S(1)}, u32[]{:S(2)}, u32[]{:S(2)}) collective-permute-start(bf16[128,1024]{1,0:T(8,128)(2,1)S(1)} %collective-permute-done.1), channel_id=1, source_target_pairs={{0,1},{1,0},{2,3},{3,2},{4,5},{5,4},{6,7},{7,6},{8,9},{9,8},{10,11... | collective-permute-start | bytes 786440 | tf_op jit(solution)/shard_map/ppermute | solution.py:35
  31.9 18.2 %collective-permute-start.11 = (bf16[512,1024]{1,0:T(8,128)(2,1)S(1)}, bf16[512,1024]{1,0:T(8,128)(2,1)S(1)}, u32[]{:S(2)}, u32[]{:S(2)}) collective-permute-start(bf16[512,1024]{1,0:T(8,128)(2,1)S(1)} %convolution_convert_fusion), channel_id=1, source_target_pairs={{0,4},{4,8},{8,12},{12,0},{1,5},{5,9},{9,13},{13,1},{2,6},{6,10},{... | collective-permute-start | bytes 3145736 | tf_op jit(solution)/shard_map/ppermute | solution.py:38
  31.9 14.2 %collective-permute-start.8 = (bf16[32,1024]{1,0:T(8,128)(2,1)S(1)}, bf16[32,1024]{1,0:T(8,128)(2,1)S(1)}, u32[]{:S(2)}, u32[]{:S(2)}) collective-permute-start(bf16[32,1024]{1,0:T(8,128)(2,1)S(1)} %slice.56), channel_id=1, source_target_pairs={{0,3},{1,2},{2,1},{3,0},{4,7},{5,6},{6,5},{7,4},{8,11},{9,10},{10,... | collective-permute-start | bytes 196616 | tf_op jit(solution)/shard_map/ppermute | solution.py:35
  34.7 9.7 %collective-permute-start.7 = (bf16[96,1024]{1,0:T(8,128)(2,1)S(1)}, bf16[96,1024]{1,0:T(8,128)(2,1)S(1)}, u32[]{:S(2)}, u32[]{:S(2)}) collective-permute-start(bf16[96,1024]{1,0:T(8,128)(2,1)S(1)} %slice.54), channel_id=1, source_target_pairs={{0,1},{1,0},{2,3},{3,2},{4,5},{5,4},{6,7},{7,6},{8,9},{9,8},{10,11... | collective-permute-start | bytes 589832 | tf_op jit(solution)/shard_map/ppermute | solution.py:35
  36.5 9.3 %collective-permute-start.9 = (bf16[32,1024]{1,0:T(8,128)(2,1)S(1)}, bf16[32,1024]{1,0:T(8,128)(2,1)S(1)}, u32[]{:S(2)}, u32[]{:S(2)}) collective-permute-start(bf16[32,1024]{1,0:T(8,128)(2,1)S(1)} %slice.75), channel_id=1, source_target_pairs={{0,2},{1,3},{2,0},{3,1},{4,6},{5,7},{6,4},{7,5},{8,10},{9,11},{10,... | collective-permute-start | bytes 196616 | tf_op jit(solution)/shard_map/ppermute | solution.py:35
  38.7 11.2 %collective-permute-start.6 = (bf16[128,1024]{1,0:T(8,128)(2,1)S(1)}, bf16[128,1024]{1,0:T(8,128)(2,1)S(1)}, u32[]{:S(2)}, u32[]{:S(2)}) collective-permute-start(bf16[128,1024]{1,0:T(8,128)(2,1)S(1)} %multiply_convert_fusion.1), channel_id=1, source_target_pairs={{0,1},{1,0},{2,3},{3,2},{4,5},{5,4},{6,7},{7,6},{8,9},{9,8},{10,11... | collective-permute-start | bytes 786440 | tf_op jit(solution)/shard_map/ppermute | solution.py:35
  44.3 14.8 %collective-permute-start.12 = (bf16[256,1024]{1,0:T(8,128)(2,1)S(1)}, bf16[256,1024]{1,0:T(8,128)(2,1)S(1)}, u32[]{:S(2)}, u32[]{:S(2)}) collective-permute-start(bf16[256,1024]{1,0:T(8,128)(2,1)S(1)} %convolution_convert_fusion.1), channel_id=1, source_target_pairs={{0,4},{4,8},{8,12},{12,0},{1,5},{5,9},{9,13},{13,1},{2,6},{6,10},{... | collective-permute-start | bytes 1572872 | tf_op jit(solution)/shard_map/ppermute | solution.py:38
  45.8 12.5 %collective-permute-start.10 = (bf16[96,1024]{1,0:T(8,128)(2,1)S(1)}, bf16[96,1024]{1,0:T(8,128)(2,1)S(1)}, u32[]{:S(2)}, u32[]{:S(2)}) collective-permute-start(bf16[96,1024]{1,0:T(8,128)(2,1)S(1)} %fusion.71), channel_id=1, source_target_pairs={{0,2},{1,3},{2,0},{3,1},{4,6},{5,7},{6,4},{7,5},{8,10},{9,11},{10,... | collective-permute-start | bytes 589832 | tf_op jit(solution)/shard_map/ppermute | solution.py:35
  59.2 1.1 %copy-start.1 = (bf16[768,1024]{1,0:T(8,128)(2,1)}, bf16[768,1024]{1,0:T(8,128)(2,1)S(1)}, u32[]{:S(2)}) copy-start(bf16[768,1024]{1,0:T(8,128)(2,1)S(1)} %fusion.69) | copy-start | bytes 4718596

commit v9 on v6

--- a/solution.py
+++ b/solution.py
@@ -53,48 +53,64 @@
             preferred_element_type=jnp.float32,
         )
 
-    d_own, d_next, g_own, total, moved = {}, {}, {}, {}, {}
     pieces = {0: weights}
     for k in range(1, n_dp):
         step = k & -k
         pieces[k] = to_dp(pieces[k ^ step], step)
     next_rows = to_label(embeds, -1)
+    d_own, d_next, g_w = {}, {}, {}
 
     def own_step(k):
         pieces[k] = in_turn(pieces[k])
         d_own[k] = delta_of(embeds, ids, pieces[k], k)
-        g_own[k] = grad_w_of(d_own[k], embeds)
-        last[0] = g_own[k]
+        g_w[k] = grad_w_of(d_own[k], embeds)
+        last[0] = g_w[k]
 
     def next_step(k):
         d_next[k] = delta_of(next_rows, next_ids, in_turn(pieces[k]), k)
-        total[k] = (g_own[k] + grad_w_of(d_next[k], next_rows)) * scale
-        if k > 0:
-            total[k] = total[k].astype(jnp.bfloat16)
-            moved[k] = to_dp(total[k], k)
-        last[0] = total[k]
+        last[0] = d_next[k]
+        if k > 1:
+            add_next(k)
 
-    own_step(0)
+    def add_next(k):
+        g_w[k] = (g_w[k] + grad_w_of(in_turn(d_next[k]), next_rows)) * scale
+        last[0] = g_w[k]
+
+    own_step(1)
     next_ids = to_label(in_turn(ids), -1)
-    for k in range(1, n_dp - 1):
+    for k in range(2, n_dp):
         own_step(k)
     next_ids = in_turn(next_ids)
-    for k in range(n_dp - 1):
+    for k in range(n_dp - 1, -1, -1):
         next_step(k)
-    if n_dp > 1:
-        own_step(n_dp - 1)
-        next_step(n_dp - 1)
     theirs = grad_x_of(d_next).astype(jnp.bfloat16)
     last[0] = theirs
     back = to_label(theirs, 1)
+
+    add_next(1)
+    relayed, moved = {}, []
+    for k in range(n_dp - 1, 0, -1):
+        step = k & -k
+        for term in relayed.get(k, ()):
+            g_w[k] = g_w[k] + term.astype(jnp.float32)
+        part = g_w[k].astype(jnp.bfloat16)
+        if k in relayed:
+            last[0] = part
+        if step == k:
+            moved.append(to_dp(part, k))
+        else:
+            relayed.setdefault(k ^ step, []).append(in_turn(to_dp(part, step)))
+    own_step(0)
     grad_x = grad_x_of(d_own)
     last[0] = grad_x
+    add_next(0)
+    grad_w = g_w[0]
+    for term in reversed(moved):
+        grad_w = grad_w + in_turn(term).astype(jnp.float32)
+    grad_w = grad_w.astype(jnp.bfloat16)
+    last[0] = grad_w
     grad_x = (grad_x + in_turn(back).astype(jnp.float32)).astype(jnp.bfloat16)
-    last[0] = grad_x
-    grad_w = total[0]
-    for k in range(1, n_dp):
-        grad_w = grad_w + in_turn(moved[k]).astype(jnp.float32)
-    return (grad_w.astype(jnp.bfloat16), grad_x)
+    return (grad_w, grad_x)
 
 
 def solution(mesh):

time: 63.1 us -> 55.5 us (0.88)
  the two profiles are of different devices: /device:TPU:9 before, /device:TPU:0 now
where the time goes in v9:
time: 55.5 us; the launch traced here: 55.3 us
  waiting for transfers between devices  27.7 us (50%)
  matrix products  12.3 us (22%)
  starting transfers between devices  10.5 us (19%)
  other arithmetic  3.48 us (6%)
  between operations  0.97 us (2%)
    ppermute x6, waiting for transfers between devices, to_dp(): return lax.ppermute(x, 'dp', [(i, i ^ k) for i in range(n_dp)])  27.3 us
    ppermute x6, starting transfers between devices, to_dp(): return lax.ppermute(x, 'dp', [(i, i ^ k) for i in range(n_dp)])  9.83 us
    dot_general x8, matrix products, delta_of(): lax.dot_general(rows, piece, (((1,), (1,)), ((), ())), preferred_element_...  7.17 us
    dot_general x8, matrix products, grad_w_of(): lax.dot_general(delta, rows, (((0,), (0,)), ((), ())), preferred_element_...  3.06 us
    dot_general x2, matrix products, grad_x_of(): jnp.dot(in_turn(jnp.concatenate([deltas[k] for k in range(n_dp)], axis=1)...  2.04 us
    convert_element_type x1, other arithmetic, local(): grad_x = (grad_x + in_turn(back).astype(jnp.float32)).astype(jnp.bfloat16)  1.75 us
  transfers between devices with their start and end apart: 9, of which 6 were waited for; matrix products, arithmetic and copies ran while one was open for 23% of the time, Pallas kernels for 0%

profile of v9, /device:TPU:0, one launch (start us, length us, event | category | flops | bytes accessed | tf_op | source)
XLA Modules:
  0.0 55.3 jit_solution(16026031525222514293)
XLA Ops:
  0.6 3.1 %collective-permute-start.1 = (bf16[128,1024]{1,0:T(8,128)(2,1)}, bf16[128,1024]{1,0:T(8,128)(2,1)S(1)}, u32[]{:S(2)}, u32[]{:S(2)}) collective-permute-start(bf16[128,1024]{1,0:T(8,128)(2,1)} %param.5), channel_id=1, source_target_pairs={{0,1},{1,0},{2,3},{3,2},{4,5},{5,4},{6,7},{7,6},{8,9},{9,8},{10,11... | collective-permute-start | bytes 786440 | tf_op jit(solution)/shard_map/ppermute | solution.py:29
  3.7 2.6 %collective-permute-start = (bf16[128,1024]{1,0:T(8,128)(2,1)}, bf16[128,1024]{1,0:T(8,128)(2,1)S(1)}, u32[]{:S(2)}, u32[]{:S(2)}) collective-permute-start(bf16[128,1024]{1,0:T(8,128)(2,1)} %param.5), channel_id=1, source_target_pairs={{0,2},{1,3},{2,0},{3,1},{4,6},{5,7},{6,4},{7,5},{8,10},{9,11},{10,... | collective-permute-start | bytes 786440 | tf_op jit(solution)/shard_map/ppermute | solution.py:29
  6.3 0.4 collective-permute-start.3
  6.7 0.7 %fusion.55 = s32[768,8]{0,1:T(8,128)S(1)} fusion(s32[768,8]{0,1:T(8,128)} %param.6, s32[768]{0:T(1024)} %param.7), kind=kLoop, calls=%fused_computation.80 | loop fusion | flops 12288 | bytes 52224 | tf_op jit(solution)/shard_map/jit(_where)/select_n | solution.py:21
  7.6 8.1 %collective-permute-done.1 = bf16[128,1024]{1,0:T(8,128)(2,1)S(1)} collective-permute-done((bf16[128,1024]{1,0:T(8,128)(2,1)}, bf16[128,1024]{1,0:T(8,128)(2,1)S(1)}, u32[]{:S(2)}, u32[]{:S(2)}) %collective-permute-start.1) | collective-permute-done | bytes 262176 | tf_op jit(solution)/shard_map/ppermute | solution.py:29
  15.7 0.0 copy-start
  15.7 2.2 %fusion.51 = bf16[768,128]{0,1:T(8,128)(2,1)S(1)} fusion(bf16[128,1024]{1,0:T(8,128)(2,1)S(1)} %collective-permute-done.1, bf16[768,1024]{1,0:T(8,128)(2,1)} %param.4, s32[768]{0:T(1024)S(1)} %get-tuple-element.45, s32[128]{0:T(128)S(1)} %iota_add_fusion.3), kind=kOutput, calls=%fused_computation.71 | convolution fusion | flops 202014720 | bytes 2035200 | tf_op jit(solution)/shard_map/dot_general | solution.py:39
  18.0 0.0 copy-done
  18.0 0.4 fusion.58
  18.4 0.0 collective-permute-done
  18.4 0.3 collective-permute-start.4
  18.6 0.1 collective-permute-start.2
  18.7 0.7 %fusion.50 = bf16[768,128]{0,1:T(8,128)(2,1)S(1)} fusion(bf16[128,1024]{1,0:T(8,128)(2,1)S(1)} %collective-permute-done, bf16[768,1024]{1,0:T(8,128)(2,1)S(1)} %copy-done, s32[768]{0:T(1024)S(1)} %get-tuple-element.44, s32[128]{0:T(128)S(1)} %iota_add_fusion.2), kind=kOutput, calls=%fused_computation.70 | convolution fusion | flops 202014720 | bytes 2035200 | tf_op jit(solution)/shard_map/dot_general | solution.py:39
  19.4 0.4 fusion.59
  19.8 7.3 %collective-permute-done.2 = bf16[128,1024]{1,0:T(8,128)(2,1)S(1)} collective-permute-done((bf16[128,1024]{1,0:T(8,128)(2,1)S(1)}, bf16[128,1024]{1,0:T(8,128)(2,1)S(1)}, u32[]{:S(2)}, u32[]{:S(2)}) %collective-permute-start.2) | collective-permute-done | bytes 262176 | tf_op jit(solution)/shard_map/ppermute | solution.py:29
  27.1 0.7 %fusion.49 = bf16[768,128]{0,1:T(8,128)(2,1)S(1)} fusion(bf16[128,1024]{1,0:T(8,128)(2,1)S(1)} %collective-permute-done.2, bf16[768,1024]{1,0:T(8,128)(2,1)S(1)} %copy-done, s32[768]{0:T(1024)S(1)} %get-tuple-element.43, s32[128]{0:T(128)S(1)} %iota_add_fusion.1), kind=kOutput, calls=%fused_computation.69 | convolution fusion | flops 202014720 | bytes 2035200 | tf_op jit(solution)/shard_map/dot_general | solution.py:39
  27.9 0.4 fusion.60
  28.2 0.0 collective-permute-done.4
  28.3 0.0 collective-permute-done.3
  28.3 0.7 %fusion.48 = bf16[768,128]{0,1:T(8,128)(2,1)S(1)} fusion(bf16[128,1024]{1,0:T(8,128)(2,1)S(1)} %collective-permute-done.2, bf16[768,1024]{1,0:T(8,128)(2,1)S(1)} %collective-permute-done.3, s32[768]{0:T(1024)S(1)} %get-tuple-element.49, s32[128]{0:T(128)S(1)} %iota_add_fusion.1), kind=kOutput, calls=%fused_computation.68 | convolution fusion | flops 202014720 | bytes 2035200 | tf_op jit(solution)/shard_map/dot_general | solution.py:39
  29.0 0.4 fusion.3
  29.4 0.4 collective-permute-start.5
  29.8 0.7 %fusion.47 = bf16[768,128]{0,1:T(8,128)(2,1)S(1)} fusion(bf16[128,1024]{1,0:T(8,128)(2,1)S(1)} %collective-permute-done, bf16[768,1024]{1,0:T(8,128)(2,1)S(1)} %collective-permute-done.3, s32[768]{0:T(1024)S(1)} %get-tuple-element.48, s32[128]{0:T(128)S(1)} %iota_add_fusion.2), kind=kOutput, calls=%fused_computation.67 | convolution fusion | flops 202014720 | bytes 2035200 | tf_op jit(solution)/shard_map/dot_general | solution.py:39
  30.5 0.4 fusion.2
  30.9 0.0 copy-start.1
  30.9 0.7 %fusion.46 = bf16[768,128]{0,1:T(8,128)(2,1)S(1)} fusion(bf16[128,1024]{1,0:T(8,128)(2,1)S(1)} %collective-permute-done.1, bf16[768,1024]{1,0:T(8,128)(2,1)S(1)} %collective-permute-done.3, s32[768]{0:T(1024)S(1)} %get-tuple-element.47, s32[128]{0:T(128)S(1)} %iota_add_fusion.3), kind=kOutput, calls=%fused_computation.66 | convolution fusion | flops 202014720 | bytes 2035200 | tf_op jit(solution)/shard_map/dot_general | solution.py:39
  31.6 0.2 copy-done.1
  31.8 0.7 %fusion.45 = bf16[768,128]{0,1:T(8,128)(2,1)S(1)} fusion(bf16[128,1024]{1,0:T(8,128)(2,1)S(1)} %copy-done.1, bf16[768,1024]{1,0:T(8,128)(2,1)S(1)} %collective-permute-done.3, s32[768]{0:T(1024)S(1)} %get-tuple-element.46, s32[128]{0:T(128)S(1)} %iota_add_fusion), kind=kOutput, calls=%fused_computation.65 | convolution fusion | flops 202014720 | bytes 2035200 | tf_op jit(solution)/shard_map/dot_general | solution.py:39
  32.6 0.1 pad_maximum_fusion.8
  32.6 1.0 %convolution_convert_fusion = bf16[768,1024]{1,0:T(8,128)(2,1)S(1)} fusion(bf16[768,512]{0,1:T(8,128)(2,1)S(1)} %pad_maximum_fusion.8, bf16[128,1024]{1,0:T(8,128)(2,1)S(1)} %collective-permute-done.2, bf16[128,1024]{1,0:T(8,128)(2,1)S(1)} %collective-permute-done, bf16[128,1024]{1,0:T(8,128)(2,1)S(1)} %collective-permute-done.1, ...), kind=kOutput, calls=%fused_computation.1 | convolution fusion | flops 810287104 | bytes 3407872 | tf_op jit(solution)/shard_map/dot_general | solution.py:50
  33.6 0.1 collective-permute-start.8
  33.7 0.4 fusion.1
  34.1 1.8 %collective-permute-start.6 = (bf16[128,1024]{1,0:T(8,128)(2,1)S(1)}, bf16[128,1024]{1,0:T(8,128)(2,1)S(1)}, u32[]{:S(2)}, u32[]{:S(2)}) collective-permute-start(bf16[128,1024]{1,0:T(8,128)(2,1)S(1)} %fusion.1), channel_id=1, source_target_pairs={{0,1},{1,0},{2,3},{3,2},{4,5},{5,4},{6,7},{7,6},{8,9},{9,8},{10,11... | collective-permute-start | bytes 786440 | tf_op jit(solution)/shard_map/ppermute | solution.py:29
  35.9 1.3 %collective-permute-done.5 = bf16[128,1024]{1,0:T(8,128)(2,1)S(1)} collective-permute-done((bf16[128,1024]{1,0:T(8,128)(2,1)S(1)}, bf16[128,1024]{1,0:T(8,128)(2,1)S(1)}, u32[]{:S(2)}, u32[]{:S(2)}) %collective-permute-start.5) | collective-permute-done | bytes 262176 | tf_op jit(solution)/shard_map/ppermute | solution.py:29
  37.2 0.1 add_convert_fusion.2
  37.2 1.9 %collective-permute-start.7 = (bf16[128,1024]{1,0:T(8,128)(2,1)S(1)}, bf16[128,1024]{1,0:T(8,128)(2,1)S(1)}, u32[]{:S(2)}, u32[]{:S(2)}) collective-permute-start(bf16[128,1024]{1,0:T(8,128)(2,1)S(1)} %add_convert_fusion.2), channel_id=1, source_target_pairs={{0,2},{1,3},{2,0},{3,1},{4,6},{5,7},{6,4},{7,5},{8,10},{9,11},{10,... | collective-permute-start | bytes 786440 | tf_op jit(solution)/shard_map/ppermute | solution.py:29
  39.2 0.7 %fusion.44 = bf16[768,128]{0,1:T(8,128)(2,1)S(1)} fusion(bf16[128,1024]{1,0:T(8,128)(2,1)S(1)} %copy-done.1, bf16[768,1024]{1,0:T(8,128)(2,1)S(1)} %copy-done, s32[768]{0:T(1024)S(1)} %get-tuple-element.42, s32[128]{0:T(128)S(1)} %iota_add_fusion), kind=kOutput, calls=%fused_computation.64 | convolution fusion | flops 202014720 | bytes 2035200 | tf_op jit(solution)/shard_map/dot_general | solution.py:39
  39.9 0.1 pad_maximum_fusion.9
  39.9 0.4 fusion.61
  40.3 1.0 %fusion.52 = f32[768,1024]{1,0:T(8,128)S(1)} fusion(bf16[768,512]{0,1:T(8,128)(2,1)S(1)} %pad_maximum_fusion.9, bf16[128,1024]{1,0:T(8,128)(2,1)S(1)} %collective-permute-done.2, bf16[128,1024]{1,0:T(8,128)(2,1)S(1)} %collective-permute-done, bf16[128,1024]{1,0:T(8,128)(2,1)S(1)} %collective-permute-done.1, bf16[128,1024]{1,0:T(8,128)(2,1)S(1)} %copy-done.1), kind=kOutput, calls=%fused_computation.72 | convolution fusion | flops 809500672 | bytes 4980736 | tf_op jit(solution)/shard_map/dot_general | solution.py:50
  41.3 0.4 fusion
  41.7 5.6 %collective-permute-done.6 = bf16[128,1024]{1,0:T(8,128)(2,1)S(1)} collective-permute-done((bf16[128,1024]{1,0:T(8,128)(2,1)S(1)}, bf16[128,1024]{1,0:T(8,128)(2,1)S(1)}, u32[]{:S(2)}, u32[]{:S(2)}) %collective-permute-start.6) | collective-permute-done | bytes 262176 | tf_op jit(solution)/shard_map/ppermute | solution.py:29
  47.4 4.9 %collective-permute-done.7 = bf16[128,1024]{1,0:T(8,128)(2,1)S(1)} collective-permute-done((bf16[128,1024]{1,0:T(8,128)(2,1)S(1)}, bf16[128,1024]{1,0:T(8,128)(2,1)S(1)}, u32[]{:S(2)}, u32[]{:S(2)}) %collective-permute-start.7) | collective-permute-done | bytes 262176 | tf_op jit(solution)/shard_map/ppermute | solution.py:29
  52.3 0.8 %add_convert_fusion.1 = bf16[128,1024]{1,0:T(8,128)(2,1)} fusion(bf16[128,1024]{1,0:T(8,128)(2,1)S(1)} %collective-permute-done.7, f32[128,1024]{1,0:T(8,128)S(1)} %fusion, bf16[128,1024]{1,0:T(8,128)(2,1)S(1)} %collective-permute-done.6), kind=kLoop, calls=%fused_computation.77 | loop fusion | flops 655360 | bytes 1310720 | tf_op jit(solution)/shard_map/convert_element_type | solution.py:110
  53.1 0.4 collective-permute-done.8
  53.5 1.8 %add_convert_fusion = bf16[768,1024]{1,0:T(8,128)(2,1)} fusion(f32[768,1024]{1,0:T(8,128)S(1)} %fusion.52, bf16[768,1024]{1,0:T(8,128)(2,1)S(1)} %collective-permute-done.8), kind=kLoop, calls=%fused_computation | loop fusion | flops 2359296 | bytes 6291456 | tf_op jit(solution)/shard_map/convert_element_type | solution.py:112
  (6 shorter events, 0.1 us)
Async XLA Ops:
  0.6 15.1 %collective-permute-start.1 = (bf16[128,1024]{1,0:T(8,128)(2,1)}, bf16[128,1024]{1,0:T(8,128)(2,1)S(1)}, u32[]{:S(2)}, u32[]{:S(2)}) collective-permute-start(bf16[128,1024]{1,0:T(8,128)(2,1)} %param.5), channel_id=1, source_target_pairs={{0,1},{1,0},{2,3},{3,2},{4,5},{5,4},{6,7},{7,6},{8,9},{9,8},{10,11... | collective-permute-start | bytes 786440 | tf_op jit(solution)/shard_map/ppermute | solution.py:29
  3.7 14.6 %collective-permute-start = (bf16[128,1024]{1,0:T(8,128)(2,1)}, bf16[128,1024]{1,0:T(8,128)(2,1)S(1)}, u32[]{:S(2)}, u32[]{:S(2)}) collective-permute-start(bf16[128,1024]{1,0:T(8,128)(2,1)} %param.5), channel_id=1, source_target_pairs={{0,2},{1,3},{2,0},{3,1},{4,6},{5,7},{6,4},{7,5},{8,10},{9,11},{10,... | collective-permute-start | bytes 786440 | tf_op jit(solution)/shard_map/ppermute | solution.py:29
  6.3 22.0 %collective-permute-start.3 = (bf16[768,1024]{1,0:T(8,128)(2,1)}, bf16[768,1024]{1,0:T(8,128)(2,1)S(1)}, u32[]{:S(2)}, u32[]{:S(2)}) collective-permute-start(bf16[768,1024]{1,0:T(8,128)(2,1)} %param.4), channel_id=1, source_target_pairs={{0,12},{4,0},{8,4},{12,8},{1,13},{5,1},{9,5},{13,9},{2,14},{6,2},{... | collective-permute-start | bytes 4718600 | tf_op jit(solution)/shard_map/ppermute | solution.py:32
  15.7 2.2 %copy-start = (bf16[768,1024]{1,0:T(8,128)(2,1)S(1)}, bf16[768,1024]{1,0:T(8,128)(2,1)}, u32[]{:S(2)}) copy-start(bf16[768,1024]{1,0:T(8,128)(2,1)} %param.4) | copy-start | bytes 4718596
  18.4 9.9 %collective-permute-start.4 = (s32[768,8]{0,1:T(8,128)S(1)}, s32[768,8]{0,1:T(8,128)S(1)}, u32[]{:S(2)}, u32[]{:S(2)}) collective-permute-start(s32[768,8]{0,1:T(8,128)S(1)} %fusion.55), channel_id=1, source_target_pairs={{0,12},{4,0},{8,4},{12,8},{1,13},{5,1},{9,5},{13,9},{2,14},{6,2},{... | collective-permute-start | bytes 73736 | tf_op jit(solution)/shard_map/ppermute | solution.py:32
  18.6 8.5 %collective-permute-start.2 = (bf16[128,1024]{1,0:T(8,128)(2,1)S(1)}, bf16[128,1024]{1,0:T(8,128)(2,1)S(1)}, u32[]{:S(2)}, u32[]{:S(2)}) collective-permute-start(bf16[128,1024]{1,0:T(8,128)(2,1)S(1)} %collective-permute-done), channel_id=1, source_target_pairs={{0,1},{1,0},{2,3},{3,2},{4,5},{5,4},{6,7},{7,6},{8,9},{9,8},{10,11... | collective-permute-start | bytes 786440 | tf_op jit(solution)/shard_map/ppermute | solution.py:29
  29.4 7.8 %collective-permute-start.5 = (bf16[128,1024]{1,0:T(8,128)(2,1)S(1)}, bf16[128,1024]{1,0:T(8,128)(2,1)S(1)}, u32[]{:S(2)}, u32[]{:S(2)}) collective-permute-start(bf16[128,1024]{1,0:T(8,128)(2,1)S(1)} %fusion.3), channel_id=1, source_target_pairs={{0,1},{1,0},{2,3},{3,2},{4,5},{5,4},{6,7},{7,6},{8,9},{9,8},{10,11... | collective-permute-start | bytes 786440 | tf_op jit(solution)/shard_map/ppermute | solution.py:29
  30.9 1.0 %copy-start.1 = (bf16[128,1024]{1,0:T(8,128)(2,1)S(1)}, bf16[128,1024]{1,0:T(8,128)(2,1)}, u32[]{:S(2)}) copy-start(bf16[128,1024]{1,0:T(8,128)(2,1)} %param.5) | copy-start | bytes 786436
  33.6 19.9 %collective-permute-start.8 = (bf16[768,1024]{1,0:T(8,128)(2,1)S(1)}, bf16[768,1024]{1,0:T(8,128)(2,1)S(1)}, u32[]{:S(2)}, u32[]{:S(2)}) collective-permute-start(bf16[768,1024]{1,0:T(8,128)(2,1)S(1)} %convolution_convert_fusion), channel_id=1, source_target_pairs={{0,4},{4,8},{8,12},{12,0},{1,5},{5,9},{9,13},{13,1},{2,6},{6,10},{... | collective-permute-start | bytes 4718600 | tf_op jit(solution)/shard_map/ppermute | solution.py:32
  34.1 13.3 %collective-permute-start.6 = (bf16[128,1024]{1,0:T(8,128)(2,1)S(1)}, bf16[128,1024]{1,0:T(8,128)(2,1)S(1)}, u32[]{:S(2)}, u32[]{:S(2)}) collective-permute-start(bf16[128,1024]{1,0:T(8,128)(2,1)S(1)} %fusion.1), channel_id=1, source_target_pairs={{0,1},{1,0},{2,3},{3,2},{4,5},{5,4},{6,7},{7,6},{8,9},{9,8},{10,11... | collective-permute-start | bytes 786440 | tf_op jit(solution)/shard_map/ppermute | solution.py:29
  37.2 15.0 %collective-permute-start.7 = (bf16[128,1024]{1,0:T(8,128)(2,1)S(1)}, bf16[128,1024]{1,0:T(8,128)(2,1)S(1)}, u32[]{:S(2)}, u32[]{:S(2)}) collective-permute-start(bf16[128,1024]{1,0:T(8,128)(2,1)S(1)} %add_convert_fusion.2), channel_id=1, source_target_pairs={{0,2},{1,3},{2,0},{3,1},{4,6},{5,7},{6,4},{7,5},{8,10},{9,11},{10,... | collective-permute-start | bytes 786440 | tf_op jit(solution)/shard_map/ppermute | solution.py:29

commit v10 on v7

--- a/solution.py
+++ b/solution.py
@@ -5,7 +5,7 @@
 from jax import lax
 from jax.sharding import PartitionSpec as P
 
-CHUNKS = 1
+
 DIRECT_EIGHTHS = 2
 
 
@@ -20,10 +20,9 @@
     slots = pos_ids.shape[1]
     span = stretch * n_label // slots
     scale = 1.0 / math.sqrt(rows_dev * n_dp)
-    run = rows_dev // CHUNKS
-    direct = ch_dev * DIRECT_EIGHTHS // 8
     valid = jnp.arange(slots, dtype=jnp.int32)[None, :] < pos_count[:, None]
     ids = jnp.where(valid, pos_ids, -1)
+    direct = ch_dev * DIRECT_EIGHTHS // 8
     last = [embeds]
 
     def in_turn(x):
@@ -36,11 +35,13 @@
     def to_label(x, by):
         return lax.ppermute(x, "label", [(i, (i + by) % n_label) for i in range(n_label)])
 
-    def delta_of(rows, row_ids, piece, k):
-        start = me_label * stretch + (me_dp ^ k) * ch_dev
-        column = lax.dynamic_slice_in_dim(row_ids, start // span, 1, axis=1)
-        labels = start + jnp.arange(ch_dev, dtype=jnp.int32)
-        target = (column == labels[None, :]).astype(jnp.float32)
+    def delta_of(rows, row_ids, piece, ks):
+        starts = [me_label * stretch + (me_dp ^ k) * ch_dev for k in ks]
+        place = jnp.arange(len(ks) * ch_dev, dtype=jnp.int32)[None, :]
+        for i, start in enumerate(starts):
+            column = lax.dynamic_slice_in_dim(row_ids, start // span, 1, axis=1) - (start - i * ch_dev)
+            sought = column if i == 0 else jnp.where(place < i * ch_dev, sought, column)
+        target = (sought == place).astype(jnp.float32)
         logits = lax.dot_general(
             rows, piece, (((1,), (1,)), ((), ())), preferred_element_type=jnp.float32
         )
@@ -62,37 +63,43 @@
     for k in range(1, n_dp):
         step = k & -k
         pieces[k] = to_dp(pieces[k ^ step], step)
-    next_rows = [to_label(embeds[c * run:(c + 1) * run], -1) for c in range(CHUNKS)]
-    d_own, g_own = {}, {}
-    d_next = [{} for _ in range(CHUNKS)]
+    next_rows = to_label(embeds, -1)
+    d_own, g_own, g_w = {}, {}, {}
 
     def own_step(k):
         pieces[k] = in_turn(pieces[k])
-        d_own[k] = delta_of(embeds, ids, pieces[k], k)
+        d_own[k] = delta_of(embeds, ids, pieces[k], [k])
         g_own[k] = grad_w_of(d_own[k], embeds)
         last[0] = g_own[k]
 
-    def next_step(c, k):
-        d_next[c][k] = delta_of(next_rows[c], next_ids[c * run:(c + 1) * run], in_turn(pieces[k]), k)
-        g_own[k] = g_own[k] + grad_w_of(d_next[c][k], next_rows[c])
-        last[0] = g_own[k]
+    def add_next(k):
+        g_w[k] = (g_own[k] + grad_w_of(in_turn(d_next[:, k * ch_dev:(k + 1) * ch_dev]), next_rows)) * scale
+        last[0] = g_w[k]
 
+    early, late = list(range(n_dp - 1)), n_dp - 1
     own_step(0)
     next_ids = to_label(in_turn(ids), -1)
-    for k in range(1, n_dp):
-        own_step(k)
-    next_ids = in_turn(next_ids)
-    for c in range(CHUNKS):
-        for k in range(n_dp - 1, -1, -1):
-            next_step(c, k)
-    theirs = [grad_x_of([d_next[c][k] for k in range(n_dp)]).astype(jnp.bfloat16) for c in range(CHUNKS)]
-    last[0] = theirs[-1]
-    back = [to_label(t, 1) for t in theirs]
+    own_step(1)
+    next_rows, next_ids, _ = lax.optimization_barrier((next_rows, next_ids, last[0]))
+    d_early = delta_of(
+        in_turn(next_rows), next_ids, jnp.concatenate([pieces[k] for k in early], axis=0), early
+    )
+    last[0] = d_early
+    d_late = delta_of(next_rows, next_ids, in_turn(pieces[late]), [late])
+    d_next = jnp.concatenate([d_early, d_late], axis=1)
+    last[0] = d_next
+    theirs = grad_x_of([d_next]).astype(jnp.bfloat16)
+    last[0] = theirs
+    back = to_label(theirs, 1)
 
     relayed, moved, low, high = {}, [], [], []
-    for k in range(n_dp - 1, 0, -1):
+    for k in [k for k in range(late, 0, -1) if k not in g_own] + [1]:
+        if k not in g_own:
+            own_step(k)
+        add_next(k)
+    for k in range(late, 0, -1):
         step = k & -k
-        whole = g_own[k] * scale
+        whole = g_w[k]
         if step == k and k not in relayed:
             moved.append(to_dp(whole.astype(jnp.bfloat16), k))
             continue
@@ -105,10 +112,12 @@
             high.append(to_dp(part, k))
         else:
             relayed.setdefault(k ^ step, []).append(in_turn(to_dp(part, step)))
-        low.append(to_dp(whole[:direct].astype(jnp.bfloat16), k))
+        if direct:
+            low.append(to_dp(in_turn(whole)[:direct].astype(jnp.bfloat16), k))
     grad_x = grad_x_of([d_own[k] for k in range(n_dp)])
     last[0] = grad_x
-    grad_w = g_own[0] * scale
+    add_next(0)
+    grad_w = g_w[0]
     for term in moved:
         grad_w = grad_w + in_turn(term).astype(jnp.float32)
     if high:
@@ -120,7 +129,7 @@
         grad_w = jnp.concatenate([rest, grad_w], axis=0)
     grad_w = grad_w.astype(jnp.bfloat16)
     last[0] = grad_w
-    grad_x = (grad_x + jnp.concatenate([in_turn(b) for b in back], axis=0).astype(jnp.float32)).astype(jnp.bfloat16)
+    grad_x = (grad_x + in_turn(back).astype(jnp.float32)).astype(jnp.bfloat16)
     return (grad_w, grad_x)
 
 

time: 55.6 us -> 56.4 us (1.014)
  matrix products: 12.3 us -> 17.1 us
  waiting for transfers between devices: 21.8 us -> 19 us
  starting transfers between devices: 16.6 us -> 15.4 us
    ppermute x8, starting transfers between devices: 14.9 us -> 12.8 us  [to_dp(): return lax.ppermute(x, 'dp', [(i, i ^ k) for i in range(n_dp)])]
    dot_general x2, matrix products: 2.02 us -> 4.09 us  [grad_x_of(): jnp.dot(in_turn(jnp.concatenate(deltas, axis=1)), jnp.concatenate([pieces...]
    ppermute x8, waiting for transfers between devices: 21 us -> 19 us  [to_dp(): return lax.ppermute(x, 'dp', [(i, i ^ k) for i in range(n_dp)])]
    dot_general x8 -> x6, matrix products: 7.22 us -> 9.15 us  [delta_of(): lax.dot_general(rows, piece, (((1,), (1,)), ((), ())), preferred_element_...]
    ppermute x3, starting transfers between devices: 1.72 us -> 2.56 us  [to_label(): lax.ppermute(x, 'label', [(i, (i + by) % n_label) for i in range(n_label)])]
    ppermute x3, waiting for transfers between devices: 0.83 us -> 0.01 us  [to_label(): lax.ppermute(x, 'label', [(i, (i + by) % n_label) for i in range(n_label)])]
    dot_general x8, matrix products: 3.06 us -> 3.86 us  [grad_w_of(): lax.dot_general(delta, rows, (((0,), (0,)), ((), ())), preferred_element_...]
  transfers between devices with their start and end apart: 11 -> 11, of which waited for: 5 -> 3; matrix products, arithmetic and copies ran while one was open for 24% -> 26% of each run, Pallas kernels for 0% -> 0%
where the time goes in v10:
time: 56.4 us; the launch traced here: 56.1 us
  waiting for transfers between devices  19 us (34%)
  matrix products  17.1 us (30%)
  starting transfers between devices  15.4 us (27%)
  other arithmetic  3.59 us (6%)
  between operations  0.89 us (2%)
    ppermute x8, waiting for transfers between devices, to_dp(): return lax.ppermute(x, 'dp', [(i, i ^ k) for i in range(n_dp)])  19 us
    ppermute x8, starting transfers between devices, to_dp(): return lax.ppermute(x, 'dp', [(i, i ^ k) for i in range(n_dp)])  12.8 us
    dot_general x6, matrix products, delta_of(): lax.dot_general(rows, piece, (((1,), (1,)), ((), ())), preferred_element_...  9.15 us
    dot_general x2, matrix products, grad_x_of(): jnp.dot(in_turn(jnp.concatenate(deltas, axis=1)), jnp.concatenate([pieces...  4.09 us
    dot_general x8, matrix products, grad_w_of(): lax.dot_general(delta, rows, (((0,), (0,)), ((), ())), preferred_element_...  3.86 us
    ppermute x3, starting transfers between devices, to_label(): lax.ppermute(x, 'label', [(i, (i + by) % n_label) for i in range(n_label)])  2.56 us
    convert_element_type x1, other arithmetic, local(): grad_x = (grad_x + in_turn(back).astype(jnp.float32)).astype(jnp.bfloat16)  1.75 us
  transfers between devices with their start and end apart: 11, of which 3 were waited for; matrix products, arithmetic and copies ran while one was open for 26% of the time, Pallas kernels for 0%

profile of v10, /device:TPU:0, one launch (start us, length us, event | category | flops | bytes accessed | tf_op | source)
XLA Modules:
  0.0 56.1 jit_solution(11202508314661822512)
XLA Ops:
  0.6 2.4 %collective-permute-start = (bf16[768,1024]{1,0:T(8,128)(2,1)}, bf16[768,1024]{1,0:T(8,128)(2,1)S(1)}, u32[]{:S(2)}, u32[]{:S(2)}) collective-permute-start(bf16[768,1024]{1,0:T(8,128)(2,1)} %param.4), channel_id=1, source_target_pairs={{0,12},{4,0},{8,4},{12,8},{1,13},{5,1},{9,5},{13,9},{2,14},{6,2},{... | collective-permute-start | bytes 4718600 | tf_op jit(solution)/shard_map/ppermute | solution.py:36
  3.1 2.6 %collective-permute-start.3 = (bf16[128,1024]{1,0:T(8,128)(2,1)}, bf16[128,1024]{1,0:T(8,128)(2,1)}, u32[]{:S(2)}, u32[]{:S(2)}) collective-permute-start(bf16[128,1024]{1,0:T(8,128)(2,1)} %param.5), channel_id=1, source_target_pairs={{0,2},{1,3},{2,0},{3,1},{4,6},{5,7},{6,4},{7,5},{8,10},{9,11},{10,... | collective-permute-start | bytes 786440 | tf_op jit(solution)/shard_map/ppermute | solution.py:33
  5.7 1.6 %collective-permute-start.2 = (bf16[128,1024]{1,0:T(8,128)(2,1)}, bf16[128,1024]{1,0:T(8,128)(2,1)}, u32[]{:S(2)}, u32[]{:S(2)}) collective-permute-start(bf16[128,1024]{1,0:T(8,128)(2,1)} %param.5), channel_id=1, source_target_pairs={{0,1},{1,0},{2,3},{3,2},{4,5},{5,4},{6,7},{7,6},{8,9},{9,8},{10,11... | collective-permute-start | bytes 786440 | tf_op jit(solution)/shard_map/ppermute | solution.py:33
  7.2 0.7 %fusion.57 = s32[768,8]{0,1:T(8,128)S(1)} fusion(s32[768,8]{0,1:T(8,128)} %param.6, s32[768]{0:T(1024)} %param.7), kind=kLoop, calls=%fused_computation.87 | loop fusion | flops 12288 | bytes 52224 | tf_op jit(solution)/shard_map/jit(_where)/select_n | solution.py:24
  8.0 0.0 copy-start
  8.0 2.3 %fusion.38 = bf16[768,128]{0,1:T(8,128)(2,1)S(1)} fusion(bf16[128,1024]{1,0:T(8,128)(2,1)} %param.5, bf16[768,1024]{1,0:T(8,128)(2,1)} %param.4, s32[768]{0:T(1024)S(1)} %get-tuple-element.49), kind=kOutput, calls=%fused_computation.51 | convolution fusion | flops 202014720 | bytes 2034688 | tf_op jit(solution)/shard_map/dot_general | solution.py:45
  10.3 0.0 copy-done
  10.4 1.2 %fusion.62 = f32[128,1024]{1,0:T(8,128)} fusion(bf16[768,128]{0,1:T(8,128)(2,1)S(1)} %fusion.38, bf16[768,1024]{1,0:T(8,128)(2,1)S(1)} %copy-done), kind=kOutput, calls=%fused_computation.102 | convolution fusion | flops 201326592 | bytes 2293760 | tf_op jit(solution)/shard_map/dot_general | solution.py:51
  11.5 0.1 collective-permute-start.1
  11.7 6.3 %collective-permute-done.2 = bf16[128,1024]{1,0:T(8,128)(2,1)} collective-permute-done((bf16[128,1024]{1,0:T(8,128)(2,1)}, bf16[128,1024]{1,0:T(8,128)(2,1)}, u32[]{:S(2)}, u32[]{:S(2)}) %collective-permute-start.2) | collective-permute-done | bytes 262176 | tf_op jit(solution)/shard_map/ppermute | solution.py:33
  17.9 1.6 %fusion.37 = bf16[768,128]{0,1:T(8,128)(2,1)S(1)} fusion(bf16[128,1024]{1,0:T(8,128)(2,1)} %collective-permute-done.2, bf16[768,1024]{1,0:T(8,128)(2,1)S(1)} %copy-done, s32[768]{0:T(1024)S(1)} %get-tuple-element.48), kind=kOutput, calls=%fused_computation.50 | convolution fusion | flops 202014720 | bytes 2034688 | tf_op jit(solution)/shard_map/dot_general | solution.py:45
  19.6 0.0 copy-start.2
  19.6 0.4 fusion.63
  20.0 0.0 collective-permute-done.3
  20.0 1.6 %collective-permute-start.4 = (bf16[128,1024]{1,0:T(8,128)(2,1)}, bf16[128,1024]{1,0:T(8,128)(2,1)S(1)}, u32[]{:S(2)}, u32[]{:S(2)}) collective-permute-start(bf16[128,1024]{1,0:T(8,128)(2,1)} %collective-permute-done.3), channel_id=1, source_target_pairs={{0,1},{1,0},{2,3},{3,2},{4,5},{5,4},{6,7},{7,6},{8,9},{9,8},{10,11... | collective-permute-start | bytes 786440 | tf_op jit(solution)/shard_map/ppermute | solution.py:33
  21.6 0.0 collective-permute-done.1
  21.6 0.0 collective-permute-done
  21.6 0.0 copy-done.2
  21.6 2.1 %fusion.4 = bf16[768,384]{0,1:T(8,128)(2,1)S(1)} fusion(bf16[768,1024]{1,0:T(8,128)(2,1)S(1)} %collective-permute-done, bf16[128,1024]{1,0:T(8,128)(2,1)} %collective-permute-done.3, bf16[128,1024]{1,0:T(8,128)(2,1)} %collective-permute-done.2, bf16[128,1024]{1,0:T(8,128)(2,1)S(1)} %copy-done.2, s32[768]{0:T(1024)S(1)} %get-tuple-element.51, ...), kind=kOutput, calls=%fused_computation.7 | convolution fusion | flops 608993280 | bytes 2959104 | tf_op jit(solution)/shard_map/dot_general | solution.py:45
  23.8 3.1 %collective-permute-done.4 = bf16[128,1024]{1,0:T(8,128)(2,1)S(1)} collective-permute-done((bf16[128,1024]{1,0:T(8,128)(2,1)}, bf16[128,1024]{1,0:T(8,128)(2,1)S(1)}, u32[]{:S(2)}, u32[]{:S(2)}) %collective-permute-start.4) | collective-permute-done | bytes 262176 | tf_op jit(solution)/shard_map/ppermute | solution.py:33
  26.9 0.7 %fusion.36 = bf16[768,128]{0,1:T(8,128)(2,1)S(1)} fusion(bf16[768,1024]{1,0:T(8,128)(2,1)S(1)} %collective-permute-done, bf16[128,1024]{1,0:T(8,128)(2,1)S(1)} %collective-permute-done.4, s32[768]{0:T(1024)S(1)} %get-tuple-element.50), kind=kOutput, calls=%fused_computation.49 | convolution fusion | flops 202014720 | bytes 2034688 | tf_op jit(solution)/shard_map/dot_general | solution.py:45
  27.6 0.1 pad_maximum_fusion.3
  27.7 2.0 %convolution_convert_fusion = bf16[768,1024]{1,0:T(8,128)(2,1)S(1)} fusion(bf16[768,512]{0,1:T(8,128)(2,1)S(1)} %pad_maximum_fusion.3, bf16[128,1024]{1,0:T(8,128)(2,1)S(1)} %collective-permute-done.4, bf16[128,1024]{1,0:T(8,128)(2,1)} %collective-permute-done.3, bf16[128,1024]{1,0:T(8,128)(2,1)} %collective-permute-done.2, bf16[128,1024]{1,0:T(8,128)(2,1)S(1)} %copy-done.2), kind=kOutput, calls=%fused_computation.1 | convolution fusion | flops 810287104 | bytes 3407872 | tf_op jit(solution)/shard_map/dot_general | solution.py:56
  29.7 0.7 %fusion.35 = bf16[768,128]{0,1:T(8,128)(2,1)S(1)} fusion(bf16[128,1024]{1,0:T(8,128)(2,1)S(1)} %collective-permute-done.4, bf16[768,1024]{1,0:T(8,128)(2,1)S(1)} %copy-done, s32[768]{0:T(1024)S(1)} %get-tuple-element.47), kind=kOutput, calls=%fused_computation.48 | convolution fusion | flops 202014720 | bytes 2034688 | tf_op jit(solution)/shard_map/dot_general | solution.py:45
  30.4 0.4 fusion.64
  30.8 0.4 fusion.8
  31.2 1.8 %collective-permute-start.5 = (bf16[96,1024]{1,0:T(8,128)(2,1)S(1)}, bf16[96,1024]{1,0:T(8,128)(2,1)S(1)}, u32[]{:S(2)}, u32[]{:S(2)}) collective-permute-start(bf16[96,1024]{1,0:T(8,128)(2,1)S(1)} %slice.62), channel_id=1, source_target_pairs={{0,1},{1,0},{2,3},{3,2},{4,5},{5,4},{6,7},{7,6},{8,9},{9,8},{10,11... | collective-permute-start | bytes 589832 | tf_op jit(solution)/shard_map/ppermute | solution.py:33
  33.1 0.0 collective-permute-start.10
  33.1 1.5 %collective-permute-start.7 = (bf16[32,1024]{1,0:T(8,128)(2,1)S(1)}, bf16[32,1024]{1,0:T(8,128)(2,1)S(1)}, u32[]{:S(2)}, u32[]{:S(2)}) collective-permute-start(bf16[32,1024]{1,0:T(8,128)(2,1)S(1)} %slice.64), channel_id=1, source_target_pairs={{0,3},{1,2},{2,1},{3,0},{4,7},{5,6},{6,5},{7,4},{8,11},{9,10},{10,... | collective-permute-start | bytes 196616 | tf_op jit(solution)/shard_map/ppermute | solution.py:33
  34.5 1.6 %fusion.34 = bf16[768,128]{0,1:T(8,128)(2,1)S(1)} fusion(bf16[128,1024]{1,0:T(8,128)(2,1)} %collective-permute-done.3, bf16[768,1024]{1,0:T(8,128)(2,1)S(1)} %copy-done, s32[768]{0:T(1024)S(1)} %get-tuple-element.46), kind=kOutput, calls=%fused_computation.47 | convolution fusion | flops 202014720 | bytes 2034688 | tf_op jit(solution)/shard_map/dot_general | solution.py:45
  36.2 0.4 fusion.65
  36.6 0.4 fusion.7
  37.0 0.4 fusion.9
  37.4 0.8 %collective-permute-start.6 = (bf16[128,1024]{1,0:T(8,128)(2,1)S(1)}, bf16[128,1024]{1,0:T(8,128)(2,1)S(1)}, u32[]{:S(2)}, u32[]{:S(2)}) collective-permute-start(bf16[128,1024]{1,0:T(8,128)(2,1)S(1)} %fusion.9), channel_id=1, source_target_pairs={{0,1},{1,0},{2,3},{3,2},{4,5},{5,4},{6,7},{7,6},{8,9},{9,8},{10,11... | collective-permute-start | bytes 786440 | tf_op jit(solution)/shard_map/ppermute | solution.py:33
  38.1 0.1 pad_maximum_fusion.4
  38.2 0.0 collective-permute-done.5
  38.2 2.4 %collective-permute-start.9 = (bf16[96,1024]{1,0:T(8,128)(2,1)S(1)}, bf16[96,1024]{1,0:T(8,128)(2,1)S(1)}, u32[]{:S(2)}, u32[]{:S(2)}) collective-permute-start(bf16[96,1024]{1,0:T(8,128)(2,1)S(1)} %fusion.54), channel_id=1, source_target_pairs={{0,2},{1,3},{2,0},{3,1},{4,6},{5,7},{6,4},{7,5},{8,10},{9,11},{10,... | collective-permute-start | bytes 589832 | tf_op jit(solution)/shard_map/ppermute | solution.py:33
  40.6 0.0 copy-start.1
  40.6 0.7 %collective-permute-start.8 = (bf16[32,1024]{1,0:T(8,128)(2,1)S(1)}, bf16[32,1024]{1,0:T(8,128)(2,1)S(1)}, u32[]{:S(2)}, u32[]{:S(2)}) collective-permute-start(bf16[32,1024]{1,0:T(8,128)(2,1)S(1)} %slice.63), channel_id=1, source_target_pairs={{0,2},{1,3},{2,0},{3,1},{4,6},{5,7},{6,4},{7,5},{8,10},{9,11},{10,... | collective-permute-start | bytes 196616 | tf_op jit(solution)/shard_map/ppermute | solution.py:33
  41.3 2.0 %fusion.43 = f32[768,1024]{1,0:T(8,128)S(1)} fusion(bf16[768,512]{0,1:T(8,128)(2,1)S(1)} %pad_maximum_fusion.4, bf16[128,1024]{1,0:T(8,128)(2,1)S(1)} %collective-permute-done.4, bf16[128,1024]{1,0:T(8,128)(2,1)} %collective-permute-done.3, bf16[128,1024]{1,0:T(8,128)(2,1)} %collective-permute-done.2, bf16[128,1024]{1,0:T(8,128)(2,1)S(1)} %copy-done.2), kind=kOutput, calls=%fused_computation.57 | convolution fusion | flops 809500672 | bytes 4980736 | tf_op jit(solution)/shard_map/dot_general | solution.py:56
  43.4 0.0 copy-done.1
  43.4 0.4 fusion.6
  43.8 0.0 collective-permute-done.7
  43.8 9.7 %collective-permute-done.8 = bf16[32,1024]{1,0:T(8,128)(2,1)S(1)} collective-permute-done((bf16[32,1024]{1,0:T(8,128)(2,1)S(1)}, bf16[32,1024]{1,0:T(8,128)(2,1)S(1)}, u32[]{:S(2)}, u32[]{:S(2)}) %collective-permute-start.8) | collective-permute-done | bytes 65568 | tf_op jit(solution)/shard_map/ppermute | solution.py:33
  53.4 0.0 collective-permute-done.6
  53.4 0.1 convert_add_fusion
  53.5 0.0 collective-permute-done.9
  53.6 0.7 %pad_maximum_fusion.5 = bf16[128,1024]{1,0:T(8,128)(2,1)} fusion(bf16[96,1024]{1,0:T(8,128)(2,1)S(1)} %fusion.53, bf16[32,1024]{1,0:T(8,128)(2,1)S(1)} %fusion.56), kind=kLoop, calls=%fused_computation.80 | loop fusion | flops 524288 | bytes 524288 | tf_op jit(solution)/shard_map/concatenate | solution.py:129
  54.3 0.0 collective-permute-done.10
  54.3 1.8 %add_convert_fusion = bf16[768,1024]{1,0:T(8,128)(2,1)} fusion(f32[768,1024]{1,0:T(8,128)S(1)} %fusion.43, bf16[768,1024]{1,0:T(8,128)(2,1)S(1)} %collective-permute-done.10), kind=kLoop, calls=%fused_computation | loop fusion | flops 2359296 | bytes 6291456 | tf_op jit(solution)/shard_map/convert_element_type | solution.py:132
  (10 shorter events, 0.3 us)
Async XLA Ops:
  0.6 20.9 %collective-permute-start = (bf16[768,1024]{1,0:T(8,128)(2,1)}, bf16[768,1024]{1,0:T(8,128)(2,1)S(1)}, u32[]{:S(2)}, u32[]{:S(2)}) collective-permute-start(bf16[768,1024]{1,0:T(8,128)(2,1)} %param.4), channel_id=1, source_target_pairs={{0,12},{4,0},{8,4},{12,8},{1,13},{5,1},{9,5},{13,9},{2,14},{6,2},{... | collective-permute-start | bytes 4718600 | tf_op jit(solution)/shard_map/ppermute | solution.py:36
  3.1 16.9 %collective-permute-start.3 = (bf16[128,1024]{1,0:T(8,128)(2,1)}, bf16[128,1024]{1,0:T(8,128)(2,1)}, u32[]{:S(2)}, u32[]{:S(2)}) collective-permute-start(bf16[128,1024]{1,0:T(8,128)(2,1)} %param.5), channel_id=1, source_target_pairs={{0,2},{1,3},{2,0},{3,1},{4,6},{5,7},{6,4},{7,5},{8,10},{9,11},{10,... | collective-permute-start | bytes 786440 | tf_op jit(solution)/shard_map/ppermute | solution.py:33
  5.7 12.3 %collective-permute-start.2 = (bf16[128,1024]{1,0:T(8,128)(2,1)}, bf16[128,1024]{1,0:T(8,128)(2,1)}, u32[]{:S(2)}, u32[]{:S(2)}) collective-permute-start(bf16[128,1024]{1,0:T(8,128)(2,1)} %param.5), channel_id=1, source_target_pairs={{0,1},{1,0},{2,3},{3,2},{4,5},{5,4},{6,7},{7,6},{8,9},{9,8},{10,11... | collective-permute-start | bytes 786440 | tf_op jit(solution)/shard_map/ppermute | solution.py:33
  8.0 2.3 %copy-start = (bf16[768,1024]{1,0:T(8,128)(2,1)S(1)}, bf16[768,1024]{1,0:T(8,128)(2,1)}, u32[]{:S(2)}) copy-start(bf16[768,1024]{1,0:T(8,128)(2,1)} %param.4) | copy-start | bytes 4718596
  11.5 10.0 %collective-permute-start.1 = (s32[768,8]{0,1:T(8,128)S(1)}, s32[768,8]{0,1:T(8,128)S(1)}, u32[]{:S(2)}, u32[]{:S(2)}) collective-permute-start(s32[768,8]{0,1:T(8,128)S(1)} %fusion.57), channel_id=1, source_target_pairs={{0,12},{4,0},{8,4},{12,8},{1,13},{5,1},{9,5},{13,9},{2,14},{6,2},{... | collective-permute-start | bytes 73736 | tf_op jit(solution)/shard_map/ppermute | solution.py:36
  19.6 2.0 %copy-start.2 = (bf16[128,1024]{1,0:T(8,128)(2,1)S(1)}, bf16[128,1024]{1,0:T(8,128)(2,1)}, u32[]{:S(2)}) copy-start(bf16[128,1024]{1,0:T(8,128)(2,1)} %param.5) | copy-start | bytes 786436
  20.0 6.9 %collective-permute-start.4 = (bf16[128,1024]{1,0:T(8,128)(2,1)}, bf16[128,1024]{1,0:T(8,128)(2,1)S(1)}, u32[]{:S(2)}, u32[]{:S(2)}) collective-permute-start(bf16[128,1024]{1,0:T(8,128)(2,1)} %collective-permute-done.3), channel_id=1, source_target_pairs={{0,1},{1,0},{2,3},{3,2},{4,5},{5,4},{6,7},{7,6},{8,9},{9,8},{10,11... | collective-permute-start | bytes 786440 | tf_op jit(solution)/shard_map/ppermute | solution.py:33
  31.2 6.9 %collective-permute-start.5 = (bf16[96,1024]{1,0:T(8,128)(2,1)S(1)}, bf16[96,1024]{1,0:T(8,128)(2,1)S(1)}, u32[]{:S(2)}, u32[]{:S(2)}) collective-permute-start(bf16[96,1024]{1,0:T(8,128)(2,1)S(1)} %slice.62), channel_id=1, source_target_pairs={{0,1},{1,0},{2,3},{3,2},{4,5},{5,4},{6,7},{7,6},{8,9},{9,8},{10,11... | collective-permute-start | bytes 589832 | tf_op jit(solution)/shard_map/ppermute | solution.py:33
  33.1 21.3 %collective-permute-start.10 = (bf16[768,1024]{1,0:T(8,128)(2,1)S(1)}, bf16[768,1024]{1,0:T(8,128)(2,1)S(1)}, u32[]{:S(2)}, u32[]{:S(2)}) collective-permute-start(bf16[768,1024]{1,0:T(8,128)(2,1)S(1)} %convolution_convert_fusion), channel_id=1, source_target_pairs={{0,4},{4,8},{8,12},{12,0},{1,5},{5,9},{9,13},{13,1},{2,6},{6,10},{... | collective-permute-start | bytes 4718600 | tf_op jit(solution)/shard_map/ppermute | solution.py:36
  33.1 10.7 %collective-permute-start.7 = (bf16[32,1024]{1,0:T(8,128)(2,1)S(1)}, bf16[32,1024]{1,0:T(8,128)(2,1)S(1)}, u32[]{:S(2)}, u32[]{:S(2)}) collective-permute-start(bf16[32,1024]{1,0:T(8,128)(2,1)S(1)} %slice.64), channel_id=1, source_target_pairs={{0,3},{1,2},{2,1},{3,0},{4,7},{5,6},{6,5},{7,4},{8,11},{9,10},{10,... | collective-permute-start | bytes 196616 | tf_op jit(solution)/shard_map/ppermute | solution.py:33
  37.4 16.1 %collective-permute-start.6 = (bf16[128,1024]{1,0:T(8,128)(2,1)S(1)}, bf16[128,1024]{1,0:T(8,128)(2,1)S(1)}, u32[]{:S(2)}, u32[]{:S(2)}) collective-permute-start(bf16[128,1024]{1,0:T(8,128)(2,1)S(1)} %fusion.9), channel_id=1, source_target_pairs={{0,1},{1,0},{2,3},{3,2},{4,5},{5,4},{6,7},{7,6},{8,9},{9,8},{10,11... | collective-permute-start | bytes 786440 | tf_op jit(solution)/shard_map/ppermute | solution.py:33
  38.2 15.3 %collective-permute-start.9 = (bf16[96,1024]{1,0:T(8,128)(2,1)S(1)}, bf16[96,1024]{1,0:T(8,128)(2,1)S(1)}, u32[]{:S(2)}, u32[]{:S(2)}) collective-permute-start(bf16[96,1024]{1,0:T(8,128)(2,1)S(1)} %fusion.54), channel_id=1, source_target_pairs={{0,2},{1,3},{2,0},{3,1},{4,6},{5,7},{6,4},{7,5},{8,10},{9,11},{10,... | collective-permute-start | bytes 589832 | tf_op jit(solution)/shard_map/ppermute | solution.py:33
  40.6 2.8 %copy-start.1 = (f32[128,1024]{1,0:T(8,128)S(1)}, f32[128,1024]{1,0:T(8,128)}, u32[]{:S(2)}) copy-start(f32[128,1024]{1,0:T(8,128)} %fusion.62) | copy-start | bytes 1572868
  40.6 12.8 %collective-permute-start.8 = (bf16[32,1024]{1,0:T(8,128)(2,1)S(1)}, bf16[32,1024]{1,0:T(8,128)(2,1)S(1)}, u32[]{:S(2)}, u32[]{:S(2)}) collective-permute-start(bf16[32,1024]{1,0:T(8,128)(2,1)S(1)} %slice.63), channel_id=1, source_target_pairs={{0,2},{1,3},{2,0},{3,1},{4,6},{5,7},{6,4},{7,5},{8,10},{9,11},{10,... | collective-permute-start | bytes 196616 | tf_op jit(solution)/shard_map/ppermute | solution.py:33

commit v11 on v10

--- a/solution.py
+++ b/solution.py
@@ -6,7 +6,8 @@
 from jax.sharding import PartitionSpec as P
 
 
-DIRECT_EIGHTHS = 2
+SCATTER_DIRECT_EIGHTHS = 2
+GATHER_DIRECT_EIGHTHS = 4
 
 
 def local(embeds, weights, pos_ids, pos_count):
@@ -22,7 +23,8 @@
     scale = 1.0 / math.sqrt(rows_dev * n_dp)
     valid = jnp.arange(slots, dtype=jnp.int32)[None, :] < pos_count[:, None]
     ids = jnp.where(valid, pos_ids, -1)
-    direct = ch_dev * DIRECT_EIGHTHS // 8
+    direct = ch_dev * SCATTER_DIRECT_EIGHTHS // 8
+    ahead = ch_dev * GATHER_DIRECT_EIGHTHS // 8
     last = [embeds]
 
     def in_turn(x):
@@ -35,13 +37,11 @@
     def to_label(x, by):
         return lax.ppermute(x, "label", [(i, (i + by) % n_label) for i in range(n_label)])
 
-    def delta_of(rows, row_ids, piece, ks):
-        starts = [me_label * stretch + (me_dp ^ k) * ch_dev for k in ks]
-        place = jnp.arange(len(ks) * ch_dev, dtype=jnp.int32)[None, :]
-        for i, start in enumerate(starts):
-            column = lax.dynamic_slice_in_dim(row_ids, start // span, 1, axis=1) - (start - i * ch_dev)
-            sought = column if i == 0 else jnp.where(place < i * ch_dev, sought, column)
-        target = (sought == place).astype(jnp.float32)
+    def delta_of(rows, row_ids, piece, k):
+        start = me_label * stretch + (me_dp ^ k) * ch_dev
+        column = lax.dynamic_slice_in_dim(row_ids, start // span, 1, axis=1)
+        labels = start + jnp.arange(ch_dev, dtype=jnp.int32)
+        target = (column == labels[None, :]).astype(jnp.float32)
         logits = lax.dot_general(
             rows, piece, (((1,), (1,)), ((), ())), preferred_element_type=jnp.float32
         )
@@ -54,48 +54,52 @@
 
     def grad_x_of(deltas):
         return jnp.dot(
-            in_turn(jnp.concatenate(deltas, axis=1)),
+            in_turn(jnp.concatenate([deltas[k] for k in range(n_dp)], axis=1)),
             jnp.concatenate([pieces[k] for k in range(n_dp)], axis=0),
             preferred_element_type=jnp.float32,
         )
 
     pieces = {0: weights}
-    for k in range(1, n_dp):
-        step = k & -k
-        pieces[k] = to_dp(pieces[k ^ step], step)
+    for k in range(2, n_dp):
+        if k & -k == k:
+            pieces[k] = to_dp(weights, k)
     next_rows = to_label(embeds, -1)
     d_own, g_own, g_w = {}, {}, {}
 
     def own_step(k):
         pieces[k] = in_turn(pieces[k])
-        d_own[k] = delta_of(embeds, ids, pieces[k], [k])
+        d_own[k] = delta_of(embeds, ids, pieces[k], k)
         g_own[k] = grad_w_of(d_own[k], embeds)
         last[0] = g_own[k]
 
     def add_next(k):
-        g_w[k] = (g_own[k] + grad_w_of(in_turn(d_next[:, k * ch_dev:(k + 1) * ch_dev]), next_rows)) * scale
+        g_w[k] = (g_own[k] + grad_w_of(in_turn(d_next[k]), next_rows)) * scale
         last[0] = g_w[k]
 
-    early, late = list(range(n_dp - 1)), n_dp - 1
+    late = n_dp - 1
     own_step(0)
+    later = in_turn(weights)
+    pieces[1] = to_dp(later, 1)
+    for k in range(2, n_dp):
+        step = k & -k
+        if step < k:
+            pieces[k] = jnp.concatenate(
+                [to_dp(later[:ahead], k), to_dp(pieces[k ^ step][ahead:], step)], axis=0
+            )
     next_ids = to_label(in_turn(ids), -1)
-    own_step(1)
+    for k in range(1, n_dp):
+        own_step(k)
     next_rows, next_ids, _ = lax.optimization_barrier((next_rows, next_ids, last[0]))
-    d_early = delta_of(
-        in_turn(next_rows), next_ids, jnp.concatenate([pieces[k] for k in early], axis=0), early
-    )
-    last[0] = d_early
-    d_late = delta_of(next_rows, next_ids, in_turn(pieces[late]), [late])
-    d_next = jnp.concatenate([d_early, d_late], axis=1)
-    last[0] = d_next
-    theirs = grad_x_of([d_next]).astype(jnp.bfloat16)
+    d_next = {}
+    for k in range(late, -1, -1):
+        d_next[k] = delta_of(next_rows, next_ids, in_turn(pieces[k]), k)
+        last[0] = d_next[k]
+    theirs = grad_x_of(d_next).astype(jnp.bfloat16)
     last[0] = theirs
     back = to_label(theirs, 1)
 
     relayed, moved, low, high = {}, [], [], []
-    for k in [k for k in range(late, 0, -1) if k not in g_own] + [1]:
-        if k not in g_own:
-            own_step(k)
+    for k in range(late, 0, -1):
         add_next(k)
     for k in range(late, 0, -1):
         step = k & -k
@@ -114,7 +118,7 @@
             relayed.setdefault(k ^ step, []).append(in_turn(to_dp(part, step)))
         if direct:
             low.append(to_dp(in_turn(whole)[:direct].astype(jnp.bfloat16), k))
-    grad_x = grad_x_of([d_own[k] for k in range(n_dp)])
+    grad_x = grad_x_of(d_own)
     last[0] = grad_x
     add_next(0)
     grad_w = g_w[0]

time: 56.4 us -> 56.5 us (level)
  waiting for transfers between devices: 19 us -> 23.9 us
  matrix products: 17.1 us -> 12.3 us
    ppermute x8 -> x9, waiting for transfers between devices: 19 us -> 23.9 us  [to_dp(): return lax.ppermute(x, 'dp', [(i, i ^ k) for i in range(n_dp)])]
    dot_general x2, matrix products: 4.09 us -> 2.02 us  [grad_x_of(): jnp.dot(in_turn(jnp.concatenate([deltas[k] for k in range(n_dp)], axis=1)...]
    dot_general x6 -> x8, matrix products: 9.15 us -> 7.26 us  [delta_of(): lax.dot_general(rows, piece, (((1,), (1,)), ((), ())), preferred_element_...]
    ppermute x8 -> x9, starting transfers between devices: 12.8 us -> 13.7 us  [to_dp(): return lax.ppermute(x, 'dp', [(i, i ^ k) for i in range(n_dp)])]
    ppermute x3, starting transfers between devices: 2.56 us -> 1.71 us  [to_label(): lax.ppermute(x, 'label', [(i, (i + by) % n_label) for i in range(n_label)])]
    dot_general x8, matrix products: 3.86 us -> 3.05 us  [grad_w_of(): lax.dot_general(delta, rows, (((0,), (0,)), ((), ())), preferred_element_...]
  transfers between devices with their start and end apart: 11 -> 12, of which waited for: 3 -> 4; matrix products, arithmetic and copies ran while one was open for 26% -> 18% of each run, Pallas kernels for 0% -> 0%
where the time goes in v11:
time: 56.5 us; the launch traced here: 56.3 us
  waiting for transfers between devices  23.9 us (42%)
  starting transfers between devices  15.4 us (27%)
  matrix products  12.3 us (22%)
  other arithmetic  3.54 us (6%)
  between operations  0.96 us (2%)
    ppermute x9, waiting for transfers between devices, to_dp(): return lax.ppermute(x, 'dp', [(i, i ^ k) for i in range(n_dp)])  23.9 us
    ppermute x9, starting transfers between devices, to_dp(): return lax.ppermute(x, 'dp', [(i, i ^ k) for i in range(n_dp)])  13.7 us
    dot_general x8, matrix products, delta_of(): lax.dot_general(rows, piece, (((1,), (1,)), ((), ())), preferred_element_...  7.26 us
    dot_general x8, matrix products, grad_w_of(): lax.dot_general(delta, rows, (((0,), (0,)), ((), ())), preferred_element_...  3.05 us
    dot_general x2, matrix products, grad_x_of(): jnp.dot(in_turn(jnp.concatenate([deltas[k] for k in range(n_dp)], axis=1)...  2.02 us
    convert_element_type x1, other arithmetic, local(): grad_x = (grad_x + in_turn(back).astype(jnp.float32)).astype(jnp.bfloat16)  1.75 us
    ppermute x3, starting transfers between devices, to_label(): lax.ppermute(x, 'label', [(i, (i + by) % n_label) for i in range(n_label)])  1.71 us
  transfers between devices with their start and end apart: 12, of which 4 were waited for; matrix products, arithmetic and copies ran while one was open for 18% of the time, Pallas kernels for 0%

profile of v11, /device:TPU:0, one launch (start us, length us, event | category | flops | bytes accessed | tf_op | source)
XLA Modules:
  0.0 56.3 jit_solution(7031116758796529157)
XLA Ops:
  0.6 4.1 %collective-permute-start.3 = (bf16[128,1024]{1,0:T(8,128)(2,1)}, bf16[128,1024]{1,0:T(8,128)(2,1)S(1)}, u32[]{:S(2)}, u32[]{:S(2)}) collective-permute-start(bf16[128,1024]{1,0:T(8,128)(2,1)} %param.5), channel_id=1, source_target_pairs={{0,2},{1,3},{2,0},{3,1},{4,6},{5,7},{6,4},{7,5},{8,10},{9,11},{10,... | collective-permute-start | bytes 786440 | tf_op jit(solution)/shard_map/ppermute | solution.py:35
  4.7 0.7 %collective-permute-start = (bf16[768,1024]{1,0:T(8,128)(2,1)}, bf16[768,1024]{1,0:T(8,128)(2,1)S(1)}, u32[]{:S(2)}, u32[]{:S(2)}) collective-permute-start(bf16[768,1024]{1,0:T(8,128)(2,1)} %param.4), channel_id=1, source_target_pairs={{0,12},{4,0},{8,4},{12,8},{1,13},{5,1},{9,5},{13,9},{2,14},{6,2},{... | collective-permute-start | bytes 4718600 | tf_op jit(solution)/shard_map/ppermute | solution.py:38
  5.4 0.7 %fusion.53 = s32[768,8]{0,1:T(8,128)S(1)} fusion(s32[768,8]{0,1:T(8,128)} %param.6, s32[768]{0:T(1024)} %param.7), kind=kLoop, calls=%fused_computation.79 | loop fusion | flops 12288 | bytes 52224 | tf_op jit(solution)/shard_map/jit(_where)/select_n | solution.py:25
  6.2 0.0 copy-start
  6.2 2.3 %fusion.48 = bf16[768,128]{0,1:T(8,128)(2,1)S(1)} fusion(bf16[128,1024]{1,0:T(8,128)(2,1)} %param.5, bf16[768,1024]{1,0:T(8,128)(2,1)} %param.4, s32[768]{0:T(1024)S(1)} %get-tuple-element.61, s32[128]{0:T(128)S(1)} %iota_add_fusion.3), kind=kOutput, calls=%fused_computation.62 | convolution fusion | flops 202014720 | bytes 2035200 | tf_op jit(solution)/shard_map/dot_general | solution.py:45
  8.5 0.0 copy-done
  8.5 0.0 copy-start.1
  8.5 0.4 fusion.54
  8.9 1.0 %collective-permute-start.1 = (s32[768,8]{0,1:T(8,128)S(1)}, s32[768,8]{0,1:T(8,128)S(1)}, u32[]{:S(2)}, u32[]{:S(2)}) collective-permute-start(s32[768,8]{0,1:T(8,128)S(1)} %fusion.53), channel_id=1, source_target_pairs={{0,12},{4,0},{8,4},{12,8},{1,13},{5,1},{9,5},{13,9},{2,14},{6,2},{... | collective-permute-start | bytes 73736 | tf_op jit(solution)/shard_map/ppermute | solution.py:38
  9.9 0.0 copy-done.1
  9.9 1.6 %collective-permute-start.5 = (bf16[128,1024]{1,0:T(8,128)(2,1)S(1)}, bf16[128,1024]{1,0:T(8,128)(2,1)S(1)}, u32[]{:S(2)}, u32[]{:S(2)}) collective-permute-start(bf16[128,1024]{1,0:T(8,128)(2,1)S(1)} %copy-done.1), channel_id=1, source_target_pairs={{0,1},{1,0},{2,3},{3,2},{4,5},{5,4},{6,7},{7,6},{8,9},{9,8},{10,11... | collective-permute-start | bytes 786440 | tf_op jit(solution)/shard_map/ppermute | solution.py:35
  11.5 0.3 collective-permute-start.2
  11.8 6.6 %collective-permute-done.3 = bf16[128,1024]{1,0:T(8,128)(2,1)S(1)} collective-permute-done((bf16[128,1024]{1,0:T(8,128)(2,1)}, bf16[128,1024]{1,0:T(8,128)(2,1)S(1)}, u32[]{:S(2)}, u32[]{:S(2)}) %collective-permute-start.3) | collective-permute-done | bytes 262176 | tf_op jit(solution)/shard_map/ppermute | solution.py:35
  18.5 0.1 collective-permute-start.4
  18.5 6.9 %collective-permute-done.5 = bf16[128,1024]{1,0:T(8,128)(2,1)S(1)} collective-permute-done((bf16[128,1024]{1,0:T(8,128)(2,1)S(1)}, bf16[128,1024]{1,0:T(8,128)(2,1)S(1)}, u32[]{:S(2)}, u32[]{:S(2)}) %collective-permute-start.5) | collective-permute-done | bytes 262176 | tf_op jit(solution)/shard_map/ppermute | solution.py:35
  25.4 0.7 %fusion.47 = bf16[768,128]{0,1:T(8,128)(2,1)S(1)} fusion(bf16[128,1024]{1,0:T(8,128)(2,1)S(1)} %collective-permute-done.5, bf16[768,1024]{1,0:T(8,128)(2,1)S(1)} %copy-done, s32[768]{0:T(1024)S(1)} %get-tuple-element.60, s32[128]{0:T(128)S(1)} %iota_add_fusion.2), kind=kOutput, calls=%fused_computation.61 | convolution fusion | flops 202014720 | bytes 2035200 | tf_op jit(solution)/shard_map/dot_general | solution.py:45
  26.2 0.4 fusion.55
  26.5 0.7 %fusion.46 = bf16[768,128]{0,1:T(8,128)(2,1)S(1)} fusion(bf16[128,1024]{1,0:T(8,128)(2,1)S(1)} %collective-permute-done.3, bf16[768,1024]{1,0:T(8,128)(2,1)S(1)} %copy-done, s32[768]{0:T(1024)S(1)} %get-tuple-element.59, s32[128]{0:T(128)S(1)} %iota_add_fusion.1), kind=kOutput, calls=%fused_computation.60 | convolution fusion | flops 202014720 | bytes 2035200 | tf_op jit(solution)/shard_map/dot_general | solution.py:45
  27.3 0.4 fusion.56
  27.7 0.0 collective-permute-done.2
  27.7 0.0 collective-permute-done.4
  27.8 0.7 %fusion.45 = bf16[768,128]{0,1:T(8,128)(2,1)S(1)} fusion(bf16[128,1024]{1,0:T(8,128)(2,1)S(1)} %pad_maximum_fusion.2, bf16[768,1024]{1,0:T(8,128)(2,1)S(1)} %copy-done, s32[768]{0:T(1024)S(1)} %get-tuple-element.58, s32[128]{0:T(128)S(1)} %iota_add_fusion), kind=kOutput, calls=%fused_computation.59 | convolution fusion | flops 202014720 | bytes 2035200 | tf_op jit(solution)/shard_map/dot_general | solution.py:45
  28.5 0.1 pad_maximum_fusion
  28.5 0.4 fusion.57
  28.9 0.0 collective-permute-done.1
  28.9 0.0 collective-permute-done
  29.0 0.7 %fusion.44 = bf16[768,128]{0,1:T(8,128)(2,1)S(1)} fusion(bf16[768,1024]{1,0:T(8,128)(2,1)S(1)} %collective-permute-done, bf16[128,1024]{1,0:T(8,128)(2,1)S(1)} %pad_maximum_fusion.2, s32[768]{0:T(1024)S(1)} %get-tuple-element.57, s32[128]{0:T(128)S(1)} %iota_add_fusion), kind=kOutput, calls=%fused_computation.58 | convolution fusion | flops 202014720 | bytes 2035200 | tf_op jit(solution)/shard_map/dot_general | solution.py:45
  29.7 0.7 %fusion.43 = bf16[768,128]{0,1:T(8,128)(2,1)S(1)} fusion(bf16[768,1024]{1,0:T(8,128)(2,1)S(1)} %collective-permute-done, bf16[128,1024]{1,0:T(8,128)(2,1)S(1)} %collective-permute-done.3, s32[768]{0:T(1024)S(1)} %get-tuple-element.56, s32[128]{0:T(128)S(1)} %iota_add_fusion.1), kind=kOutput, calls=%fused_computation.57 | convolution fusion | flops 202014720 | bytes 2035200 | tf_op jit(solution)/shard_map/dot_general | solution.py:45
  30.4 0.7 %fusion.42 = bf16[768,128]{0,1:T(8,128)(2,1)S(1)} fusion(bf16[768,1024]{1,0:T(8,128)(2,1)S(1)} %collective-permute-done, bf16[128,1024]{1,0:T(8,128)(2,1)S(1)} %collective-permute-done.5, s32[768]{0:T(1024)S(1)} %get-tuple-element.55, s32[128]{0:T(128)S(1)} %iota_add_fusion.2), kind=kOutput, calls=%fused_computation.56 | convolution fusion | flops 202014720 | bytes 2035200 | tf_op jit(solution)/shard_map/dot_general | solution.py:45
  31.2 0.7 %fusion.41 = bf16[768,128]{0,1:T(8,128)(2,1)S(1)} fusion(bf16[768,1024]{1,0:T(8,128)(2,1)S(1)} %collective-permute-done, bf16[128,1024]{1,0:T(8,128)(2,1)S(1)} %copy-done.1, s32[768]{0:T(1024)S(1)} %get-tuple-element.54, s32[128]{0:T(128)S(1)} %iota_add_fusion.3), kind=kOutput, calls=%fused_computation.55 | convolution fusion | flops 202014720 | bytes 2035200 | tf_op jit(solution)/shard_map/dot_general | solution.py:45
  31.9 0.1 pad_maximum_fusion.1
  31.9 1.0 %convolution_convert_fusion = bf16[768,1024]{1,0:T(8,128)(2,1)S(1)} fusion(bf16[768,512]{0,1:T(8,128)(2,1)S(1)} %pad_maximum_fusion.1, bf16[512,1024]{1,0:T(8,128)(2,1)S(1)} %constant_dynamic-update-slice_fusion), kind=kOutput, calls=%fused_computation.1 | convolution fusion | flops 806092800 | bytes 3407872 | tf_op jit(solution)/shard_map/dot_general | solution.py:56
  32.9 0.4 fusion.3
  33.4 0.1 collective-permute-start.6
  33.4 0.1 collective-permute-start.11
  33.5 0.4 fusion.2
  33.9 3.4 %collective-permute-start.8 = (bf16[32,1024]{1,0:T(8,128)(2,1)S(1)}, bf16[32,1024]{1,0:T(8,128)(2,1)S(1)}, u32[]{:S(2)}, u32[]{:S(2)}) collective-permute-start(bf16[32,1024]{1,0:T(8,128)(2,1)S(1)} %slice.58), channel_id=1, source_target_pairs={{0,3},{1,2},{2,1},{3,0},{4,7},{5,6},{6,5},{7,4},{8,11},{9,10},{10,... | collective-permute-start | bytes 196616 | tf_op jit(solution)/shard_map/ppermute | solution.py:35
  37.3 0.4 fusion.4
  37.7 1.1 %collective-permute-start.7 = (bf16[128,1024]{1,0:T(8,128)(2,1)S(1)}, bf16[128,1024]{1,0:T(8,128)(2,1)S(1)}, u32[]{:S(2)}, u32[]{:S(2)}) collective-permute-start(bf16[128,1024]{1,0:T(8,128)(2,1)S(1)} %fusion.4), channel_id=1, source_target_pairs={{0,1},{1,0},{2,3},{3,2},{4,5},{5,4},{6,7},{7,6},{8,9},{9,8},{10,11... | collective-permute-start | bytes 786440 | tf_op jit(solution)/shard_map/ppermute | solution.py:35
  38.8 1.0 %collective-permute-done.6 = bf16[96,1024]{1,0:T(8,128)(2,1)S(1)} collective-permute-done((bf16[96,1024]{1,0:T(8,128)(2,1)S(1)}, bf16[96,1024]{1,0:T(8,128)(2,1)S(1)}, u32[]{:S(2)}, u32[]{:S(2)}) %collective-permute-start.6) | collective-permute-done | bytes 196640 | tf_op jit(solution)/shard_map/ppermute | solution.py:35
  39.9 1.7 %collective-permute-start.10 = (bf16[96,1024]{1,0:T(8,128)(2,1)S(1)}, bf16[96,1024]{1,0:T(8,128)(2,1)S(1)}, u32[]{:S(2)}, u32[]{:S(2)}) collective-permute-start(bf16[96,1024]{1,0:T(8,128)(2,1)S(1)} %fusion.50), channel_id=1, source_target_pairs={{0,2},{1,3},{2,0},{3,1},{4,6},{5,7},{6,4},{7,5},{8,10},{9,11},{10,... | collective-permute-start | bytes 589832 | tf_op jit(solution)/shard_map/ppermute | solution.py:35
  41.6 1.4 %collective-permute-start.9 = (bf16[32,1024]{1,0:T(8,128)(2,1)S(1)}, bf16[32,1024]{1,0:T(8,128)(2,1)S(1)}, u32[]{:S(2)}, u32[]{:S(2)}) collective-permute-start(bf16[32,1024]{1,0:T(8,128)(2,1)S(1)} %slice.57), channel_id=1, source_target_pairs={{0,2},{1,3},{2,0},{3,1},{4,6},{5,7},{6,4},{7,5},{8,10},{9,11},{10,... | collective-permute-start | bytes 196616 | tf_op jit(solution)/shard_map/ppermute | solution.py:35
  42.9 1.0 %fusion.58 = f32[768,1024]{1,0:T(8,128)S(1)} fusion(bf16[768,512]{0,1:T(8,128)(2,1)S(1)} %pad_maximum_fusion, bf16[512,1024]{1,0:T(8,128)(2,1)S(1)} %constant_dynamic-update-slice_fusion), kind=kOutput, calls=%fused_computation.100 | convolution fusion | flops 805306368 | bytes 4980736 | tf_op jit(solution)/shard_map/dot_general | solution.py:56
  43.9 0.4 fusion.1
  44.3 0.0 collective-permute-done.8
  44.3 9.4 %collective-permute-done.9 = bf16[32,1024]{1,0:T(8,128)(2,1)S(1)} collective-permute-done((bf16[32,1024]{1,0:T(8,128)(2,1)S(1)}, bf16[32,1024]{1,0:T(8,128)(2,1)S(1)}, u32[]{:S(2)}, u32[]{:S(2)}) %collective-permute-start.9) | collective-permute-done | bytes 65568 | tf_op jit(solution)/shard_map/ppermute | solution.py:35
  53.7 0.0 collective-permute-done.7
  53.7 0.1 convert_add_fusion
  53.8 0.0 collective-permute-done.10
  53.8 0.1 fusion.49
  53.9 0.7 %pad_maximum_fusion.3 = bf16[128,1024]{1,0:T(8,128)(2,1)} fusion(bf16[96,1024]{1,0:T(8,128)(2,1)S(1)} %fusion.49, bf16[32,1024]{1,0:T(8,128)(2,1)S(1)} %fusion.52), kind=kLoop, calls=%fused_computation.72 | loop fusion | flops 524288 | bytes 524288 | tf_op jit(solution)/shard_map/concatenate | solution.py:133
  54.6 0.0 collective-permute-done.11
  54.6 1.8 %add_convert_fusion = bf16[768,1024]{1,0:T(8,128)(2,1)} fusion(f32[768,1024]{1,0:T(8,128)S(1)} %fusion.58, bf16[768,1024]{1,0:T(8,128)(2,1)S(1)} %collective-permute-done.11), kind=kLoop, calls=%fused_computation | loop fusion | flops 2359296 | bytes 6291456 | tf_op jit(solution)/shard_map/convert_element_type | solution.py:136
  (18 shorter events, 0.3 us)
Async XLA Ops:
  0.6 17.8 %collective-permute-start.3 = (bf16[128,1024]{1,0:T(8,128)(2,1)}, bf16[128,1024]{1,0:T(8,128)(2,1)S(1)}, u32[]{:S(2)}, u32[]{:S(2)}) collective-permute-start(bf16[128,1024]{1,0:T(8,128)(2,1)} %param.5), channel_id=1, source_target_pairs={{0,2},{1,3},{2,0},{3,1},{4,6},{5,7},{6,4},{7,5},{8,10},{9,11},{10,... | collective-permute-start | bytes 786440 | tf_op jit(solution)/shard_map/ppermute | solution.py:35
  4.7 24.2 %collective-permute-start = (bf16[768,1024]{1,0:T(8,128)(2,1)}, bf16[768,1024]{1,0:T(8,128)(2,1)S(1)}, u32[]{:S(2)}, u32[]{:S(2)}) collective-permute-start(bf16[768,1024]{1,0:T(8,128)(2,1)} %param.4), channel_id=1, source_target_pairs={{0,12},{4,0},{8,4},{12,8},{1,13},{5,1},{9,5},{13,9},{2,14},{6,2},{... | collective-permute-start | bytes 4718600 | tf_op jit(solution)/shard_map/ppermute | solution.py:38
  6.2 2.3 %copy-start = (bf16[768,1024]{1,0:T(8,128)(2,1)S(1)}, bf16[768,1024]{1,0:T(8,128)(2,1)}, u32[]{:S(2)}) copy-start(bf16[768,1024]{1,0:T(8,128)(2,1)} %param.4) | copy-start | bytes 4718596
  8.5 1.4 %copy-start.1 = (bf16[128,1024]{1,0:T(8,128)(2,1)S(1)}, bf16[128,1024]{1,0:T(8,128)(2,1)}, u32[]{:S(2)}) copy-start(bf16[128,1024]{1,0:T(8,128)(2,1)} %param.5) | copy-start | bytes 786436
  8.9 20.0 %collective-permute-start.1 = (s32[768,8]{0,1:T(8,128)S(1)}, s32[768,8]{0,1:T(8,128)S(1)}, u32[]{:S(2)}, u32[]{:S(2)}) collective-permute-start(s32[768,8]{0,1:T(8,128)S(1)} %fusion.53), channel_id=1, source_target_pairs={{0,12},{4,0},{8,4},{12,8},{1,13},{5,1},{9,5},{13,9},{2,14},{6,2},{... | collective-permute-start | bytes 73736 | tf_op jit(solution)/shard_map/ppermute | solution.py:38
  9.9 15.5 %collective-permute-start.5 = (bf16[128,1024]{1,0:T(8,128)(2,1)S(1)}, bf16[128,1024]{1,0:T(8,128)(2,1)S(1)}, u32[]{:S(2)}, u32[]{:S(2)}) collective-permute-start(bf16[128,1024]{1,0:T(8,128)(2,1)S(1)} %copy-done.1), channel_id=1, source_target_pairs={{0,1},{1,0},{2,3},{3,2},{4,5},{5,4},{6,7},{7,6},{8,9},{9,8},{10,11... | collective-permute-start | bytes 786440 | tf_op jit(solution)/shard_map/ppermute | solution.py:35
  11.5 16.2 %collective-permute-start.2 = (bf16[64,1024]{1,0:T(8,128)(2,1)S(1)}, bf16[64,1024]{1,0:T(8,128)(2,1)S(1)}, u32[]{:S(2)}, u32[]{:S(2)}) collective-permute-start(bf16[64,1024]{1,0:T(8,128)(2,1)S(1)} %slice.27), channel_id=1, source_target_pairs={{0,3},{1,2},{2,1},{3,0},{4,7},{5,6},{6,5},{7,4},{8,11},{9,10},{10,... | collective-permute-start | bytes 393224 | tf_op jit(solution)/shard_map/ppermute | solution.py:35
  18.5 9.3 %collective-permute-start.4 = (bf16[64,1024]{1,0:T(8,128)(2,1)S(1)}, bf16[64,1024]{1,0:T(8,128)(2,1)S(1)}, u32[]{:S(2)}, u32[]{:S(2)}) collective-permute-start(bf16[64,1024]{1,0:T(8,128)(2,1)S(1)} %slice.35), channel_id=1, source_target_pairs={{0,1},{1,0},{2,3},{3,2},{4,5},{5,4},{6,7},{7,6},{8,9},{9,8},{10,11... | collective-permute-start | bytes 393224 | tf_op jit(solution)/shard_map/ppermute | solution.py:35
  33.4 6.4 %collective-permute-start.6 = (bf16[96,1024]{1,0:T(8,128)(2,1)S(1)}, bf16[96,1024]{1,0:T(8,128)(2,1)S(1)}, u32[]{:S(2)}, u32[]{:S(2)}) collective-permute-start(bf16[96,1024]{1,0:T(8,128)(2,1)S(1)} %slice.56), channel_id=1, source_target_pairs={{0,1},{1,0},{2,3},{3,2},{4,5},{5,4},{6,7},{7,6},{8,9},{9,8},{10,11... | collective-permute-start | bytes 589832 | tf_op jit(solution)/shard_map/ppermute | solution.py:35
  33.4 21.2 %collective-permute-start.11 = (bf16[768,1024]{1,0:T(8,128)(2,1)S(1)}, bf16[768,1024]{1,0:T(8,128)(2,1)S(1)}, u32[]{:S(2)}, u32[]{:S(2)}) collective-permute-start(bf16[768,1024]{1,0:T(8,128)(2,1)S(1)} %convolution_convert_fusion), channel_id=1, source_target_pairs={{0,4},{4,8},{8,12},{12,0},{1,5},{5,9},{9,13},{13,1},{2,6},{6,10},{... | collective-permute-start | bytes 4718600 | tf_op jit(solution)/shard_map/ppermute | solution.py:38
  33.9 10.4 %collective-permute-start.8 = (bf16[32,1024]{1,0:T(8,128)(2,1)S(1)}, bf16[32,1024]{1,0:T(8,128)(2,1)S(1)}, u32[]{:S(2)}, u32[]{:S(2)}) collective-permute-start(bf16[32,1024]{1,0:T(8,128)(2,1)S(1)} %slice.58), channel_id=1, source_target_pairs={{0,3},{1,2},{2,1},{3,0},{4,7},{5,6},{6,5},{7,4},{8,11},{9,10},{10,... | collective-permute-start | bytes 196616 | tf_op jit(solution)/shard_map/ppermute | solution.py:35
  37.7 16.0 %collective-permute-start.7 = (bf16[128,1024]{1,0:T(8,128)(2,1)S(1)}, bf16[128,1024]{1,0:T(8,128)(2,1)S(1)}, u32[]{:S(2)}, u32[]{:S(2)}) collective-permute-start(bf16[128,1024]{1,0:T(8,128)(2,1)S(1)} %fusion.4), channel_id=1, source_target_pairs={{0,1},{1,0},{2,3},{3,2},{4,5},{5,4},{6,7},{7,6},{8,9},{9,8},{10,11... | collective-permute-start | bytes 786440 | tf_op jit(solution)/shard_map/ppermute | solution.py:35
  39.9 13.9 %collective-permute-start.10 = (bf16[96,1024]{1,0:T(8,128)(2,1)S(1)}, bf16[96,1024]{1,0:T(8,128)(2,1)S(1)}, u32[]{:S(2)}, u32[]{:S(2)}) collective-permute-start(bf16[96,1024]{1,0:T(8,128)(2,1)S(1)} %fusion.50), channel_id=1, source_target_pairs={{0,2},{1,3},{2,0},{3,1},{4,6},{5,7},{6,4},{7,5},{8,10},{9,11},{10,... | collective-permute-start | bytes 589832 | tf_op jit(solution)/shard_map/ppermute | solution.py:35
  41.6 12.1 %collective-permute-start.9 = (bf16[32,1024]{1,0:T(8,128)(2,1)S(1)}, bf16[32,1024]{1,0:T(8,128)(2,1)S(1)}, u32[]{:S(2)}, u32[]{:S(2)}) collective-permute-start(bf16[32,1024]{1,0:T(8,128)(2,1)S(1)} %slice.57), channel_id=1, source_target_pairs={{0,2},{1,3},{2,0},{3,1},{4,6},{5,7},{6,4},{7,5},{8,10},{9,11},{10,... | collective-permute-start | bytes 196616 | tf_op jit(solution)/shard_map/ppermute | solution.py:35

commit v12 on v11

--- a/solution.py
+++ b/solution.py
@@ -11,8 +11,10 @@
 
 
 def local(embeds, weights, pos_ids, pos_count):
+    n_groups = lax.axis_size("groups")
     n_label = lax.axis_size("label")
     n_dp = lax.axis_size("dp")
+    me_group = lax.axis_index("groups")
     me_label = lax.axis_index("label")
     me_dp = lax.axis_index("dp")
     rows_dev, width = embeds.shape
@@ -63,6 +65,9 @@
     for k in range(2, n_dp):
         if k & -k == k:
             pieces[k] = to_dp(weights, k)
+    half = ch_dev // 2
+    after_ids, _ = lax.optimization_barrier((weights, ids))
+    near = to_dp(jnp.where(me_group == 0, after_ids[:half], after_ids[half:]), 1)
     next_rows = to_label(embeds, -1)
     d_own, g_own, g_w = {}, {}, {}
 
@@ -79,7 +84,11 @@
     late = n_dp - 1
     own_step(0)
     later = in_turn(weights)
-    pieces[1] = to_dp(later, 1)
+    near = in_turn(near)
+    other = lax.ppermute(near, "groups", [(i, i ^ 1) for i in range(n_groups)])
+    pieces[1] = jnp.where(
+        me_group == 0, jnp.concatenate([near, other], axis=0), jnp.concatenate([other, near], axis=0)
+    )
     for k in range(2, n_dp):
         step = k & -k
         if step < k:

time: 56.5 us -> 58 us (1.027)
  starting transfers between devices: 15.4 us -> 16.8 us
  other arithmetic: 3.54 us -> 4.57 us
  waiting for transfers between devices: 23.9 us -> 23 us
    ppermute x0 -> x1, starting transfers between devices: none -> 1.52 us  [local(): other = lax.ppermute(near, 'groups', [(i, i ^ 1) for i in range(n_groups)])]
    ppermute x9, starting transfers between devices: 13.7 us -> 12.5 us  [to_dp(): return lax.ppermute(x, 'dp', [(i, i ^ k) for i in range(n_dp)])]
    ppermute x3, starting transfers between devices: 1.71 us -> 2.78 us  [to_label(): lax.ppermute(x, 'label', [(i, (i + by) % n_label) for i in range(n_label)])]
    ppermute x9, waiting for transfers between devices: 23.9 us -> 22.8 us  [to_dp(): return lax.ppermute(x, 'dp', [(i, i ^ k) for i in range(n_dp)])]
    select_n x0 -> x2, other arithmetic: none -> 1.03 us  [the longest x1 0.98 us: local(): jnp.where(me_group == 0, after_ids[:half], after_ids[half:])]
  transfers between devices with their start and end apart: 12 -> 13, of which waited for: 4 -> 6; matrix products, arithmetic and copies ran while one was open for 18% -> 19% of each run, Pallas kernels for 0% -> 0%
where the time goes in v12:
time: 58 us; the launch traced here: 57.8 us
  waiting for transfers between devices  23 us (40%)
  starting transfers between devices  16.8 us (29%)
  matrix products  12.3 us (21%)
  other arithmetic  4.57 us (8%)
  between operations  0.92 us (2%)
    ppermute x9, waiting for transfers between devices, to_dp(): return lax.ppermute(x, 'dp', [(i, i ^ k) for i in range(n_dp)])  22.8 us
    ppermute x9, starting transfers between devices, to_dp(): return lax.ppermute(x, 'dp', [(i, i ^ k) for i in range(n_dp)])  12.5 us
    dot_general x8, matrix products, delta_of(): lax.dot_general(rows, piece, (((1,), (1,)), ((), ())), preferred_element_...  7.26 us
    dot_general x8, matrix products, grad_w_of(): lax.dot_general(delta, rows, (((0,), (0,)), ((), ())), preferred_element_...  3.05 us
    ppermute x3, starting transfers between devices, to_label(): lax.ppermute(x, 'label', [(i, (i + by) % n_label) for i in range(n_label)])  2.78 us
    dot_general x2, matrix products, grad_x_of(): jnp.dot(in_turn(jnp.concatenate([deltas[k] for k in range(n_dp)], axis=1)...  2.02 us
    convert_element_type x1, other arithmetic, local(): grad_x = (grad_x + in_turn(back).astype(jnp.float32)).astype(jnp.bfloat16)  1.75 us
    ppermute x1, starting transfers between devices, local(): other = lax.ppermute(near, 'groups', [(i, i ^ 1) for i in range(n_groups)])  1.52 us
  transfers between devices with their start and end apart: 13, of which 6 were waited for; matrix products, arithmetic and copies ran while one was open for 19% of the time, Pallas kernels for 0%

profile of v12, /device:TPU:0, one launch (start us, length us, event | category | flops | bytes accessed | tf_op | source)
XLA Modules:
  0.0 57.8 jit_solution(13522207405148608135)
XLA Ops:
  0.6 4.1 %collective-permute-start.3 = (bf16[128,1024]{1,0:T(8,128)(2,1)}, bf16[128,1024]{1,0:T(8,128)(2,1)S(1)}, u32[]{:S(2)}, u32[]{:S(2)}) collective-permute-start(bf16[128,1024]{1,0:T(8,128)(2,1)} %param.5), channel_id=1, source_target_pairs={{0,2},{1,3},{2,0},{3,1},{4,6},{5,7},{6,4},{7,5},{8,10},{9,11},{10,... | collective-permute-start | bytes 786440 | tf_op jit(solution)/shard_map/ppermute | solution.py:37
  4.7 0.7 %fusion.53 = s32[768,8]{0,1:T(8,128)S(1)} fusion(s32[768,8]{0,1:T(8,128)} %param.6, s32[768]{0:T(1024)} %param.7), kind=kLoop, calls=%fused_computation.81 | loop fusion | flops 12288 | bytes 52224 | tf_op jit(solution)/shard_map/jit(_where)/select_n | solution.py:27
  5.5 1.0 %slice_select_fusion = bf16[64,1024]{1,0:T(8,128)(2,1)S(1)} fusion(bf16[128,1024]{1,0:T(8,128)(2,1)} %param.5, pred[]{:T(512)S(6)} %eq.120), kind=kLoop, calls=%fused_computation.79 | loop fusion | flops 65536 | bytes 393217 | tf_op jit(solution)/shard_map/jit(_where)/select_n | solution.py:70
  6.5 1.6 %collective-permute-start.5 = (bf16[64,1024]{1,0:T(8,128)(2,1)S(1)}, bf16[64,1024]{1,0:T(8,128)(2,1)S(1)}, u32[]{:S(2)}, u32[]{:S(2)}) collective-permute-start(bf16[64,1024]{1,0:T(8,128)(2,1)S(1)} %slice_select_fusion), channel_id=1, source_target_pairs={{0,1},{1,0},{2,3},{3,2},{4,5},{5,4},{6,7},{7,6},{8,9},{9,8},{10,11... | collective-permute-start | bytes 393224 | tf_op jit(solution)/shard_map/ppermute | solution.py:37
  8.1 0.4 collective-permute-start
  8.5 0.0 copy-start
  8.5 2.3 %fusion.48 = bf16[768,128]{0,1:T(8,128)(2,1)S(1)} fusion(bf16[128,1024]{1,0:T(8,128)(2,1)} %param.5, bf16[768,1024]{1,0:T(8,128)(2,1)} %param.4, s32[768]{0:T(1024)S(1)} %get-tuple-element.65, s32[128]{0:T(128)S(1)} %iota_add_fusion.3), kind=kOutput, calls=%fused_computation.62 | convolution fusion | flops 202014720 | bytes 2035200 | tf_op jit(solution)/shard_map/dot_general | solution.py:47
  10.8 0.0 copy-done
  10.9 0.0 copy-start.1
  10.9 0.4 fusion.54
  11.2 1.3 %collective-permute-start.1 = (s32[768,8]{0,1:T(8,128)S(1)}, s32[768,8]{0,1:T(8,128)S(1)}, u32[]{:S(2)}, u32[]{:S(2)}) collective-permute-start(s32[768,8]{0,1:T(8,128)S(1)} %fusion.53), channel_id=1, source_target_pairs={{0,12},{4,0},{8,4},{12,8},{1,13},{5,1},{9,5},{13,9},{2,14},{6,2},{... | collective-permute-start | bytes 73736 | tf_op jit(solution)/shard_map/ppermute | solution.py:40
  12.5 0.0 copy-done.1
  12.6 0.3 collective-permute-start.2
  12.8 1.4 %collective-permute-done.5 = bf16[64,1024]{1,0:T(8,128)(2,1)S(1)} collective-permute-done((bf16[64,1024]{1,0:T(8,128)(2,1)S(1)}, bf16[64,1024]{1,0:T(8,128)(2,1)S(1)}, u32[]{:S(2)}, u32[]{:S(2)}) %collective-permute-start.5) | collective-permute-done | bytes 131104 | tf_op jit(solution)/shard_map/ppermute | solution.py:37
  14.2 1.5 %collective-permute-start.6 = (bf16[64,1024]{1,0:T(8,128)(2,1)S(1)}, bf16[64,1024]{1,0:T(8,128)(2,1)S(1)}, u32[]{:S(2)}, u32[]{:S(2)}) collective-permute-start(bf16[64,1024]{1,0:T(8,128)(2,1)S(1)} %collective-permute-done.5), channel_id=1, source_target_pairs={{0,16},{16,0},{1,17},{17,1},{2,18},{18,2},{3,19},{19,3},{4,20},{20... | collective-permute-start | bytes 393224 | tf_op jit(solution)/shard_map/ppermute | solution.py:88
  15.8 4.7 %collective-permute-done.3 = bf16[128,1024]{1,0:T(8,128)(2,1)S(1)} collective-permute-done((bf16[128,1024]{1,0:T(8,128)(2,1)}, bf16[128,1024]{1,0:T(8,128)(2,1)S(1)}, u32[]{:S(2)}, u32[]{:S(2)}) %collective-permute-start.3) | collective-permute-done | bytes 262176 | tf_op jit(solution)/shard_map/ppermute | solution.py:37
  20.5 0.2 collective-permute-start.4
  20.7 0.0 collective-permute-done.6
  20.7 0.1 maximum_select_fusion
  20.7 0.7 %fusion.47 = bf16[768,128]{0,1:T(8,128)(2,1)S(1)} fusion(bf16[128,1024]{1,0:T(8,128)(2,1)S(1)} %maximum_select_fusion, bf16[768,1024]{1,0:T(8,128)(2,1)S(1)} %copy-done, s32[768]{0:T(1024)S(1)} %get-tuple-element.64, s32[128]{0:T(128)S(1)} %iota_add_fusion.2), kind=kOutput, calls=%fused_computation.61 | convolution fusion | flops 202014720 | bytes 2035200 | tf_op jit(solution)/shard_map/dot_general | solution.py:47
  21.4 0.4 fusion.55
  21.8 0.7 %fusion.46 = bf16[768,128]{0,1:T(8,128)(2,1)S(1)} fusion(bf16[128,1024]{1,0:T(8,128)(2,1)S(1)} %collective-permute-done.3, bf16[768,1024]{1,0:T(8,128)(2,1)S(1)} %copy-done, s32[768]{0:T(1024)S(1)} %get-tuple-element.63, s32[128]{0:T(128)S(1)} %iota_add_fusion.1), kind=kOutput, calls=%fused_computation.60 | convolution fusion | flops 202014720 | bytes 2035200 | tf_op jit(solution)/shard_map/dot_general | solution.py:47
  22.6 0.4 fusion.56
  23.0 0.0 collective-permute-done.2
  23.0 2.6 %collective-permute-done.4 = bf16[64,1024]{1,0:T(8,128)(2,1)S(1)} collective-permute-done((bf16[64,1024]{1,0:T(8,128)(2,1)S(1)}, bf16[64,1024]{1,0:T(8,128)(2,1)S(1)}, u32[]{:S(2)}, u32[]{:S(2)}) %collective-permute-start.4) | collective-permute-done | bytes 131104 | tf_op jit(solution)/shard_map/ppermute | solution.py:37
  25.6 0.7 %fusion.45 = bf16[768,128]{0,1:T(8,128)(2,1)S(1)} fusion(bf16[128,1024]{1,0:T(8,128)(2,1)S(1)} %pad_maximum_fusion.2, bf16[768,1024]{1,0:T(8,128)(2,1)S(1)} %copy-done, s32[768]{0:T(1024)S(1)} %get-tuple-element.62, s32[128]{0:T(128)S(1)} %iota_add_fusion), kind=kOutput, calls=%fused_computation.59 | convolution fusion | flops 202014720 | bytes 2035200 | tf_op jit(solution)/shard_map/dot_general | solution.py:47
  26.3 0.1 pad_maximum_fusion
  26.4 0.4 fusion.57
  26.8 0.1 collective-permute-done.1
  26.9 0.0 collective-permute-done
  26.9 0.7 %fusion.44 = bf16[768,128]{0,1:T(8,128)(2,1)S(1)} fusion(bf16[768,1024]{1,0:T(8,128)(2,1)S(1)} %collective-permute-done, bf16[128,1024]{1,0:T(8,128)(2,1)S(1)} %pad_maximum_fusion.2, s32[768]{0:T(1024)S(1)} %get-tuple-element.61, s32[128]{0:T(128)S(1)} %iota_add_fusion), kind=kOutput, calls=%fused_computation.58 | convolution fusion | flops 202014720 | bytes 2035200 | tf_op jit(solution)/shard_map/dot_general | solution.py:47
  27.7 0.7 %fusion.43 = bf16[768,128]{0,1:T(8,128)(2,1)S(1)} fusion(bf16[768,1024]{1,0:T(8,128)(2,1)S(1)} %collective-permute-done, bf16[128,1024]{1,0:T(8,128)(2,1)S(1)} %collective-permute-done.3, s32[768]{0:T(1024)S(1)} %get-tuple-element.60, s32[128]{0:T(128)S(1)} %iota_add_fusion.1), kind=kOutput, calls=%fused_computation.57 | convolution fusion | flops 202014720 | bytes 2035200 | tf_op jit(solution)/shard_map/dot_general | solution.py:47
  28.4 0.7 %fusion.42 = bf16[768,128]{0,1:T(8,128)(2,1)S(1)} fusion(bf16[768,1024]{1,0:T(8,128)(2,1)S(1)} %collective-permute-done, bf16[128,1024]{1,0:T(8,128)(2,1)S(1)} %maximum_select_fusion, s32[768]{0:T(1024)S(1)} %get-tuple-element.59, s32[128]{0:T(128)S(1)} %iota_add_fusion.2), kind=kOutput, calls=%fused_computation.56 | convolution fusion | flops 202014720 | bytes 2035200 | tf_op jit(solution)/shard_map/dot_general | solution.py:47
  29.1 0.7 %fusion.41 = bf16[768,128]{0,1:T(8,128)(2,1)S(1)} fusion(bf16[768,1024]{1,0:T(8,128)(2,1)S(1)} %collective-permute-done, bf16[128,1024]{1,0:T(8,128)(2,1)S(1)} %copy-done.1, s32[768]{0:T(1024)S(1)} %get-tuple-element.58, s32[128]{0:T(128)S(1)} %iota_add_fusion.3), kind=kOutput, calls=%fused_computation.55 | convolution fusion | flops 202014720 | bytes 2035200 | tf_op jit(solution)/shard_map/dot_general | solution.py:47
  29.8 0.1 pad_maximum_fusion.1
  29.9 1.0 %convolution_convert_fusion = bf16[768,1024]{1,0:T(8,128)(2,1)S(1)} fusion(bf16[768,512]{0,1:T(8,128)(2,1)S(1)} %pad_maximum_fusion.1, bf16[512,1024]{1,0:T(8,128)(2,1)S(1)} %constant_dynamic-update-slice_fusion), kind=kOutput, calls=%fused_computation.1 | convolution fusion | flops 806092800 | bytes 3407872 | tf_op jit(solution)/shard_map/dot_general | solution.py:58
  30.9 0.4 fusion.3
  31.3 0.5 collective-permute-start.7
  31.8 1.1 %collective-permute-start.12 = (bf16[768,1024]{1,0:T(8,128)(2,1)S(1)}, bf16[768,1024]{1,0:T(8,128)(2,1)S(1)}, u32[]{:S(2)}, u32[]{:S(2)}) collective-permute-start(bf16[768,1024]{1,0:T(8,128)(2,1)S(1)} %convolution_convert_fusion), channel_id=1, source_target_pairs={{0,4},{4,8},{8,12},{12,0},{1,5},{5,9},{9,13},{13,1},{2,6},{6,10},{... | collective-permute-start | bytes 4718600 | tf_op jit(solution)/shard_map/ppermute | solution.py:40
  32.9 0.4 fusion.2
  33.3 1.9 %collective-permute-start.9 = (bf16[32,1024]{1,0:T(8,128)(2,1)S(1)}, bf16[32,1024]{1,0:T(8,128)(2,1)S(1)}, u32[]{:S(2)}, u32[]{:S(2)}) collective-permute-start(bf16[32,1024]{1,0:T(8,128)(2,1)S(1)} %slice.68), channel_id=1, source_target_pairs={{0,3},{1,2},{2,1},{3,0},{4,7},{5,6},{6,5},{7,4},{8,11},{9,10},{10,... | collective-permute-start | bytes 196616 | tf_op jit(solution)/shard_map/ppermute | solution.py:37
  35.2 0.4 fusion.4
  35.6 0.9 %collective-permute-start.8 = (bf16[128,1024]{1,0:T(8,128)(2,1)S(1)}, bf16[128,1024]{1,0:T(8,128)(2,1)S(1)}, u32[]{:S(2)}, u32[]{:S(2)}) collective-permute-start(bf16[128,1024]{1,0:T(8,128)(2,1)S(1)} %fusion.4), channel_id=1, source_target_pairs={{0,1},{1,0},{2,3},{3,2},{4,5},{5,4},{6,7},{7,6},{8,9},{9,8},{10,11... | collective-permute-start | bytes 786440 | tf_op jit(solution)/shard_map/ppermute | solution.py:37
  36.5 2.9 %collective-permute-done.7 = bf16[96,1024]{1,0:T(8,128)(2,1)S(1)} collective-permute-done((bf16[96,1024]{1,0:T(8,128)(2,1)S(1)}, bf16[96,1024]{1,0:T(8,128)(2,1)S(1)}, u32[]{:S(2)}, u32[]{:S(2)}) %collective-permute-start.7) | collective-permute-done | bytes 196640 | tf_op jit(solution)/shard_map/ppermute | solution.py:37
  39.4 1.7 %collective-permute-start.11 = (bf16[96,1024]{1,0:T(8,128)(2,1)S(1)}, bf16[96,1024]{1,0:T(8,128)(2,1)S(1)}, u32[]{:S(2)}, u32[]{:S(2)}) collective-permute-start(bf16[96,1024]{1,0:T(8,128)(2,1)S(1)} %fusion.50), channel_id=1, source_target_pairs={{0,2},{1,3},{2,0},{3,1},{4,6},{5,7},{6,4},{7,5},{8,10},{9,11},{10,... | collective-permute-start | bytes 589832 | tf_op jit(solution)/shard_map/ppermute | solution.py:37
  41.1 1.3 %collective-permute-start.10 = (bf16[32,1024]{1,0:T(8,128)(2,1)S(1)}, bf16[32,1024]{1,0:T(8,128)(2,1)S(1)}, u32[]{:S(2)}, u32[]{:S(2)}) collective-permute-start(bf16[32,1024]{1,0:T(8,128)(2,1)S(1)} %slice.67), channel_id=1, source_target_pairs={{0,2},{1,3},{2,0},{3,1},{4,6},{5,7},{6,4},{7,5},{8,10},{9,11},{10,... | collective-permute-start | bytes 196616 | tf_op jit(solution)/shard_map/ppermute | solution.py:37
  42.5 1.0 %fusion.58 = f32[768,1024]{1,0:T(8,128)S(1)} fusion(bf16[768,512]{0,1:T(8,128)(2,1)S(1)} %pad_maximum_fusion, bf16[512,1024]{1,0:T(8,128)(2,1)S(1)} %constant_dynamic-update-slice_fusion), kind=kOutput, calls=%fused_computation.102 | convolution fusion | flops 805306368 | bytes 4980736 | tf_op jit(solution)/shard_map/dot_general | solution.py:58
  43.5 0.4 fusion.1
  43.9 0.0 collective-permute-done.9
  43.9 11.3 %collective-permute-done.10 = bf16[32,1024]{1,0:T(8,128)(2,1)S(1)} collective-permute-done((bf16[32,1024]{1,0:T(8,128)(2,1)S(1)}, bf16[32,1024]{1,0:T(8,128)(2,1)S(1)}, u32[]{:S(2)}, u32[]{:S(2)}) %collective-permute-start.10) | collective-permute-done | bytes 65568 | tf_op jit(solution)/shard_map/ppermute | solution.py:37
  55.2 0.0 collective-permute-done.8
  55.2 0.1 convert_add_fusion
  55.3 0.0 collective-permute-done.11
  55.3 0.1 fusion.49
  55.3 0.7 %pad_maximum_fusion.3 = bf16[128,1024]{1,0:T(8,128)(2,1)} fusion(bf16[96,1024]{1,0:T(8,128)(2,1)S(1)} %fusion.49, bf16[32,1024]{1,0:T(8,128)(2,1)S(1)} %fusion.52), kind=kLoop, calls=%fused_computation.73 | loop fusion | flops 524288 | bytes 524288 | tf_op jit(solution)/shard_map/concatenate | solution.py:142
  56.1 0.0 collective-permute-done.12
  56.1 1.8 %add_convert_fusion = bf16[768,1024]{1,0:T(8,128)(2,1)} fusion(f32[768,1024]{1,0:T(8,128)S(1)} %fusion.58, bf16[768,1024]{1,0:T(8,128)(2,1)S(1)} %collective-permute-done.12), kind=kLoop, calls=%fused_computation | loop fusion | flops 2359296 | bytes 6291456 | tf_op jit(solution)/shard_map/convert_element_type | solution.py:145
  (18 shorter events, 0.3 us)
Async XLA Ops:
  0.6 19.9 %collective-permute-start.3 = (bf16[128,1024]{1,0:T(8,128)(2,1)}, bf16[128,1024]{1,0:T(8,128)(2,1)S(1)}, u32[]{:S(2)}, u32[]{:S(2)}) collective-permute-start(bf16[128,1024]{1,0:T(8,128)(2,1)} %param.5), channel_id=1, source_target_pairs={{0,2},{1,3},{2,0},{3,1},{4,6},{5,7},{6,4},{7,5},{8,10},{9,11},{10,... | collective-permute-start | bytes 786440 | tf_op jit(solution)/shard_map/ppermute | solution.py:37
  6.5 7.8 %collective-permute-start.5 = (bf16[64,1024]{1,0:T(8,128)(2,1)S(1)}, bf16[64,1024]{1,0:T(8,128)(2,1)S(1)}, u32[]{:S(2)}, u32[]{:S(2)}) collective-permute-start(bf16[64,1024]{1,0:T(8,128)(2,1)S(1)} %slice_select_fusion), channel_id=1, source_target_pairs={{0,1},{1,0},{2,3},{3,2},{4,5},{5,4},{6,7},{7,6},{8,9},{9,8},{10,11... | collective-permute-start | bytes 393224 | tf_op jit(solution)/shard_map/ppermute | solution.py:37
  8.1 18.8 %collective-permute-start = (bf16[768,1024]{1,0:T(8,128)(2,1)}, bf16[768,1024]{1,0:T(8,128)(2,1)S(1)}, u32[]{:S(2)}, u32[]{:S(2)}) collective-permute-start(bf16[768,1024]{1,0:T(8,128)(2,1)} %param.4), channel_id=1, source_target_pairs={{0,12},{4,0},{8,4},{12,8},{1,13},{5,1},{9,5},{13,9},{2,14},{6,2},{... | collective-permute-start | bytes 4718600 | tf_op jit(solution)/shard_map/ppermute | solution.py:40
  8.5 2.3 %copy-start = (bf16[768,1024]{1,0:T(8,128)(2,1)S(1)}, bf16[768,1024]{1,0:T(8,128)(2,1)}, u32[]{:S(2)}) copy-start(bf16[768,1024]{1,0:T(8,128)(2,1)} %param.4) | copy-start | bytes 4718596
  10.9 1.7 %copy-start.1 = (bf16[128,1024]{1,0:T(8,128)(2,1)S(1)}, bf16[128,1024]{1,0:T(8,128)(2,1)}, u32[]{:S(2)}) copy-start(bf16[128,1024]{1,0:T(8,128)(2,1)} %param.5) | copy-start | bytes 786436
  11.2 15.6 %collective-permute-start.1 = (s32[768,8]{0,1:T(8,128)S(1)}, s32[768,8]{0,1:T(8,128)S(1)}, u32[]{:S(2)}, u32[]{:S(2)}) collective-permute-start(s32[768,8]{0,1:T(8,128)S(1)} %fusion.53), channel_id=1, source_target_pairs={{0,12},{4,0},{8,4},{12,8},{1,13},{5,1},{9,5},{13,9},{2,14},{6,2},{... | collective-permute-start | bytes 73736 | tf_op jit(solution)/shard_map/ppermute | solution.py:40
  12.6 10.4 %collective-permute-start.2 = (bf16[64,1024]{1,0:T(8,128)(2,1)S(1)}, bf16[64,1024]{1,0:T(8,128)(2,1)S(1)}, u32[]{:S(2)}, u32[]{:S(2)}) collective-permute-start(bf16[64,1024]{1,0:T(8,128)(2,1)S(1)} %slice.33), channel_id=1, source_target_pairs={{0,3},{1,2},{2,1},{3,0},{4,7},{5,6},{6,5},{7,4},{8,11},{9,10},{10,... | collective-permute-start | bytes 393224 | tf_op jit(solution)/shard_map/ppermute | solution.py:37
  14.2 6.5 %collective-permute-start.6 = (bf16[64,1024]{1,0:T(8,128)(2,1)S(1)}, bf16[64,1024]{1,0:T(8,128)(2,1)S(1)}, u32[]{:S(2)}, u32[]{:S(2)}) collective-permute-start(bf16[64,1024]{1,0:T(8,128)(2,1)S(1)} %collective-permute-done.5), channel_id=1, source_target_pairs={{0,16},{16,0},{1,17},{17,1},{2,18},{18,2},{3,19},{19,3},{4,20},{20... | collective-permute-start | bytes 393224 | tf_op jit(solution)/shard_map/ppermute | solution.py:88
  20.5 5.0 %collective-permute-start.4 = (bf16[64,1024]{1,0:T(8,128)(2,1)S(1)}, bf16[64,1024]{1,0:T(8,128)(2,1)S(1)}, u32[]{:S(2)}, u32[]{:S(2)}) collective-permute-start(bf16[64,1024]{1,0:T(8,128)(2,1)S(1)} %slice.43), channel_id=1, source_target_pairs={{0,1},{1,0},{2,3},{3,2},{4,5},{5,4},{6,7},{7,6},{8,9},{9,8},{10,11... | collective-permute-start | bytes 393224 | tf_op jit(solution)/shard_map/ppermute | solution.py:37
  31.3 8.1 %collective-permute-start.7 = (bf16[96,1024]{1,0:T(8,128)(2,1)S(1)}, bf16[96,1024]{1,0:T(8,128)(2,1)S(1)}, u32[]{:S(2)}, u32[]{:S(2)}) collective-permute-start(bf16[96,1024]{1,0:T(8,128)(2,1)S(1)} %slice.66), channel_id=1, source_target_pairs={{0,1},{1,0},{2,3},{3,2},{4,5},{5,4},{6,7},{7,6},{8,9},{9,8},{10,11... | collective-permute-start | bytes 589832 | tf_op jit(solution)/shard_map/ppermute | solution.py:37
  31.8 24.3 %collective-permute-start.12 = (bf16[768,1024]{1,0:T(8,128)(2,1)S(1)}, bf16[768,1024]{1,0:T(8,128)(2,1)S(1)}, u32[]{:S(2)}, u32[]{:S(2)}) collective-permute-start(bf16[768,1024]{1,0:T(8,128)(2,1)S(1)} %convolution_convert_fusion), channel_id=1, source_target_pairs={{0,4},{4,8},{8,12},{12,0},{1,5},{5,9},{9,13},{13,1},{2,6},{6,10},{... | collective-permute-start | bytes 4718600 | tf_op jit(solution)/shard_map/ppermute | solution.py:40
  33.3 10.6 %collective-permute-start.9 = (bf16[32,1024]{1,0:T(8,128)(2,1)S(1)}, bf16[32,1024]{1,0:T(8,128)(2,1)S(1)}, u32[]{:S(2)}, u32[]{:S(2)}) collective-permute-start(bf16[32,1024]{1,0:T(8,128)(2,1)S(1)} %slice.68), channel_id=1, source_target_pairs={{0,3},{1,2},{2,1},{3,0},{4,7},{5,6},{6,5},{7,4},{8,11},{9,10},{10,... | collective-permute-start | bytes 196616 | tf_op jit(solution)/shard_map/ppermute | solution.py:37
  35.6 19.6 %collective-permute-start.8 = (bf16[128,1024]{1,0:T(8,128)(2,1)S(1)}, bf16[128,1024]{1,0:T(8,128)(2,1)S(1)}, u32[]{:S(2)}, u32[]{:S(2)}) collective-permute-start(bf16[128,1024]{1,0:T(8,128)(2,1)S(1)} %fusion.4), channel_id=1, source_target_pairs={{0,1},{1,0},{2,3},{3,2},{4,5},{5,4},{6,7},{7,6},{8,9},{9,8},{10,11... | collective-permute-start | bytes 786440 | tf_op jit(solution)/shard_map/ppermute | solution.py:37
  39.4 15.9 %collective-permute-start.11 = (bf16[96,1024]{1,0:T(8,128)(2,1)S(1)}, bf16[96,1024]{1,0:T(8,128)(2,1)S(1)}, u32[]{:S(2)}, u32[]{:S(2)}) collective-permute-start(bf16[96,1024]{1,0:T(8,128)(2,1)S(1)} %fusion.50), channel_id=1, source_target_pairs={{0,2},{1,3},{2,0},{3,1},{4,6},{5,7},{6,4},{7,5},{8,10},{9,11},{10,... | collective-permute-start | bytes 589832 | tf_op jit(solution)/shard_map/ppermute | solution.py:37
  41.1 14.0 %collective-permute-start.10 = (bf16[32,1024]{1,0:T(8,128)(2,1)S(1)}, bf16[32,1024]{1,0:T(8,128)(2,1)S(1)}, u32[]{:S(2)}, u32[]{:S(2)}) collective-permute-start(bf16[32,1024]{1,0:T(8,128)(2,1)S(1)} %slice.67), channel_id=1, source_target_pairs={{0,2},{1,3},{2,0},{3,1},{4,6},{5,7},{6,4},{7,5},{8,10},{9,11},{10,... | collective-permute-start | bytes 196616 | tf_op jit(solution)/shard_map/ppermute | solution.py:37

commit v13 on v9

--- a/solution.py
+++ b/solution.py
@@ -4,6 +4,9 @@
 import jax.numpy as jnp
 from jax import lax
 from jax.sharding import PartitionSpec as P
+
+
+SCATTER_DIRECT_EIGHTHS = 2
 
 
 def local(embeds, weights, pos_ids, pos_count):
@@ -19,6 +22,7 @@
     scale = 1.0 / math.sqrt(rows_dev * n_dp)
     valid = jnp.arange(slots, dtype=jnp.int32)[None, :] < pos_count[:, None]
     ids = jnp.where(valid, pos_ids, -1)
+    direct = ch_dev * SCATTER_DIRECT_EIGHTHS // 8
     last = [embeds]
 
     def in_turn(x):
@@ -53,61 +57,81 @@
             preferred_element_type=jnp.float32,
         )
 
+    late = n_dp - 1
     pieces = {0: weights}
-    for k in range(1, n_dp):
+    for k in range(2, n_dp):
         step = k & -k
         pieces[k] = to_dp(pieces[k ^ step], step)
     next_rows = to_label(embeds, -1)
-    d_own, d_next, g_w = {}, {}, {}
+    d_own, g_own, g_w = {}, {}, {}
 
     def own_step(k):
         pieces[k] = in_turn(pieces[k])
         d_own[k] = delta_of(embeds, ids, pieces[k], k)
-        g_w[k] = grad_w_of(d_own[k], embeds)
+        last[0] = d_own[k]
+        if k == 0:
+            pieces[1] = to_dp(in_turn(weights), 1)
+        g_own[k] = grad_w_of(d_own[k], embeds)
+        last[0] = g_own[k]
+
+    def add_next(k):
+        g_w[k] = (g_own[k] + grad_w_of(in_turn(d_next[k]), next_rows)) * scale
         last[0] = g_w[k]
 
-    def next_step(k):
+    late = n_dp - 1
+    def next_delta(k):
         d_next[k] = delta_of(next_rows, next_ids, in_turn(pieces[k]), k)
         last[0] = d_next[k]
-        if k > 1:
-            add_next(k)
 
-    def add_next(k):
-        g_w[k] = (g_w[k] + grad_w_of(in_turn(d_next[k]), next_rows)) * scale
-        last[0] = g_w[k]
-
+    d_next = {}
+    own_step(0)
+    next_ids = to_label(in_turn(ids), -1)
     own_step(1)
-    next_ids = to_label(in_turn(ids), -1)
-    for k in range(2, n_dp):
+    next_rows, next_ids, _ = lax.optimization_barrier((next_rows, next_ids, last[0]))
+    for k in range(late):
+        next_delta(k)
+    for k in range(2, late):
         own_step(k)
-    next_ids = in_turn(next_ids)
-    for k in range(n_dp - 1, -1, -1):
-        next_step(k)
+    next_delta(late)
+    own_step(late)
+    add_next(late)
     theirs = grad_x_of(d_next).astype(jnp.bfloat16)
     last[0] = theirs
     back = to_label(theirs, 1)
 
-    add_next(1)
-    relayed, moved = {}, []
-    for k in range(n_dp - 1, 0, -1):
+    relayed, moved, low, high = {}, [], [], []
+    for k in range(late - 1, 1, -1):
+        add_next(k)
+    for k in range(late, 1, -1):
+        low.append(to_dp(in_turn(g_w[k])[:direct].astype(jnp.bfloat16), k))
+    for k in range(late, 0, -1):
         step = k & -k
+        if k == 1:
+            add_next(k)
+            moved.append(to_dp(g_w[k].astype(jnp.bfloat16), k))
+            continue
+        part = g_w[k][direct:]
         for term in relayed.get(k, ()):
-            g_w[k] = g_w[k] + term.astype(jnp.float32)
-        part = g_w[k].astype(jnp.bfloat16)
+            part = part + term.astype(jnp.float32)
+        part = part.astype(jnp.bfloat16)
         if k in relayed:
             last[0] = part
         if step == k:
-            moved.append(to_dp(part, k))
+            high.append(to_dp(part, k))
         else:
             relayed.setdefault(k ^ step, []).append(in_turn(to_dp(part, step)))
-    own_step(0)
     grad_x = grad_x_of(d_own)
     last[0] = grad_x
     add_next(0)
     grad_w = g_w[0]
-    for term in reversed(moved):
+    for term in moved:
         grad_w = grad_w + in_turn(term).astype(jnp.float32)
-    grad_w = grad_w.astype(jnp.bfloat16)
+    rest, grad_w = grad_w[:direct], grad_w[direct:]
+    for term in low:
+        rest = rest + in_turn(term).astype(jnp.float32)
+    for term in high:
+        grad_w = grad_w + in_turn(term).astype(jnp.float32)
+    grad_w = jnp.concatenate([rest, grad_w], axis=0).astype(jnp.bfloat16)
     last[0] = grad_w
     grad_x = (grad_x + in_turn(back).astype(jnp.float32)).astype(jnp.bfloat16)
     return (grad_w, grad_x)

time: 55.5 us -> 56.1 us (1.011)
  starting transfers between devices: 10.5 us -> 14.5 us
  waiting for transfers between devices: 27.7 us -> 24.5 us
    ppermute x6 -> x8, waiting for transfers between devices: 27.3 us -> 23 us  [to_dp(): return lax.ppermute(x, 'dp', [(i, i ^ k) for i in range(n_dp)])]
    ppermute x6 -> x8, starting transfers between devices: 9.83 us -> 13 us  [to_dp(): return lax.ppermute(x, 'dp', [(i, i ^ k) for i in range(n_dp)])]
    ppermute x3, waiting for transfers between devices: 0.45 us -> 1.46 us  [to_label(): lax.ppermute(x, 'label', [(i, (i + by) % n_label) for i in range(n_label)])]
    convert_element_type x2 -> x1, other arithmetic: 0.86 us -> 0.04 us  [local(): part = part.astype(jnp.bfloat16)]
    ppermute x3, starting transfers between devices: 0.7 us -> 1.44 us  [to_label(): lax.ppermute(x, 'label', [(i, (i + by) % n_label) for i in range(n_label)])]
    concatenate x0 -> x1, other arithmetic: none -> 0.72 us  [local(): grad_w = jnp.concatenate([rest, grad_w], axis=0).astype(jnp.bfloat16)]
  transfers between devices with their start and end apart: 9 -> 11, of which waited for: 6 -> 5; matrix products, arithmetic and copies ran while one was open for 23% -> 22% of each run, Pallas kernels for 0% -> 0%
where the time goes in v13:
time: 56.1 us; the launch traced here: 55.9 us
  waiting for transfers between devices  24.5 us (44%)
  starting transfers between devices  14.5 us (26%)
  matrix products  12.3 us (22%)
  other arithmetic  3.52 us (6%)
  between operations  0.93 us (2%)
    ppermute x8, waiting for transfers between devices, to_dp(): return lax.ppermute(x, 'dp', [(i, i ^ k) for i in range(n_dp)])  23 us
    ppermute x8, starting transfers between devices, to_dp(): return lax.ppermute(x, 'dp', [(i, i ^ k) for i in range(n_dp)])  13 us
    dot_general x8, matrix products, delta_of(): lax.dot_general(rows, piece, (((1,), (1,)), ((), ())), preferred_element_...  7.27 us
    dot_general x8, matrix products, grad_w_of(): lax.dot_general(delta, rows, (((0,), (0,)), ((), ())), preferred_element_...  3.05 us
    dot_general x2, matrix products, grad_x_of(): jnp.dot(in_turn(jnp.concatenate([deltas[k] for k in range(n_dp)], axis=1)...  2.02 us
    convert_element_type x1, other arithmetic, local(): grad_x = (grad_x + in_turn(back).astype(jnp.float32)).astype(jnp.bfloat16)  1.75 us
    ppermute x3, waiting for transfers between devices, to_label(): lax.ppermute(x, 'label', [(i, (i + by) % n_label) for i in range(n_label)])  1.46 us
    ppermute x3, starting transfers between devices, to_label(): lax.ppermute(x, 'label', [(i, (i + by) % n_label) for i in range(n_label)])  1.44 us
  transfers between devices with their start and end apart: 11, of which 5 were waited for; matrix products, arithmetic and copies ran while one was open for 22% of the time, Pallas kernels for 0%

profile of v13, /device:TPU:0, one launch (start us, length us, event | category | flops | bytes accessed | tf_op | source)
XLA Modules:
  0.0 55.9 jit_solution(14997531239835330359)
XLA Ops:
  0.6 4.1 %collective-permute-start.3 = (bf16[128,1024]{1,0:T(8,128)(2,1)}, bf16[128,1024]{1,0:T(8,128)(2,1)S(1)}, u32[]{:S(2)}, u32[]{:S(2)}) collective-permute-start(bf16[128,1024]{1,0:T(8,128)(2,1)} %param.5), channel_id=1, source_target_pairs={{0,2},{1,3},{2,0},{3,1},{4,6},{5,7},{6,4},{7,5},{8,10},{9,11},{10,... | collective-permute-start | bytes 786440 | tf_op jit(solution)/shard_map/ppermute | solution.py:33
  4.7 0.7 %collective-permute-start = (bf16[768,1024]{1,0:T(8,128)(2,1)}, bf16[768,1024]{1,0:T(8,128)(2,1)S(1)}, u32[]{:S(2)}, u32[]{:S(2)}) collective-permute-start(bf16[768,1024]{1,0:T(8,128)(2,1)} %param.4), channel_id=1, source_target_pairs={{0,12},{4,0},{8,4},{12,8},{1,13},{5,1},{9,5},{13,9},{2,14},{6,2},{... | collective-permute-start | bytes 4718600 | tf_op jit(solution)/shard_map/ppermute | solution.py:36
  5.4 0.7 %fusion.52 = s32[768,8]{0,1:T(8,128)S(1)} fusion(s32[768,8]{0,1:T(8,128)} %param.6, s32[768]{0:T(1024)} %param.7), kind=kLoop, calls=%fused_computation.77 | loop fusion | flops 12288 | bytes 52224 | tf_op jit(solution)/shard_map/jit(_where)/select_n | solution.py:24
  6.2 0.0 copy-start.1
  6.2 0.0 copy-start
  6.2 2.3 %fusion.47 = bf16[768,128]{0,1:T(8,128)(2,1)S(1)} fusion(bf16[128,1024]{1,0:T(8,128)(2,1)} %param.5, bf16[768,1024]{1,0:T(8,128)(2,1)} %param.4, s32[768]{0:T(1024)S(1)} %get-tuple-element.57, s32[128]{0:T(128)S(1)} %iota_add_fusion.3), kind=kOutput, calls=%fused_computation.61 | convolution fusion | flops 202014720 | bytes 2035200 | tf_op jit(solution)/shard_map/dot_general | solution.py:43
  8.5 0.0 copy-done.1
  8.5 1.6 %collective-permute-start.2 = (bf16[128,1024]{1,0:T(8,128)(2,1)S(1)}, bf16[128,1024]{1,0:T(8,128)(2,1)S(1)}, u32[]{:S(2)}, u32[]{:S(2)}) collective-permute-start(bf16[128,1024]{1,0:T(8,128)(2,1)S(1)} %copy-done.1), channel_id=1, source_target_pairs={{0,1},{1,0},{2,3},{3,2},{4,5},{5,4},{6,7},{7,6},{8,9},{9,8},{10,11... | collective-permute-start | bytes 786440 | tf_op jit(solution)/shard_map/ppermute | solution.py:33
  10.2 0.0 copy-done
  10.2 0.4 fusion.53
  10.6 0.7 %collective-permute-start.1 = (s32[768,8]{0,1:T(8,128)S(1)}, s32[768,8]{0,1:T(8,128)S(1)}, u32[]{:S(2)}, u32[]{:S(2)}) collective-permute-start(s32[768,8]{0,1:T(8,128)S(1)} %fusion.52), channel_id=1, source_target_pairs={{0,12},{4,0},{8,4},{12,8},{1,13},{5,1},{9,5},{13,9},{2,14},{6,2},{... | collective-permute-start | bytes 73736 | tf_op jit(solution)/shard_map/ppermute | solution.py:36
  11.3 9.8 %collective-permute-done.2 = bf16[128,1024]{1,0:T(8,128)(2,1)S(1)} collective-permute-done((bf16[128,1024]{1,0:T(8,128)(2,1)S(1)}, bf16[128,1024]{1,0:T(8,128)(2,1)S(1)}, u32[]{:S(2)}, u32[]{:S(2)}) %collective-permute-start.2) | collective-permute-done | bytes 262176 | tf_op jit(solution)/shard_map/ppermute | solution.py:33
  21.1 0.7 %fusion.46 = bf16[768,128]{0,1:T(8,128)(2,1)S(1)} fusion(bf16[128,1024]{1,0:T(8,128)(2,1)S(1)} %collective-permute-done.2, bf16[768,1024]{1,0:T(8,128)(2,1)S(1)} %copy-done, s32[768]{0:T(1024)S(1)} %get-tuple-element.56, s32[128]{0:T(128)S(1)} %iota_add_fusion.2), kind=kOutput, calls=%fused_computation.60 | convolution fusion | flops 202014720 | bytes 2035200 | tf_op jit(solution)/shard_map/dot_general | solution.py:43
  21.8 0.4 fusion.54
  22.2 0.0 collective-permute-done.3
  22.3 0.1 collective-permute-start.4
  22.3 1.5 %collective-permute-done.1 = s32[768,8]{0,1:T(8,128)S(1)} collective-permute-done((s32[768,8]{0,1:T(8,128)S(1)}, s32[768,8]{0,1:T(8,128)S(1)}, u32[]{:S(2)}, u32[]{:S(2)}) %collective-permute-start.1) | collective-permute-done | bytes 24608 | tf_op jit(solution)/shard_map/ppermute | solution.py:36
  23.8 0.0 collective-permute-done
  23.8 0.7 %fusion.45 = bf16[768,128]{0,1:T(8,128)(2,1)S(1)} fusion(bf16[768,1024]{1,0:T(8,128)(2,1)S(1)} %collective-permute-done, bf16[128,1024]{1,0:T(8,128)(2,1)S(1)} %copy-done.1, s32[768]{0:T(1024)S(1)} %get-tuple-element.61, s32[128]{0:T(128)S(1)} %iota_add_fusion.3), kind=kOutput, calls=%fused_computation.59 | convolution fusion | flops 202014720 | bytes 2035200 | tf_op jit(solution)/shard_map/dot_general | solution.py:43
  24.6 0.7 %fusion.44 = bf16[768,128]{0,1:T(8,128)(2,1)S(1)} fusion(bf16[768,1024]{1,0:T(8,128)(2,1)S(1)} %collective-permute-done, bf16[128,1024]{1,0:T(8,128)(2,1)S(1)} %collective-permute-done.2, s32[768]{0:T(1024)S(1)} %get-tuple-element.60, s32[128]{0:T(128)S(1)} %iota_add_fusion.2), kind=kOutput, calls=%fused_computation.58 | convolution fusion | flops 202014720 | bytes 2035200 | tf_op jit(solution)/shard_map/dot_general | solution.py:43
  25.3 0.7 %fusion.43 = bf16[768,128]{0,1:T(8,128)(2,1)S(1)} fusion(bf16[768,1024]{1,0:T(8,128)(2,1)S(1)} %collective-permute-done, bf16[128,1024]{1,0:T(8,128)(2,1)S(1)} %collective-permute-done.3, s32[768]{0:T(1024)S(1)} %get-tuple-element.59, s32[128]{0:T(128)S(1)} %iota_add_fusion.1), kind=kOutput, calls=%fused_computation.57 | convolution fusion | flops 202014720 | bytes 2035200 | tf_op jit(solution)/shard_map/dot_general | solution.py:43
  26.0 0.7 %fusion.42 = bf16[768,128]{0,1:T(8,128)(2,1)S(1)} fusion(bf16[128,1024]{1,0:T(8,128)(2,1)S(1)} %collective-permute-done.3, bf16[768,1024]{1,0:T(8,128)(2,1)S(1)} %copy-done, s32[768]{0:T(1024)S(1)} %get-tuple-element.55, s32[128]{0:T(128)S(1)} %iota_add_fusion.1), kind=kOutput, calls=%fused_computation.56 | convolution fusion | flops 202014720 | bytes 2035200 | tf_op jit(solution)/shard_map/dot_general | solution.py:43
  26.7 0.4 fusion.55
  27.1 2.8 %collective-permute-done.4 = bf16[128,1024]{1,0:T(8,128)(2,1)S(1)} collective-permute-done((bf16[128,1024]{1,0:T(8,128)(2,1)S(1)}, bf16[128,1024]{1,0:T(8,128)(2,1)S(1)}, u32[]{:S(2)}, u32[]{:S(2)}) %collective-permute-start.4) | collective-permute-done | bytes 262176 | tf_op jit(solution)/shard_map/ppermute | solution.py:33
  29.9 0.7 %fusion.41 = bf16[768,128]{0,1:T(8,128)(2,1)S(1)} fusion(bf16[768,1024]{1,0:T(8,128)(2,1)S(1)} %collective-permute-done, bf16[128,1024]{1,0:T(8,128)(2,1)S(1)} %collective-permute-done.4, s32[768]{0:T(1024)S(1)} %get-tuple-element.58, s32[128]{0:T(128)S(1)} %iota_add_fusion), kind=kOutput, calls=%fused_computation.55 | convolution fusion | flops 202014720 | bytes 2035200 | tf_op jit(solution)/shard_map/dot_general | solution.py:43
  30.6 0.1 pad_maximum_fusion.1
  30.7 0.7 %fusion.40 = bf16[768,128]{0,1:T(8,128)(2,1)S(1)} fusion(bf16[128,1024]{1,0:T(8,128)(2,1)S(1)} %collective-permute-done.4, bf16[768,1024]{1,0:T(8,128)(2,1)S(1)} %copy-done, s32[768]{0:T(1024)S(1)} %get-tuple-element.54, s32[128]{0:T(128)S(1)} %iota_add_fusion), kind=kOutput, calls=%fused_computation.54 | convolution fusion | flops 202014720 | bytes 2035200 | tf_op jit(solution)/shard_map/dot_general | solution.py:43
  31.4 0.4 fusion.56
  31.8 0.4 fusion.3
  32.2 0.3 collective-permute-start.5
  32.6 1.0 %convolution_convert_fusion = bf16[768,1024]{1,0:T(8,128)(2,1)S(1)} fusion(bf16[768,512]{0,1:T(8,128)(2,1)S(1)} %pad_maximum_fusion.1, bf16[512,1024]{1,0:T(8,128)(2,1)S(1)} %constant_dynamic-update-slice_fusion), kind=kOutput, calls=%fused_computation.1 | convolution fusion | flops 806092800 | bytes 3407872 | tf_op jit(solution)/shard_map/dot_general | solution.py:54
  33.6 0.4 fusion.2
  34.0 0.1 collective-permute-start.10
  34.1 2.3 %collective-permute-start.8 = (bf16[32,1024]{1,0:T(8,128)(2,1)S(1)}, bf16[32,1024]{1,0:T(8,128)(2,1)S(1)}, u32[]{:S(2)}, u32[]{:S(2)}) collective-permute-start(bf16[32,1024]{1,0:T(8,128)(2,1)S(1)} %slice.48), channel_id=1, source_target_pairs={{0,2},{1,3},{2,0},{3,1},{4,6},{5,7},{6,4},{7,5},{8,10},{9,11},{10,... | collective-permute-start | bytes 196616 | tf_op jit(solution)/shard_map/ppermute | solution.py:33
  36.4 1.8 %collective-permute-start.7 = (bf16[32,1024]{1,0:T(8,128)(2,1)S(1)}, bf16[32,1024]{1,0:T(8,128)(2,1)S(1)}, u32[]{:S(2)}, u32[]{:S(2)}) collective-permute-start(bf16[32,1024]{1,0:T(8,128)(2,1)S(1)} %slice.49), channel_id=1, source_target_pairs={{0,3},{1,2},{2,1},{3,0},{4,7},{5,6},{6,5},{7,4},{8,11},{9,10},{10,... | collective-permute-start | bytes 196616 | tf_op jit(solution)/shard_map/ppermute | solution.py:33
  38.3 0.1 pad_maximum_fusion
  38.3 0.0 collective-permute-done.5
  38.4 0.5 collective-permute-start.9
  38.9 0.4 fusion.1
  39.3 2.2 %collective-permute-start.6 = (bf16[128,1024]{1,0:T(8,128)(2,1)S(1)}, bf16[128,1024]{1,0:T(8,128)(2,1)S(1)}, u32[]{:S(2)}, u32[]{:S(2)}) collective-permute-start(bf16[128,1024]{1,0:T(8,128)(2,1)S(1)} %fusion.1), channel_id=1, source_target_pairs={{0,1},{1,0},{2,3},{3,2},{4,5},{5,4},{6,7},{7,6},{8,9},{9,8},{10,11... | collective-permute-start | bytes 786440 | tf_op jit(solution)/shard_map/ppermute | solution.py:33
  41.5 1.0 %fusion.57 = f32[768,1024]{1,0:T(8,128)S(1)} fusion(bf16[768,512]{0,1:T(8,128)(2,1)S(1)} %pad_maximum_fusion, bf16[512,1024]{1,0:T(8,128)(2,1)S(1)} %constant_dynamic-update-slice_fusion), kind=kOutput, calls=%fused_computation.98 | convolution fusion | flops 805306368 | bytes 4980736 | tf_op jit(solution)/shard_map/dot_general | solution.py:54
  42.5 0.4 fusion
  42.9 0.0 collective-permute-done.8
  42.9 0.0 collective-permute-done.7
  42.9 9.6 %collective-permute-done.9 = bf16[96,1024]{1,0:T(8,128)(2,1)S(1)} collective-permute-done((bf16[96,1024]{1,0:T(8,128)(2,1)S(1)}, bf16[96,1024]{1,0:T(8,128)(2,1)S(1)}, u32[]{:S(2)}, u32[]{:S(2)}) %collective-permute-start.9) | collective-permute-done | bytes 196640 | tf_op jit(solution)/shard_map/ppermute | solution.py:33
  52.5 0.8 %collective-permute-done.6 = bf16[128,1024]{1,0:T(8,128)(2,1)S(1)} collective-permute-done((bf16[128,1024]{1,0:T(8,128)(2,1)S(1)}, bf16[128,1024]{1,0:T(8,128)(2,1)S(1)}, u32[]{:S(2)}, u32[]{:S(2)}) %collective-permute-start.6) | collective-permute-done | bytes 262176 | tf_op jit(solution)/shard_map/ppermute | solution.py:33
  53.3 0.1 convert_add_fusion
  53.4 0.1 fusion.48
  53.4 0.7 %pad_maximum_fusion.2 = bf16[128,1024]{1,0:T(8,128)(2,1)} fusion(bf16[96,1024]{1,0:T(8,128)(2,1)S(1)} %fusion.48, bf16[32,1024]{1,0:T(8,128)(2,1)S(1)} %fusion.51), kind=kLoop, calls=%fused_computation.70 | loop fusion | flops 524288 | bytes 524288 | tf_op jit(solution)/shard_map/concatenate | solution.py:134
  54.2 0.0 collective-permute-done.10
  54.2 1.8 %add_convert_fusion = bf16[768,1024]{1,0:T(8,128)(2,1)} fusion(f32[768,1024]{1,0:T(8,128)S(1)} %fusion.57, bf16[768,1024]{1,0:T(8,128)(2,1)S(1)} %collective-permute-done.10), kind=kLoop, calls=%fused_computation | loop fusion | flops 2359296 | bytes 6291456 | tf_op jit(solution)/shard_map/convert_element_type | solution.py:136
  (15 shorter events, 0.3 us)
Async XLA Ops:
  0.6 21.6 %collective-permute-start.3 = (bf16[128,1024]{1,0:T(8,128)(2,1)}, bf16[128,1024]{1,0:T(8,128)(2,1)S(1)}, u32[]{:S(2)}, u32[]{:S(2)}) collective-permute-start(bf16[128,1024]{1,0:T(8,128)(2,1)} %param.5), channel_id=1, source_target_pairs={{0,2},{1,3},{2,0},{3,1},{4,6},{5,7},{6,4},{7,5},{8,10},{9,11},{10,... | collective-permute-start | bytes 786440 | tf_op jit(solution)/shard_map/ppermute | solution.py:33
  4.7 19.1 %collective-permute-start = (bf16[768,1024]{1,0:T(8,128)(2,1)}, bf16[768,1024]{1,0:T(8,128)(2,1)S(1)}, u32[]{:S(2)}, u32[]{:S(2)}) collective-permute-start(bf16[768,1024]{1,0:T(8,128)(2,1)} %param.4), channel_id=1, source_target_pairs={{0,12},{4,0},{8,4},{12,8},{1,13},{5,1},{9,5},{13,9},{2,14},{6,2},{... | collective-permute-start | bytes 4718600 | tf_op jit(solution)/shard_map/ppermute | solution.py:36
  6.2 2.3 %copy-start.1 = (bf16[128,1024]{1,0:T(8,128)(2,1)S(1)}, bf16[128,1024]{1,0:T(8,128)(2,1)}, u32[]{:S(2)}) copy-start(bf16[128,1024]{1,0:T(8,128)(2,1)} %param.5) | copy-start | bytes 786436
  6.2 4.0 %copy-start = (bf16[768,1024]{1,0:T(8,128)(2,1)S(1)}, bf16[768,1024]{1,0:T(8,128)(2,1)}, u32[]{:S(2)}) copy-start(bf16[768,1024]{1,0:T(8,128)(2,1)} %param.4) | copy-start | bytes 4718596
  8.5 12.6 %collective-permute-start.2 = (bf16[128,1024]{1,0:T(8,128)(2,1)S(1)}, bf16[128,1024]{1,0:T(8,128)(2,1)S(1)}, u32[]{:S(2)}, u32[]{:S(2)}) collective-permute-start(bf16[128,1024]{1,0:T(8,128)(2,1)S(1)} %copy-done.1), channel_id=1, source_target_pairs={{0,1},{1,0},{2,3},{3,2},{4,5},{5,4},{6,7},{7,6},{8,9},{9,8},{10,11... | collective-permute-start | bytes 786440 | tf_op jit(solution)/shard_map/ppermute | solution.py:33
  10.6 13.2 %collective-permute-start.1 = (s32[768,8]{0,1:T(8,128)S(1)}, s32[768,8]{0,1:T(8,128)S(1)}, u32[]{:S(2)}, u32[]{:S(2)}) collective-permute-start(s32[768,8]{0,1:T(8,128)S(1)} %fusion.52), channel_id=1, source_target_pairs={{0,12},{4,0},{8,4},{12,8},{1,13},{5,1},{9,5},{13,9},{2,14},{6,2},{... | collective-permute-start | bytes 73736 | tf_op jit(solution)/shard_map/ppermute | solution.py:36
  22.3 7.7 %collective-permute-start.4 = (bf16[128,1024]{1,0:T(8,128)(2,1)S(1)}, bf16[128,1024]{1,0:T(8,128)(2,1)S(1)}, u32[]{:S(2)}, u32[]{:S(2)}) collective-permute-start(bf16[128,1024]{1,0:T(8,128)(2,1)S(1)} %collective-permute-done.3), channel_id=1, source_target_pairs={{0,1},{1,0},{2,3},{3,2},{4,5},{5,4},{6,7},{7,6},{8,9},{9,8},{10,11... | collective-permute-start | bytes 786440 | tf_op jit(solution)/shard_map/ppermute | solution.py:33
  32.2 6.1 %collective-permute-start.5 = (bf16[96,1024]{1,0:T(8,128)(2,1)S(1)}, bf16[96,1024]{1,0:T(8,128)(2,1)S(1)}, u32[]{:S(2)}, u32[]{:S(2)}) collective-permute-start(bf16[96,1024]{1,0:T(8,128)(2,1)S(1)} %slice.47), channel_id=1, source_target_pairs={{0,1},{1,0},{2,3},{3,2},{4,5},{5,4},{6,7},{7,6},{8,9},{9,8},{10,11... | collective-permute-start | bytes 589832 | tf_op jit(solution)/shard_map/ppermute | solution.py:33
  34.0 20.2 %collective-permute-start.10 = (bf16[768,1024]{1,0:T(8,128)(2,1)S(1)}, bf16[768,1024]{1,0:T(8,128)(2,1)S(1)}, u32[]{:S(2)}, u32[]{:S(2)}) collective-permute-start(bf16[768,1024]{1,0:T(8,128)(2,1)S(1)} %convolution_convert_fusion), channel_id=1, source_target_pairs={{0,4},{4,8},{8,12},{12,0},{1,5},{5,9},{9,13},{13,1},{2,6},{6,10},{... | collective-permute-start | bytes 4718600 | tf_op jit(solution)/shard_map/ppermute | solution.py:36
  34.1 8.8 %collective-permute-start.8 = (bf16[32,1024]{1,0:T(8,128)(2,1)S(1)}, bf16[32,1024]{1,0:T(8,128)(2,1)S(1)}, u32[]{:S(2)}, u32[]{:S(2)}) collective-permute-start(bf16[32,1024]{1,0:T(8,128)(2,1)S(1)} %slice.48), channel_id=1, source_target_pairs={{0,2},{1,3},{2,0},{3,1},{4,6},{5,7},{6,4},{7,5},{8,10},{9,11},{10,... | collective-permute-start | bytes 196616 | tf_op jit(solution)/shard_map/ppermute | solution.py:33
  36.4 6.5 %collective-permute-start.7 = (bf16[32,1024]{1,0:T(8,128)(2,1)S(1)}, bf16[32,1024]{1,0:T(8,128)(2,1)S(1)}, u32[]{:S(2)}, u32[]{:S(2)}) collective-permute-start(bf16[32,1024]{1,0:T(8,128)(2,1)S(1)} %slice.49), channel_id=1, source_target_pairs={{0,3},{1,2},{2,1},{3,0},{4,7},{5,6},{6,5},{7,4},{8,11},{9,10},{10,... | collective-permute-start | bytes 196616 | tf_op jit(solution)/shard_map/ppermute | solution.py:33
  38.4 14.1 %collective-permute-start.9 = (bf16[96,1024]{1,0:T(8,128)(2,1)S(1)}, bf16[96,1024]{1,0:T(8,128)(2,1)S(1)}, u32[]{:S(2)}, u32[]{:S(2)}) collective-permute-start(bf16[96,1024]{1,0:T(8,128)(2,1)S(1)} %fusion.49), channel_id=1, source_target_pairs={{0,2},{1,3},{2,0},{3,1},{4,6},{5,7},{6,4},{7,5},{8,10},{9,11},{10,... | collective-permute-start | bytes 589832 | tf_op jit(solution)/shard_map/ppermute | solution.py:33
  39.3 14.0 %collective-permute-start.6 = (bf16[128,1024]{1,0:T(8,128)(2,1)S(1)}, bf16[128,1024]{1,0:T(8,128)(2,1)S(1)}, u32[]{:S(2)}, u32[]{:S(2)}) collective-permute-start(bf16[128,1024]{1,0:T(8,128)(2,1)S(1)} %fusion.1), channel_id=1, source_target_pairs={{0,1},{1,0},{2,3},{3,2},{4,5},{5,4},{6,7},{7,6},{8,9},{9,8},{10,11... | collective-permute-start | bytes 786440 | tf_op jit(solution)/shard_map/ppermute | solution.py:33

commit v14 on v9

--- a/solution.py
+++ b/solution.py
@@ -31,11 +31,13 @@
     def to_label(x, by):
         return lax.ppermute(x, "label", [(i, (i + by) % n_label) for i in range(n_label)])
 
-    def delta_of(rows, row_ids, piece, k):
-        start = me_label * stretch + (me_dp ^ k) * ch_dev
-        column = lax.dynamic_slice_in_dim(row_ids, start // span, 1, axis=1)
-        labels = start + jnp.arange(ch_dev, dtype=jnp.int32)
-        target = (column == labels[None, :]).astype(jnp.float32)
+    def delta_of(rows, row_ids, piece, ks):
+        starts = [me_label * stretch + (me_dp ^ k) * ch_dev for k in ks]
+        place = jnp.arange(len(ks) * ch_dev, dtype=jnp.int32)[None, :]
+        for i, start in enumerate(starts):
+            column = lax.dynamic_slice_in_dim(row_ids, start // span, 1, axis=1) - (start - i * ch_dev)
+            sought = column if i == 0 else jnp.where(place < i * ch_dev, sought, column)
+        target = (sought == place).astype(jnp.float32)
         logits = lax.dot_general(
             rows, piece, (((1,), (1,)), ((), ())), preferred_element_type=jnp.float32
         )
@@ -46,50 +48,44 @@
             delta, rows, (((0,), (0,)), ((), ())), preferred_element_type=jnp.float32
         )
 
-    def grad_x_of(deltas):
-        return jnp.dot(
-            in_turn(jnp.concatenate([deltas[k] for k in range(n_dp)], axis=1)),
-            jnp.concatenate([pieces[k] for k in range(n_dp)], axis=0),
-            preferred_element_type=jnp.float32,
-        )
-
+    late = n_dp - 1
     pieces = {0: weights}
     for k in range(1, n_dp):
         step = k & -k
         pieces[k] = to_dp(pieces[k ^ step], step)
     next_rows = to_label(embeds, -1)
-    d_own, d_next, g_w = {}, {}, {}
+    d_own, g_w = {}, {}
 
     def own_step(k):
         pieces[k] = in_turn(pieces[k])
-        d_own[k] = delta_of(embeds, ids, pieces[k], k)
+        d_own[k] = delta_of(embeds, ids, pieces[k], [k])
         g_w[k] = grad_w_of(d_own[k], embeds)
         last[0] = g_w[k]
 
-    def next_step(k):
-        d_next[k] = delta_of(next_rows, next_ids, in_turn(pieces[k]), k)
-        last[0] = d_next[k]
-        if k > 1:
-            add_next(k)
-
     def add_next(k):
-        g_w[k] = (g_w[k] + grad_w_of(in_turn(d_next[k]), next_rows)) * scale
+        delta = in_turn(d_next)[:, k * ch_dev:(k + 1) * ch_dev]
+        g_w[k] = (g_w[k] + grad_w_of(delta, next_rows)) * scale
         last[0] = g_w[k]
 
-    own_step(1)
+    own_step(0)
     next_ids = to_label(in_turn(ids), -1)
-    for k in range(2, n_dp):
+    for k in range(1, n_dp):
         own_step(k)
+    joined = in_turn(jnp.concatenate([pieces[k] for k in range(n_dp)], axis=0))
+    joined = lax.optimization_barrier(joined)
+    last[0] = joined
     next_ids = in_turn(next_ids)
-    for k in range(n_dp - 1, -1, -1):
-        next_step(k)
-    theirs = grad_x_of(d_next).astype(jnp.bfloat16)
+    d_next = delta_of(next_rows, next_ids, joined, list(range(n_dp)))
+    last[0] = d_next
+    add_next(late)
+    theirs = jnp.dot(in_turn(d_next), joined, preferred_element_type=jnp.float32).astype(jnp.bfloat16)
     last[0] = theirs
     back = to_label(theirs, 1)
+    for k in range(late - 1, 0, -1):
+        add_next(k)
 
-    add_next(1)
     relayed, moved = {}, []
-    for k in range(n_dp - 1, 0, -1):
+    for k in range(late, 0, -1):
         step = k & -k
         for term in relayed.get(k, ()):
             g_w[k] = g_w[k] + term.astype(jnp.float32)
@@ -100,8 +96,11 @@
             moved.append(to_dp(part, k))
         else:
             relayed.setdefault(k ^ step, []).append(in_turn(to_dp(part, step)))
-    own_step(0)
-    grad_x = grad_x_of(d_own)
+    grad_x = jnp.dot(
+        in_turn(jnp.concatenate([d_own[k] for k in range(n_dp)], axis=1)),
+        joined,
+        preferred_element_type=jnp.float32,
+    )
     last[0] = grad_x
     add_next(0)
     grad_w = g_w[0]

time: 55.5 us -> 56.1 us (1.011)
  waiting for transfers between devices: 27.7 us -> 22.7 us
  starting transfers between devices: 10.5 us -> 13.4 us
  matrix products: 12.3 us -> 13.7 us
  other arithmetic: 3.48 us -> 4.6 us
    ppermute x6, waiting for transfers between devices: 27.3 us -> 21 us  [to_dp(): return lax.ppermute(x, 'dp', [(i, i ^ k) for i in range(n_dp)])]
    ppermute x6, starting transfers between devices: 9.83 us -> 11.7 us  [to_dp(): return lax.ppermute(x, 'dp', [(i, i ^ k) for i in range(n_dp)])]
    ppermute x3, waiting for transfers between devices: 0.45 us -> 1.66 us  [to_label(): lax.ppermute(x, 'label', [(i, (i + by) % n_label) for i in range(n_label)])]
    concatenate x2, other arithmetic: 0.11 us -> 1.15 us  [the longest x1 1.1 us: local(): joined = in_turn(jnp.concatenate([pieces[k] for k in range(n_dp)], axis=0))]
    ppermute x3, starting transfers between devices: 0.7 us -> 1.67 us  [to_label(): lax.ppermute(x, 'label', [(i, (i + by) % n_label) for i in range(n_label)])]
    dot_general x8, matrix products: 3.06 us -> 3.86 us  [grad_w_of(): lax.dot_general(delta, rows, (((0,), (0,)), ((), ())), preferred_element_...]
    dot_general x8 -> x5, matrix products: 7.17 us -> 7.86 us  [delta_of(): lax.dot_general(rows, piece, (((1,), (1,)), ((), ())), preferred_element_...]
  transfers between devices with their start and end apart: 9 -> 9, of which waited for: 6 -> 6; matrix products, arithmetic and copies ran while one was open for 23% -> 26% of each run, Pallas kernels for 0% -> 0%
where the time goes in v14:
time: 56.1 us; the launch traced here: 55.8 us
  waiting for transfers between devices  22.7 us (40%)
  matrix products  13.7 us (24%)
  starting transfers between devices  13.4 us (24%)
  other arithmetic  4.6 us (8%)
  between operations  0.84 us (1%)
  local copies, waits for them, and re-layouts  0.57 us (1%)
    ppermute x6, waiting for transfers between devices, to_dp(): return lax.ppermute(x, 'dp', [(i, i ^ k) for i in range(n_dp)])  21 us
    ppermute x6, starting transfers between devices, to_dp(): return lax.ppermute(x, 'dp', [(i, i ^ k) for i in range(n_dp)])  11.7 us
    dot_general x5, matrix products, delta_of(): lax.dot_general(rows, piece, (((1,), (1,)), ((), ())), preferred_element_...  7.86 us
    dot_general x8, matrix products, grad_w_of(): lax.dot_general(delta, rows, (((0,), (0,)), ((), ())), preferred_element_...  3.86 us
    convert_element_type x1, other arithmetic, local(): grad_x = (grad_x + in_turn(back).astype(jnp.float32)).astype(jnp.bfloat16)  1.75 us
    ppermute x3, starting transfers between devices, to_label(): lax.ppermute(x, 'label', [(i, (i + by) % n_label) for i in range(n_label)])  1.67 us
    ppermute x3, waiting for transfers between devices, to_label(): lax.ppermute(x, 'label', [(i, (i + by) % n_label) for i in range(n_label)])  1.66 us
  transfers between devices with their start and end apart: 9, of which 6 were waited for; matrix products, arithmetic and copies ran while one was open for 26% of the time, Pallas kernels for 0%

profile of v14, /device:TPU:0, one launch (start us, length us, event | category | flops | bytes accessed | tf_op | source)
XLA Modules:
  0.0 55.8 jit_solution(10045560048176986328)
XLA Ops:
  0.6 4.1 %collective-permute-start.1 = (bf16[128,1024]{1,0:T(8,128)(2,1)}, bf16[128,1024]{1,0:T(8,128)(2,1)}, u32[]{:S(2)}, u32[]{:S(2)}) collective-permute-start(bf16[128,1024]{1,0:T(8,128)(2,1)} %param.5), channel_id=1, source_target_pairs={{0,2},{1,3},{2,0},{3,1},{4,6},{5,7},{6,4},{7,5},{8,10},{9,11},{10,... | collective-permute-start | bytes 786440 | tf_op jit(solution)/shard_map/ppermute | solution.py:29
  4.7 1.6 %collective-permute-start = (bf16[128,1024]{1,0:T(8,128)(2,1)}, bf16[128,1024]{1,0:T(8,128)(2,1)}, u32[]{:S(2)}, u32[]{:S(2)}) collective-permute-start(bf16[128,1024]{1,0:T(8,128)(2,1)} %param.5), channel_id=1, source_target_pairs={{0,1},{1,0},{2,3},{3,2},{4,5},{5,4},{6,7},{7,6},{8,9},{9,8},{10,11... | collective-permute-start | bytes 786440 | tf_op jit(solution)/shard_map/ppermute | solution.py:29
  6.3 0.4 collective-permute-start.3
  6.7 0.7 %fusion.33 = s32[768,8]{0,1:T(8,128)S(1)} fusion(s32[768,8]{0,1:T(8,128)} %param.6, s32[768]{0:T(1024)} %param.7), kind=kLoop, calls=%fused_computation.54 | loop fusion | flops 12288 | bytes 52224 | tf_op jit(solution)/shard_map/jit(_where)/select_n | solution.py:21
  7.5 0.0 copy-start
  7.5 2.3 %fusion.28 = bf16[768,128]{0,1:T(8,128)(2,1)S(1)} fusion(bf16[128,1024]{1,0:T(8,128)(2,1)} %param.5, bf16[768,1024]{1,0:T(8,128)(2,1)} %param.4, s32[768]{0:T(1024)S(1)} %get-tuple-element.43), kind=kOutput, calls=%fused_computation.40 | convolution fusion | flops 202014720 | bytes 2034688 | tf_op jit(solution)/shard_map/dot_general | solution.py:41
  9.8 0.0 copy-done
  9.8 1.2 %fusion.34 = f32[128,1024]{1,0:T(8,128)} fusion(bf16[768,128]{0,1:T(8,128)(2,1)S(1)} %fusion.28, bf16[768,1024]{1,0:T(8,128)(2,1)S(1)} %copy-done), kind=kOutput, calls=%fused_computation.66 | convolution fusion | flops 201326592 | bytes 2293760 | tf_op jit(solution)/shard_map/dot_general | solution.py:47
  11.0 1.2 %collective-permute-start.4 = (s32[768,8]{0,1:T(8,128)S(1)}, s32[768,8]{0,1:T(8,128)S(1)}, u32[]{:S(2)}, u32[]{:S(2)}) collective-permute-start(s32[768,8]{0,1:T(8,128)S(1)} %fusion.33), channel_id=1, source_target_pairs={{0,12},{4,0},{8,4},{12,8},{1,13},{5,1},{9,5},{13,9},{2,14},{6,2},{... | collective-permute-start | bytes 73736 | tf_op jit(solution)/shard_map/ppermute | solution.py:32
  12.2 5.0 %collective-permute-done = bf16[128,1024]{1,0:T(8,128)(2,1)} collective-permute-done((bf16[128,1024]{1,0:T(8,128)(2,1)}, bf16[128,1024]{1,0:T(8,128)(2,1)}, u32[]{:S(2)}, u32[]{:S(2)}) %collective-permute-start) | collective-permute-done | bytes 262176 | tf_op jit(solution)/shard_map/ppermute | solution.py:29
  17.3 1.7 %fusion.27 = bf16[768,128]{0,1:T(8,128)(2,1)S(1)} fusion(bf16[128,1024]{1,0:T(8,128)(2,1)} %collective-permute-done, bf16[768,1024]{1,0:T(8,128)(2,1)S(1)} %copy-done, s32[768]{0:T(1024)S(1)} %get-tuple-element.42), kind=kOutput, calls=%fused_computation.39 | convolution fusion | flops 202014720 | bytes 2034688 | tf_op jit(solution)/shard_map/dot_general | solution.py:41
  18.9 0.4 fusion.35
  19.3 0.0 collective-permute-done.1
  19.3 1.5 %collective-permute-start.2 = (bf16[128,1024]{1,0:T(8,128)(2,1)}, bf16[128,1024]{1,0:T(8,128)(2,1)S(1)}, u32[]{:S(2)}, u32[]{:S(2)}) collective-permute-start(bf16[128,1024]{1,0:T(8,128)(2,1)} %collective-permute-done.1), channel_id=1, source_target_pairs={{0,1},{1,0},{2,3},{3,2},{4,5},{5,4},{6,7},{7,6},{8,9},{9,8},{10,11... | collective-permute-start | bytes 786440 | tf_op jit(solution)/shard_map/ppermute | solution.py:29
  20.9 1.7 %fusion.26 = bf16[768,128]{0,1:T(8,128)(2,1)S(1)} fusion(bf16[128,1024]{1,0:T(8,128)(2,1)} %collective-permute-done.1, bf16[768,1024]{1,0:T(8,128)(2,1)S(1)} %copy-done, s32[768]{0:T(1024)S(1)} %get-tuple-element.41), kind=kOutput, calls=%fused_computation.38 | convolution fusion | flops 202014720 | bytes 2034688 | tf_op jit(solution)/shard_map/dot_general | solution.py:41
  22.6 0.4 fusion.36
  23.0 3.6 %collective-permute-done.2 = bf16[128,1024]{1,0:T(8,128)(2,1)S(1)} collective-permute-done((bf16[128,1024]{1,0:T(8,128)(2,1)}, bf16[128,1024]{1,0:T(8,128)(2,1)S(1)}, u32[]{:S(2)}, u32[]{:S(2)}) %collective-permute-start.2) | collective-permute-done | bytes 262176 | tf_op jit(solution)/shard_map/ppermute | solution.py:29
  26.5 0.7 %fusion.25 = bf16[768,128]{0,1:T(8,128)(2,1)S(1)} fusion(bf16[128,1024]{1,0:T(8,128)(2,1)S(1)} %collective-permute-done.2, bf16[768,1024]{1,0:T(8,128)(2,1)S(1)} %copy-done, s32[768]{0:T(1024)S(1)} %get-tuple-element.40), kind=kOutput, calls=%fused_computation.37 | convolution fusion | flops 202014720 | bytes 2034688 | tf_op jit(solution)/shard_map/dot_general | solution.py:41
  27.2 0.0 copy-start.2
  27.2 0.4 fusion.37
  27.6 0.6 copy-done.2
  28.2 1.1 %pad_maximum_fusion = bf16[512,1024]{1,0:T(8,128)(2,1)S(1)} fusion(bf16[128,1024]{1,0:T(8,128)(2,1)S(1)} %collective-permute-done.2, bf16[128,1024]{1,0:T(8,128)(2,1)} %collective-permute-done.1, bf16[128,1024]{1,0:T(8,128)(2,1)} %collective-permute-done, bf16[128,1024]{1,0:T(8,128)(2,1)S(1)} %copy-done.2), kind=kLoop, calls=%fused_computation.41 | loop fusion | flops 4194304 | bytes 2097152 | tf_op jit(solution)/shard_map/concatenate | solution.py:74
  29.3 0.0 collective-permute-done.4
  29.3 0.1 subtract_reduce_fusion.3
  29.4 0.1 pad_maximum_fusion.1
  29.4 0.0 collective-permute-done.3
  29.4 1.5 %fusion = bf16[768,512]{0,1:T(8,128)(2,1)S(1)} fusion(bf16[512,1024]{1,0:T(8,128)(2,1)S(1)} %pad_maximum_fusion, bf16[768,1024]{1,0:T(8,128)(2,1)S(1)} %collective-permute-done.3, s32[768]{0:T(1024)S(1)} %get-tuple-element.37, s32[768]{0:T(1024)S(1)} %get-tuple-element.38, s32[768]{0:T(1024)S(1)} %get-tuple-element.39, s32[768]{0:T(1024)S(1)} %get-tuple-element.36, ...), kind=kOutput, calls=%fused_computation.3 | convolution fusion | flops 809238528 | bytes 3421696 | tf_op jit(solution)/shard_map/dot_general | solution.py:41
  31.0 0.4 fusion.4
  31.3 1.8 %collective-permute-start.5 = (bf16[128,1024]{1,0:T(8,128)(2,1)S(1)}, bf16[128,1024]{1,0:T(8,128)(2,1)S(1)}, u32[]{:S(2)}, u32[]{:S(2)}) collective-permute-start(bf16[128,1024]{1,0:T(8,128)(2,1)S(1)} %fusion.4), channel_id=1, source_target_pairs={{0,1},{1,0},{2,3},{3,2},{4,5},{5,4},{6,7},{7,6},{8,9},{9,8},{10,11... | collective-permute-start | bytes 786440 | tf_op jit(solution)/shard_map/ppermute | solution.py:29
  33.2 1.0 %convolution_convert_fusion = bf16[768,1024]{1,0:T(8,128)(2,1)S(1)} fusion(bf16[768,512]{0,1:T(8,128)(2,1)S(1)} %fusion, bf16[512,1024]{1,0:T(8,128)(2,1)S(1)} %pad_maximum_fusion), kind=kOutput, calls=%fused_computation.1 | convolution fusion | flops 806092800 | bytes 3407872 | tf_op jit(solution)/shard_map/dot_general | solution.py:81
  34.2 0.1 collective-permute-start.8
  34.2 0.4 fusion.3
  34.6 0.4 fusion.2
  35.0 0.3 collective-permute-start.6
  35.4 2.4 %collective-permute-done.5 = bf16[128,1024]{1,0:T(8,128)(2,1)S(1)} collective-permute-done((bf16[128,1024]{1,0:T(8,128)(2,1)S(1)}, bf16[128,1024]{1,0:T(8,128)(2,1)S(1)}, u32[]{:S(2)}, u32[]{:S(2)}) %collective-permute-start.5) | collective-permute-done | bytes 262176 | tf_op jit(solution)/shard_map/ppermute | solution.py:29
  37.8 0.1 add_convert_fusion.2
  37.8 0.0 copy-start.1
  37.9 2.3 %collective-permute-start.7 = (bf16[128,1024]{1,0:T(8,128)(2,1)S(1)}, bf16[128,1024]{1,0:T(8,128)(2,1)S(1)}, u32[]{:S(2)}, u32[]{:S(2)}) collective-permute-start(bf16[128,1024]{1,0:T(8,128)(2,1)S(1)} %add_convert_fusion.2), channel_id=1, source_target_pairs={{0,2},{1,3},{2,0},{3,1},{4,6},{5,7},{6,4},{7,5},{8,10},{9,11},{10,... | collective-permute-start | bytes 786440 | tf_op jit(solution)/shard_map/ppermute | solution.py:29
  40.2 1.0 %fusion.38 = f32[768,1024]{1,0:T(8,128)S(1)} fusion(bf16[768,512]{0,1:T(8,128)(2,1)S(1)} %pad_maximum_fusion.1, bf16[512,1024]{1,0:T(8,128)(2,1)S(1)} %pad_maximum_fusion), kind=kOutput, calls=%fused_computation.70 | convolution fusion | flops 805306368 | bytes 4980736 | tf_op jit(solution)/shard_map/dot_general | solution.py:99
  41.2 0.0 copy-done.1
  41.2 0.4 fusion.1
  41.6 6.9 %collective-permute-done.6 = bf16[128,1024]{1,0:T(8,128)(2,1)S(1)} collective-permute-done((bf16[128,1024]{1,0:T(8,128)(2,1)S(1)}, bf16[128,1024]{1,0:T(8,128)(2,1)S(1)}, u32[]{:S(2)}, u32[]{:S(2)}) %collective-permute-start.6) | collective-permute-done | bytes 262176 | tf_op jit(solution)/shard_map/ppermute | solution.py:29
  48.5 3.1 %collective-permute-done.7 = bf16[128,1024]{1,0:T(8,128)(2,1)S(1)} collective-permute-done((bf16[128,1024]{1,0:T(8,128)(2,1)S(1)}, bf16[128,1024]{1,0:T(8,128)(2,1)S(1)}, u32[]{:S(2)}, u32[]{:S(2)}) %collective-permute-start.7) | collective-permute-done | bytes 262176 | tf_op jit(solution)/shard_map/ppermute | solution.py:29
  51.6 0.8 %add_convert_fusion.1 = bf16[128,1024]{1,0:T(8,128)(2,1)} fusion(bf16[128,1024]{1,0:T(8,128)(2,1)S(1)} %collective-permute-done.7, f32[128,1024]{1,0:T(8,128)S(1)} %fusion.1, bf16[128,1024]{1,0:T(8,128)(2,1)S(1)} %collective-permute-done.6), kind=kLoop, calls=%fused_computation.43 | loop fusion | flops 655360 | bytes 1310720 | tf_op jit(solution)/shard_map/convert_element_type | solution.py:109
  52.4 1.7 %collective-permute-done.8 = bf16[768,1024]{1,0:T(8,128)(2,1)S(1)} collective-permute-done((bf16[768,1024]{1,0:T(8,128)(2,1)S(1)}, bf16[768,1024]{1,0:T(8,128)(2,1)S(1)}, u32[]{:S(2)}, u32[]{:S(2)}) %collective-permute-start.8) | collective-permute-done | bytes 1572896 | tf_op jit(solution)/shard_map/ppermute | solution.py:32
  54.1 1.8 %add_convert_fusion = bf16[768,1024]{1,0:T(8,128)(2,1)} fusion(f32[768,1024]{1,0:T(8,128)S(1)} %fusion.38, bf16[768,1024]{1,0:T(8,128)(2,1)S(1)} %collective-permute-done.8), kind=kLoop, calls=%fused_computation | loop fusion | flops 2359296 | bytes 6291456 | tf_op jit(solution)/shard_map/convert_element_type | solution.py:111
  (3 shorter events, 0.1 us)
Async XLA Ops:
  0.6 18.7 %collective-permute-start.1 = (bf16[128,1024]{1,0:T(8,128)(2,1)}, bf16[128,1024]{1,0:T(8,128)(2,1)}, u32[]{:S(2)}, u32[]{:S(2)}) collective-permute-start(bf16[128,1024]{1,0:T(8,128)(2,1)} %param.5), channel_id=1, source_target_pairs={{0,2},{1,3},{2,0},{3,1},{4,6},{5,7},{6,4},{7,5},{8,10},{9,11},{10,... | collective-permute-start | bytes 786440 | tf_op jit(solution)/shard_map/ppermute | solution.py:29
  4.7 12.5 %collective-permute-start = (bf16[128,1024]{1,0:T(8,128)(2,1)}, bf16[128,1024]{1,0:T(8,128)(2,1)}, u32[]{:S(2)}, u32[]{:S(2)}) collective-permute-start(bf16[128,1024]{1,0:T(8,128)(2,1)} %param.5), channel_id=1, source_target_pairs={{0,1},{1,0},{2,3},{3,2},{4,5},{5,4},{6,7},{7,6},{8,9},{9,8},{10,11... | collective-permute-start | bytes 786440 | tf_op jit(solution)/shard_map/ppermute | solution.py:29
  6.3 23.1 %collective-permute-start.3 = (bf16[768,1024]{1,0:T(8,128)(2,1)}, bf16[768,1024]{1,0:T(8,128)(2,1)S(1)}, u32[]{:S(2)}, u32[]{:S(2)}) collective-permute-start(bf16[768,1024]{1,0:T(8,128)(2,1)} %param.4), channel_id=1, source_target_pairs={{0,12},{4,0},{8,4},{12,8},{1,13},{5,1},{9,5},{13,9},{2,14},{6,2},{... | collective-permute-start | bytes 4718600 | tf_op jit(solution)/shard_map/ppermute | solution.py:32
  7.5 2.3 %copy-start = (bf16[768,1024]{1,0:T(8,128)(2,1)S(1)}, bf16[768,1024]{1,0:T(8,128)(2,1)}, u32[]{:S(2)}) copy-start(bf16[768,1024]{1,0:T(8,128)(2,1)} %param.4) | copy-start | bytes 4718596
  11.0 18.3 %collective-permute-start.4 = (s32[768,8]{0,1:T(8,128)S(1)}, s32[768,8]{0,1:T(8,128)S(1)}, u32[]{:S(2)}, u32[]{:S(2)}) collective-permute-start(s32[768,8]{0,1:T(8,128)S(1)} %fusion.33), channel_id=1, source_target_pairs={{0,12},{4,0},{8,4},{12,8},{1,13},{5,1},{9,5},{13,9},{2,14},{6,2},{... | collective-permute-start | bytes 73736 | tf_op jit(solution)/shard_map/ppermute | solution.py:32
  19.3 7.2 %collective-permute-start.2 = (bf16[128,1024]{1,0:T(8,128)(2,1)}, bf16[128,1024]{1,0:T(8,128)(2,1)S(1)}, u32[]{:S(2)}, u32[]{:S(2)}) collective-permute-start(bf16[128,1024]{1,0:T(8,128)(2,1)} %collective-permute-done.1), channel_id=1, source_target_pairs={{0,1},{1,0},{2,3},{3,2},{4,5},{5,4},{6,7},{7,6},{8,9},{9,8},{10,11... | collective-permute-start | bytes 786440 | tf_op jit(solution)/shard_map/ppermute | solution.py:29
  27.2 1.0 %copy-start.2 = (bf16[128,1024]{1,0:T(8,128)(2,1)S(1)}, bf16[128,1024]{1,0:T(8,128)(2,1)}, u32[]{:S(2)}) copy-start(bf16[128,1024]{1,0:T(8,128)(2,1)} %param.5) | copy-start | bytes 786436
  31.3 6.4 %collective-permute-start.5 = (bf16[128,1024]{1,0:T(8,128)(2,1)S(1)}, bf16[128,1024]{1,0:T(8,128)(2,1)S(1)}, u32[]{:S(2)}, u32[]{:S(2)}) collective-permute-start(bf16[128,1024]{1,0:T(8,128)(2,1)S(1)} %fusion.4), channel_id=1, source_target_pairs={{0,1},{1,0},{2,3},{3,2},{4,5},{5,4},{6,7},{7,6},{8,9},{9,8},{10,11... | collective-permute-start | bytes 786440 | tf_op jit(solution)/shard_map/ppermute | solution.py:29
  34.2 19.9 %collective-permute-start.8 = (bf16[768,1024]{1,0:T(8,128)(2,1)S(1)}, bf16[768,1024]{1,0:T(8,128)(2,1)S(1)}, u32[]{:S(2)}, u32[]{:S(2)}) collective-permute-start(bf16[768,1024]{1,0:T(8,128)(2,1)S(1)} %convolution_convert_fusion), channel_id=1, source_target_pairs={{0,4},{4,8},{8,12},{12,0},{1,5},{5,9},{9,13},{13,1},{2,6},{6,10},{... | collective-permute-start | bytes 4718600 | tf_op jit(solution)/shard_map/ppermute | solution.py:32
  35.0 13.5 %collective-permute-start.6 = (bf16[128,1024]{1,0:T(8,128)(2,1)S(1)}, bf16[128,1024]{1,0:T(8,128)(2,1)S(1)}, u32[]{:S(2)}, u32[]{:S(2)}) collective-permute-start(bf16[128,1024]{1,0:T(8,128)(2,1)S(1)} %fusion.2), channel_id=1, source_target_pairs={{0,1},{1,0},{2,3},{3,2},{4,5},{5,4},{6,7},{7,6},{8,9},{9,8},{10,11... | collective-permute-start | bytes 786440 | tf_op jit(solution)/shard_map/ppermute | solution.py:29
  37.8 3.4 %copy-start.1 = (f32[128,1024]{1,0:T(8,128)S(1)}, f32[128,1024]{1,0:T(8,128)}, u32[]{:S(2)}) copy-start(f32[128,1024]{1,0:T(8,128)} %fusion.34) | copy-start | bytes 1572868
  37.9 13.8 %collective-permute-start.7 = (bf16[128,1024]{1,0:T(8,128)(2,1)S(1)}, bf16[128,1024]{1,0:T(8,128)(2,1)S(1)}, u32[]{:S(2)}, u32[]{:S(2)}) collective-permute-start(bf16[128,1024]{1,0:T(8,128)(2,1)S(1)} %add_convert_fusion.2), channel_id=1, source_target_pairs={{0,2},{1,3},{2,0},{3,1},{4,6},{5,7},{6,4},{7,5},{8,10},{9,11},{10,... | collective-permute-start | bytes 786440 | tf_op jit(solution)/shard_map/ppermute | solution.py:29

commit v15 on v14

--- a/solution.py
+++ b/solution.py
@@ -55,11 +55,13 @@
         pieces[k] = to_dp(pieces[k ^ step], step)
     next_rows = to_label(embeds, -1)
     d_own, g_w = {}, {}
+    joined = [jnp.zeros((stretch, width), weights.dtype)]
 
     def own_step(k):
         pieces[k] = in_turn(pieces[k])
         d_own[k] = delta_of(embeds, ids, pieces[k], [k])
         g_w[k] = grad_w_of(d_own[k], embeds)
+        joined[0] = lax.dynamic_update_slice_in_dim(joined[0], pieces[k], k * ch_dev, axis=0)
         last[0] = g_w[k]
 
     def add_next(k):
@@ -71,9 +73,7 @@
     next_ids = to_label(in_turn(ids), -1)
     for k in range(1, n_dp):
         own_step(k)
-    joined = in_turn(jnp.concatenate([pieces[k] for k in range(n_dp)], axis=0))
-    joined = lax.optimization_barrier(joined)
-    last[0] = joined
+    joined = joined[0]
     next_ids = in_turn(next_ids)
     d_next = delta_of(next_rows, next_ids, joined, list(range(n_dp)))
     last[0] = d_next
@@ -81,7 +81,7 @@
     theirs = jnp.dot(in_turn(d_next), joined, preferred_element_type=jnp.float32).astype(jnp.bfloat16)
     last[0] = theirs
     back = to_label(theirs, 1)
-    for k in range(late - 1, 0, -1):
+    for k in range(1, late):
         add_next(k)
 
     relayed, moved = {}, []

time: 56.1 us -> 54.5 us (0.971)
  local copies, waits for them, and re-layouts: 0.57 us -> 3.03 us
  waiting for transfers between devices: 22.7 us -> 20.4 us
  other arithmetic: 4.6 us -> 3.51 us
  starting transfers between devices: 13.4 us -> 12.7 us
    dynamic_update_slice x0 -> x4, local copies, waits for them, and re-layouts: none -> 3.02 us  [own_step(): lax.dynamic_update_slice_in_dim(joined[0], pieces[k], k * ch_dev, axis=0)]
    ppermute x6, waiting for transfers between devices: 21 us -> 18.7 us  [to_dp(): return lax.ppermute(x, 'dp', [(i, i ^ k) for i in range(n_dp)])]
    concatenate x1 -> x0, other arithmetic: 1.1 us -> none  [local(): joined = in_turn(jnp.concatenate([pieces[k] for k in range(n_dp)], axis=0))]
    ppermute x6, starting transfers between devices: 11.7 us -> 11 us  [to_dp(): return lax.ppermute(x, 'dp', [(i, i ^ k) for i in range(n_dp)])]
  transfers between devices with their start and end apart: 9 -> 9, of which waited for: 6 -> 6; matrix products, arithmetic and copies ran while one was open for 26% -> 31% of each run, Pallas kernels for 0% -> 0%
where the time goes in v15:
time: 54.5 us; the launch traced here: 54.2 us
  waiting for transfers between devices  20.4 us (37%)
  matrix products  13.7 us (25%)
  starting transfers between devices  12.7 us (23%)
  other arithmetic  3.51 us (6%)
  local copies, waits for them, and re-layouts  3.03 us (6%)
  between operations  0.86 us (2%)
    ppermute x6, waiting for transfers between devices, to_dp(): return lax.ppermute(x, 'dp', [(i, i ^ k) for i in range(n_dp)])  18.7 us
    ppermute x6, starting transfers between devices, to_dp(): return lax.ppermute(x, 'dp', [(i, i ^ k) for i in range(n_dp)])  11 us
    dot_general x5, matrix products, delta_of(): lax.dot_general(rows, piece, (((1,), (1,)), ((), ())), preferred_element_...  7.82 us
    dot_general x8, matrix products, grad_w_of(): lax.dot_general(delta, rows, (((0,), (0,)), ((), ())), preferred_element_...  3.86 us
    dynamic_update_slice x4, local copies, waits for them, and re-layouts, own_step(): lax.dynamic_update_slice_in_dim(joined[0], pieces[k], k * ch_dev, axis=0)  3.02 us
    convert_element_type x1, other arithmetic, local(): grad_x = (grad_x + in_turn(back).astype(jnp.float32)).astype(jnp.bfloat16)  1.75 us
    ppermute x3, starting transfers between devices, to_label(): lax.ppermute(x, 'label', [(i, (i + by) % n_label) for i in range(n_label)])  1.67 us
    ppermute x3, waiting for transfers between devices, to_label(): lax.ppermute(x, 'label', [(i, (i + by) % n_label) for i in range(n_label)])  1.63 us
  transfers between devices with their start and end apart: 9, of which 6 were waited for; matrix products, arithmetic and copies ran while one was open for 31% of the time, Pallas kernels for 0%

profile of v15, /device:TPU:0, one launch (start us, length us, event | category | flops | bytes accessed | tf_op | source)
XLA Modules:
  0.0 54.2 jit_solution(10281152902446358863)
XLA Ops:
  0.6 4.1 %collective-permute-start.1 = (bf16[128,1024]{1,0:T(8,128)(2,1)}, bf16[128,1024]{1,0:T(8,128)(2,1)}, u32[]{:S(2)}, u32[]{:S(2)}) collective-permute-start(bf16[128,1024]{1,0:T(8,128)(2,1)} %param.5), channel_id=1, source_target_pairs={{0,2},{1,3},{2,0},{3,1},{4,6},{5,7},{6,4},{7,5},{8,10},{9,11},{10,... | collective-permute-start | bytes 786440 | tf_op jit(solution)/shard_map/ppermute | solution.py:29
  4.7 1.6 %collective-permute-start = (bf16[128,1024]{1,0:T(8,128)(2,1)}, bf16[128,1024]{1,0:T(8,128)(2,1)}, u32[]{:S(2)}, u32[]{:S(2)}) collective-permute-start(bf16[128,1024]{1,0:T(8,128)(2,1)} %param.5), channel_id=1, source_target_pairs={{0,1},{1,0},{2,3},{3,2},{4,5},{5,4},{6,7},{7,6},{8,9},{9,8},{10,11... | collective-permute-start | bytes 786440 | tf_op jit(solution)/shard_map/ppermute | solution.py:29
  6.3 0.4 collective-permute-start.3
  6.7 0.7 %fusion.33 = s32[768,8]{0,1:T(8,128)S(1)} fusion(s32[768,8]{0,1:T(8,128)} %param.6, s32[768]{0:T(1024)} %param.7), kind=kLoop, calls=%fused_computation.53 | loop fusion | flops 12288 | bytes 52224 | tf_op jit(solution)/shard_map/jit(_where)/select_n | solution.py:21
  7.5 0.0 copy-start
  7.5 2.3 %fusion.28 = bf16[768,128]{0,1:T(8,128)(2,1)S(1)} fusion(bf16[128,1024]{1,0:T(8,128)(2,1)} %param.5, bf16[768,1024]{1,0:T(8,128)(2,1)} %param.4, s32[768]{0:T(1024)S(1)} %get-tuple-element.41), kind=kOutput, calls=%fused_computation.40 | convolution fusion | flops 202014720 | bytes 2034688 | tf_op jit(solution)/shard_map/dot_general | solution.py:41
  9.8 0.0 copy-done
  9.8 1.2 %fusion.34 = f32[128,1024]{1,0:T(8,128)} fusion(bf16[768,128]{0,1:T(8,128)(2,1)S(1)} %fusion.28, bf16[768,1024]{1,0:T(8,128)(2,1)S(1)} %copy-done), kind=kOutput, calls=%fused_computation.68 | convolution fusion | flops 201326592 | bytes 2293760 | tf_op jit(solution)/shard_map/dot_general | solution.py:47
  11.0 1.2 %collective-permute-start.4 = (s32[768,8]{0,1:T(8,128)S(1)}, s32[768,8]{0,1:T(8,128)S(1)}, u32[]{:S(2)}, u32[]{:S(2)}) collective-permute-start(s32[768,8]{0,1:T(8,128)S(1)} %fusion.33), channel_id=1, source_target_pairs={{0,12},{4,0},{8,4},{12,8},{1,13},{5,1},{9,5},{13,9},{2,14},{6,2},{... | collective-permute-start | bytes 73736 | tf_op jit(solution)/shard_map/ppermute | solution.py:32
  12.2 1.1 %dynamic_update_slice.12 = bf16[512,1024]{1,0:T(8,128)(2,1)S(1)} pad(bf16[128,1024]{1,0:T(8,128)(2,1)} %param.5, bf16[]{:T(256)} %constant.74.clone.1), padding=0_384x0_0 | pad | bytes 1310722 | tf_op jit(solution)/shard_map/dynamic_update_slice | solution.py:64
  13.3 4.0 %collective-permute-done = bf16[128,1024]{1,0:T(8,128)(2,1)} collective-permute-done((bf16[128,1024]{1,0:T(8,128)(2,1)}, bf16[128,1024]{1,0:T(8,128)(2,1)}, u32[]{:S(2)}, u32[]{:S(2)}) %collective-permute-start) | collective-permute-done | bytes 262176 | tf_op jit(solution)/shard_map/ppermute | solution.py:29
  17.3 1.7 %fusion.27 = bf16[768,128]{0,1:T(8,128)(2,1)S(1)} fusion(bf16[128,1024]{1,0:T(8,128)(2,1)} %collective-permute-done, bf16[768,1024]{1,0:T(8,128)(2,1)S(1)} %copy-done, s32[768]{0:T(1024)S(1)} %get-tuple-element.40), kind=kOutput, calls=%fused_computation.39 | convolution fusion | flops 202014720 | bytes 2034688 | tf_op jit(solution)/shard_map/dot_general | solution.py:41
  18.9 0.4 fusion.35
  19.3 0.0 collective-permute-done.1
  19.3 1.5 %collective-permute-start.2 = (bf16[128,1024]{1,0:T(8,128)(2,1)}, bf16[128,1024]{1,0:T(8,128)(2,1)S(1)}, u32[]{:S(2)}, u32[]{:S(2)}) collective-permute-start(bf16[128,1024]{1,0:T(8,128)(2,1)} %collective-permute-done.1), channel_id=1, source_target_pairs={{0,1},{1,0},{2,3},{3,2},{4,5},{5,4},{6,7},{7,6},{8,9},{9,8},{10,11... | collective-permute-start | bytes 786440 | tf_op jit(solution)/shard_map/ppermute | solution.py:29
  20.9 1.0 %constant_dynamic-update-slice_fusion.2 = bf16[512,1024]{1,0:T(8,128)(2,1)S(1)} fusion(bf16[512,1024]{1,0:T(8,128)(2,1)S(1)} %dynamic_update_slice.12, bf16[128,1024]{1,0:T(8,128)(2,1)} %collective-permute-done), kind=kLoop, calls=%fused_computation.64 | loop fusion | bytes 524288 | tf_op jit(solution)/shard_map/dynamic_update_slice | solution.py:64
  21.8 1.0 %constant_dynamic-update-slice_fusion.1 = bf16[512,1024]{1,0:T(8,128)(2,1)S(1)} fusion(bf16[512,1024]{1,0:T(8,128)(2,1)S(1)} %constant_dynamic-update-slice_fusion.2, bf16[128,1024]{1,0:T(8,128)(2,1)} %collective-permute-done.1), kind=kLoop, calls=%fused_computation.63 | loop fusion | bytes 524288 | tf_op jit(solution)/shard_map/dynamic_update_slice | solution.py:64
  22.8 1.6 %fusion.26 = bf16[768,128]{0,1:T(8,128)(2,1)S(1)} fusion(bf16[128,1024]{1,0:T(8,128)(2,1)} %collective-permute-done.1, bf16[768,1024]{1,0:T(8,128)(2,1)S(1)} %copy-done, s32[768]{0:T(1024)S(1)} %get-tuple-element.39), kind=kOutput, calls=%fused_computation.38 | convolution fusion | flops 202014720 | bytes 2034688 | tf_op jit(solution)/shard_map/dot_general | solution.py:41
  24.5 0.4 fusion.36
  24.9 1.7 %collective-permute-done.2 = bf16[128,1024]{1,0:T(8,128)(2,1)S(1)} collective-permute-done((bf16[128,1024]{1,0:T(8,128)(2,1)}, bf16[128,1024]{1,0:T(8,128)(2,1)S(1)}, u32[]{:S(2)}, u32[]{:S(2)}) %collective-permute-start.2) | collective-permute-done | bytes 262176 | tf_op jit(solution)/shard_map/ppermute | solution.py:29
  26.5 0.7 %fusion.25 = bf16[768,128]{0,1:T(8,128)(2,1)S(1)} fusion(bf16[128,1024]{1,0:T(8,128)(2,1)S(1)} %collective-permute-done.2, bf16[768,1024]{1,0:T(8,128)(2,1)S(1)} %copy-done, s32[768]{0:T(1024)S(1)} %get-tuple-element.38), kind=kOutput, calls=%fused_computation.37 | convolution fusion | flops 202014720 | bytes 2034688 | tf_op jit(solution)/shard_map/dot_general | solution.py:41
  27.2 0.4 fusion.37
  27.6 0.0 collective-permute-done.4
  27.6 0.1 subtract_reduce_fusion.3
  27.7 0.1 pad_maximum_fusion
  27.8 0.0 collective-permute-done.3
  27.8 1.5 %fusion = bf16[768,512]{0,1:T(8,128)(2,1)S(1)} fusion(bf16[512,1024]{1,0:T(8,128)(2,1)S(1)} %constant_dynamic-update-slice_fusion, bf16[768,1024]{1,0:T(8,128)(2,1)S(1)} %collective-permute-done.3, s32[768]{0:T(1024)S(1)} %get-tuple-element.35, s32[768]{0:T(1024)S(1)} %get-tuple-element.36, s32[768]{0:T(1024)S(1)} %get-tuple-element.37, ...), kind=kOutput, calls=%fused_computation.3 | convolution fusion | flops 809238528 | bytes 3421696 | tf_op jit(solution)/shard_map/dot_general | solution.py:41
  29.3 0.4 fusion.4
  29.7 1.8 %collective-permute-start.5 = (bf16[128,1024]{1,0:T(8,128)(2,1)S(1)}, bf16[128,1024]{1,0:T(8,128)(2,1)S(1)}, u32[]{:S(2)}, u32[]{:S(2)}) collective-permute-start(bf16[128,1024]{1,0:T(8,128)(2,1)S(1)} %fusion.4), channel_id=1, source_target_pairs={{0,1},{1,0},{2,3},{3,2},{4,5},{5,4},{6,7},{7,6},{8,9},{9,8},{10,11... | collective-permute-start | bytes 786440 | tf_op jit(solution)/shard_map/ppermute | solution.py:29
  31.5 1.0 %convolution_convert_fusion = bf16[768,1024]{1,0:T(8,128)(2,1)S(1)} fusion(bf16[768,512]{0,1:T(8,128)(2,1)S(1)} %fusion, bf16[512,1024]{1,0:T(8,128)(2,1)S(1)} %constant_dynamic-update-slice_fusion), kind=kOutput, calls=%fused_computation.1 | convolution fusion | flops 806092800 | bytes 3407872 | tf_op jit(solution)/shard_map/dot_general | solution.py:81
  32.5 0.1 collective-permute-start.8
  32.6 0.4 fusion.3
  33.0 0.3 collective-permute-start.6
  33.3 0.4 fusion.2
  33.7 3.3 %collective-permute-done.5 = bf16[128,1024]{1,0:T(8,128)(2,1)S(1)} collective-permute-done((bf16[128,1024]{1,0:T(8,128)(2,1)S(1)}, bf16[128,1024]{1,0:T(8,128)(2,1)S(1)}, u32[]{:S(2)}, u32[]{:S(2)}) %collective-permute-start.5) | collective-permute-done | bytes 262176 | tf_op jit(solution)/shard_map/ppermute | solution.py:29
  37.0 0.1 add_convert_fusion.2
  37.0 0.0 copy-start.1
  37.0 1.7 %collective-permute-start.7 = (bf16[128,1024]{1,0:T(8,128)(2,1)S(1)}, bf16[128,1024]{1,0:T(8,128)(2,1)S(1)}, u32[]{:S(2)}, u32[]{:S(2)}) collective-permute-start(bf16[128,1024]{1,0:T(8,128)(2,1)S(1)} %add_convert_fusion.2), channel_id=1, source_target_pairs={{0,2},{1,3},{2,0},{3,1},{4,6},{5,7},{6,4},{7,5},{8,10},{9,11},{10,... | collective-permute-start | bytes 786440 | tf_op jit(solution)/shard_map/ppermute | solution.py:29
  38.7 1.0 %fusion.38 = f32[768,1024]{1,0:T(8,128)S(1)} fusion(bf16[768,512]{0,1:T(8,128)(2,1)S(1)} %pad_maximum_fusion, bf16[512,1024]{1,0:T(8,128)(2,1)S(1)} %constant_dynamic-update-slice_fusion), kind=kOutput, calls=%fused_computation.72 | convolution fusion | flops 805306368 | bytes 4980736 | tf_op jit(solution)/shard_map/dot_general | solution.py:99
  39.7 0.0 copy-done.1
  39.7 0.4 fusion.1
  40.1 6.9 %collective-permute-done.6 = bf16[128,1024]{1,0:T(8,128)(2,1)S(1)} collective-permute-done((bf16[128,1024]{1,0:T(8,128)(2,1)S(1)}, bf16[128,1024]{1,0:T(8,128)(2,1)S(1)}, u32[]{:S(2)}, u32[]{:S(2)}) %collective-permute-start.6) | collective-permute-done | bytes 262176 | tf_op jit(solution)/shard_map/ppermute | solution.py:29
  47.1 2.9 %collective-permute-done.7 = bf16[128,1024]{1,0:T(8,128)(2,1)S(1)} collective-permute-done((bf16[128,1024]{1,0:T(8,128)(2,1)S(1)}, bf16[128,1024]{1,0:T(8,128)(2,1)S(1)}, u32[]{:S(2)}, u32[]{:S(2)}) %collective-permute-start.7) | collective-permute-done | bytes 262176 | tf_op jit(solution)/shard_map/ppermute | solution.py:29
  50.0 0.8 %add_convert_fusion.1 = bf16[128,1024]{1,0:T(8,128)(2,1)} fusion(bf16[128,1024]{1,0:T(8,128)(2,1)S(1)} %collective-permute-done.7, f32[128,1024]{1,0:T(8,128)S(1)} %fusion.1, bf16[128,1024]{1,0:T(8,128)(2,1)S(1)} %collective-permute-done.6), kind=kLoop, calls=%fused_computation.42 | loop fusion | flops 655360 | bytes 1310720 | tf_op jit(solution)/shard_map/convert_element_type | solution.py:109
  50.8 1.6 %collective-permute-done.8 = bf16[768,1024]{1,0:T(8,128)(2,1)S(1)} collective-permute-done((bf16[768,1024]{1,0:T(8,128)(2,1)S(1)}, bf16[768,1024]{1,0:T(8,128)(2,1)S(1)}, u32[]{:S(2)}, u32[]{:S(2)}) %collective-permute-start.8) | collective-permute-done | bytes 1572896 | tf_op jit(solution)/shard_map/ppermute | solution.py:32
  52.4 1.8 %add_convert_fusion = bf16[768,1024]{1,0:T(8,128)(2,1)} fusion(f32[768,1024]{1,0:T(8,128)S(1)} %fusion.38, bf16[768,1024]{1,0:T(8,128)(2,1)S(1)} %collective-permute-done.8), kind=kLoop, calls=%fused_computation | loop fusion | flops 2359296 | bytes 6291456 | tf_op jit(solution)/shard_map/convert_element_type | solution.py:111
  (4 shorter events, 0.1 us)
Async XLA Ops:
  0.6 18.7 %collective-permute-start.1 = (bf16[128,1024]{1,0:T(8,128)(2,1)}, bf16[128,1024]{1,0:T(8,128)(2,1)}, u32[]{:S(2)}, u32[]{:S(2)}) collective-permute-start(bf16[128,1024]{1,0:T(8,128)(2,1)} %param.5), channel_id=1, source_target_pairs={{0,2},{1,3},{2,0},{3,1},{4,6},{5,7},{6,4},{7,5},{8,10},{9,11},{10,... | collective-permute-start | bytes 786440 | tf_op jit(solution)/shard_map/ppermute | solution.py:29
  4.7 12.5 %collective-permute-start = (bf16[128,1024]{1,0:T(8,128)(2,1)}, bf16[128,1024]{1,0:T(8,128)(2,1)}, u32[]{:S(2)}, u32[]{:S(2)}) collective-permute-start(bf16[128,1024]{1,0:T(8,128)(2,1)} %param.5), channel_id=1, source_target_pairs={{0,1},{1,0},{2,3},{3,2},{4,5},{5,4},{6,7},{7,6},{8,9},{9,8},{10,11... | collective-permute-start | bytes 786440 | tf_op jit(solution)/shard_map/ppermute | solution.py:29
  6.3 21.5 %collective-permute-start.3 = (bf16[768,1024]{1,0:T(8,128)(2,1)}, bf16[768,1024]{1,0:T(8,128)(2,1)S(1)}, u32[]{:S(2)}, u32[]{:S(2)}) collective-permute-start(bf16[768,1024]{1,0:T(8,128)(2,1)} %param.4), channel_id=1, source_target_pairs={{0,12},{4,0},{8,4},{12,8},{1,13},{5,1},{9,5},{13,9},{2,14},{6,2},{... | collective-permute-start | bytes 4718600 | tf_op jit(solution)/shard_map/ppermute | solution.py:32
  7.5 2.3 %copy-start = (bf16[768,1024]{1,0:T(8,128)(2,1)S(1)}, bf16[768,1024]{1,0:T(8,128)(2,1)}, u32[]{:S(2)}) copy-start(bf16[768,1024]{1,0:T(8,128)(2,1)} %param.4) | copy-start | bytes 4718596
  11.0 16.6 %collective-permute-start.4 = (s32[768,8]{0,1:T(8,128)S(1)}, s32[768,8]{0,1:T(8,128)S(1)}, u32[]{:S(2)}, u32[]{:S(2)}) collective-permute-start(s32[768,8]{0,1:T(8,128)S(1)} %fusion.33), channel_id=1, source_target_pairs={{0,12},{4,0},{8,4},{12,8},{1,13},{5,1},{9,5},{13,9},{2,14},{6,2},{... | collective-permute-start | bytes 73736 | tf_op jit(solution)/shard_map/ppermute | solution.py:32
  19.3 7.2 %collective-permute-start.2 = (bf16[128,1024]{1,0:T(8,128)(2,1)}, bf16[128,1024]{1,0:T(8,128)(2,1)S(1)}, u32[]{:S(2)}, u32[]{:S(2)}) collective-permute-start(bf16[128,1024]{1,0:T(8,128)(2,1)} %collective-permute-done.1), channel_id=1, source_target_pairs={{0,1},{1,0},{2,3},{3,2},{4,5},{5,4},{6,7},{7,6},{8,9},{9,8},{10,11... | collective-permute-start | bytes 786440 | tf_op jit(solution)/shard_map/ppermute | solution.py:29
  29.7 7.3 %collective-permute-start.5 = (bf16[128,1024]{1,0:T(8,128)(2,1)S(1)}, bf16[128,1024]{1,0:T(8,128)(2,1)S(1)}, u32[]{:S(2)}, u32[]{:S(2)}) collective-permute-start(bf16[128,1024]{1,0:T(8,128)(2,1)S(1)} %fusion.4), channel_id=1, source_target_pairs={{0,1},{1,0},{2,3},{3,2},{4,5},{5,4},{6,7},{7,6},{8,9},{9,8},{10,11... | collective-permute-start | bytes 786440 | tf_op jit(solution)/shard_map/ppermute | solution.py:29
  32.5 19.9 %collective-permute-start.8 = (bf16[768,1024]{1,0:T(8,128)(2,1)S(1)}, bf16[768,1024]{1,0:T(8,128)(2,1)S(1)}, u32[]{:S(2)}, u32[]{:S(2)}) collective-permute-start(bf16[768,1024]{1,0:T(8,128)(2,1)S(1)} %convolution_convert_fusion), channel_id=1, source_target_pairs={{0,4},{4,8},{8,12},{12,0},{1,5},{5,9},{9,13},{13,1},{2,6},{6,10},{... | collective-permute-start | bytes 4718600 | tf_op jit(solution)/shard_map/ppermute | solution.py:32
  33.0 14.1 %collective-permute-start.6 = (bf16[128,1024]{1,0:T(8,128)(2,1)S(1)}, bf16[128,1024]{1,0:T(8,128)(2,1)S(1)}, u32[]{:S(2)}, u32[]{:S(2)}) collective-permute-start(bf16[128,1024]{1,0:T(8,128)(2,1)S(1)} %fusion.3), channel_id=1, source_target_pairs={{0,1},{1,0},{2,3},{3,2},{4,5},{5,4},{6,7},{7,6},{8,9},{9,8},{10,11... | collective-permute-start | bytes 786440 | tf_op jit(solution)/shard_map/ppermute | solution.py:29
  37.0 2.7 %copy-start.1 = (f32[128,1024]{1,0:T(8,128)S(1)}, f32[128,1024]{1,0:T(8,128)}, u32[]{:S(2)}) copy-start(f32[128,1024]{1,0:T(8,128)} %fusion.34) | copy-start | bytes 1572868
  37.0 13.0 %collective-permute-start.7 = (bf16[128,1024]{1,0:T(8,128)(2,1)S(1)}, bf16[128,1024]{1,0:T(8,128)(2,1)S(1)}, u32[]{:S(2)}, u32[]{:S(2)}) collective-permute-start(bf16[128,1024]{1,0:T(8,128)(2,1)S(1)} %add_convert_fusion.2), channel_id=1, source_target_pairs={{0,2},{1,3},{2,0},{3,1},{4,6},{5,7},{6,4},{7,5},{8,10},{9,11},{10,... | collective-permute-start | bytes 786440 | tf_op jit(solution)/shard_map/ppermute | solution.py:29

commit v16 on v15

--- a/solution.py
+++ b/solution.py
@@ -53,26 +53,42 @@
     for k in range(1, n_dp):
         step = k & -k
         pieces[k] = to_dp(pieces[k ^ step], step)
-    next_rows = to_label(embeds, -1)
     d_own, g_w = {}, {}
     joined = [jnp.zeros((stretch, width), weights.dtype)]
+    next_rows = to_label(embeds, -1)
 
-    def own_step(k):
-        pieces[k] = in_turn(pieces[k])
-        d_own[k] = delta_of(embeds, ids, pieces[k], [k])
-        g_w[k] = grad_w_of(d_own[k], embeds)
-        joined[0] = lax.dynamic_update_slice_in_dim(joined[0], pieces[k], k * ch_dev, axis=0)
+    def join(piece, at):
+        joined[0] = lax.dynamic_update_slice_in_dim(joined[0], piece, at, axis=0)
+
+    def own_delta(k, piece):
+        d_own[k] = delta_of(embeds, ids, in_turn(piece), [k])
+        last[0] = d_own[k]
+
+    def own_grad(k):
+        g_w[k] = grad_w_of(in_turn(d_own[k]), embeds)
         last[0] = g_w[k]
+
+    def piece_of(k):
+        whole = joined[0] if isinstance(joined, list) else joined
+        return whole[k * ch_dev:(k + 1) * ch_dev]
 
     def add_next(k):
         delta = in_turn(d_next)[:, k * ch_dev:(k + 1) * ch_dev]
         g_w[k] = (g_w[k] + grad_w_of(delta, next_rows)) * scale
         last[0] = g_w[k]
 
-    own_step(0)
-    next_ids = to_label(in_turn(ids), -1)
+    next_ids = to_label(ids, -1)
+    join(weights, 0)
+    for k in range(2, n_dp):
+        if k & -k == k:
+            pieces[k] = in_turn(pieces[k])
+            last[0] = pieces[k]
     for k in range(1, n_dp):
-        own_step(k)
+        join(in_turn(pieces[k]), k * ch_dev)
+    joined = [in_turn(joined[0])]
+    last[0] = joined[0]
+    own_delta(late, piece_of(late))
+    own_grad(late)
     joined = joined[0]
     next_ids = in_turn(next_ids)
     d_next = delta_of(next_rows, next_ids, joined, list(range(n_dp)))
@@ -81,21 +97,33 @@
     theirs = jnp.dot(in_turn(d_next), joined, preferred_element_type=jnp.float32).astype(jnp.bfloat16)
     last[0] = theirs
     back = to_label(theirs, 1)
+    second = in_turn(g_w[late])
     for k in range(1, late):
+        own_delta(k, piece_of(k))
+        own_grad(k)
         add_next(k)
 
-    relayed, moved = {}, []
-    for k in range(late, 0, -1):
-        step = k & -k
-        for term in relayed.get(k, ()):
-            g_w[k] = g_w[k] + term.astype(jnp.float32)
-        part = g_w[k].astype(jnp.bfloat16)
-        if k in relayed:
-            last[0] = part
-        if step == k:
-            moved.append(to_dp(part, k))
-        else:
-            relayed.setdefault(k ^ step, []).append(in_turn(to_dp(part, step)))
+    relayed, moved = {}, {}
+    moved[1] = to_dp(g_w[1].astype(jnp.bfloat16), 1)
+    for h, rows in enumerate((slice(0, ch_dev // 2), slice(ch_dev // 2, ch_dev))):
+        for k in range(late, 1, -1):
+            step = k & -k
+            part = (second if (k, h) == (late, 1) else g_w[k])[rows]
+            for term in relayed.get((k, h), ()):
+                part = part + in_turn(term).astype(jnp.float32)
+            part = part.astype(jnp.bfloat16)
+            if (k, h) in relayed:
+                last[0] = part
+            if step == k:
+                moved[k, h] = to_dp(part, k)
+            else:
+                relayed.setdefault((k ^ step, h), []).append(to_dp(part, step))
+    for k in range(2, n_dp):
+        if (k, 0) in moved:
+            moved[k, 0] = in_turn(moved[k, 0])
+            last[0] = moved[k, 0]
+    own_delta(0, piece_of(0))
+    own_grad(0)
     grad_x = jnp.dot(
         in_turn(jnp.concatenate([d_own[k] for k in range(n_dp)], axis=1)),
         joined,
@@ -103,9 +131,11 @@
     )
     last[0] = grad_x
     add_next(0)
-    grad_w = g_w[0]
-    for term in reversed(moved):
-        grad_w = grad_w + in_turn(term).astype(jnp.float32)
+    grad_w = g_w[0] + in_turn(moved[1]).astype(jnp.float32)
+    for k in range(2, n_dp):
+        if (k, 0) in moved:
+            whole = jnp.concatenate([moved[k, 0], in_turn(moved[k, 1])], axis=0)
+            grad_w = grad_w + whole.astype(jnp.float32)
     grad_w = grad_w.astype(jnp.bfloat16)
     last[0] = grad_w
     grad_x = (grad_x + in_turn(back).astype(jnp.float32)).astype(jnp.bfloat16)

time: 54.5 us -> 52.7 us (0.967)
  matrix products: 13.7 us -> 9.41 us
  starting transfers between devices: 12.7 us -> 16.8 us
  local copies, waits for them, and re-layouts: 3.03 us -> 1.22 us
    dot_general x5, matrix products: 7.82 us -> 4.31 us  [delta_of(): lax.dot_general(rows, piece, (((1,), (1,)), ((), ())), preferred_element_...]
    ppermute x6 -> x8, starting transfers between devices: 11 us -> 14.3 us  [to_dp(): return lax.ppermute(x, 'dp', [(i, i ^ k) for i in range(n_dp)])]
    dynamic_update_slice x4, local copies, waits for them, and re-layouts: 3.02 us -> 1.12 us  [join(): joined[0] = lax.dynamic_update_slice_in_dim(joined[0], piece, at, axis=0)]
    ppermute x3, waiting for transfers between devices: 1.63 us -> 0.01 us  [to_label(): lax.ppermute(x, 'label', [(i, (i + by) % n_label) for i in range(n_label)])]
    ppermute x6 -> x8, waiting for transfers between devices: 18.7 us -> 20.3 us  [to_dp(): return lax.ppermute(x, 'dp', [(i, i ^ k) for i in range(n_dp)])]
    ppermute x3, starting transfers between devices: 1.67 us -> 2.51 us  [to_label(): lax.ppermute(x, 'label', [(i, (i + by) % n_label) for i in range(n_label)])]
    dot_general x8, matrix products: 3.86 us -> 3.06 us  [grad_w_of(): lax.dot_general(delta, rows, (((0,), (0,)), ((), ())), preferred_element_...]
  transfers between devices with their start and end apart: 9 -> 11, of which waited for: 6 -> 6; matrix products, arithmetic and copies ran while one was open for 31% -> 18% of each run, Pallas kernels for 0% -> 0%
where the time goes in v16:
time: 52.7 us; the launch traced here: 52.1 us
  waiting for transfers between devices  20.3 us (39%)
  starting transfers between devices  16.8 us (32%)
  matrix products  9.41 us (18%)
  other arithmetic  3.53 us (7%)
  local copies, waits for them, and re-layouts  1.22 us (2%)
  between operations  0.87 us (2%)
    ppermute x8, waiting for transfers between devices, to_dp(): return lax.ppermute(x, 'dp', [(i, i ^ k) for i in range(n_dp)])  20.3 us
    ppermute x8, starting transfers between devices, to_dp(): return lax.ppermute(x, 'dp', [(i, i ^ k) for i in range(n_dp)])  14.3 us
    dot_general x5, matrix products, delta_of(): lax.dot_general(rows, piece, (((1,), (1,)), ((), ())), preferred_element_...  4.31 us
    dot_general x8, matrix products, grad_w_of(): lax.dot_general(delta, rows, (((0,), (0,)), ((), ())), preferred_element_...  3.06 us
    ppermute x3, starting transfers between devices, to_label(): lax.ppermute(x, 'label', [(i, (i + by) % n_label) for i in range(n_label)])  2.51 us
    convert_element_type x1, other arithmetic, local(): grad_x = (grad_x + in_turn(back).astype(jnp.float32)).astype(jnp.bfloat16)  1.75 us
    dynamic_update_slice x4, local copies, waits for them, and re-layouts, join(): joined[0] = lax.dynamic_update_slice_in_dim(joined[0], piece, at, axis=0)  1.12 us
  transfers between devices with their start and end apart: 11, of which 6 were waited for; matrix products, arithmetic and copies ran while one was open for 18% of the time, Pallas kernels for 0%

profile of v16, /device:TPU:0, one launch (start us, length us, event | category | flops | bytes accessed | tf_op | source)
XLA Modules:
  0.0 52.1 jit_solution(16776901024229658939)
XLA Ops:
  0.6 4.1 %collective-permute-start.1 = (bf16[128,1024]{1,0:T(8,128)(2,1)}, bf16[128,1024]{1,0:T(8,128)(2,1)S(1)}, u32[]{:S(2)}, u32[]{:S(2)}) collective-permute-start(bf16[128,1024]{1,0:T(8,128)(2,1)} %param.5), channel_id=1, source_target_pairs={{0,2},{1,3},{2,0},{3,1},{4,6},{5,7},{6,4},{7,5},{8,10},{9,11},{10,... | collective-permute-start | bytes 786440 | tf_op jit(solution)/shard_map/ppermute | solution.py:29
  4.7 1.6 %collective-permute-start = (bf16[128,1024]{1,0:T(8,128)(2,1)}, bf16[128,1024]{1,0:T(8,128)(2,1)S(1)}, u32[]{:S(2)}, u32[]{:S(2)}) collective-permute-start(bf16[128,1024]{1,0:T(8,128)(2,1)} %param.5), channel_id=1, source_target_pairs={{0,1},{1,0},{2,3},{3,2},{4,5},{5,4},{6,7},{7,6},{8,9},{9,8},{10,11... | collective-permute-start | bytes 786440 | tf_op jit(solution)/shard_map/ppermute | solution.py:29
  6.3 0.4 collective-permute-start.3
  6.7 0.7 %fusion.35 = s32[768,8]{0,1:T(8,128)S(1)} fusion(s32[768,8]{0,1:T(8,128)} %param.6, s32[768]{0:T(1024)} %param.7), kind=kLoop, calls=%fused_computation.58 | loop fusion | flops 12288 | bytes 52224 | tf_op jit(solution)/shard_map/jit(_where)/select_n | solution.py:21
  7.4 1.2 %collective-permute-start.4 = (s32[768,8]{0,1:T(8,128)S(1)}, s32[768,8]{0,1:T(8,128)S(1)}, u32[]{:S(2)}, u32[]{:S(2)}) collective-permute-start(s32[768,8]{0,1:T(8,128)S(1)} %fusion.35), channel_id=1, source_target_pairs={{0,12},{4,0},{8,4},{12,8},{1,13},{5,1},{9,5},{13,9},{2,14},{6,2},{... | collective-permute-start | bytes 73736 | tf_op jit(solution)/shard_map/ppermute | solution.py:32
  8.7 8.3 %collective-permute-done.1 = bf16[128,1024]{1,0:T(8,128)(2,1)S(1)} collective-permute-done((bf16[128,1024]{1,0:T(8,128)(2,1)}, bf16[128,1024]{1,0:T(8,128)(2,1)S(1)}, u32[]{:S(2)}, u32[]{:S(2)}) %collective-permute-start.1) | collective-permute-done | bytes 262176 | tf_op jit(solution)/shard_map/ppermute | solution.py:29
  17.0 0.7 %collective-permute-start.2 = (bf16[128,1024]{1,0:T(8,128)(2,1)S(1)}, bf16[128,1024]{1,0:T(8,128)(2,1)S(1)}, u32[]{:S(2)}, u32[]{:S(2)}) collective-permute-start(bf16[128,1024]{1,0:T(8,128)(2,1)S(1)} %collective-permute-done.1), channel_id=1, source_target_pairs={{0,1},{1,0},{2,3},{3,2},{4,5},{5,4},{6,7},{7,6},{8,9},{9,8},{10,11... | collective-permute-start | bytes 786440 | tf_op jit(solution)/shard_map/ppermute | solution.py:29
  17.7 1.1 %dynamic_update_slice.12 = bf16[512,1024]{1,0:T(8,128)(2,1)S(1)} pad(bf16[128,1024]{1,0:T(8,128)(2,1)} %param.5, bf16[]{:T(256)} %constant.65.clone.1), padding=0_384x0_0 | pad | bytes 1310722 | tf_op jit(solution)/shard_map/dynamic_update_slice | solution.py:61
  18.8 0.0 collective-permute-done
  18.9 0.0 copy-start
  18.9 5.5 %collective-permute-done.2 = bf16[128,1024]{1,0:T(8,128)(2,1)S(1)} collective-permute-done((bf16[128,1024]{1,0:T(8,128)(2,1)S(1)}, bf16[128,1024]{1,0:T(8,128)(2,1)S(1)}, u32[]{:S(2)}, u32[]{:S(2)}) %collective-permute-start.2) | collective-permute-done | bytes 262176 | tf_op jit(solution)/shard_map/ppermute | solution.py:29
  24.4 0.1 fusion.36
  24.5 0.0 copy-done
  24.5 0.7 %fusion.28 = bf16[768,128]{0,1:T(8,128)(2,1)S(1)} fusion(bf16[128,1024]{1,0:T(8,128)(2,1)S(1)} %get-tuple-element.34, bf16[768,1024]{1,0:T(8,128)(2,1)S(1)} %copy-done, s32[768]{0:T(1024)S(1)} %get-tuple-element.59), kind=kOutput, calls=%fused_computation.40 | convolution fusion | flops 202014720 | bytes 2034688 | tf_op jit(solution)/shard_map/dot_general | solution.py:41
  25.2 0.4 fusion.37
  25.6 0.0 collective-permute-done.4
  25.6 0.1 subtract_reduce_fusion.6
  25.7 0.0 collective-permute-done.3
  25.7 1.5 %fusion = bf16[768,512]{0,1:T(8,128)(2,1)S(1)} fusion(bf16[512,1024]{1,0:T(8,128)(2,1)S(1)} %constant_dynamic-update-slice_fusion, bf16[768,1024]{1,0:T(8,128)(2,1)S(1)} %collective-permute-done.3, s32[768]{0:T(1024)S(1)} %get-tuple-element.61, s32[768]{0:T(1024)S(1)} %get-tuple-element.62, s32[768]{0:T(1024)S(1)} %get-tuple-element.63, ...), kind=kOutput, calls=%fused_computation.3 | convolution fusion | flops 809238528 | bytes 3421696 | tf_op jit(solution)/shard_map/dot_general | solution.py:41
  27.2 0.4 fusion.4
  27.6 1.0 %convolution_convert_fusion = bf16[768,1024]{1,0:T(8,128)(2,1)S(1)} fusion(bf16[768,512]{0,1:T(8,128)(2,1)S(1)} %fusion, bf16[512,1024]{1,0:T(8,128)(2,1)S(1)} %constant_dynamic-update-slice_fusion), kind=kOutput, calls=%fused_computation.1 | convolution fusion | flops 806092800 | bytes 3407872 | tf_op jit(solution)/shard_map/dot_general | solution.py:97
  28.6 0.9 %collective-permute-start.10 = (bf16[768,1024]{1,0:T(8,128)(2,1)S(1)}, bf16[768,1024]{1,0:T(8,128)(2,1)S(1)}, u32[]{:S(2)}, u32[]{:S(2)}) collective-permute-start(bf16[768,1024]{1,0:T(8,128)(2,1)S(1)} %convolution_convert_fusion), channel_id=1, source_target_pairs={{0,4},{4,8},{8,12},{12,0},{1,5},{5,9},{9,13},{13,1},{2,6},{6,10},{... | collective-permute-start | bytes 4718600 | tf_op jit(solution)/shard_map/ppermute | solution.py:32
  29.5 0.7 %collective-permute-start.5 = (bf16[64,1024]{1,0:T(8,128)(2,1)S(1)}, bf16[64,1024]{1,0:T(8,128)(2,1)S(1)}, u32[]{:S(2)}, u32[]{:S(2)}) collective-permute-start(bf16[64,1024]{1,0:T(8,128)(2,1)S(1)} %slice.71), channel_id=1, source_target_pairs={{0,1},{1,0},{2,3},{3,2},{4,5},{5,4},{6,7},{7,6},{8,9},{9,8},{10,11... | collective-permute-start | bytes 393224 | tf_op jit(solution)/shard_map/ppermute | solution.py:29
  30.3 0.7 %fusion.27 = bf16[768,128]{0,1:T(8,128)(2,1)S(1)} fusion(bf16[128,1024]{1,0:T(8,128)(2,1)S(1)} %get-tuple-element.39, bf16[768,1024]{1,0:T(8,128)(2,1)S(1)} %copy-done, s32[768]{0:T(1024)S(1)} %get-tuple-element.58), kind=kOutput, calls=%fused_computation.39 | convolution fusion | flops 202014720 | bytes 2034688 | tf_op jit(solution)/shard_map/dot_general | solution.py:41
  31.0 1.4 %collective-permute-start.7 = (bf16[64,1024]{1,0:T(8,128)(2,1)S(1)}, bf16[64,1024]{1,0:T(8,128)(2,1)S(1)}, u32[]{:S(2)}, u32[]{:S(2)}) collective-permute-start(bf16[64,1024]{1,0:T(8,128)(2,1)S(1)} %slice.70), channel_id=1, source_target_pairs={{0,1},{1,0},{2,3},{3,2},{4,5},{5,4},{6,7},{7,6},{8,9},{9,8},{10,11... | collective-permute-start | bytes 393224 | tf_op jit(solution)/shard_map/ppermute | solution.py:29
  32.4 0.4 fusion.38
  32.7 0.4 fusion.3
  33.1 0.8 %collective-permute-start.8 = (bf16[128,1024]{1,0:T(8,128)(2,1)S(1)}, bf16[128,1024]{1,0:T(8,128)(2,1)S(1)}, u32[]{:S(2)}, u32[]{:S(2)}) collective-permute-start(bf16[128,1024]{1,0:T(8,128)(2,1)S(1)} %fusion.3), channel_id=1, source_target_pairs={{0,1},{1,0},{2,3},{3,2},{4,5},{5,4},{6,7},{7,6},{8,9},{9,8},{10,11... | collective-permute-start | bytes 786440 | tf_op jit(solution)/shard_map/ppermute | solution.py:29
  33.9 0.7 %fusion.26 = bf16[768,128]{0,1:T(8,128)(2,1)S(1)} fusion(bf16[128,1024]{1,0:T(8,128)(2,1)S(1)} %get-tuple-element.42, bf16[768,1024]{1,0:T(8,128)(2,1)S(1)} %copy-done, s32[768]{0:T(1024)S(1)} %get-tuple-element.57), kind=kOutput, calls=%fused_computation.38 | convolution fusion | flops 202014720 | bytes 2034688 | tf_op jit(solution)/shard_map/dot_general | solution.py:41
  34.6 0.4 fusion.39
  35.0 0.4 fusion.2
  35.4 0.4 collective-permute-done.5
  35.9 3.0 %collective-permute-start.6 = (bf16[64,1024]{1,0:T(8,128)(2,1)S(1)}, bf16[64,1024]{1,0:T(8,128)(2,1)S(1)}, u32[]{:S(2)}, u32[]{:S(2)}) collective-permute-start(bf16[64,1024]{1,0:T(8,128)(2,1)S(1)} %fusion.30), channel_id=1, source_target_pairs={{0,2},{1,3},{2,0},{3,1},{4,6},{5,7},{6,4},{7,5},{8,10},{9,11},{10,... | collective-permute-start | bytes 393224 | tf_op jit(solution)/shard_map/ppermute | solution.py:29
  38.8 0.0 collective-permute-done.7
  38.9 2.0 %collective-permute-start.9 = (bf16[64,1024]{1,0:T(8,128)(2,1)S(1)}, bf16[64,1024]{1,0:T(8,128)(2,1)S(1)}, u32[]{:S(2)}, u32[]{:S(2)}) collective-permute-start(bf16[64,1024]{1,0:T(8,128)(2,1)S(1)} %fusion.29), channel_id=1, source_target_pairs={{0,2},{1,3},{2,0},{3,1},{4,6},{5,7},{6,4},{7,5},{8,10},{9,11},{10,... | collective-permute-start | bytes 393224 | tf_op jit(solution)/shard_map/ppermute | solution.py:29
  40.9 4.0 %collective-permute-done.6 = bf16[64,1024]{1,0:T(8,128)(2,1)S(1)} collective-permute-done((bf16[64,1024]{1,0:T(8,128)(2,1)S(1)}, bf16[64,1024]{1,0:T(8,128)(2,1)S(1)}, u32[]{:S(2)}, u32[]{:S(2)}) %collective-permute-start.6) | collective-permute-done | bytes 131104 | tf_op jit(solution)/shard_map/ppermute | solution.py:29
  44.9 0.7 %fusion.25 = bf16[768,128]{0,1:T(8,128)(2,1)S(1)} fusion(bf16[128,1024]{1,0:T(8,128)(2,1)S(1)} %get-tuple-element.49, bf16[768,1024]{1,0:T(8,128)(2,1)S(1)} %copy-done, s32[768]{0:T(1024)S(1)} %get-tuple-element.56), kind=kOutput, calls=%fused_computation.37 | convolution fusion | flops 202014720 | bytes 2034688 | tf_op jit(solution)/shard_map/dot_general | solution.py:41
  45.6 0.1 pad_maximum_fusion
  45.7 0.4 fusion.40
  46.1 1.0 %fusion.41 = f32[768,1024]{1,0:T(8,128)S(1)} fusion(bf16[768,512]{0,1:T(8,128)(2,1)S(1)} %pad_maximum_fusion, bf16[512,1024]{1,0:T(8,128)(2,1)S(1)} %constant_dynamic-update-slice_fusion), kind=kOutput, calls=%fused_computation.78 | convolution fusion | flops 805306368 | bytes 4980736 | tf_op jit(solution)/shard_map/dot_general | solution.py:127
  47.1 0.4 fusion.1
  47.5 0.2 collective-permute-done.9
  47.7 1.8 %collective-permute-done.8 = bf16[128,1024]{1,0:T(8,128)(2,1)S(1)} collective-permute-done((bf16[128,1024]{1,0:T(8,128)(2,1)S(1)}, bf16[128,1024]{1,0:T(8,128)(2,1)S(1)}, u32[]{:S(2)}, u32[]{:S(2)}) %collective-permute-start.8) | collective-permute-done | bytes 262176 | tf_op jit(solution)/shard_map/ppermute | solution.py:29
  49.5 0.8 %add_convert_fusion.1 = bf16[128,1024]{1,0:T(8,128)(2,1)} fusion(f32[128,1024]{1,0:T(8,128)S(1)} %fusion.1, bf16[128,1024]{1,0:T(8,128)(2,1)S(1)} %collective-permute-done.8, bf16[64,1024]{1,0:T(8,128)(2,1)S(1)} %collective-permute-done.9, bf16[64,1024]{1,0:T(8,128)(2,1)S(1)} %collective-permute-done.6), kind=kLoop, calls=%fused_computation.42 | loop fusion | flops 1048576 | bytes 1310720 | tf_op jit(solution)/shard_map/convert_element_type | solution.py:139
  50.3 0.0 collective-permute-done.10
  50.3 1.8 %add_convert_fusion = bf16[768,1024]{1,0:T(8,128)(2,1)} fusion(f32[768,1024]{1,0:T(8,128)S(1)} %fusion.41, bf16[768,1024]{1,0:T(8,128)(2,1)S(1)} %collective-permute-done.10), kind=kLoop, calls=%fused_computation | loop fusion | flops 2359296 | bytes 6291456 | tf_op jit(solution)/shard_map/convert_element_type | solution.py:141
  (10 shorter events, 0.2 us)
Async XLA Ops:
  0.6 16.3 %collective-permute-start.1 = (bf16[128,1024]{1,0:T(8,128)(2,1)}, bf16[128,1024]{1,0:T(8,128)(2,1)S(1)}, u32[]{:S(2)}, u32[]{:S(2)}) collective-permute-start(bf16[128,1024]{1,0:T(8,128)(2,1)} %param.5), channel_id=1, source_target_pairs={{0,2},{1,3},{2,0},{3,1},{4,6},{5,7},{6,4},{7,5},{8,10},{9,11},{10,... | collective-permute-start | bytes 786440 | tf_op jit(solution)/shard_map/ppermute | solution.py:29
  4.7 14.1 %collective-permute-start = (bf16[128,1024]{1,0:T(8,128)(2,1)}, bf16[128,1024]{1,0:T(8,128)(2,1)S(1)}, u32[]{:S(2)}, u32[]{:S(2)}) collective-permute-start(bf16[128,1024]{1,0:T(8,128)(2,1)} %param.5), channel_id=1, source_target_pairs={{0,1},{1,0},{2,3},{3,2},{4,5},{5,4},{6,7},{7,6},{8,9},{9,8},{10,11... | collective-permute-start | bytes 786440 | tf_op jit(solution)/shard_map/ppermute | solution.py:29
  6.3 19.4 %collective-permute-start.3 = (bf16[768,1024]{1,0:T(8,128)(2,1)}, bf16[768,1024]{1,0:T(8,128)(2,1)S(1)}, u32[]{:S(2)}, u32[]{:S(2)}) collective-permute-start(bf16[768,1024]{1,0:T(8,128)(2,1)} %param.4), channel_id=1, source_target_pairs={{0,12},{4,0},{8,4},{12,8},{1,13},{5,1},{9,5},{13,9},{2,14},{6,2},{... | collective-permute-start | bytes 4718600 | tf_op jit(solution)/shard_map/ppermute | solution.py:32
  7.4 18.2 %collective-permute-start.4 = (s32[768,8]{0,1:T(8,128)S(1)}, s32[768,8]{0,1:T(8,128)S(1)}, u32[]{:S(2)}, u32[]{:S(2)}) collective-permute-start(s32[768,8]{0,1:T(8,128)S(1)} %fusion.35), channel_id=1, source_target_pairs={{0,12},{4,0},{8,4},{12,8},{1,13},{5,1},{9,5},{13,9},{2,14},{6,2},{... | collective-permute-start | bytes 73736 | tf_op jit(solution)/shard_map/ppermute | solution.py:32
  17.0 7.4 %collective-permute-start.2 = (bf16[128,1024]{1,0:T(8,128)(2,1)S(1)}, bf16[128,1024]{1,0:T(8,128)(2,1)S(1)}, u32[]{:S(2)}, u32[]{:S(2)}) collective-permute-start(bf16[128,1024]{1,0:T(8,128)(2,1)S(1)} %collective-permute-done.1), channel_id=1, source_target_pairs={{0,1},{1,0},{2,3},{3,2},{4,5},{5,4},{6,7},{7,6},{8,9},{9,8},{10,11... | collective-permute-start | bytes 786440 | tf_op jit(solution)/shard_map/ppermute | solution.py:29
  18.9 5.6 %copy-start = (bf16[768,1024]{1,0:T(8,128)(2,1)S(1)}, bf16[768,1024]{1,0:T(8,128)(2,1)}, u32[]{:S(2)}) copy-start(bf16[768,1024]{1,0:T(8,128)(2,1)} %param.4) | copy-start | bytes 4718596
  28.6 21.7 %collective-permute-start.10 = (bf16[768,1024]{1,0:T(8,128)(2,1)S(1)}, bf16[768,1024]{1,0:T(8,128)(2,1)S(1)}, u32[]{:S(2)}, u32[]{:S(2)}) collective-permute-start(bf16[768,1024]{1,0:T(8,128)(2,1)S(1)} %convolution_convert_fusion), channel_id=1, source_target_pairs={{0,4},{4,8},{8,12},{12,0},{1,5},{5,9},{9,13},{13,1},{2,6},{6,10},{... | collective-permute-start | bytes 4718600 | tf_op jit(solution)/shard_map/ppermute | solution.py:32
  29.5 6.3 %collective-permute-start.5 = (bf16[64,1024]{1,0:T(8,128)(2,1)S(1)}, bf16[64,1024]{1,0:T(8,128)(2,1)S(1)}, u32[]{:S(2)}, u32[]{:S(2)}) collective-permute-start(bf16[64,1024]{1,0:T(8,128)(2,1)S(1)} %slice.71), channel_id=1, source_target_pairs={{0,1},{1,0},{2,3},{3,2},{4,5},{5,4},{6,7},{7,6},{8,9},{9,8},{10,11... | collective-permute-start | bytes 393224 | tf_op jit(solution)/shard_map/ppermute | solution.py:29
  31.0 7.8 %collective-permute-start.7 = (bf16[64,1024]{1,0:T(8,128)(2,1)S(1)}, bf16[64,1024]{1,0:T(8,128)(2,1)S(1)}, u32[]{:S(2)}, u32[]{:S(2)}) collective-permute-start(bf16[64,1024]{1,0:T(8,128)(2,1)S(1)} %slice.70), channel_id=1, source_target_pairs={{0,1},{1,0},{2,3},{3,2},{4,5},{5,4},{6,7},{7,6},{8,9},{9,8},{10,11... | collective-permute-start | bytes 393224 | tf_op jit(solution)/shard_map/ppermute | solution.py:29
  33.1 16.4 %collective-permute-start.8 = (bf16[128,1024]{1,0:T(8,128)(2,1)S(1)}, bf16[128,1024]{1,0:T(8,128)(2,1)S(1)}, u32[]{:S(2)}, u32[]{:S(2)}) collective-permute-start(bf16[128,1024]{1,0:T(8,128)(2,1)S(1)} %fusion.3), channel_id=1, source_target_pairs={{0,1},{1,0},{2,3},{3,2},{4,5},{5,4},{6,7},{7,6},{8,9},{9,8},{10,11... | collective-permute-start | bytes 786440 | tf_op jit(solution)/shard_map/ppermute | solution.py:29
  35.9 9.1 %collective-permute-start.6 = (bf16[64,1024]{1,0:T(8,128)(2,1)S(1)}, bf16[64,1024]{1,0:T(8,128)(2,1)S(1)}, u32[]{:S(2)}, u32[]{:S(2)}) collective-permute-start(bf16[64,1024]{1,0:T(8,128)(2,1)S(1)} %fusion.30), channel_id=1, source_target_pairs={{0,2},{1,3},{2,0},{3,1},{4,6},{5,7},{6,4},{7,5},{8,10},{9,11},{10,... | collective-permute-start | bytes 393224 | tf_op jit(solution)/shard_map/ppermute | solution.py:29
  38.9 8.9 %collective-permute-start.9 = (bf16[64,1024]{1,0:T(8,128)(2,1)S(1)}, bf16[64,1024]{1,0:T(8,128)(2,1)S(1)}, u32[]{:S(2)}, u32[]{:S(2)}) collective-permute-start(bf16[64,1024]{1,0:T(8,128)(2,1)S(1)} %fusion.29), channel_id=1, source_target_pairs={{0,2},{1,3},{2,0},{3,1},{4,6},{5,7},{6,4},{7,5},{8,10},{9,11},{10,... | collective-permute-start | bytes 393224 | tf_op jit(solution)/shard_map/ppermute | solution.py:29

commit v17 on v16

--- a/solution.py
+++ b/solution.py
@@ -118,10 +118,6 @@
                 moved[k, h] = to_dp(part, k)
             else:
                 relayed.setdefault((k ^ step, h), []).append(to_dp(part, step))
-    for k in range(2, n_dp):
-        if (k, 0) in moved:
-            moved[k, 0] = in_turn(moved[k, 0])
-            last[0] = moved[k, 0]
     own_delta(0, piece_of(0))
     own_grad(0)
     grad_x = jnp.dot(
@@ -131,14 +127,18 @@
     )
     last[0] = grad_x
     add_next(0)
+    for k in range(2, n_dp):
+        if (k, 0) in moved:
+            moved[k, 0] = in_turn(moved[k, 0])
+            last[0] = moved[k, 0]
+    grad_x = (grad_x + in_turn(back).astype(jnp.float32)).astype(jnp.bfloat16)
+    last[0] = grad_x
     grad_w = g_w[0] + in_turn(moved[1]).astype(jnp.float32)
     for k in range(2, n_dp):
         if (k, 0) in moved:
             whole = jnp.concatenate([moved[k, 0], in_turn(moved[k, 1])], axis=0)
             grad_w = grad_w + whole.astype(jnp.float32)
     grad_w = grad_w.astype(jnp.bfloat16)
-    last[0] = grad_w
-    grad_x = (grad_x + in_turn(back).astype(jnp.float32)).astype(jnp.bfloat16)
     return (grad_w, grad_x)
 
 

time: 52.7 us -> 51.3 us (0.973)
  waiting for transfers between devices: 20.3 us -> 19.3 us
    ppermute x8, waiting for transfers between devices: 20.3 us -> 15.7 us  [to_dp(): return lax.ppermute(x, 'dp', [(i, i ^ k) for i in range(n_dp)])]
    ppermute x3, waiting for transfers between devices: 0.01 us -> 3.6 us  [to_label(): lax.ppermute(x, 'label', [(i, (i + by) % n_label) for i in range(n_label)])]
  transfers between devices with their start and end apart: 11 -> 11, of which waited for: 6 -> 5; matrix products, arithmetic and copies ran while one was open for 18% -> 20% of each run, Pallas kernels for 0% -> 0%
where the time goes in v17:
time: 51.3 us; the launch traced here: 51.1 us
  waiting for transfers between devices  19.3 us (38%)
  starting transfers between devices  16.8 us (33%)
  matrix products  9.41 us (18%)
  other arithmetic  3.53 us (7%)
  local copies, waits for them, and re-layouts  1.22 us (2%)
  between operations  0.88 us (2%)
    ppermute x8, waiting for transfers between devices, to_dp(): return lax.ppermute(x, 'dp', [(i, i ^ k) for i in range(n_dp)])  15.7 us
    ppermute x8, starting transfers between devices, to_dp(): return lax.ppermute(x, 'dp', [(i, i ^ k) for i in range(n_dp)])  14.3 us
    dot_general x5, matrix products, delta_of(): lax.dot_general(rows, piece, (((1,), (1,)), ((), ())), preferred_element_...  4.31 us
    ppermute x3, waiting for transfers between devices, to_label(): lax.ppermute(x, 'label', [(i, (i + by) % n_label) for i in range(n_label)])  3.6 us
    dot_general x8, matrix products, grad_w_of(): lax.dot_general(delta, rows, (((0,), (0,)), ((), ())), preferred_element_...  3.06 us
    ppermute x3, starting transfers between devices, to_label(): lax.ppermute(x, 'label', [(i, (i + by) % n_label) for i in range(n_label)])  2.51 us
    convert_element_type x1, other arithmetic, local(): grad_x = (grad_x + in_turn(back).astype(jnp.float32)).astype(jnp.bfloat16)  1.75 us
    dynamic_update_slice x4, local copies, waits for them, and re-layouts, join(): joined[0] = lax.dynamic_update_slice_in_dim(joined[0], piece, at, axis=0)  1.12 us
  transfers between devices with their start and end apart: 11, of which 5 were waited for; matrix products, arithmetic and copies ran while one was open for 20% of the time, Pallas kernels for 0%

profile of v17, /device:TPU:0, one launch (start us, length us, event | category | flops | bytes accessed | tf_op | source)
XLA Modules:
  0.0 51.1 jit_solution(4031831070805192446)
XLA Ops:
  0.6 4.1 %collective-permute-start.1 = (bf16[128,1024]{1,0:T(8,128)(2,1)}, bf16[128,1024]{1,0:T(8,128)(2,1)S(1)}, u32[]{:S(2)}, u32[]{:S(2)}) collective-permute-start(bf16[128,1024]{1,0:T(8,128)(2,1)} %param.5), channel_id=1, source_target_pairs={{0,2},{1,3},{2,0},{3,1},{4,6},{5,7},{6,4},{7,5},{8,10},{9,11},{10,... | collective-permute-start | bytes 786440 | tf_op jit(solution)/shard_map/ppermute | solution.py:29
  4.7 1.6 %collective-permute-start = (bf16[128,1024]{1,0:T(8,128)(2,1)}, bf16[128,1024]{1,0:T(8,128)(2,1)S(1)}, u32[]{:S(2)}, u32[]{:S(2)}) collective-permute-start(bf16[128,1024]{1,0:T(8,128)(2,1)} %param.5), channel_id=1, source_target_pairs={{0,1},{1,0},{2,3},{3,2},{4,5},{5,4},{6,7},{7,6},{8,9},{9,8},{10,11... | collective-permute-start | bytes 786440 | tf_op jit(solution)/shard_map/ppermute | solution.py:29
  6.3 0.4 collective-permute-start.3
  6.7 0.7 %fusion.35 = s32[768,8]{0,1:T(8,128)S(1)} fusion(s32[768,8]{0,1:T(8,128)} %param.6, s32[768]{0:T(1024)} %param.7), kind=kLoop, calls=%fused_computation.58 | loop fusion | flops 12288 | bytes 52224 | tf_op jit(solution)/shard_map/jit(_where)/select_n | solution.py:21
  7.4 1.2 %collective-permute-start.4 = (s32[768,8]{0,1:T(8,128)S(1)}, s32[768,8]{0,1:T(8,128)S(1)}, u32[]{:S(2)}, u32[]{:S(2)}) collective-permute-start(s32[768,8]{0,1:T(8,128)S(1)} %fusion.35), channel_id=1, source_target_pairs={{0,12},{4,0},{8,4},{12,8},{1,13},{5,1},{9,5},{13,9},{2,14},{6,2},{... | collective-permute-start | bytes 73736 | tf_op jit(solution)/shard_map/ppermute | solution.py:32
  8.7 8.3 %collective-permute-done.1 = bf16[128,1024]{1,0:T(8,128)(2,1)S(1)} collective-permute-done((bf16[128,1024]{1,0:T(8,128)(2,1)}, bf16[128,1024]{1,0:T(8,128)(2,1)S(1)}, u32[]{:S(2)}, u32[]{:S(2)}) %collective-permute-start.1) | collective-permute-done | bytes 262176 | tf_op jit(solution)/shard_map/ppermute | solution.py:29
  17.0 0.7 %collective-permute-start.2 = (bf16[128,1024]{1,0:T(8,128)(2,1)S(1)}, bf16[128,1024]{1,0:T(8,128)(2,1)S(1)}, u32[]{:S(2)}, u32[]{:S(2)}) collective-permute-start(bf16[128,1024]{1,0:T(8,128)(2,1)S(1)} %collective-permute-done.1), channel_id=1, source_target_pairs={{0,1},{1,0},{2,3},{3,2},{4,5},{5,4},{6,7},{7,6},{8,9},{9,8},{10,11... | collective-permute-start | bytes 786440 | tf_op jit(solution)/shard_map/ppermute | solution.py:29
  17.7 1.1 %dynamic_update_slice.12 = bf16[512,1024]{1,0:T(8,128)(2,1)S(1)} pad(bf16[128,1024]{1,0:T(8,128)(2,1)} %param.5, bf16[]{:T(256)} %constant.65.clone.1), padding=0_384x0_0 | pad | bytes 1310722 | tf_op jit(solution)/shard_map/dynamic_update_slice | solution.py:61
  18.8 0.0 collective-permute-done
  18.9 0.0 copy-start
  18.9 5.5 %collective-permute-done.2 = bf16[128,1024]{1,0:T(8,128)(2,1)S(1)} collective-permute-done((bf16[128,1024]{1,0:T(8,128)(2,1)S(1)}, bf16[128,1024]{1,0:T(8,128)(2,1)S(1)}, u32[]{:S(2)}, u32[]{:S(2)}) %collective-permute-start.2) | collective-permute-done | bytes 262176 | tf_op jit(solution)/shard_map/ppermute | solution.py:29
  24.4 0.1 fusion.36
  24.5 0.0 copy-done
  24.5 0.7 %fusion.28 = bf16[768,128]{0,1:T(8,128)(2,1)S(1)} fusion(bf16[128,1024]{1,0:T(8,128)(2,1)S(1)} %get-tuple-element.34, bf16[768,1024]{1,0:T(8,128)(2,1)S(1)} %copy-done, s32[768]{0:T(1024)S(1)} %get-tuple-element.59), kind=kOutput, calls=%fused_computation.40 | convolution fusion | flops 202014720 | bytes 2034688 | tf_op jit(solution)/shard_map/dot_general | solution.py:41
  25.2 0.4 fusion.37
  25.6 0.0 collective-permute-done.4
  25.6 0.1 subtract_reduce_fusion.6
  25.7 0.0 collective-permute-done.3
  25.7 1.5 %fusion = bf16[768,512]{0,1:T(8,128)(2,1)S(1)} fusion(bf16[512,1024]{1,0:T(8,128)(2,1)S(1)} %constant_dynamic-update-slice_fusion, bf16[768,1024]{1,0:T(8,128)(2,1)S(1)} %collective-permute-done.3, s32[768]{0:T(1024)S(1)} %get-tuple-element.61, s32[768]{0:T(1024)S(1)} %get-tuple-element.62, s32[768]{0:T(1024)S(1)} %get-tuple-element.63, ...), kind=kOutput, calls=%fused_computation.3 | convolution fusion | flops 809238528 | bytes 3421696 | tf_op jit(solution)/shard_map/dot_general | solution.py:41
  27.2 0.4 fusion.4
  27.6 1.0 %convolution_convert_fusion = bf16[768,1024]{1,0:T(8,128)(2,1)S(1)} fusion(bf16[768,512]{0,1:T(8,128)(2,1)S(1)} %fusion, bf16[512,1024]{1,0:T(8,128)(2,1)S(1)} %constant_dynamic-update-slice_fusion), kind=kOutput, calls=%fused_computation.1 | convolution fusion | flops 806092800 | bytes 3407872 | tf_op jit(solution)/shard_map/dot_general | solution.py:97
  28.6 0.9 %collective-permute-start.8 = (bf16[768,1024]{1,0:T(8,128)(2,1)S(1)}, bf16[768,1024]{1,0:T(8,128)(2,1)S(1)}, u32[]{:S(2)}, u32[]{:S(2)}) collective-permute-start(bf16[768,1024]{1,0:T(8,128)(2,1)S(1)} %convolution_convert_fusion), channel_id=1, source_target_pairs={{0,4},{4,8},{8,12},{12,0},{1,5},{5,9},{9,13},{13,1},{2,6},{6,10},{... | collective-permute-start | bytes 4718600 | tf_op jit(solution)/shard_map/ppermute | solution.py:32
  29.5 0.7 %collective-permute-start.6 = (bf16[64,1024]{1,0:T(8,128)(2,1)S(1)}, bf16[64,1024]{1,0:T(8,128)(2,1)S(1)}, u32[]{:S(2)}, u32[]{:S(2)}) collective-permute-start(bf16[64,1024]{1,0:T(8,128)(2,1)S(1)} %slice.70), channel_id=1, source_target_pairs={{0,1},{1,0},{2,3},{3,2},{4,5},{5,4},{6,7},{7,6},{8,9},{9,8},{10,11... | collective-permute-start | bytes 393224 | tf_op jit(solution)/shard_map/ppermute | solution.py:29
  30.3 0.7 %fusion.27 = bf16[768,128]{0,1:T(8,128)(2,1)S(1)} fusion(bf16[128,1024]{1,0:T(8,128)(2,1)S(1)} %get-tuple-element.39, bf16[768,1024]{1,0:T(8,128)(2,1)S(1)} %copy-done, s32[768]{0:T(1024)S(1)} %get-tuple-element.58), kind=kOutput, calls=%fused_computation.39 | convolution fusion | flops 202014720 | bytes 2034688 | tf_op jit(solution)/shard_map/dot_general | solution.py:41
  31.0 1.4 %collective-permute-start.5 = (bf16[64,1024]{1,0:T(8,128)(2,1)S(1)}, bf16[64,1024]{1,0:T(8,128)(2,1)S(1)}, u32[]{:S(2)}, u32[]{:S(2)}) collective-permute-start(bf16[64,1024]{1,0:T(8,128)(2,1)S(1)} %slice.71), channel_id=1, source_target_pairs={{0,1},{1,0},{2,3},{3,2},{4,5},{5,4},{6,7},{7,6},{8,9},{9,8},{10,11... | collective-permute-start | bytes 393224 | tf_op jit(solution)/shard_map/ppermute | solution.py:29
  32.4 0.4 fusion.38
  32.7 0.4 fusion.3
  33.1 0.8 %collective-permute-start.7 = (bf16[128,1024]{1,0:T(8,128)(2,1)S(1)}, bf16[128,1024]{1,0:T(8,128)(2,1)S(1)}, u32[]{:S(2)}, u32[]{:S(2)}) collective-permute-start(bf16[128,1024]{1,0:T(8,128)(2,1)S(1)} %fusion.3), channel_id=1, source_target_pairs={{0,1},{1,0},{2,3},{3,2},{4,5},{5,4},{6,7},{7,6},{8,9},{9,8},{10,11... | collective-permute-start | bytes 786440 | tf_op jit(solution)/shard_map/ppermute | solution.py:29
  33.9 0.7 %fusion.26 = bf16[768,128]{0,1:T(8,128)(2,1)S(1)} fusion(bf16[128,1024]{1,0:T(8,128)(2,1)S(1)} %get-tuple-element.42, bf16[768,1024]{1,0:T(8,128)(2,1)S(1)} %copy-done, s32[768]{0:T(1024)S(1)} %get-tuple-element.57), kind=kOutput, calls=%fused_computation.38 | convolution fusion | flops 202014720 | bytes 2034688 | tf_op jit(solution)/shard_map/dot_general | solution.py:41
  34.6 0.4 fusion.39
  35.0 0.4 fusion.2
  35.4 0.4 collective-permute-done.6
  35.9 3.0 %collective-permute-start.9 = (bf16[64,1024]{1,0:T(8,128)(2,1)S(1)}, bf16[64,1024]{1,0:T(8,128)(2,1)S(1)}, u32[]{:S(2)}, u32[]{:S(2)}) collective-permute-start(bf16[64,1024]{1,0:T(8,128)(2,1)S(1)} %fusion.29), channel_id=1, source_target_pairs={{0,2},{1,3},{2,0},{3,1},{4,6},{5,7},{6,4},{7,5},{8,10},{9,11},{10,... | collective-permute-start | bytes 393224 | tf_op jit(solution)/shard_map/ppermute | solution.py:29
  38.8 0.0 collective-permute-done.5
  38.9 2.0 %collective-permute-start.10 = (bf16[64,1024]{1,0:T(8,128)(2,1)S(1)}, bf16[64,1024]{1,0:T(8,128)(2,1)S(1)}, u32[]{:S(2)}, u32[]{:S(2)}) collective-permute-start(bf16[64,1024]{1,0:T(8,128)(2,1)S(1)} %fusion.30), channel_id=1, source_target_pairs={{0,2},{1,3},{2,0},{3,1},{4,6},{5,7},{6,4},{7,5},{8,10},{9,11},{10,... | collective-permute-start | bytes 393224 | tf_op jit(solution)/shard_map/ppermute | solution.py:29
  40.9 0.7 %fusion.25 = bf16[768,128]{0,1:T(8,128)(2,1)S(1)} fusion(bf16[128,1024]{1,0:T(8,128)(2,1)S(1)} %get-tuple-element.48, bf16[768,1024]{1,0:T(8,128)(2,1)S(1)} %copy-done, s32[768]{0:T(1024)S(1)} %get-tuple-element.56), kind=kOutput, calls=%fused_computation.37 | convolution fusion | flops 202014720 | bytes 2034688 | tf_op jit(solution)/shard_map/dot_general | solution.py:41
  41.6 0.1 pad_maximum_fusion
  41.7 0.4 fusion.40
  42.0 1.0 %fusion.41 = f32[768,1024]{1,0:T(8,128)S(1)} fusion(bf16[768,512]{0,1:T(8,128)(2,1)S(1)} %pad_maximum_fusion, bf16[512,1024]{1,0:T(8,128)(2,1)S(1)} %constant_dynamic-update-slice_fusion), kind=kOutput, calls=%fused_computation.78 | convolution fusion | flops 805306368 | bytes 4980736 | tf_op jit(solution)/shard_map/dot_general | solution.py:123
  43.1 0.4 fusion.1
  43.5 1.5 %collective-permute-done.9 = bf16[64,1024]{1,0:T(8,128)(2,1)S(1)} collective-permute-done((bf16[64,1024]{1,0:T(8,128)(2,1)S(1)}, bf16[64,1024]{1,0:T(8,128)(2,1)S(1)}, u32[]{:S(2)}, u32[]{:S(2)}) %collective-permute-start.9) | collective-permute-done | bytes 131104 | tf_op jit(solution)/shard_map/ppermute | solution.py:29
  44.9 3.6 %collective-permute-done.8 = bf16[768,1024]{1,0:T(8,128)(2,1)S(1)} collective-permute-done((bf16[768,1024]{1,0:T(8,128)(2,1)S(1)}, bf16[768,1024]{1,0:T(8,128)(2,1)S(1)}, u32[]{:S(2)}, u32[]{:S(2)}) %collective-permute-start.8) | collective-permute-done | bytes 1572896 | tf_op jit(solution)/shard_map/ppermute | solution.py:32
  48.5 1.8 %add_convert_fusion = bf16[768,1024]{1,0:T(8,128)(2,1)} fusion(f32[768,1024]{1,0:T(8,128)S(1)} %fusion.41, bf16[768,1024]{1,0:T(8,128)(2,1)S(1)} %collective-permute-done.8), kind=kLoop, calls=%fused_computation | loop fusion | flops 2359296 | bytes 6291456 | tf_op jit(solution)/shard_map/convert_element_type | solution.py:134
  50.3 0.0 collective-permute-done.10
  50.3 0.0 collective-permute-done.7
  50.3 0.8 %add_convert_fusion.1 = bf16[128,1024]{1,0:T(8,128)(2,1)} fusion(f32[128,1024]{1,0:T(8,128)S(1)} %fusion.1, bf16[128,1024]{1,0:T(8,128)(2,1)S(1)} %collective-permute-done.7, bf16[64,1024]{1,0:T(8,128)(2,1)S(1)} %collective-permute-done.10, bf16[64,1024]{1,0:T(8,128)(2,1)S(1)} %collective-permute-done.9), kind=kLoop, calls=%fused_computation.42 | loop fusion | flops 1048576 | bytes 1310720 | tf_op jit(solution)/shard_map/convert_element_type | solution.py:141
  (10 shorter events, 0.2 us)
Async XLA Ops:
  0.6 16.3 %collective-permute-start.1 = (bf16[128,1024]{1,0:T(8,128)(2,1)}, bf16[128,1024]{1,0:T(8,128)(2,1)S(1)}, u32[]{:S(2)}, u32[]{:S(2)}) collective-permute-start(bf16[128,1024]{1,0:T(8,128)(2,1)} %param.5), channel_id=1, source_target_pairs={{0,2},{1,3},{2,0},{3,1},{4,6},{5,7},{6,4},{7,5},{8,10},{9,11},{10,... | collective-permute-start | bytes 786440 | tf_op jit(solution)/shard_map/ppermute | solution.py:29
  4.7 14.1 %collective-permute-start = (bf16[128,1024]{1,0:T(8,128)(2,1)}, bf16[128,1024]{1,0:T(8,128)(2,1)S(1)}, u32[]{:S(2)}, u32[]{:S(2)}) collective-permute-start(bf16[128,1024]{1,0:T(8,128)(2,1)} %param.5), channel_id=1, source_target_pairs={{0,1},{1,0},{2,3},{3,2},{4,5},{5,4},{6,7},{7,6},{8,9},{9,8},{10,11... | collective-permute-start | bytes 786440 | tf_op jit(solution)/shard_map/ppermute | solution.py:29
  6.3 19.4 %collective-permute-start.3 = (bf16[768,1024]{1,0:T(8,128)(2,1)}, bf16[768,1024]{1,0:T(8,128)(2,1)S(1)}, u32[]{:S(2)}, u32[]{:S(2)}) collective-permute-start(bf16[768,1024]{1,0:T(8,128)(2,1)} %param.4), channel_id=1, source_target_pairs={{0,12},{4,0},{8,4},{12,8},{1,13},{5,1},{9,5},{13,9},{2,14},{6,2},{... | collective-permute-start | bytes 4718600 | tf_op jit(solution)/shard_map/ppermute | solution.py:32
  7.4 18.2 %collective-permute-start.4 = (s32[768,8]{0,1:T(8,128)S(1)}, s32[768,8]{0,1:T(8,128)S(1)}, u32[]{:S(2)}, u32[]{:S(2)}) collective-permute-start(s32[768,8]{0,1:T(8,128)S(1)} %fusion.35), channel_id=1, source_target_pairs={{0,12},{4,0},{8,4},{12,8},{1,13},{5,1},{9,5},{13,9},{2,14},{6,2},{... | collective-permute-start | bytes 73736 | tf_op jit(solution)/shard_map/ppermute | solution.py:32
  17.0 7.4 %collective-permute-start.2 = (bf16[128,1024]{1,0:T(8,128)(2,1)S(1)}, bf16[128,1024]{1,0:T(8,128)(2,1)S(1)}, u32[]{:S(2)}, u32[]{:S(2)}) collective-permute-start(bf16[128,1024]{1,0:T(8,128)(2,1)S(1)} %collective-permute-done.1), channel_id=1, source_target_pairs={{0,1},{1,0},{2,3},{3,2},{4,5},{5,4},{6,7},{7,6},{8,9},{9,8},{10,11... | collective-permute-start | bytes 786440 | tf_op jit(solution)/shard_map/ppermute | solution.py:29
  18.9 5.6 %copy-start = (bf16[768,1024]{1,0:T(8,128)(2,1)S(1)}, bf16[768,1024]{1,0:T(8,128)(2,1)}, u32[]{:S(2)}) copy-start(bf16[768,1024]{1,0:T(8,128)(2,1)} %param.4) | copy-start | bytes 4718596
  28.6 19.9 %collective-permute-start.8 = (bf16[768,1024]{1,0:T(8,128)(2,1)S(1)}, bf16[768,1024]{1,0:T(8,128)(2,1)S(1)}, u32[]{:S(2)}, u32[]{:S(2)}) collective-permute-start(bf16[768,1024]{1,0:T(8,128)(2,1)S(1)} %convolution_convert_fusion), channel_id=1, source_target_pairs={{0,4},{4,8},{8,12},{12,0},{1,5},{5,9},{9,13},{13,1},{2,6},{6,10},{... | collective-permute-start | bytes 4718600 | tf_op jit(solution)/shard_map/ppermute | solution.py:32
  29.5 6.3 %collective-permute-start.6 = (bf16[64,1024]{1,0:T(8,128)(2,1)S(1)}, bf16[64,1024]{1,0:T(8,128)(2,1)S(1)}, u32[]{:S(2)}, u32[]{:S(2)}) collective-permute-start(bf16[64,1024]{1,0:T(8,128)(2,1)S(1)} %slice.70), channel_id=1, source_target_pairs={{0,1},{1,0},{2,3},{3,2},{4,5},{5,4},{6,7},{7,6},{8,9},{9,8},{10,11... | collective-permute-start | bytes 393224 | tf_op jit(solution)/shard_map/ppermute | solution.py:29
  31.0 7.8 %collective-permute-start.5 = (bf16[64,1024]{1,0:T(8,128)(2,1)S(1)}, bf16[64,1024]{1,0:T(8,128)(2,1)S(1)}, u32[]{:S(2)}, u32[]{:S(2)}) collective-permute-start(bf16[64,1024]{1,0:T(8,128)(2,1)S(1)} %slice.71), channel_id=1, source_target_pairs={{0,1},{1,0},{2,3},{3,2},{4,5},{5,4},{6,7},{7,6},{8,9},{9,8},{10,11... | collective-permute-start | bytes 393224 | tf_op jit(solution)/shard_map/ppermute | solution.py:29
  33.1 17.2 %collective-permute-start.7 = (bf16[128,1024]{1,0:T(8,128)(2,1)S(1)}, bf16[128,1024]{1,0:T(8,128)(2,1)S(1)}, u32[]{:S(2)}, u32[]{:S(2)}) collective-permute-start(bf16[128,1024]{1,0:T(8,128)(2,1)S(1)} %fusion.3), channel_id=1, source_target_pairs={{0,1},{1,0},{2,3},{3,2},{4,5},{5,4},{6,7},{7,6},{8,9},{9,8},{10,11... | collective-permute-start | bytes 786440 | tf_op jit(solution)/shard_map/ppermute | solution.py:29
  35.9 9.1 %collective-permute-start.9 = (bf16[64,1024]{1,0:T(8,128)(2,1)S(1)}, bf16[64,1024]{1,0:T(8,128)(2,1)S(1)}, u32[]{:S(2)}, u32[]{:S(2)}) collective-permute-start(bf16[64,1024]{1,0:T(8,128)(2,1)S(1)} %fusion.29), channel_id=1, source_target_pairs={{0,2},{1,3},{2,0},{3,1},{4,6},{5,7},{6,4},{7,5},{8,10},{9,11},{10,... | collective-permute-start | bytes 393224 | tf_op jit(solution)/shard_map/ppermute | solution.py:29
  38.9 11.4 %collective-permute-start.10 = (bf16[64,1024]{1,0:T(8,128)(2,1)S(1)}, bf16[64,1024]{1,0:T(8,128)(2,1)S(1)}, u32[]{:S(2)}, u32[]{:S(2)}) collective-permute-start(bf16[64,1024]{1,0:T(8,128)(2,1)S(1)} %fusion.30), channel_id=1, source_target_pairs={{0,2},{1,3},{2,0},{3,1},{4,6},{5,7},{6,4},{7,5},{8,10},{9,11},{10,... | collective-permute-start | bytes 393224 | tf_op jit(solution)/shard_map/ppermute | solution.py:29

commit v18 on v17

--- a/solution.py
+++ b/solution.py
@@ -52,7 +52,10 @@
     pieces = {0: weights}
     for k in range(1, n_dp):
         step = k & -k
-        pieces[k] = to_dp(pieces[k ^ step], step)
+        source = pieces[k ^ step]
+        if k == 1:
+            source, _ = lax.optimization_barrier((source, ids))
+        pieces[k] = to_dp(source, step)
     d_own, g_w = {}, {}
     joined = [jnp.zeros((stretch, width), weights.dtype)]
     next_rows = to_label(embeds, -1)
@@ -73,7 +76,7 @@
         return whole[k * ch_dev:(k + 1) * ch_dev]
 
     def add_next(k):
-        delta = in_turn(d_next)[:, k * ch_dev:(k + 1) * ch_dev]
+        delta = in_turn(d_late if k == late else d_early[:, k * ch_dev:(k + 1) * ch_dev])
         g_w[k] = (g_w[k] + grad_w_of(delta, next_rows)) * scale
         last[0] = g_w[k]
 
@@ -83,16 +86,20 @@
         if k & -k == k:
             pieces[k] = in_turn(pieces[k])
             last[0] = pieces[k]
-    for k in range(1, n_dp):
-        join(in_turn(pieces[k]), k * ch_dev)
-    joined = [in_turn(joined[0])]
-    last[0] = joined[0]
-    own_delta(late, piece_of(late))
+    next_rows, next_ids, pieces[1], _ = lax.optimization_barrier((next_rows, next_ids, pieces[1], last[0]))
+    for k in range(1, late):
+        join(pieces[k], k * ch_dev)
+    early = joined[0][:late * ch_dev]
+    d_early = delta_of(next_rows, next_ids, early, list(range(late)))
+    last[0] = d_early
+    pieces[late] = in_turn(pieces[late])
+    join(pieces[late], late * ch_dev)
+    joined = joined[0]
+    own_delta(late, pieces[late])
     own_grad(late)
-    joined = joined[0]
-    next_ids = in_turn(next_ids)
-    d_next = delta_of(next_rows, next_ids, joined, list(range(n_dp)))
-    last[0] = d_next
+    d_late = delta_of(next_rows, next_ids, in_turn(pieces[late]), [late])
+    d_next = jnp.concatenate([d_early, d_late], axis=1)
+    last[0] = d_late
     add_next(late)
     theirs = jnp.dot(in_turn(d_next), joined, preferred_element_type=jnp.float32).astype(jnp.bfloat16)
     last[0] = theirs

time: 51.3 us -> 50.9 us (level)
    ppermute x8, waiting for transfers between devices: 15.7 us -> 12.5 us  [to_dp(): return lax.ppermute(x, 'dp', [(i, i ^ k) for i in range(n_dp)])]
    ppermute x3, waiting for transfers between devices: 3.6 us -> 6.37 us  [to_label(): lax.ppermute(x, 'label', [(i, (i + by) % n_label) for i in range(n_label)])]
    ppermute x8, starting transfers between devices: 14.3 us -> 13.6 us  [to_dp(): return lax.ppermute(x, 'dp', [(i, i ^ k) for i in range(n_dp)])]
    dot_general x5 -> x6, matrix products: 4.31 us -> 4.62 us  [delta_of(): lax.dot_general(rows, piece, (((1,), (1,)), ((), ())), preferred_element_...]
where the time goes in v18:
time: 50.9 us; the launch traced here: 50.7 us
  waiting for transfers between devices  18.8 us (37%)
  starting transfers between devices  16.5 us (32%)
  matrix products  9.72 us (19%)
  other arithmetic  3.58 us (7%)
  local copies, waits for them, and re-layouts  1.24 us (2%)
  between operations  0.88 us (2%)
    ppermute x8, starting transfers between devices, to_dp(): return lax.ppermute(x, 'dp', [(i, i ^ k) for i in range(n_dp)])  13.6 us
    ppermute x8, waiting for transfers between devices, to_dp(): return lax.ppermute(x, 'dp', [(i, i ^ k) for i in range(n_dp)])  12.5 us
    ppermute x3, waiting for transfers between devices, to_label(): lax.ppermute(x, 'label', [(i, (i + by) % n_label) for i in range(n_label)])  6.37 us
    dot_general x6, matrix products, delta_of(): lax.dot_general(rows, piece, (((1,), (1,)), ((), ())), preferred_element_...  4.62 us
    dot_general x8, matrix products, grad_w_of(): lax.dot_general(delta, rows, (((0,), (0,)), ((), ())), preferred_element_...  3.05 us
    ppermute x3, starting transfers between devices, to_label(): lax.ppermute(x, 'label', [(i, (i + by) % n_label) for i in range(n_label)])  2.93 us
    convert_element_type x1, other arithmetic, local(): grad_x = (grad_x + in_turn(back).astype(jnp.float32)).astype(jnp.bfloat16)  1.75 us
    dynamic_update_slice x4, local copies, waits for them, and re-layouts, join(): joined[0] = lax.dynamic_update_slice_in_dim(joined[0], piece, at, axis=0)  1.12 us
  transfers between devices with their start and end apart: 11, of which 5 were waited for; matrix products, arithmetic and copies ran while one was open for 20% of the time, Pallas kernels for 0%

profile of v18, /device:TPU:0, one launch (start us, length us, event | category | flops | bytes accessed | tf_op | source)
XLA Modules:
  0.0 50.7 jit_solution(4846316721251732723)
XLA Ops:
  0.6 2.4 %collective-permute-start = (bf16[768,1024]{1,0:T(8,128)(2,1)}, bf16[768,1024]{1,0:T(8,128)(2,1)S(1)}, u32[]{:S(2)}, u32[]{:S(2)}) collective-permute-start(bf16[768,1024]{1,0:T(8,128)(2,1)} %param.4), channel_id=1, source_target_pairs={{0,12},{4,0},{8,4},{12,8},{1,13},{5,1},{9,5},{13,9},{2,14},{6,2},{... | collective-permute-start | bytes 4718600 | tf_op jit(solution)/shard_map/ppermute | solution.py:32
  3.1 2.6 %collective-permute-start.3 = (bf16[128,1024]{1,0:T(8,128)(2,1)}, bf16[128,1024]{1,0:T(8,128)(2,1)S(1)}, u32[]{:S(2)}, u32[]{:S(2)}) collective-permute-start(bf16[128,1024]{1,0:T(8,128)(2,1)} %param.5), channel_id=1, source_target_pairs={{0,2},{1,3},{2,0},{3,1},{4,6},{5,7},{6,4},{7,5},{8,10},{9,11},{10,... | collective-permute-start | bytes 786440 | tf_op jit(solution)/shard_map/ppermute | solution.py:29
  5.7 0.7 %fusion.41 = s32[768,8]{0,1:T(8,128)S(1)} fusion(s32[768,8]{0,1:T(8,128)} %param.6, s32[768]{0:T(1024)} %param.7), kind=kLoop, calls=%fused_computation.67 | loop fusion | flops 12288 | bytes 52224 | tf_op jit(solution)/shard_map/jit(_where)/select_n | solution.py:21
  6.4 1.6 %collective-permute-start.2 = (bf16[128,1024]{1,0:T(8,128)(2,1)}, bf16[128,1024]{1,0:T(8,128)(2,1)S(1)}, u32[]{:S(2)}, u32[]{:S(2)}) collective-permute-start(bf16[128,1024]{1,0:T(8,128)(2,1)} %param.5), channel_id=1, source_target_pairs={{0,1},{1,0},{2,3},{3,2},{4,5},{5,4},{6,7},{7,6},{8,9},{9,8},{10,11... | collective-permute-start | bytes 786440 | tf_op jit(solution)/shard_map/ppermute | solution.py:29
  8.0 0.1 collective-permute-start.1
  8.1 1.1 %dynamic_update_slice.12 = bf16[512,1024]{1,0:T(8,128)(2,1)S(1)} pad(bf16[128,1024]{1,0:T(8,128)(2,1)} %param.5, bf16[]{:T(256)} %constant.63.clone.1), padding=0_384x0_0 | pad | bytes 1310722 | tf_op jit(solution)/shard_map/dynamic_update_slice | solution.py:64
  9.3 8.4 %collective-permute-done.3 = bf16[128,1024]{1,0:T(8,128)(2,1)S(1)} collective-permute-done((bf16[128,1024]{1,0:T(8,128)(2,1)}, bf16[128,1024]{1,0:T(8,128)(2,1)S(1)}, u32[]{:S(2)}, u32[]{:S(2)}) %collective-permute-start.3) | collective-permute-done | bytes 262176 | tf_op jit(solution)/shard_map/ppermute | solution.py:29
  17.6 0.7 %collective-permute-start.4 = (bf16[128,1024]{1,0:T(8,128)(2,1)S(1)}, bf16[128,1024]{1,0:T(8,128)(2,1)S(1)}, u32[]{:S(2)}, u32[]{:S(2)}) collective-permute-start(bf16[128,1024]{1,0:T(8,128)(2,1)S(1)} %collective-permute-done.3), channel_id=1, source_target_pairs={{0,1},{1,0},{2,3},{3,2},{4,5},{5,4},{6,7},{7,6},{8,9},{9,8},{10,11... | collective-permute-start | bytes 786440 | tf_op jit(solution)/shard_map/ppermute | solution.py:29
  18.4 3.1 %collective-permute-done.1 = s32[768,8]{0,1:T(8,128)S(1)} collective-permute-done((s32[768,8]{0,1:T(8,128)S(1)}, s32[768,8]{0,1:T(8,128)S(1)}, u32[]{:S(2)}, u32[]{:S(2)}) %collective-permute-start.1) | collective-permute-done | bytes 24608 | tf_op jit(solution)/shard_map/ppermute | solution.py:32
  21.5 0.0 collective-permute-done.2
  21.5 0.0 collective-permute-done
  21.5 0.1 subtract_reduce_fusion.3
  21.6 1.1 %fusion.4 = bf16[768,384]{0,1:T(8,128)(2,1)S(1)} fusion(bf16[768,1024]{1,0:T(8,128)(2,1)S(1)} %collective-permute-done, bf16[512,1024]{1,0:T(8,128)(2,1)S(1)} %constant_dynamic-update-slice_fusion.1, s32[768]{0:T(1024)S(1)} %get-tuple-element.63, s32[768]{0:T(1024)S(1)} %get-tuple-element.64, s32[768]{0:T(1024)S(1)} %get-tuple-element.65, ...), kind=kOutput, calls=%fused_computation.7 | convolution fusion | flops 606633984 | bytes 2962432 | tf_op jit(solution)/shard_map/dot_general | solution.py:41
  22.7 0.0 copy-start
  22.7 2.1 %collective-permute-done.4 = bf16[128,1024]{1,0:T(8,128)(2,1)S(1)} collective-permute-done((bf16[128,1024]{1,0:T(8,128)(2,1)S(1)}, bf16[128,1024]{1,0:T(8,128)(2,1)S(1)}, u32[]{:S(2)}, u32[]{:S(2)}) %collective-permute-start.4) | collective-permute-done | bytes 262176 | tf_op jit(solution)/shard_map/ppermute | solution.py:29
  24.9 0.0 copy-done
  24.9 0.7 %fusion.37 = bf16[768,128]{0,1:T(8,128)(2,1)S(1)} fusion(bf16[128,1024]{1,0:T(8,128)(2,1)S(1)} %collective-permute-done.4, bf16[768,1024]{1,0:T(8,128)(2,1)S(1)} %copy-done, s32[768]{0:T(1024)S(1)} %get-tuple-element.61), kind=kOutput, calls=%fused_computation.50 | convolution fusion | flops 202014720 | bytes 2034688 | tf_op jit(solution)/shard_map/dot_general | solution.py:41
  25.6 0.4 fusion.44
  26.0 0.7 %fusion.36 = bf16[768,128]{0,1:T(8,128)(2,1)S(1)} fusion(bf16[768,1024]{1,0:T(8,128)(2,1)S(1)} %collective-permute-done, bf16[128,1024]{1,0:T(8,128)(2,1)S(1)} %collective-permute-done.4, s32[768]{0:T(1024)S(1)} %get-tuple-element.62), kind=kOutput, calls=%fused_computation.49 | convolution fusion | flops 202014720 | bytes 2034688 | tf_op jit(solution)/shard_map/dot_general | solution.py:41
  26.7 0.1 pad_maximum_fusion
  26.8 0.4 fusion.8
  27.2 0.1 fusion.42
  27.3 1.0 %convolution_convert_fusion = bf16[768,1024]{1,0:T(8,128)(2,1)S(1)} fusion(bf16[768,512]{0,1:T(8,128)(2,1)S(1)} %pad_maximum_fusion, bf16[512,1024]{1,0:T(8,128)(2,1)S(1)} %constant_dynamic-update-slice_fusion), kind=kOutput, calls=%fused_computation.1 | convolution fusion | flops 806092800 | bytes 3407872 | tf_op jit(solution)/shard_map/dot_general | solution.py:104
  28.3 0.4 collective-permute-start.8
  28.7 1.6 %collective-permute-start.6 = (bf16[64,1024]{1,0:T(8,128)(2,1)S(1)}, bf16[64,1024]{1,0:T(8,128)(2,1)S(1)}, u32[]{:S(2)}, u32[]{:S(2)}) collective-permute-start(bf16[64,1024]{1,0:T(8,128)(2,1)S(1)} %slice.67), channel_id=1, source_target_pairs={{0,1},{1,0},{2,3},{3,2},{4,5},{5,4},{6,7},{7,6},{8,9},{9,8},{10,11... | collective-permute-start | bytes 393224 | tf_op jit(solution)/shard_map/ppermute | solution.py:29
  30.2 0.5 %collective-permute-start.5 = (bf16[64,1024]{1,0:T(8,128)(2,1)S(1)}, bf16[64,1024]{1,0:T(8,128)(2,1)S(1)}, u32[]{:S(2)}, u32[]{:S(2)}) collective-permute-start(bf16[64,1024]{1,0:T(8,128)(2,1)S(1)} %slice.68), channel_id=1, source_target_pairs={{0,1},{1,0},{2,3},{3,2},{4,5},{5,4},{6,7},{7,6},{8,9},{9,8},{10,11... | collective-permute-start | bytes 393224 | tf_op jit(solution)/shard_map/ppermute | solution.py:29
  30.8 0.7 %fusion.35 = bf16[768,128]{0,1:T(8,128)(2,1)S(1)} fusion(bf16[128,1024]{1,0:T(8,128)(2,1)S(1)} %get-tuple-element.41, bf16[768,1024]{1,0:T(8,128)(2,1)S(1)} %copy-done, s32[768]{0:T(1024)S(1)} %get-tuple-element.60), kind=kOutput, calls=%fused_computation.48 | convolution fusion | flops 202014720 | bytes 2034688 | tf_op jit(solution)/shard_map/dot_general | solution.py:41
  31.5 0.4 fusion.45
  31.9 0.4 fusion.7
  32.3 1.6 %collective-permute-start.7 = (bf16[128,1024]{1,0:T(8,128)(2,1)S(1)}, bf16[128,1024]{1,0:T(8,128)(2,1)S(1)}, u32[]{:S(2)}, u32[]{:S(2)}) collective-permute-start(bf16[128,1024]{1,0:T(8,128)(2,1)S(1)} %fusion.7), channel_id=1, source_target_pairs={{0,1},{1,0},{2,3},{3,2},{4,5},{5,4},{6,7},{7,6},{8,9},{9,8},{10,11... | collective-permute-start | bytes 786440 | tf_op jit(solution)/shard_map/ppermute | solution.py:29
  33.9 0.7 %fusion.34 = bf16[768,128]{0,1:T(8,128)(2,1)S(1)} fusion(bf16[128,1024]{1,0:T(8,128)(2,1)S(1)} %get-tuple-element.44, bf16[768,1024]{1,0:T(8,128)(2,1)S(1)} %copy-done, s32[768]{0:T(1024)S(1)} %get-tuple-element.59), kind=kOutput, calls=%fused_computation.47 | convolution fusion | flops 202014720 | bytes 2034688 | tf_op jit(solution)/shard_map/dot_general | solution.py:41
  34.6 0.4 fusion.46
  35.0 0.4 fusion.6
  35.4 0.0 collective-permute-done.6
  35.4 3.3 %collective-permute-start.9 = (bf16[64,1024]{1,0:T(8,128)(2,1)S(1)}, bf16[64,1024]{1,0:T(8,128)(2,1)S(1)}, u32[]{:S(2)}, u32[]{:S(2)}) collective-permute-start(bf16[64,1024]{1,0:T(8,128)(2,1)S(1)} %fusion.39), channel_id=1, source_target_pairs={{0,2},{1,3},{2,0},{3,1},{4,6},{5,7},{6,4},{7,5},{8,10},{9,11},{10,... | collective-permute-start | bytes 393224 | tf_op jit(solution)/shard_map/ppermute | solution.py:29
  38.7 0.0 collective-permute-done.5
  38.7 1.7 %collective-permute-start.10 = (bf16[64,1024]{1,0:T(8,128)(2,1)S(1)}, bf16[64,1024]{1,0:T(8,128)(2,1)S(1)}, u32[]{:S(2)}, u32[]{:S(2)}) collective-permute-start(bf16[64,1024]{1,0:T(8,128)(2,1)S(1)} %fusion.40), channel_id=1, source_target_pairs={{0,2},{1,3},{2,0},{3,1},{4,6},{5,7},{6,4},{7,5},{8,10},{9,11},{10,... | collective-permute-start | bytes 393224 | tf_op jit(solution)/shard_map/ppermute | solution.py:29
  40.4 0.7 %fusion.33 = bf16[768,128]{0,1:T(8,128)(2,1)S(1)} fusion(bf16[128,1024]{1,0:T(8,128)(2,1)S(1)} %get-tuple-element.50, bf16[768,1024]{1,0:T(8,128)(2,1)S(1)} %copy-done, s32[768]{0:T(1024)S(1)} %get-tuple-element.58), kind=kOutput, calls=%fused_computation.46 | convolution fusion | flops 202014720 | bytes 2034688 | tf_op jit(solution)/shard_map/dot_general | solution.py:41
  41.1 0.1 pad_maximum_fusion.1
  41.2 0.4 fusion.47
  41.6 1.0 %fusion.48 = f32[768,1024]{1,0:T(8,128)S(1)} fusion(bf16[768,512]{0,1:T(8,128)(2,1)S(1)} %pad_maximum_fusion.1, bf16[512,1024]{1,0:T(8,128)(2,1)S(1)} %constant_dynamic-update-slice_fusion), kind=kOutput, calls=%fused_computation.87 | convolution fusion | flops 805306368 | bytes 4980736 | tf_op jit(solution)/shard_map/dot_general | solution.py:130
  42.6 0.4 fusion.5
  43.0 1.9 %collective-permute-done.9 = bf16[64,1024]{1,0:T(8,128)(2,1)S(1)} collective-permute-done((bf16[64,1024]{1,0:T(8,128)(2,1)S(1)}, bf16[64,1024]{1,0:T(8,128)(2,1)S(1)}, u32[]{:S(2)}, u32[]{:S(2)}) %collective-permute-start.9) | collective-permute-done | bytes 131104 | tf_op jit(solution)/shard_map/ppermute | solution.py:29
  44.9 3.3 %collective-permute-done.8 = bf16[768,1024]{1,0:T(8,128)(2,1)S(1)} collective-permute-done((bf16[768,1024]{1,0:T(8,128)(2,1)S(1)}, bf16[768,1024]{1,0:T(8,128)(2,1)S(1)}, u32[]{:S(2)}, u32[]{:S(2)}) %collective-permute-start.8) | collective-permute-done | bytes 1572896 | tf_op jit(solution)/shard_map/ppermute | solution.py:32
  48.2 1.8 %add_convert_fusion = bf16[768,1024]{1,0:T(8,128)(2,1)} fusion(f32[768,1024]{1,0:T(8,128)S(1)} %fusion.48, bf16[768,1024]{1,0:T(8,128)(2,1)S(1)} %collective-permute-done.8), kind=kLoop, calls=%fused_computation | loop fusion | flops 2359296 | bytes 6291456 | tf_op jit(solution)/shard_map/convert_element_type | solution.py:141
  49.9 0.0 collective-permute-done.10
  49.9 0.0 collective-permute-done.7
  49.9 0.8 %add_convert_fusion.1 = bf16[128,1024]{1,0:T(8,128)(2,1)} fusion(f32[128,1024]{1,0:T(8,128)S(1)} %fusion.5, bf16[128,1024]{1,0:T(8,128)(2,1)S(1)} %collective-permute-done.7, bf16[64,1024]{1,0:T(8,128)(2,1)S(1)} %collective-permute-done.10, bf16[64,1024]{1,0:T(8,128)(2,1)S(1)} %collective-permute-done.9), kind=kLoop, calls=%fused_computation.54 | loop fusion | flops 1048576 | bytes 1310720 | tf_op jit(solution)/shard_map/convert_element_type | solution.py:148
  (10 shorter events, 0.2 us)
Async XLA Ops:
  0.6 20.8 %collective-permute-start = (bf16[768,1024]{1,0:T(8,128)(2,1)}, bf16[768,1024]{1,0:T(8,128)(2,1)S(1)}, u32[]{:S(2)}, u32[]{:S(2)}) collective-permute-start(bf16[768,1024]{1,0:T(8,128)(2,1)} %param.4), channel_id=1, source_target_pairs={{0,12},{4,0},{8,4},{12,8},{1,13},{5,1},{9,5},{13,9},{2,14},{6,2},{... | collective-permute-start | bytes 4718600 | tf_op jit(solution)/shard_map/ppermute | solution.py:32
  3.1 14.6 %collective-permute-start.3 = (bf16[128,1024]{1,0:T(8,128)(2,1)}, bf16[128,1024]{1,0:T(8,128)(2,1)S(1)}, u32[]{:S(2)}, u32[]{:S(2)}) collective-permute-start(bf16[128,1024]{1,0:T(8,128)(2,1)} %param.5), channel_id=1, source_target_pairs={{0,2},{1,3},{2,0},{3,1},{4,6},{5,7},{6,4},{7,5},{8,10},{9,11},{10,... | collective-permute-start | bytes 786440 | tf_op jit(solution)/shard_map/ppermute | solution.py:29
  6.4 15.1 %collective-permute-start.2 = (bf16[128,1024]{1,0:T(8,128)(2,1)}, bf16[128,1024]{1,0:T(8,128)(2,1)S(1)}, u32[]{:S(2)}, u32[]{:S(2)}) collective-permute-start(bf16[128,1024]{1,0:T(8,128)(2,1)} %param.5), channel_id=1, source_target_pairs={{0,1},{1,0},{2,3},{3,2},{4,5},{5,4},{6,7},{7,6},{8,9},{9,8},{10,11... | collective-permute-start | bytes 786440 | tf_op jit(solution)/shard_map/ppermute | solution.py:29
  8.0 13.5 %collective-permute-start.1 = (s32[768,8]{0,1:T(8,128)S(1)}, s32[768,8]{0,1:T(8,128)S(1)}, u32[]{:S(2)}, u32[]{:S(2)}) collective-permute-start(s32[768,8]{0,1:T(8,128)S(1)} %fusion.41), channel_id=1, source_target_pairs={{0,12},{4,0},{8,4},{12,8},{1,13},{5,1},{9,5},{13,9},{2,14},{6,2},{... | collective-permute-start | bytes 73736 | tf_op jit(solution)/shard_map/ppermute | solution.py:32
  17.6 7.2 %collective-permute-start.4 = (bf16[128,1024]{1,0:T(8,128)(2,1)S(1)}, bf16[128,1024]{1,0:T(8,128)(2,1)S(1)}, u32[]{:S(2)}, u32[]{:S(2)}) collective-permute-start(bf16[128,1024]{1,0:T(8,128)(2,1)S(1)} %collective-permute-done.3), channel_id=1, source_target_pairs={{0,1},{1,0},{2,3},{3,2},{4,5},{5,4},{6,7},{7,6},{8,9},{9,8},{10,11... | collective-permute-start | bytes 786440 | tf_op jit(solution)/shard_map/ppermute | solution.py:29
  22.7 2.2 %copy-start = (bf16[768,1024]{1,0:T(8,128)(2,1)S(1)}, bf16[768,1024]{1,0:T(8,128)(2,1)}, u32[]{:S(2)}) copy-start(bf16[768,1024]{1,0:T(8,128)(2,1)} %param.4) | copy-start | bytes 4718596
  28.3 19.9 %collective-permute-start.8 = (bf16[768,1024]{1,0:T(8,128)(2,1)S(1)}, bf16[768,1024]{1,0:T(8,128)(2,1)S(1)}, u32[]{:S(2)}, u32[]{:S(2)}) collective-permute-start(bf16[768,1024]{1,0:T(8,128)(2,1)S(1)} %convolution_convert_fusion), channel_id=1, source_target_pairs={{0,4},{4,8},{8,12},{12,0},{1,5},{5,9},{9,13},{13,1},{2,6},{6,10},{... | collective-permute-start | bytes 4718600 | tf_op jit(solution)/shard_map/ppermute | solution.py:32
  28.7 6.7 %collective-permute-start.6 = (bf16[64,1024]{1,0:T(8,128)(2,1)S(1)}, bf16[64,1024]{1,0:T(8,128)(2,1)S(1)}, u32[]{:S(2)}, u32[]{:S(2)}) collective-permute-start(bf16[64,1024]{1,0:T(8,128)(2,1)S(1)} %slice.67), channel_id=1, source_target_pairs={{0,1},{1,0},{2,3},{3,2},{4,5},{5,4},{6,7},{7,6},{8,9},{9,8},{10,11... | collective-permute-start | bytes 393224 | tf_op jit(solution)/shard_map/ppermute | solution.py:29
  30.2 8.4 %collective-permute-start.5 = (bf16[64,1024]{1,0:T(8,128)(2,1)S(1)}, bf16[64,1024]{1,0:T(8,128)(2,1)S(1)}, u32[]{:S(2)}, u32[]{:S(2)}) collective-permute-start(bf16[64,1024]{1,0:T(8,128)(2,1)S(1)} %slice.68), channel_id=1, source_target_pairs={{0,1},{1,0},{2,3},{3,2},{4,5},{5,4},{6,7},{7,6},{8,9},{9,8},{10,11... | collective-permute-start | bytes 393224 | tf_op jit(solution)/shard_map/ppermute | solution.py:29
  32.3 17.7 %collective-permute-start.7 = (bf16[128,1024]{1,0:T(8,128)(2,1)S(1)}, bf16[128,1024]{1,0:T(8,128)(2,1)S(1)}, u32[]{:S(2)}, u32[]{:S(2)}) collective-permute-start(bf16[128,1024]{1,0:T(8,128)(2,1)S(1)} %fusion.7), channel_id=1, source_target_pairs={{0,1},{1,0},{2,3},{3,2},{4,5},{5,4},{6,7},{7,6},{8,9},{9,8},{10,11... | collective-permute-start | bytes 786440 | tf_op jit(solution)/shard_map/ppermute | solution.py:29
  35.4 9.5 %collective-permute-start.9 = (bf16[64,1024]{1,0:T(8,128)(2,1)S(1)}, bf16[64,1024]{1,0:T(8,128)(2,1)S(1)}, u32[]{:S(2)}, u32[]{:S(2)}) collective-permute-start(bf16[64,1024]{1,0:T(8,128)(2,1)S(1)} %fusion.39), channel_id=1, source_target_pairs={{0,2},{1,3},{2,0},{3,1},{4,6},{5,7},{6,4},{7,5},{8,10},{9,11},{10,... | collective-permute-start | bytes 393224 | tf_op jit(solution)/shard_map/ppermute | solution.py:29
  38.7 11.2 %collective-permute-start.10 = (bf16[64,1024]{1,0:T(8,128)(2,1)S(1)}, bf16[64,1024]{1,0:T(8,128)(2,1)S(1)}, u32[]{:S(2)}, u32[]{:S(2)}) collective-permute-start(bf16[64,1024]{1,0:T(8,128)(2,1)S(1)} %fusion.40), channel_id=1, source_target_pairs={{0,2},{1,3},{2,0},{3,1},{4,6},{5,7},{6,4},{7,5},{8,10},{9,11},{10,... | collective-permute-start | bytes 393224 | tf_op jit(solution)/shard_map/ppermute | solution.py:29

commit v19 on v18

--- a/solution.py
+++ b/solution.py
@@ -7,8 +7,10 @@
 
 
 def local(embeds, weights, pos_ids, pos_count):
+    n_groups = lax.axis_size("groups")
     n_label = lax.axis_size("label")
     n_dp = lax.axis_size("dp")
+    me_group = lax.axis_index("groups")
     me_label = lax.axis_index("label")
     me_dp = lax.axis_index("dp")
     rows_dev, width = embeds.shape
@@ -27,6 +29,9 @@
 
     def to_dp(x, k):
         return lax.ppermute(x, "dp", [(i, i ^ k) for i in range(n_dp)])
+
+    def to_group(x):
+        return lax.ppermute(x, "groups", [(i, i ^ 1) for i in range(n_groups)])
 
     def to_label(x, by):
         return lax.ppermute(x, "label", [(i, (i + by) % n_label) for i in range(n_label)])
@@ -49,13 +54,16 @@
         )
 
     late = n_dp - 1
-    pieces = {0: weights}
-    for k in range(1, n_dp):
+    half = ch_dev // 2
+    mine_at, other_at = me_group * half, (1 - me_group) * half
+    mine = lax.dynamic_slice_in_dim(weights, mine_at, half, axis=0)
+    near_source, _ = lax.optimization_barrier((weights, ids))
+    near = to_dp(near_source, 1)
+    parts, others = {}, {}
+    for k in range(2, n_dp):
         step = k & -k
-        source = pieces[k ^ step]
-        if k == 1:
-            source, _ = lax.optimization_barrier((source, ids))
-        pieces[k] = to_dp(source, step)
+        if step == k:
+            parts[k] = to_dp(mine, k)
     d_own, g_w = {}, {}
     joined = [jnp.zeros((stretch, width), weights.dtype)]
     next_rows = to_label(embeds, -1)
@@ -83,21 +91,34 @@
     next_ids = to_label(ids, -1)
     join(weights, 0)
     for k in range(2, n_dp):
-        if k & -k == k:
-            pieces[k] = in_turn(pieces[k])
-            last[0] = pieces[k]
-    next_rows, next_ids, pieces[1], _ = lax.optimization_barrier((next_rows, next_ids, pieces[1], last[0]))
-    for k in range(1, late):
-        join(pieces[k], k * ch_dev)
+        step = k & -k
+        if step < k:
+            parts[k] = to_dp(parts[k ^ step], step)
+        parts[k] = in_turn(parts[k])
+        last[0] = parts[k]
+        others[k] = to_group(parts[k])
+
+    def join_halves(k):
+        join(parts[k], k * ch_dev + mine_at)
+        join(others[k], k * ch_dev + other_at)
+
+    received = [others[k] for k in range(2, late)]
+    next_rows, next_ids, near, received, _ = lax.optimization_barrier(
+        (next_rows, next_ids, near, received, last[0])
+    )
+    join(near, ch_dev)
+    for k in range(2, late):
+        others[k] = received[k - 2]
+        join_halves(k)
     early = joined[0][:late * ch_dev]
     d_early = delta_of(next_rows, next_ids, early, list(range(late)))
     last[0] = d_early
-    pieces[late] = in_turn(pieces[late])
-    join(pieces[late], late * ch_dev)
+    others[late] = in_turn(others[late])
+    join_halves(late)
     joined = joined[0]
-    own_delta(late, pieces[late])
+    own_delta(late, piece_of(late))
     own_grad(late)
-    d_late = delta_of(next_rows, next_ids, in_turn(pieces[late]), [late])
+    d_late = delta_of(next_rows, next_ids, in_turn(piece_of(late)), [late])
     d_next = jnp.concatenate([d_early, d_late], axis=1)
     last[0] = d_late
     add_next(late)

time: 50.9 us -> 50.6 us (level)
  waiting for transfers between devices: 18.8 us -> 13.1 us
  starting transfers between devices: 16.5 us -> 20.9 us
  local copies, waits for them, and re-layouts: 1.24 us -> 2.22 us
    ppermute x8, waiting for transfers between devices: 12.5 us -> 8.6 us  [to_dp(): return lax.ppermute(x, 'dp', [(i, i ^ k) for i in range(n_dp)])]
    ppermute x3, waiting for transfers between devices: 6.37 us -> 2.79 us  [to_label(): lax.ppermute(x, 'label', [(i, (i + by) % n_label) for i in range(n_label)])]
    ppermute x0 -> x2, starting transfers between devices: none -> 3.09 us  [to_group(): return lax.ppermute(x, 'groups', [(i, i ^ 1) for i in range(n_groups)])]
    ppermute x0 -> x2, waiting for transfers between devices: none -> 1.71 us  [to_group(): return lax.ppermute(x, 'groups', [(i, i ^ 1) for i in range(n_groups)])]
    dynamic_slice x0 -> x1, local copies, waits for them, and re-layouts: none -> 0.91 us  [local(): mine = lax.dynamic_slice_in_dim(weights, mine_at, half, axis=0)]
    ppermute x8, starting transfers between devices: 13.6 us -> 14.3 us  [to_dp(): return lax.ppermute(x, 'dp', [(i, i ^ k) for i in range(n_dp)])]
    ppermute x3, starting transfers between devices: 2.93 us -> 3.47 us  [to_label(): lax.ppermute(x, 'label', [(i, (i + by) % n_label) for i in range(n_label)])]
    dynamic_update_slice x4 -> x6, local copies, waits for them, and re-layouts: 1.12 us -> 1.15 us  [join(): joined[0] = lax.dynamic_update_slice_in_dim(joined[0], piece, at, axis=0)]
  transfers between devices with their start and end apart: 11 -> 13, of which waited for: 5 -> 6; matrix products, arithmetic and copies ran while one was open for 20% -> 23% of each run, Pallas kernels for 0% -> 0%
where the time goes in v19:
time: 50.6 us; the launch traced here: 50.4 us
  starting transfers between devices  20.9 us (41%)
  waiting for transfers between devices  13.1 us (26%)
  matrix products  9.72 us (19%)
  other arithmetic  3.58 us (7%)
  local copies, waits for them, and re-layouts  2.22 us (4%)
  between operations  0.9 us (2%)
    ppermute x8, starting transfers between devices, to_dp(): return lax.ppermute(x, 'dp', [(i, i ^ k) for i in range(n_dp)])  14.3 us
    ppermute x8, waiting for transfers between devices, to_dp(): return lax.ppermute(x, 'dp', [(i, i ^ k) for i in range(n_dp)])  8.6 us
    dot_general x6, matrix products, delta_of(): lax.dot_general(rows, piece, (((1,), (1,)), ((), ())), preferred_element_...  4.63 us
    ppermute x3, starting transfers between devices, to_label(): lax.ppermute(x, 'label', [(i, (i + by) % n_label) for i in range(n_label)])  3.47 us
    ppermute x2, starting transfers between devices, to_group(): return lax.ppermute(x, 'groups', [(i, i ^ 1) for i in range(n_groups)])  3.09 us
    dot_general x8, matrix products, grad_w_of(): lax.dot_general(delta, rows, (((0,), (0,)), ((), ())), preferred_element_...  3.05 us
    ppermute x3, waiting for transfers between devices, to_label(): lax.ppermute(x, 'label', [(i, (i + by) % n_label) for i in range(n_label)])  2.79 us
    convert_element_type x1, other arithmetic, local(): grad_x = (grad_x + in_turn(back).astype(jnp.float32)).astype(jnp.bfloat16)  1.75 us
  transfers between devices with their start and end apart: 13, of which 6 were waited for; matrix products, arithmetic and copies ran while one was open for 23% of the time, Pallas kernels for 0%

profile of v19, /device:TPU:0, one launch (start us, length us, event | category | flops | bytes accessed | tf_op | source)
XLA Modules:
  0.0 50.4 jit_solution(6169026786657790756)
XLA Ops:
  0.6 2.4 %collective-permute-start = (bf16[768,1024]{1,0:T(8,128)(2,1)}, bf16[768,1024]{1,0:T(8,128)(2,1)S(1)}, u32[]{:S(2)}, u32[]{:S(2)}) collective-permute-start(bf16[768,1024]{1,0:T(8,128)(2,1)} %param.4), channel_id=1, source_target_pairs={{0,12},{4,0},{8,4},{12,8},{1,13},{5,1},{9,5},{13,9},{2,14},{6,2},{... | collective-permute-start | bytes 4718600 | tf_op jit(solution)/shard_map/ppermute | solution.py:37
  3.1 0.9 %constant_dynamic-slice_fusion.8 = bf16[64,1024]{1,0:T(8,128)(2,1)S(1)} fusion(bf16[128,1024]{1,0:T(8,128)(2,1)} %param.5, s32[]{:T(128)S(6)} %select_n.62), kind=kLoop, calls=%fused_computation.81 | loop fusion | bytes 262148 | tf_op jit(solution)/shard_map/dynamic_slice | solution.py:59
  4.0 2.7 %collective-permute-start.3 = (bf16[64,1024]{1,0:T(8,128)(2,1)S(1)}, bf16[64,1024]{1,0:T(8,128)(2,1)S(1)}, u32[]{:S(2)}, u32[]{:S(2)}) collective-permute-start(bf16[64,1024]{1,0:T(8,128)(2,1)S(1)} %constant_dynamic-slice_fusion.8), channel_id=1, source_target_pairs={{0,2},{1,3},{2,0},{3,1},{4,6},{5,7},{6,4},{7,5},{8,10},{9,11},{10,... | collective-permute-start | bytes 393224 | tf_op jit(solution)/shard_map/ppermute | solution.py:31
  6.6 0.7 %fusion.41 = s32[768,8]{0,1:T(8,128)S(1)} fusion(s32[768,8]{0,1:T(8,128)} %param.6, s32[768]{0:T(1024)} %param.7), kind=kLoop, calls=%fused_computation.67 | loop fusion | flops 12288 | bytes 52224 | tf_op jit(solution)/shard_map/jit(_where)/select_n | solution.py:23
  7.4 1.6 %collective-permute-start.2 = (bf16[128,1024]{1,0:T(8,128)(2,1)}, bf16[128,1024]{1,0:T(8,128)(2,1)S(1)}, u32[]{:S(2)}, u32[]{:S(2)}) collective-permute-start(bf16[128,1024]{1,0:T(8,128)(2,1)} %param.5), channel_id=1, source_target_pairs={{0,1},{1,0},{2,3},{3,2},{4,5},{5,4},{6,7},{7,6},{8,9},{9,8},{10,11... | collective-permute-start | bytes 786440 | tf_op jit(solution)/shard_map/ppermute | solution.py:31
  9.0 3.8 %collective-permute-done.3 = bf16[64,1024]{1,0:T(8,128)(2,1)S(1)} collective-permute-done((bf16[64,1024]{1,0:T(8,128)(2,1)S(1)}, bf16[64,1024]{1,0:T(8,128)(2,1)S(1)}, u32[]{:S(2)}, u32[]{:S(2)}) %collective-permute-start.3) | collective-permute-done | bytes 131104 | tf_op jit(solution)/shard_map/ppermute | solution.py:31
  12.8 0.7 %collective-permute-start.5 = (bf16[64,1024]{1,0:T(8,128)(2,1)S(1)}, bf16[64,1024]{1,0:T(8,128)(2,1)S(1)}, u32[]{:S(2)}, u32[]{:S(2)}) collective-permute-start(bf16[64,1024]{1,0:T(8,128)(2,1)S(1)} %collective-permute-done.3), channel_id=1, source_target_pairs={{0,1},{1,0},{2,3},{3,2},{4,5},{5,4},{6,7},{7,6},{8,9},{9,8},{10,11... | collective-permute-start | bytes 393224 | tf_op jit(solution)/shard_map/ppermute | solution.py:31
  13.5 1.5 %collective-permute-start.4 = (bf16[64,1024]{1,0:T(8,128)(2,1)S(1)}, bf16[64,1024]{1,0:T(8,128)(2,1)S(1)}, u32[]{:S(2)}, u32[]{:S(2)}) collective-permute-start(bf16[64,1024]{1,0:T(8,128)(2,1)S(1)} %collective-permute-done.3), channel_id=1, source_target_pairs={{0,16},{16,0},{1,17},{17,1},{2,18},{18,2},{3,19},{19,3},{4,20},{20... | collective-permute-start | bytes 393224 | tf_op jit(solution)/shard_map/ppermute | solution.py:34
  15.0 0.6 %collective-permute-start.1 = (s32[768,8]{0,1:T(8,128)S(1)}, s32[768,8]{0,1:T(8,128)S(1)}, u32[]{:S(2)}, u32[]{:S(2)}) collective-permute-start(s32[768,8]{0,1:T(8,128)S(1)} %fusion.41), channel_id=1, source_target_pairs={{0,12},{4,0},{8,4},{12,8},{1,13},{5,1},{9,5},{13,9},{2,14},{6,2},{... | collective-permute-start | bytes 73736 | tf_op jit(solution)/shard_map/ppermute | solution.py:37
  15.6 1.1 %dynamic_update_slice.18 = bf16[512,1024]{1,0:T(8,128)(2,1)S(1)} pad(bf16[128,1024]{1,0:T(8,128)(2,1)} %param.5, bf16[]{:T(256)} %constant.72.clone.1), padding=0_384x0_0 | pad | bytes 1310722 | tf_op jit(solution)/shard_map/dynamic_update_slice | solution.py:72
  16.7 0.1 fusion.57
  16.7 2.8 %collective-permute-done.5 = bf16[64,1024]{1,0:T(8,128)(2,1)S(1)} collective-permute-done((bf16[64,1024]{1,0:T(8,128)(2,1)S(1)}, bf16[64,1024]{1,0:T(8,128)(2,1)S(1)}, u32[]{:S(2)}, u32[]{:S(2)}) %collective-permute-start.5) | collective-permute-done | bytes 131104 | tf_op jit(solution)/shard_map/ppermute | solution.py:31
  19.6 1.6 %collective-permute-start.6 = (bf16[64,1024]{1,0:T(8,128)(2,1)S(1)}, bf16[64,1024]{1,0:T(8,128)(2,1)S(1)}, u32[]{:S(2)}, u32[]{:S(2)}) collective-permute-start(bf16[64,1024]{1,0:T(8,128)(2,1)S(1)} %collective-permute-done.5), channel_id=1, source_target_pairs={{0,16},{16,0},{1,17},{17,1},{2,18},{18,2},{3,19},{19,3},{4,20},{20... | collective-permute-start | bytes 393224 | tf_op jit(solution)/shard_map/ppermute | solution.py:34
  21.1 0.3 collective-permute-done.1
  21.5 0.0 collective-permute-done.4
  21.5 0.0 collective-permute-done.2
  21.5 0.0 collective-permute-done
  21.6 0.1 fusion.51
  21.6 1.1 %fusion.4 = bf16[768,384]{0,1:T(8,128)(2,1)S(1)} fusion(bf16[768,1024]{1,0:T(8,128)(2,1)S(1)} %collective-permute-done, bf16[512,1024]{1,0:T(8,128)(2,1)S(1)} %constant_dynamic-update-slice_fusion.2, s32[768]{0:T(1024)S(1)} %get-tuple-element.67, s32[768]{0:T(1024)S(1)} %get-tuple-element.68, s32[768]{0:T(1024)S(1)} %get-tuple-element.69, ...), kind=kOutput, calls=%fused_computation.7 | convolution fusion | flops 606633984 | bytes 2962432 | tf_op jit(solution)/shard_map/dot_general | solution.py:46
  22.8 0.0 copy-start
  22.8 1.7 %collective-permute-done.6 = bf16[64,1024]{1,0:T(8,128)(2,1)S(1)} collective-permute-done((bf16[64,1024]{1,0:T(8,128)(2,1)S(1)}, bf16[64,1024]{1,0:T(8,128)(2,1)S(1)}, u32[]{:S(2)}, u32[]{:S(2)}) %collective-permute-start.6) | collective-permute-done | bytes 131104 | tf_op jit(solution)/shard_map/ppermute | solution.py:34
  24.5 0.1 fusion.58
  24.6 0.0 copy-done
  24.6 0.7 %fusion.37 = bf16[768,128]{0,1:T(8,128)(2,1)S(1)} fusion(bf16[128,1024]{1,0:T(8,128)(2,1)S(1)} %get-tuple-element.42, bf16[768,1024]{1,0:T(8,128)(2,1)S(1)} %copy-done, s32[768]{0:T(1024)S(1)} %get-tuple-element.65), kind=kOutput, calls=%fused_computation.50 | convolution fusion | flops 202014720 | bytes 2034688 | tf_op jit(solution)/shard_map/dot_general | solution.py:46
  25.4 0.4 fusion.60
  25.7 0.7 %fusion.36 = bf16[768,128]{0,1:T(8,128)(2,1)S(1)} fusion(bf16[768,1024]{1,0:T(8,128)(2,1)S(1)} %collective-permute-done, bf16[128,1024]{1,0:T(8,128)(2,1)S(1)} %get-tuple-element.42, s32[768]{0:T(1024)S(1)} %get-tuple-element.66), kind=kOutput, calls=%fused_computation.49 | convolution fusion | flops 202014720 | bytes 2034688 | tf_op jit(solution)/shard_map/dot_general | solution.py:46
  26.5 0.1 pad_maximum_fusion
  26.5 0.4 fusion.8
  26.9 1.0 %convolution_convert_fusion = bf16[768,1024]{1,0:T(8,128)(2,1)S(1)} fusion(bf16[768,512]{0,1:T(8,128)(2,1)S(1)} %pad_maximum_fusion, bf16[512,1024]{1,0:T(8,128)(2,1)S(1)} %constant_dynamic-update-slice_fusion), kind=kOutput, calls=%fused_computation.1 | convolution fusion | flops 806092800 | bytes 3407872 | tf_op jit(solution)/shard_map/dot_general | solution.py:125
  27.9 0.4 collective-permute-start.10
  28.4 1.9 %collective-permute-start.8 = (bf16[64,1024]{1,0:T(8,128)(2,1)S(1)}, bf16[64,1024]{1,0:T(8,128)(2,1)S(1)}, u32[]{:S(2)}, u32[]{:S(2)}) collective-permute-start(bf16[64,1024]{1,0:T(8,128)(2,1)S(1)} %slice.73), channel_id=1, source_target_pairs={{0,1},{1,0},{2,3},{3,2},{4,5},{5,4},{6,7},{7,6},{8,9},{9,8},{10,11... | collective-permute-start | bytes 393224 | tf_op jit(solution)/shard_map/ppermute | solution.py:31
  30.3 0.7 %fusion.35 = bf16[768,128]{0,1:T(8,128)(2,1)S(1)} fusion(bf16[128,1024]{1,0:T(8,128)(2,1)S(1)} %get-tuple-element.45, bf16[768,1024]{1,0:T(8,128)(2,1)S(1)} %copy-done, s32[768]{0:T(1024)S(1)} %get-tuple-element.64), kind=kOutput, calls=%fused_computation.48 | convolution fusion | flops 202014720 | bytes 2034688 | tf_op jit(solution)/shard_map/dot_general | solution.py:46
  31.0 0.2 collective-permute-start.7
  31.2 0.4 fusion.61
  31.6 0.4 fusion.7
  32.0 1.9 %collective-permute-start.9 = (bf16[128,1024]{1,0:T(8,128)(2,1)S(1)}, bf16[128,1024]{1,0:T(8,128)(2,1)S(1)}, u32[]{:S(2)}, u32[]{:S(2)}) collective-permute-start(bf16[128,1024]{1,0:T(8,128)(2,1)S(1)} %fusion.7), channel_id=1, source_target_pairs={{0,1},{1,0},{2,3},{3,2},{4,5},{5,4},{6,7},{7,6},{8,9},{9,8},{10,11... | collective-permute-start | bytes 786440 | tf_op jit(solution)/shard_map/ppermute | solution.py:31
  33.9 0.7 %fusion.34 = bf16[768,128]{0,1:T(8,128)(2,1)S(1)} fusion(bf16[128,1024]{1,0:T(8,128)(2,1)S(1)} %get-tuple-element.48, bf16[768,1024]{1,0:T(8,128)(2,1)S(1)} %copy-done, s32[768]{0:T(1024)S(1)} %get-tuple-element.63), kind=kOutput, calls=%fused_computation.47 | convolution fusion | flops 202014720 | bytes 2034688 | tf_op jit(solution)/shard_map/dot_general | solution.py:46
  34.6 0.4 fusion.62
  35.0 0.4 fusion.6
  35.4 0.0 collective-permute-done.8
  35.4 2.7 %collective-permute-start.11 = (bf16[64,1024]{1,0:T(8,128)(2,1)S(1)}, bf16[64,1024]{1,0:T(8,128)(2,1)S(1)}, u32[]{:S(2)}, u32[]{:S(2)}) collective-permute-start(bf16[64,1024]{1,0:T(8,128)(2,1)S(1)} %fusion.39), channel_id=1, source_target_pairs={{0,2},{1,3},{2,0},{3,1},{4,6},{5,7},{6,4},{7,5},{8,10},{9,11},{10,... | collective-permute-start | bytes 393224 | tf_op jit(solution)/shard_map/ppermute | solution.py:31
  38.1 0.0 collective-permute-done.7
  38.1 2.7 %collective-permute-start.12 = (bf16[64,1024]{1,0:T(8,128)(2,1)S(1)}, bf16[64,1024]{1,0:T(8,128)(2,1)S(1)}, u32[]{:S(2)}, u32[]{:S(2)}) collective-permute-start(bf16[64,1024]{1,0:T(8,128)(2,1)S(1)} %fusion.40), channel_id=1, source_target_pairs={{0,2},{1,3},{2,0},{3,1},{4,6},{5,7},{6,4},{7,5},{8,10},{9,11},{10,... | collective-permute-start | bytes 393224 | tf_op jit(solution)/shard_map/ppermute | solution.py:31
  40.9 0.7 %fusion.33 = bf16[768,128]{0,1:T(8,128)(2,1)S(1)} fusion(bf16[128,1024]{1,0:T(8,128)(2,1)S(1)} %get-tuple-element.54, bf16[768,1024]{1,0:T(8,128)(2,1)S(1)} %copy-done, s32[768]{0:T(1024)S(1)} %get-tuple-element.62), kind=kOutput, calls=%fused_computation.46 | convolution fusion | flops 202014720 | bytes 2034688 | tf_op jit(solution)/shard_map/dot_general | solution.py:46
  41.6 0.1 pad_maximum_fusion.1
  41.7 0.4 fusion.63
  42.0 1.0 %fusion.64 = f32[768,1024]{1,0:T(8,128)S(1)} fusion(bf16[768,512]{0,1:T(8,128)(2,1)S(1)} %pad_maximum_fusion.1, bf16[512,1024]{1,0:T(8,128)(2,1)S(1)} %constant_dynamic-update-slice_fusion), kind=kOutput, calls=%fused_computation.106 | convolution fusion | flops 805306368 | bytes 4980736 | tf_op jit(solution)/shard_map/dot_general | solution.py:151
  43.1 0.4 fusion.5
  43.5 1.9 %collective-permute-done.11 = bf16[64,1024]{1,0:T(8,128)(2,1)S(1)} collective-permute-done((bf16[64,1024]{1,0:T(8,128)(2,1)S(1)}, bf16[64,1024]{1,0:T(8,128)(2,1)S(1)}, u32[]{:S(2)}, u32[]{:S(2)}) %collective-permute-start.11) | collective-permute-done | bytes 131104 | tf_op jit(solution)/shard_map/ppermute | solution.py:31
  45.4 2.4 %collective-permute-done.10 = bf16[768,1024]{1,0:T(8,128)(2,1)S(1)} collective-permute-done((bf16[768,1024]{1,0:T(8,128)(2,1)S(1)}, bf16[768,1024]{1,0:T(8,128)(2,1)S(1)}, u32[]{:S(2)}, u32[]{:S(2)}) %collective-permute-start.10) | collective-permute-done | bytes 1572896 | tf_op jit(solution)/shard_map/ppermute | solution.py:37
  47.8 1.8 %add_convert_fusion = bf16[768,1024]{1,0:T(8,128)(2,1)} fusion(f32[768,1024]{1,0:T(8,128)S(1)} %fusion.64, bf16[768,1024]{1,0:T(8,128)(2,1)S(1)} %collective-permute-done.10), kind=kLoop, calls=%fused_computation | loop fusion | flops 2359296 | bytes 6291456 | tf_op jit(solution)/shard_map/convert_element_type | solution.py:162
  49.6 0.0 collective-permute-done.12
  49.6 0.0 collective-permute-done.9
  49.6 0.8 %add_convert_fusion.1 = bf16[128,1024]{1,0:T(8,128)(2,1)} fusion(f32[128,1024]{1,0:T(8,128)S(1)} %fusion.5, bf16[128,1024]{1,0:T(8,128)(2,1)S(1)} %collective-permute-done.9, bf16[64,1024]{1,0:T(8,128)(2,1)S(1)} %collective-permute-done.12, bf16[64,1024]{1,0:T(8,128)(2,1)S(1)} %collective-permute-done.11), kind=kLoop, calls=%fused_computation.54 | loop fusion | flops 1048576 | bytes 1310720 | tf_op jit(solution)/shard_map/convert_element_type | solution.py:169
  (11 shorter events, 0.2 us)
Async XLA Ops:
  0.6 20.8 %collective-permute-start = (bf16[768,1024]{1,0:T(8,128)(2,1)}, bf16[768,1024]{1,0:T(8,128)(2,1)S(1)}, u32[]{:S(2)}, u32[]{:S(2)}) collective-permute-start(bf16[768,1024]{1,0:T(8,128)(2,1)} %param.4), channel_id=1, source_target_pairs={{0,12},{4,0},{8,4},{12,8},{1,13},{5,1},{9,5},{13,9},{2,14},{6,2},{... | collective-permute-start | bytes 4718600 | tf_op jit(solution)/shard_map/ppermute | solution.py:37
  4.0 8.8 %collective-permute-start.3 = (bf16[64,1024]{1,0:T(8,128)(2,1)S(1)}, bf16[64,1024]{1,0:T(8,128)(2,1)S(1)}, u32[]{:S(2)}, u32[]{:S(2)}) collective-permute-start(bf16[64,1024]{1,0:T(8,128)(2,1)S(1)} %constant_dynamic-slice_fusion.8), channel_id=1, source_target_pairs={{0,2},{1,3},{2,0},{3,1},{4,6},{5,7},{6,4},{7,5},{8,10},{9,11},{10,... | collective-permute-start | bytes 393224 | tf_op jit(solution)/shard_map/ppermute | solution.py:31
  7.4 14.1 %collective-permute-start.2 = (bf16[128,1024]{1,0:T(8,128)(2,1)}, bf16[128,1024]{1,0:T(8,128)(2,1)S(1)}, u32[]{:S(2)}, u32[]{:S(2)}) collective-permute-start(bf16[128,1024]{1,0:T(8,128)(2,1)} %param.5), channel_id=1, source_target_pairs={{0,1},{1,0},{2,3},{3,2},{4,5},{5,4},{6,7},{7,6},{8,9},{9,8},{10,11... | collective-permute-start | bytes 786440 | tf_op jit(solution)/shard_map/ppermute | solution.py:31
  12.8 6.8 %collective-permute-start.5 = (bf16[64,1024]{1,0:T(8,128)(2,1)S(1)}, bf16[64,1024]{1,0:T(8,128)(2,1)S(1)}, u32[]{:S(2)}, u32[]{:S(2)}) collective-permute-start(bf16[64,1024]{1,0:T(8,128)(2,1)S(1)} %collective-permute-done.3), channel_id=1, source_target_pairs={{0,1},{1,0},{2,3},{3,2},{4,5},{5,4},{6,7},{7,6},{8,9},{9,8},{10,11... | collective-permute-start | bytes 393224 | tf_op jit(solution)/shard_map/ppermute | solution.py:31
  13.5 8.0 %collective-permute-start.4 = (bf16[64,1024]{1,0:T(8,128)(2,1)S(1)}, bf16[64,1024]{1,0:T(8,128)(2,1)S(1)}, u32[]{:S(2)}, u32[]{:S(2)}) collective-permute-start(bf16[64,1024]{1,0:T(8,128)(2,1)S(1)} %collective-permute-done.3), channel_id=1, source_target_pairs={{0,16},{16,0},{1,17},{17,1},{2,18},{18,2},{3,19},{19,3},{4,20},{20... | collective-permute-start | bytes 393224 | tf_op jit(solution)/shard_map/ppermute | solution.py:34
  15.0 6.5 %collective-permute-start.1 = (s32[768,8]{0,1:T(8,128)S(1)}, s32[768,8]{0,1:T(8,128)S(1)}, u32[]{:S(2)}, u32[]{:S(2)}) collective-permute-start(s32[768,8]{0,1:T(8,128)S(1)} %fusion.41), channel_id=1, source_target_pairs={{0,12},{4,0},{8,4},{12,8},{1,13},{5,1},{9,5},{13,9},{2,14},{6,2},{... | collective-permute-start | bytes 73736 | tf_op jit(solution)/shard_map/ppermute | solution.py:37
  19.6 5.0 %collective-permute-start.6 = (bf16[64,1024]{1,0:T(8,128)(2,1)S(1)}, bf16[64,1024]{1,0:T(8,128)(2,1)S(1)}, u32[]{:S(2)}, u32[]{:S(2)}) collective-permute-start(bf16[64,1024]{1,0:T(8,128)(2,1)S(1)} %collective-permute-done.5), channel_id=1, source_target_pairs={{0,16},{16,0},{1,17},{17,1},{2,18},{18,2},{3,19},{19,3},{4,20},{20... | collective-permute-start | bytes 393224 | tf_op jit(solution)/shard_map/ppermute | solution.py:34
  22.8 1.9 %copy-start = (bf16[768,1024]{1,0:T(8,128)(2,1)S(1)}, bf16[768,1024]{1,0:T(8,128)(2,1)}, u32[]{:S(2)}) copy-start(bf16[768,1024]{1,0:T(8,128)(2,1)} %param.4) | copy-start | bytes 4718596
  27.9 19.9 %collective-permute-start.10 = (bf16[768,1024]{1,0:T(8,128)(2,1)S(1)}, bf16[768,1024]{1,0:T(8,128)(2,1)S(1)}, u32[]{:S(2)}, u32[]{:S(2)}) collective-permute-start(bf16[768,1024]{1,0:T(8,128)(2,1)S(1)} %convolution_convert_fusion), channel_id=1, source_target_pairs={{0,4},{4,8},{8,12},{12,0},{1,5},{5,9},{9,13},{13,1},{2,6},{6,10},{... | collective-permute-start | bytes 4718600 | tf_op jit(solution)/shard_map/ppermute | solution.py:37
  28.4 7.0 %collective-permute-start.8 = (bf16[64,1024]{1,0:T(8,128)(2,1)S(1)}, bf16[64,1024]{1,0:T(8,128)(2,1)S(1)}, u32[]{:S(2)}, u32[]{:S(2)}) collective-permute-start(bf16[64,1024]{1,0:T(8,128)(2,1)S(1)} %slice.73), channel_id=1, source_target_pairs={{0,1},{1,0},{2,3},{3,2},{4,5},{5,4},{6,7},{7,6},{8,9},{9,8},{10,11... | collective-permute-start | bytes 393224 | tf_op jit(solution)/shard_map/ppermute | solution.py:31
  31.0 7.1 %collective-permute-start.7 = (bf16[64,1024]{1,0:T(8,128)(2,1)S(1)}, bf16[64,1024]{1,0:T(8,128)(2,1)S(1)}, u32[]{:S(2)}, u32[]{:S(2)}) collective-permute-start(bf16[64,1024]{1,0:T(8,128)(2,1)S(1)} %slice.74), channel_id=1, source_target_pairs={{0,1},{1,0},{2,3},{3,2},{4,5},{5,4},{6,7},{7,6},{8,9},{9,8},{10,11... | collective-permute-start | bytes 393224 | tf_op jit(solution)/shard_map/ppermute | solution.py:31
  32.0 17.6 %collective-permute-start.9 = (bf16[128,1024]{1,0:T(8,128)(2,1)S(1)}, bf16[128,1024]{1,0:T(8,128)(2,1)S(1)}, u32[]{:S(2)}, u32[]{:S(2)}) collective-permute-start(bf16[128,1024]{1,0:T(8,128)(2,1)S(1)} %fusion.7), channel_id=1, source_target_pairs={{0,1},{1,0},{2,3},{3,2},{4,5},{5,4},{6,7},{7,6},{8,9},{9,8},{10,11... | collective-permute-start | bytes 786440 | tf_op jit(solution)/shard_map/ppermute | solution.py:31
  35.4 10.0 %collective-permute-start.11 = (bf16[64,1024]{1,0:T(8,128)(2,1)S(1)}, bf16[64,1024]{1,0:T(8,128)(2,1)S(1)}, u32[]{:S(2)}, u32[]{:S(2)}) collective-permute-start(bf16[64,1024]{1,0:T(8,128)(2,1)S(1)} %fusion.39), channel_id=1, source_target_pairs={{0,2},{1,3},{2,0},{3,1},{4,6},{5,7},{6,4},{7,5},{8,10},{9,11},{10,... | collective-permute-start | bytes 393224 | tf_op jit(solution)/shard_map/ppermute | solution.py:31
  38.1 11.4 %collective-permute-start.12 = (bf16[64,1024]{1,0:T(8,128)(2,1)S(1)}, bf16[64,1024]{1,0:T(8,128)(2,1)S(1)}, u32[]{:S(2)}, u32[]{:S(2)}) collective-permute-start(bf16[64,1024]{1,0:T(8,128)(2,1)S(1)} %fusion.40), channel_id=1, source_target_pairs={{0,2},{1,3},{2,0},{3,1},{4,6},{5,7},{6,4},{7,5},{8,10},{9,11},{10,... | collective-permute-start | bytes 393224 | tf_op jit(solution)/shard_map/ppermute | solution.py:31

commit v20 on v19

--- a/solution.py
+++ b/solution.py
@@ -113,6 +113,7 @@
     early = joined[0][:late * ch_dev]
     d_early = delta_of(next_rows, next_ids, early, list(range(late)))
     last[0] = d_early
+    own_delta(1, piece_of(1))
     others[late] = in_turn(others[late])
     join_halves(late)
     joined = joined[0]
@@ -127,7 +128,8 @@
     back = to_label(theirs, 1)
     second = in_turn(g_w[late])
     for k in range(1, late):
-        own_delta(k, piece_of(k))
+        if k > 1:
+            own_delta(k, piece_of(k))
         own_grad(k)
         add_next(k)
 

time: 50.6 us -> 50.6 us (level)
  waiting for transfers between devices: 13.1 us -> 12.3 us
    ppermute x2, waiting for transfers between devices: 1.71 us -> 0.69 us  [to_group(): return lax.ppermute(x, 'groups', [(i, i ^ 1) for i in range(n_groups)])]
    ppermute x8, starting transfers between devices: 14.3 us -> 15 us  [to_dp(): return lax.ppermute(x, 'dp', [(i, i ^ k) for i in range(n_dp)])]
where the time goes in v20:
time: 50.6 us; the launch traced here: 50.4 us
  starting transfers between devices  21.4 us (42%)
  waiting for transfers between devices  12.3 us (24%)
  matrix products  9.7 us (19%)
  other arithmetic  3.58 us (7%)
  local copies, waits for them, and re-layouts  2.49 us (5%)
  between operations  0.9 us (2%)
    ppermute x8, starting transfers between devices, to_dp(): return lax.ppermute(x, 'dp', [(i, i ^ k) for i in range(n_dp)])  15 us
    ppermute x8, waiting for transfers between devices, to_dp(): return lax.ppermute(x, 'dp', [(i, i ^ k) for i in range(n_dp)])  8.58 us
    dot_general x6, matrix products, delta_of(): lax.dot_general(rows, piece, (((1,), (1,)), ((), ())), preferred_element_...  4.62 us
    ppermute x3, starting transfers between devices, to_label(): lax.ppermute(x, 'label', [(i, (i + by) % n_label) for i in range(n_label)])  3.27 us
    ppermute x2, starting transfers between devices, to_group(): return lax.ppermute(x, 'groups', [(i, i ^ 1) for i in range(n_groups)])  3.09 us
    dot_general x8, matrix products, grad_w_of(): lax.dot_general(delta, rows, (((0,), (0,)), ((), ())), preferred_element_...  3.05 us
    ppermute x3, waiting for transfers between devices, to_label(): lax.ppermute(x, 'label', [(i, (i + by) % n_label) for i in range(n_label)])  3.01 us
    convert_element_type x1, other arithmetic, local(): grad_x = (grad_x + in_turn(back).astype(jnp.float32)).astype(jnp.bfloat16)  1.75 us
  transfers between devices with their start and end apart: 13, of which 6 were waited for; matrix products, arithmetic and copies ran while one was open for 23% of the time, Pallas kernels for 0%

profile of v20, /device:TPU:0, one launch (start us, length us, event | category | flops | bytes accessed | tf_op | source)
XLA Modules:
  0.0 50.4 jit_solution(15241748377705513836)
XLA Ops:
  0.6 2.4 %collective-permute-start = (bf16[768,1024]{1,0:T(8,128)(2,1)}, bf16[768,1024]{1,0:T(8,128)(2,1)S(1)}, u32[]{:S(2)}, u32[]{:S(2)}) collective-permute-start(bf16[768,1024]{1,0:T(8,128)(2,1)} %param.4), channel_id=1, source_target_pairs={{0,12},{4,0},{8,4},{12,8},{1,13},{5,1},{9,5},{13,9},{2,14},{6,2},{... | collective-permute-start | bytes 4718600 | tf_op jit(solution)/shard_map/ppermute | solution.py:37
  3.1 0.9 %constant_dynamic-slice_fusion.8 = bf16[64,1024]{1,0:T(8,128)(2,1)S(1)} fusion(bf16[128,1024]{1,0:T(8,128)(2,1)} %param.5, s32[]{:T(128)S(6)} %select_n.62), kind=kLoop, calls=%fused_computation.81 | loop fusion | bytes 262148 | tf_op jit(solution)/shard_map/dynamic_slice | solution.py:59
  4.0 2.7 %collective-permute-start.3 = (bf16[64,1024]{1,0:T(8,128)(2,1)S(1)}, bf16[64,1024]{1,0:T(8,128)(2,1)S(1)}, u32[]{:S(2)}, u32[]{:S(2)}) collective-permute-start(bf16[64,1024]{1,0:T(8,128)(2,1)S(1)} %constant_dynamic-slice_fusion.8), channel_id=1, source_target_pairs={{0,2},{1,3},{2,0},{3,1},{4,6},{5,7},{6,4},{7,5},{8,10},{9,11},{10,... | collective-permute-start | bytes 393224 | tf_op jit(solution)/shard_map/ppermute | solution.py:31
  6.6 0.7 %fusion.41 = s32[768,8]{0,1:T(8,128)S(1)} fusion(s32[768,8]{0,1:T(8,128)} %param.6, s32[768]{0:T(1024)} %param.7), kind=kLoop, calls=%fused_computation.67 | loop fusion | flops 12288 | bytes 52224 | tf_op jit(solution)/shard_map/jit(_where)/select_n | solution.py:23
  7.4 1.6 %collective-permute-start.2 = (bf16[128,1024]{1,0:T(8,128)(2,1)}, bf16[128,1024]{1,0:T(8,128)(2,1)S(1)}, u32[]{:S(2)}, u32[]{:S(2)}) collective-permute-start(bf16[128,1024]{1,0:T(8,128)(2,1)} %param.5), channel_id=1, source_target_pairs={{0,1},{1,0},{2,3},{3,2},{4,5},{5,4},{6,7},{7,6},{8,9},{9,8},{10,11... | collective-permute-start | bytes 786440 | tf_op jit(solution)/shard_map/ppermute | solution.py:31
  9.0 3.8 %collective-permute-done.3 = bf16[64,1024]{1,0:T(8,128)(2,1)S(1)} collective-permute-done((bf16[64,1024]{1,0:T(8,128)(2,1)S(1)}, bf16[64,1024]{1,0:T(8,128)(2,1)S(1)}, u32[]{:S(2)}, u32[]{:S(2)}) %collective-permute-start.3) | collective-permute-done | bytes 131104 | tf_op jit(solution)/shard_map/ppermute | solution.py:31
  12.8 0.7 %collective-permute-start.5 = (bf16[64,1024]{1,0:T(8,128)(2,1)S(1)}, bf16[64,1024]{1,0:T(8,128)(2,1)S(1)}, u32[]{:S(2)}, u32[]{:S(2)}) collective-permute-start(bf16[64,1024]{1,0:T(8,128)(2,1)S(1)} %collective-permute-done.3), channel_id=1, source_target_pairs={{0,1},{1,0},{2,3},{3,2},{4,5},{5,4},{6,7},{7,6},{8,9},{9,8},{10,11... | collective-permute-start | bytes 393224 | tf_op jit(solution)/shard_map/ppermute | solution.py:31
  13.5 1.5 %collective-permute-start.4 = (bf16[64,1024]{1,0:T(8,128)(2,1)S(1)}, bf16[64,1024]{1,0:T(8,128)(2,1)S(1)}, u32[]{:S(2)}, u32[]{:S(2)}) collective-permute-start(bf16[64,1024]{1,0:T(8,128)(2,1)S(1)} %collective-permute-done.3), channel_id=1, source_target_pairs={{0,16},{16,0},{1,17},{17,1},{2,18},{18,2},{3,19},{19,3},{4,20},{20... | collective-permute-start | bytes 393224 | tf_op jit(solution)/shard_map/ppermute | solution.py:34
  15.0 0.6 %collective-permute-start.1 = (s32[768,8]{0,1:T(8,128)S(1)}, s32[768,8]{0,1:T(8,128)S(1)}, u32[]{:S(2)}, u32[]{:S(2)}) collective-permute-start(s32[768,8]{0,1:T(8,128)S(1)} %fusion.41), channel_id=1, source_target_pairs={{0,12},{4,0},{8,4},{12,8},{1,13},{5,1},{9,5},{13,9},{2,14},{6,2},{... | collective-permute-start | bytes 73736 | tf_op jit(solution)/shard_map/ppermute | solution.py:37
  15.6 1.1 %dynamic_update_slice.18 = bf16[512,1024]{1,0:T(8,128)(2,1)S(1)} pad(bf16[128,1024]{1,0:T(8,128)(2,1)} %param.5, bf16[]{:T(256)} %constant.72.clone.1), padding=0_384x0_0 | pad | bytes 1310722 | tf_op jit(solution)/shard_map/dynamic_update_slice | solution.py:72
  16.7 0.1 fusion.57
  16.7 2.8 %collective-permute-done.5 = bf16[64,1024]{1,0:T(8,128)(2,1)S(1)} collective-permute-done((bf16[64,1024]{1,0:T(8,128)(2,1)S(1)}, bf16[64,1024]{1,0:T(8,128)(2,1)S(1)}, u32[]{:S(2)}, u32[]{:S(2)}) %collective-permute-start.5) | collective-permute-done | bytes 131104 | tf_op jit(solution)/shard_map/ppermute | solution.py:31
  19.6 1.6 %collective-permute-start.6 = (bf16[64,1024]{1,0:T(8,128)(2,1)S(1)}, bf16[64,1024]{1,0:T(8,128)(2,1)S(1)}, u32[]{:S(2)}, u32[]{:S(2)}) collective-permute-start(bf16[64,1024]{1,0:T(8,128)(2,1)S(1)} %collective-permute-done.5), channel_id=1, source_target_pairs={{0,16},{16,0},{1,17},{17,1},{2,18},{18,2},{3,19},{19,3},{4,20},{20... | collective-permute-start | bytes 393224 | tf_op jit(solution)/shard_map/ppermute | solution.py:34
  21.1 0.3 collective-permute-done.1
  21.5 0.0 collective-permute-done.4
  21.5 0.0 collective-permute-done.2
  21.5 0.0 collective-permute-done
  21.6 0.1 fusion.53
  21.6 0.0 copy-start
  21.7 1.1 %fusion.4 = bf16[768,384]{0,1:T(8,128)(2,1)S(1)} fusion(bf16[768,1024]{1,0:T(8,128)(2,1)S(1)} %collective-permute-done, bf16[512,1024]{1,0:T(8,128)(2,1)S(1)} %constant_dynamic-update-slice_fusion.2, s32[768]{0:T(1024)S(1)} %get-tuple-element.67, s32[768]{0:T(1024)S(1)} %get-tuple-element.68, s32[768]{0:T(1024)S(1)} %get-tuple-element.69, ...), kind=kOutput, calls=%fused_computation.7 | convolution fusion | flops 606633984 | bytes 2962432 | tf_op jit(solution)/shard_map/dot_general | solution.py:46
  22.8 0.3 copy-done
  23.1 0.7 %fusion.37 = bf16[768,128]{0,1:T(8,128)(2,1)S(1)} fusion(bf16[128,1024]{1,0:T(8,128)(2,1)S(1)} %slice.51, bf16[768,1024]{1,0:T(8,128)(2,1)S(1)} %copy-done, s32[768]{0:T(1024)S(1)} %get-tuple-element.65), kind=kOutput, calls=%fused_computation.50 | convolution fusion | flops 202014720 | bytes 2034688 | tf_op jit(solution)/shard_map/dot_general | solution.py:46
  23.8 0.7 %collective-permute-done.6 = bf16[64,1024]{1,0:T(8,128)(2,1)S(1)} collective-permute-done((bf16[64,1024]{1,0:T(8,128)(2,1)S(1)}, bf16[64,1024]{1,0:T(8,128)(2,1)S(1)}, u32[]{:S(2)}, u32[]{:S(2)}) %collective-permute-start.6) | collective-permute-done | bytes 131104 | tf_op jit(solution)/shard_map/ppermute | solution.py:34
  24.5 0.1 fusion.58
  24.6 0.7 %fusion.36 = bf16[768,128]{0,1:T(8,128)(2,1)S(1)} fusion(bf16[128,1024]{1,0:T(8,128)(2,1)S(1)} %get-tuple-element.43, bf16[768,1024]{1,0:T(8,128)(2,1)S(1)} %copy-done, s32[768]{0:T(1024)S(1)} %get-tuple-element.64), kind=kOutput, calls=%fused_computation.49 | convolution fusion | flops 202014720 | bytes 2034688 | tf_op jit(solution)/shard_map/dot_general | solution.py:46
  25.3 0.4 fusion.60
  25.7 0.7 %fusion.35 = bf16[768,128]{0,1:T(8,128)(2,1)S(1)} fusion(bf16[768,1024]{1,0:T(8,128)(2,1)S(1)} %collective-permute-done, bf16[128,1024]{1,0:T(8,128)(2,1)S(1)} %get-tuple-element.43, s32[768]{0:T(1024)S(1)} %get-tuple-element.66), kind=kOutput, calls=%fused_computation.48 | convolution fusion | flops 202014720 | bytes 2034688 | tf_op jit(solution)/shard_map/dot_general | solution.py:46
  26.4 0.1 pad_maximum_fusion
  26.5 0.4 fusion.8
  26.9 1.0 %convolution_convert_fusion = bf16[768,1024]{1,0:T(8,128)(2,1)S(1)} fusion(bf16[768,512]{0,1:T(8,128)(2,1)S(1)} %pad_maximum_fusion, bf16[512,1024]{1,0:T(8,128)(2,1)S(1)} %constant_dynamic-update-slice_fusion), kind=kOutput, calls=%fused_computation.1 | convolution fusion | flops 806092800 | bytes 3407872 | tf_op jit(solution)/shard_map/dot_general | solution.py:126
  27.9 0.2 collective-permute-start.10
  28.1 1.9 %collective-permute-start.8 = (bf16[64,1024]{1,0:T(8,128)(2,1)S(1)}, bf16[64,1024]{1,0:T(8,128)(2,1)S(1)}, u32[]{:S(2)}, u32[]{:S(2)}) collective-permute-start(bf16[64,1024]{1,0:T(8,128)(2,1)S(1)} %slice.73), channel_id=1, source_target_pairs={{0,1},{1,0},{2,3},{3,2},{4,5},{5,4},{6,7},{7,6},{8,9},{9,8},{10,11... | collective-permute-start | bytes 393224 | tf_op jit(solution)/shard_map/ppermute | solution.py:31
  30.0 0.2 collective-permute-start.7
  30.2 0.4 fusion.61
  30.6 0.4 fusion.7
  31.0 1.9 %collective-permute-start.9 = (bf16[128,1024]{1,0:T(8,128)(2,1)S(1)}, bf16[128,1024]{1,0:T(8,128)(2,1)S(1)}, u32[]{:S(2)}, u32[]{:S(2)}) collective-permute-start(bf16[128,1024]{1,0:T(8,128)(2,1)S(1)} %fusion.7), channel_id=1, source_target_pairs={{0,1},{1,0},{2,3},{3,2},{4,5},{5,4},{6,7},{7,6},{8,9},{9,8},{10,11... | collective-permute-start | bytes 786440 | tf_op jit(solution)/shard_map/ppermute | solution.py:31
  32.9 0.7 %fusion.34 = bf16[768,128]{0,1:T(8,128)(2,1)S(1)} fusion(bf16[128,1024]{1,0:T(8,128)(2,1)S(1)} %get-tuple-element.48, bf16[768,1024]{1,0:T(8,128)(2,1)S(1)} %copy-done, s32[768]{0:T(1024)S(1)} %get-tuple-element.63), kind=kOutput, calls=%fused_computation.47 | convolution fusion | flops 202014720 | bytes 2034688 | tf_op jit(solution)/shard_map/dot_general | solution.py:46
  33.7 0.4 fusion.62
  34.0 0.4 fusion.6
  34.4 0.0 collective-permute-done.8
  34.5 3.0 %collective-permute-start.11 = (bf16[64,1024]{1,0:T(8,128)(2,1)S(1)}, bf16[64,1024]{1,0:T(8,128)(2,1)S(1)}, u32[]{:S(2)}, u32[]{:S(2)}) collective-permute-start(bf16[64,1024]{1,0:T(8,128)(2,1)S(1)} %fusion.39), channel_id=1, source_target_pairs={{0,2},{1,3},{2,0},{3,1},{4,6},{5,7},{6,4},{7,5},{8,10},{9,11},{10,... | collective-permute-start | bytes 393224 | tf_op jit(solution)/shard_map/ppermute | solution.py:31
  37.5 0.0 collective-permute-done.7
  37.5 3.1 %collective-permute-start.12 = (bf16[64,1024]{1,0:T(8,128)(2,1)S(1)}, bf16[64,1024]{1,0:T(8,128)(2,1)S(1)}, u32[]{:S(2)}, u32[]{:S(2)}) collective-permute-start(bf16[64,1024]{1,0:T(8,128)(2,1)S(1)} %fusion.40), channel_id=1, source_target_pairs={{0,2},{1,3},{2,0},{3,1},{4,6},{5,7},{6,4},{7,5},{8,10},{9,11},{10,... | collective-permute-start | bytes 393224 | tf_op jit(solution)/shard_map/ppermute | solution.py:31
  40.6 0.7 %fusion.33 = bf16[768,128]{0,1:T(8,128)(2,1)S(1)} fusion(bf16[128,1024]{1,0:T(8,128)(2,1)S(1)} %get-tuple-element.54, bf16[768,1024]{1,0:T(8,128)(2,1)S(1)} %copy-done, s32[768]{0:T(1024)S(1)} %get-tuple-element.62), kind=kOutput, calls=%fused_computation.46 | convolution fusion | flops 202014720 | bytes 2034688 | tf_op jit(solution)/shard_map/dot_general | solution.py:46
  41.4 0.1 pad_maximum_fusion.1
  41.4 0.4 fusion.63
  41.8 1.0 %fusion.64 = f32[768,1024]{1,0:T(8,128)S(1)} fusion(bf16[768,512]{0,1:T(8,128)(2,1)S(1)} %pad_maximum_fusion.1, bf16[512,1024]{1,0:T(8,128)(2,1)S(1)} %constant_dynamic-update-slice_fusion), kind=kOutput, calls=%fused_computation.106 | convolution fusion | flops 805306368 | bytes 4980736 | tf_op jit(solution)/shard_map/dot_general | solution.py:153
  42.8 0.4 fusion.5
  43.2 1.9 %collective-permute-done.11 = bf16[64,1024]{1,0:T(8,128)(2,1)S(1)} collective-permute-done((bf16[64,1024]{1,0:T(8,128)(2,1)S(1)}, bf16[64,1024]{1,0:T(8,128)(2,1)S(1)}, u32[]{:S(2)}, u32[]{:S(2)}) %collective-permute-start.11) | collective-permute-done | bytes 131104 | tf_op jit(solution)/shard_map/ppermute | solution.py:31
  45.1 2.7 %collective-permute-done.10 = bf16[768,1024]{1,0:T(8,128)(2,1)S(1)} collective-permute-done((bf16[768,1024]{1,0:T(8,128)(2,1)S(1)}, bf16[768,1024]{1,0:T(8,128)(2,1)S(1)}, u32[]{:S(2)}, u32[]{:S(2)}) %collective-permute-start.10) | collective-permute-done | bytes 1572896 | tf_op jit(solution)/shard_map/ppermute | solution.py:37
  47.8 1.8 %add_convert_fusion = bf16[768,1024]{1,0:T(8,128)(2,1)} fusion(f32[768,1024]{1,0:T(8,128)S(1)} %fusion.64, bf16[768,1024]{1,0:T(8,128)(2,1)S(1)} %collective-permute-done.10), kind=kLoop, calls=%fused_computation | loop fusion | flops 2359296 | bytes 6291456 | tf_op jit(solution)/shard_map/convert_element_type | solution.py:164
  49.5 0.0 collective-permute-done.12
  49.5 0.0 collective-permute-done.9
  49.5 0.8 %add_convert_fusion.1 = bf16[128,1024]{1,0:T(8,128)(2,1)} fusion(f32[128,1024]{1,0:T(8,128)S(1)} %fusion.5, bf16[128,1024]{1,0:T(8,128)(2,1)S(1)} %collective-permute-done.9, bf16[64,1024]{1,0:T(8,128)(2,1)S(1)} %collective-permute-done.12, bf16[64,1024]{1,0:T(8,128)(2,1)S(1)} %collective-permute-done.11), kind=kLoop, calls=%fused_computation.54 | loop fusion | flops 1048576 | bytes 1310720 | tf_op jit(solution)/shard_map/convert_element_type | solution.py:171
  (12 shorter events, 0.2 us)
Async XLA Ops:
  0.6 20.8 %collective-permute-start = (bf16[768,1024]{1,0:T(8,128)(2,1)}, bf16[768,1024]{1,0:T(8,128)(2,1)S(1)}, u32[]{:S(2)}, u32[]{:S(2)}) collective-permute-start(bf16[768,1024]{1,0:T(8,128)(2,1)} %param.4), channel_id=1, source_target_pairs={{0,12},{4,0},{8,4},{12,8},{1,13},{5,1},{9,5},{13,9},{2,14},{6,2},{... | collective-permute-start | bytes 4718600 | tf_op jit(solution)/shard_map/ppermute | solution.py:37
  4.0 8.8 %collective-permute-start.3 = (bf16[64,1024]{1,0:T(8,128)(2,1)S(1)}, bf16[64,1024]{1,0:T(8,128)(2,1)S(1)}, u32[]{:S(2)}, u32[]{:S(2)}) collective-permute-start(bf16[64,1024]{1,0:T(8,128)(2,1)S(1)} %constant_dynamic-slice_fusion.8), channel_id=1, source_target_pairs={{0,2},{1,3},{2,0},{3,1},{4,6},{5,7},{6,4},{7,5},{8,10},{9,11},{10,... | collective-permute-start | bytes 393224 | tf_op jit(solution)/shard_map/ppermute | solution.py:31
  7.4 14.1 %collective-permute-start.2 = (bf16[128,1024]{1,0:T(8,128)(2,1)}, bf16[128,1024]{1,0:T(8,128)(2,1)S(1)}, u32[]{:S(2)}, u32[]{:S(2)}) collective-permute-start(bf16[128,1024]{1,0:T(8,128)(2,1)} %param.5), channel_id=1, source_target_pairs={{0,1},{1,0},{2,3},{3,2},{4,5},{5,4},{6,7},{7,6},{8,9},{9,8},{10,11... | collective-permute-start | bytes 786440 | tf_op jit(solution)/shard_map/ppermute | solution.py:31
  12.8 6.8 %collective-permute-start.5 = (bf16[64,1024]{1,0:T(8,128)(2,1)S(1)}, bf16[64,1024]{1,0:T(8,128)(2,1)S(1)}, u32[]{:S(2)}, u32[]{:S(2)}) collective-permute-start(bf16[64,1024]{1,0:T(8,128)(2,1)S(1)} %collective-permute-done.3), channel_id=1, source_target_pairs={{0,1},{1,0},{2,3},{3,2},{4,5},{5,4},{6,7},{7,6},{8,9},{9,8},{10,11... | collective-permute-start | bytes 393224 | tf_op jit(solution)/shard_map/ppermute | solution.py:31
  13.5 8.0 %collective-permute-start.4 = (bf16[64,1024]{1,0:T(8,128)(2,1)S(1)}, bf16[64,1024]{1,0:T(8,128)(2,1)S(1)}, u32[]{:S(2)}, u32[]{:S(2)}) collective-permute-start(bf16[64,1024]{1,0:T(8,128)(2,1)S(1)} %collective-permute-done.3), channel_id=1, source_target_pairs={{0,16},{16,0},{1,17},{17,1},{2,18},{18,2},{3,19},{19,3},{4,20},{20... | collective-permute-start | bytes 393224 | tf_op jit(solution)/shard_map/ppermute | solution.py:34
  15.0 6.5 %collective-permute-start.1 = (s32[768,8]{0,1:T(8,128)S(1)}, s32[768,8]{0,1:T(8,128)S(1)}, u32[]{:S(2)}, u32[]{:S(2)}) collective-permute-start(s32[768,8]{0,1:T(8,128)S(1)} %fusion.41), channel_id=1, source_target_pairs={{0,12},{4,0},{8,4},{12,8},{1,13},{5,1},{9,5},{13,9},{2,14},{6,2},{... | collective-permute-start | bytes 73736 | tf_op jit(solution)/shard_map/ppermute | solution.py:37
  19.6 5.0 %collective-permute-start.6 = (bf16[64,1024]{1,0:T(8,128)(2,1)S(1)}, bf16[64,1024]{1,0:T(8,128)(2,1)S(1)}, u32[]{:S(2)}, u32[]{:S(2)}) collective-permute-start(bf16[64,1024]{1,0:T(8,128)(2,1)S(1)} %collective-permute-done.5), channel_id=1, source_target_pairs={{0,16},{16,0},{1,17},{17,1},{2,18},{18,2},{3,19},{19,3},{4,20},{20... | collective-permute-start | bytes 393224 | tf_op jit(solution)/shard_map/ppermute | solution.py:34
  21.6 1.4 %copy-start = (bf16[768,1024]{1,0:T(8,128)(2,1)S(1)}, bf16[768,1024]{1,0:T(8,128)(2,1)}, u32[]{:S(2)}) copy-start(bf16[768,1024]{1,0:T(8,128)(2,1)} %param.4) | copy-start | bytes 4718596
  27.9 19.9 %collective-permute-start.10 = (bf16[768,1024]{1,0:T(8,128)(2,1)S(1)}, bf16[768,1024]{1,0:T(8,128)(2,1)S(1)}, u32[]{:S(2)}, u32[]{:S(2)}) collective-permute-start(bf16[768,1024]{1,0:T(8,128)(2,1)S(1)} %convolution_convert_fusion), channel_id=1, source_target_pairs={{0,4},{4,8},{8,12},{12,0},{1,5},{5,9},{9,13},{13,1},{2,6},{6,10},{... | collective-permute-start | bytes 4718600 | tf_op jit(solution)/shard_map/ppermute | solution.py:37
  28.1 6.3 %collective-permute-start.8 = (bf16[64,1024]{1,0:T(8,128)(2,1)S(1)}, bf16[64,1024]{1,0:T(8,128)(2,1)S(1)}, u32[]{:S(2)}, u32[]{:S(2)}) collective-permute-start(bf16[64,1024]{1,0:T(8,128)(2,1)S(1)} %slice.73), channel_id=1, source_target_pairs={{0,1},{1,0},{2,3},{3,2},{4,5},{5,4},{6,7},{7,6},{8,9},{9,8},{10,11... | collective-permute-start | bytes 393224 | tf_op jit(solution)/shard_map/ppermute | solution.py:31
  30.0 7.5 %collective-permute-start.7 = (bf16[64,1024]{1,0:T(8,128)(2,1)S(1)}, bf16[64,1024]{1,0:T(8,128)(2,1)S(1)}, u32[]{:S(2)}, u32[]{:S(2)}) collective-permute-start(bf16[64,1024]{1,0:T(8,128)(2,1)S(1)} %slice.74), channel_id=1, source_target_pairs={{0,1},{1,0},{2,3},{3,2},{4,5},{5,4},{6,7},{7,6},{8,9},{9,8},{10,11... | collective-permute-start | bytes 393224 | tf_op jit(solution)/shard_map/ppermute | solution.py:31
  31.0 18.5 %collective-permute-start.9 = (bf16[128,1024]{1,0:T(8,128)(2,1)S(1)}, bf16[128,1024]{1,0:T(8,128)(2,1)S(1)}, u32[]{:S(2)}, u32[]{:S(2)}) collective-permute-start(bf16[128,1024]{1,0:T(8,128)(2,1)S(1)} %fusion.7), channel_id=1, source_target_pairs={{0,1},{1,0},{2,3},{3,2},{4,5},{5,4},{6,7},{7,6},{8,9},{9,8},{10,11... | collective-permute-start | bytes 786440 | tf_op jit(solution)/shard_map/ppermute | solution.py:31
  34.5 10.6 %collective-permute-start.11 = (bf16[64,1024]{1,0:T(8,128)(2,1)S(1)}, bf16[64,1024]{1,0:T(8,128)(2,1)S(1)}, u32[]{:S(2)}, u32[]{:S(2)}) collective-permute-start(bf16[64,1024]{1,0:T(8,128)(2,1)S(1)} %fusion.39), channel_id=1, source_target_pairs={{0,2},{1,3},{2,0},{3,1},{4,6},{5,7},{6,4},{7,5},{8,10},{9,11},{10,... | collective-permute-start | bytes 393224 | tf_op jit(solution)/shard_map/ppermute | solution.py:31
  37.5 12.0 %collective-permute-start.12 = (bf16[64,1024]{1,0:T(8,128)(2,1)S(1)}, bf16[64,1024]{1,0:T(8,128)(2,1)S(1)}, u32[]{:S(2)}, u32[]{:S(2)}) collective-permute-start(bf16[64,1024]{1,0:T(8,128)(2,1)S(1)} %fusion.40), channel_id=1, source_target_pairs={{0,2},{1,3},{2,0},{3,1},{4,6},{5,7},{6,4},{7,5},{8,10},{9,11},{10,... | collective-permute-start | bytes 393224 | tf_op jit(solution)/shard_map/ppermute | solution.py:31

commit v21 on v20

--- a/solution.py
+++ b/solution.py
@@ -57,8 +57,7 @@
     half = ch_dev // 2
     mine_at, other_at = me_group * half, (1 - me_group) * half
     mine = lax.dynamic_slice_in_dim(weights, mine_at, half, axis=0)
-    near_source, _ = lax.optimization_barrier((weights, ids))
-    near = to_dp(near_source, 1)
+    near = to_dp(weights, 1)
     parts, others = {}, {}
     for k in range(2, n_dp):
         step = k & -k

time: 50.6 us -> 50.4 us (level)
    ppermute x3, starting transfers between devices: 3.27 us -> 4.23 us  [to_label(): lax.ppermute(x, 'label', [(i, (i + by) % n_label) for i in range(n_label)])]
    ppermute x8, starting transfers between devices: 15 us -> 14.3 us  [to_dp(): return lax.ppermute(x, 'dp', [(i, i ^ k) for i in range(n_dp)])]
    ppermute x2, waiting for transfers between devices: 0.69 us -> 0.01 us  [to_group(): return lax.ppermute(x, 'groups', [(i, i ^ 1) for i in range(n_groups)])]
    ppermute x3, waiting for transfers between devices: 3.01 us -> 3.55 us  [to_label(): lax.ppermute(x, 'label', [(i, (i + by) % n_label) for i in range(n_label)])]
  transfers between devices with their start and end apart: 13 -> 13, of which waited for: 6 -> 7; matrix products, arithmetic and copies ran while one was open for 23% -> 23% of each run, Pallas kernels for 0% -> 0%
where the time goes in v21:
time: 50.4 us; the launch traced here: 50.1 us
  starting transfers between devices  21.7 us (43%)
  waiting for transfers between devices  11.8 us (23%)
  matrix products  9.7 us (19%)
  other arithmetic  3.58 us (7%)
  local copies, waits for them, and re-layouts  2.49 us (5%)
  between operations  0.91 us (2%)
    ppermute x8, starting transfers between devices, to_dp(): return lax.ppermute(x, 'dp', [(i, i ^ k) for i in range(n_dp)])  14.3 us
    ppermute x8, waiting for transfers between devices, to_dp(): return lax.ppermute(x, 'dp', [(i, i ^ k) for i in range(n_dp)])  8.24 us
    dot_general x6, matrix products, delta_of(): lax.dot_general(rows, piece, (((1,), (1,)), ((), ())), preferred_element_...  4.62 us
    ppermute x3, starting transfers between devices, to_label(): lax.ppermute(x, 'label', [(i, (i + by) % n_label) for i in range(n_label)])  4.23 us
    ppermute x3, waiting for transfers between devices, to_label(): lax.ppermute(x, 'label', [(i, (i + by) % n_label) for i in range(n_label)])  3.55 us
    ppermute x2, starting transfers between devices, to_group(): return lax.ppermute(x, 'groups', [(i, i ^ 1) for i in range(n_groups)])  3.09 us
    dot_general x8, matrix products, grad_w_of(): lax.dot_general(delta, rows, (((0,), (0,)), ((), ())), preferred_element_...  3.04 us
    convert_element_type x1, other arithmetic, local(): grad_x = (grad_x + in_turn(back).astype(jnp.float32)).astype(jnp.bfloat16)  1.75 us
  transfers between devices with their start and end apart: 13, of which 7 were waited for; matrix products, arithmetic and copies ran while one was open for 23% of the time, Pallas kernels for 0%

profile of v21, /device:TPU:0, one launch (start us, length us, event | category | flops | bytes accessed | tf_op | source)
XLA Modules:
  0.0 50.1 jit_solution(18012042950239112143)
XLA Ops:
  0.6 2.4 %collective-permute-start = (bf16[768,1024]{1,0:T(8,128)(2,1)}, bf16[768,1024]{1,0:T(8,128)(2,1)S(1)}, u32[]{:S(2)}, u32[]{:S(2)}) collective-permute-start(bf16[768,1024]{1,0:T(8,128)(2,1)} %param.4), channel_id=1, source_target_pairs={{0,12},{4,0},{8,4},{12,8},{1,13},{5,1},{9,5},{13,9},{2,14},{6,2},{... | collective-permute-start | bytes 4718600 | tf_op jit(solution)/shard_map/ppermute | solution.py:37
  3.1 0.9 %constant_dynamic-slice_fusion.8 = bf16[64,1024]{1,0:T(8,128)(2,1)S(1)} fusion(bf16[128,1024]{1,0:T(8,128)(2,1)} %param.5, s32[]{:T(128)S(6)} %select_n.62), kind=kLoop, calls=%fused_computation.81 | loop fusion | bytes 262148 | tf_op jit(solution)/shard_map/dynamic_slice | solution.py:59
  4.0 2.7 %collective-permute-start.3 = (bf16[64,1024]{1,0:T(8,128)(2,1)S(1)}, bf16[64,1024]{1,0:T(8,128)(2,1)S(1)}, u32[]{:S(2)}, u32[]{:S(2)}) collective-permute-start(bf16[64,1024]{1,0:T(8,128)(2,1)S(1)} %constant_dynamic-slice_fusion.8), channel_id=1, source_target_pairs={{0,2},{1,3},{2,0},{3,1},{4,6},{5,7},{6,4},{7,5},{8,10},{9,11},{10,... | collective-permute-start | bytes 393224 | tf_op jit(solution)/shard_map/ppermute | solution.py:31
  6.6 1.6 %collective-permute-start.2 = (bf16[128,1024]{1,0:T(8,128)(2,1)}, bf16[128,1024]{1,0:T(8,128)(2,1)S(1)}, u32[]{:S(2)}, u32[]{:S(2)}) collective-permute-start(bf16[128,1024]{1,0:T(8,128)(2,1)} %param.5), channel_id=1, source_target_pairs={{0,1},{1,0},{2,3},{3,2},{4,5},{5,4},{6,7},{7,6},{8,9},{9,8},{10,11... | collective-permute-start | bytes 786440 | tf_op jit(solution)/shard_map/ppermute | solution.py:31
  8.2 4.6 %collective-permute-done.3 = bf16[64,1024]{1,0:T(8,128)(2,1)S(1)} collective-permute-done((bf16[64,1024]{1,0:T(8,128)(2,1)S(1)}, bf16[64,1024]{1,0:T(8,128)(2,1)S(1)}, u32[]{:S(2)}, u32[]{:S(2)}) %collective-permute-start.3) | collective-permute-done | bytes 131104 | tf_op jit(solution)/shard_map/ppermute | solution.py:31
  12.8 0.7 %collective-permute-start.5 = (bf16[64,1024]{1,0:T(8,128)(2,1)S(1)}, bf16[64,1024]{1,0:T(8,128)(2,1)S(1)}, u32[]{:S(2)}, u32[]{:S(2)}) collective-permute-start(bf16[64,1024]{1,0:T(8,128)(2,1)S(1)} %collective-permute-done.3), channel_id=1, source_target_pairs={{0,1},{1,0},{2,3},{3,2},{4,5},{5,4},{6,7},{7,6},{8,9},{9,8},{10,11... | collective-permute-start | bytes 393224 | tf_op jit(solution)/shard_map/ppermute | solution.py:31
  13.4 1.5 %collective-permute-start.4 = (bf16[64,1024]{1,0:T(8,128)(2,1)S(1)}, bf16[64,1024]{1,0:T(8,128)(2,1)S(1)}, u32[]{:S(2)}, u32[]{:S(2)}) collective-permute-start(bf16[64,1024]{1,0:T(8,128)(2,1)S(1)} %collective-permute-done.3), channel_id=1, source_target_pairs={{0,16},{16,0},{1,17},{17,1},{2,18},{18,2},{3,19},{19,3},{4,20},{20... | collective-permute-start | bytes 393224 | tf_op jit(solution)/shard_map/ppermute | solution.py:34
  15.0 0.7 %fusion.41 = s32[768,8]{0,1:T(8,128)S(1)} fusion(s32[768,8]{0,1:T(8,128)} %param.6, s32[768]{0:T(1024)} %param.7), kind=kLoop, calls=%fused_computation.67 | loop fusion | flops 12288 | bytes 52224 | tf_op jit(solution)/shard_map/jit(_where)/select_n | solution.py:23
  15.7 0.6 %collective-permute-start.1 = (s32[768,8]{0,1:T(8,128)S(1)}, s32[768,8]{0,1:T(8,128)S(1)}, u32[]{:S(2)}, u32[]{:S(2)}) collective-permute-start(s32[768,8]{0,1:T(8,128)S(1)} %fusion.41), channel_id=1, source_target_pairs={{0,12},{4,0},{8,4},{12,8},{1,13},{5,1},{9,5},{13,9},{2,14},{6,2},{... | collective-permute-start | bytes 73736 | tf_op jit(solution)/shard_map/ppermute | solution.py:37
  16.3 1.1 %dynamic_update_slice.18 = bf16[512,1024]{1,0:T(8,128)(2,1)S(1)} pad(bf16[128,1024]{1,0:T(8,128)(2,1)} %param.5, bf16[]{:T(256)} %constant.72.clone.1), padding=0_384x0_0 | pad | bytes 1310722 | tf_op jit(solution)/shard_map/dynamic_update_slice | solution.py:71
  17.5 1.3 %collective-permute-done.5 = bf16[64,1024]{1,0:T(8,128)(2,1)S(1)} collective-permute-done((bf16[64,1024]{1,0:T(8,128)(2,1)S(1)}, bf16[64,1024]{1,0:T(8,128)(2,1)S(1)}, u32[]{:S(2)}, u32[]{:S(2)}) %collective-permute-start.5) | collective-permute-done | bytes 131104 | tf_op jit(solution)/shard_map/ppermute | solution.py:31
  18.8 1.6 %collective-permute-start.6 = (bf16[64,1024]{1,0:T(8,128)(2,1)S(1)}, bf16[64,1024]{1,0:T(8,128)(2,1)S(1)}, u32[]{:S(2)}, u32[]{:S(2)}) collective-permute-start(bf16[64,1024]{1,0:T(8,128)(2,1)S(1)} %collective-permute-done.5), channel_id=1, source_target_pairs={{0,16},{16,0},{1,17},{17,1},{2,18},{18,2},{3,19},{19,3},{4,20},{20... | collective-permute-start | bytes 393224 | tf_op jit(solution)/shard_map/ppermute | solution.py:34
  20.4 1.1 %collective-permute-done.1 = s32[768,8]{0,1:T(8,128)S(1)} collective-permute-done((s32[768,8]{0,1:T(8,128)S(1)}, s32[768,8]{0,1:T(8,128)S(1)}, u32[]{:S(2)}, u32[]{:S(2)}) %collective-permute-start.1) | collective-permute-done | bytes 24608 | tf_op jit(solution)/shard_map/ppermute | solution.py:37
  21.5 0.0 collective-permute-done.4
  21.5 0.0 collective-permute-done.2
  21.5 0.0 collective-permute-done
  21.6 0.1 fusion.53
  21.6 0.0 copy-start
  21.7 1.1 %fusion.4 = bf16[768,384]{0,1:T(8,128)(2,1)S(1)} fusion(bf16[768,1024]{1,0:T(8,128)(2,1)S(1)} %collective-permute-done, bf16[512,1024]{1,0:T(8,128)(2,1)S(1)} %constant_dynamic-update-slice_fusion.2, s32[768]{0:T(1024)S(1)} %get-tuple-element.65, s32[768]{0:T(1024)S(1)} %get-tuple-element.66, s32[768]{0:T(1024)S(1)} %get-tuple-element.67, ...), kind=kOutput, calls=%fused_computation.7 | convolution fusion | flops 606633984 | bytes 2962432 | tf_op jit(solution)/shard_map/dot_general | solution.py:46
  22.8 0.3 copy-done
  23.1 0.7 %fusion.37 = bf16[768,128]{0,1:T(8,128)(2,1)S(1)} fusion(bf16[128,1024]{1,0:T(8,128)(2,1)S(1)} %slice.51, bf16[768,1024]{1,0:T(8,128)(2,1)S(1)} %copy-done, s32[768]{0:T(1024)S(1)} %get-tuple-element.63), kind=kOutput, calls=%fused_computation.50 | convolution fusion | flops 202014720 | bytes 2034688 | tf_op jit(solution)/shard_map/dot_general | solution.py:46
  23.8 0.0 collective-permute-done.6
  23.9 0.1 fusion.58
  23.9 0.7 %fusion.36 = bf16[768,128]{0,1:T(8,128)(2,1)S(1)} fusion(bf16[128,1024]{1,0:T(8,128)(2,1)S(1)} %get-tuple-element.41, bf16[768,1024]{1,0:T(8,128)(2,1)S(1)} %copy-done, s32[768]{0:T(1024)S(1)} %get-tuple-element.62), kind=kOutput, calls=%fused_computation.49 | convolution fusion | flops 202014720 | bytes 2034688 | tf_op jit(solution)/shard_map/dot_general | solution.py:46
  24.6 0.4 fusion.60
  25.0 0.7 %fusion.35 = bf16[768,128]{0,1:T(8,128)(2,1)S(1)} fusion(bf16[768,1024]{1,0:T(8,128)(2,1)S(1)} %collective-permute-done, bf16[128,1024]{1,0:T(8,128)(2,1)S(1)} %get-tuple-element.41, s32[768]{0:T(1024)S(1)} %get-tuple-element.64), kind=kOutput, calls=%fused_computation.48 | convolution fusion | flops 202014720 | bytes 2034688 | tf_op jit(solution)/shard_map/dot_general | solution.py:46
  25.7 0.1 pad_maximum_fusion
  25.8 0.4 fusion.8
  26.2 1.0 %convolution_convert_fusion = bf16[768,1024]{1,0:T(8,128)(2,1)S(1)} fusion(bf16[768,512]{0,1:T(8,128)(2,1)S(1)} %pad_maximum_fusion, bf16[512,1024]{1,0:T(8,128)(2,1)S(1)} %constant_dynamic-update-slice_fusion), kind=kOutput, calls=%fused_computation.1 | convolution fusion | flops 806092800 | bytes 3407872 | tf_op jit(solution)/shard_map/dot_general | solution.py:125
  27.2 1.2 %collective-permute-start.10 = (bf16[768,1024]{1,0:T(8,128)(2,1)S(1)}, bf16[768,1024]{1,0:T(8,128)(2,1)S(1)}, u32[]{:S(2)}, u32[]{:S(2)}) collective-permute-start(bf16[768,1024]{1,0:T(8,128)(2,1)S(1)} %convolution_convert_fusion), channel_id=1, source_target_pairs={{0,4},{4,8},{8,12},{12,0},{1,5},{5,9},{9,13},{13,1},{2,6},{6,10},{... | collective-permute-start | bytes 4718600 | tf_op jit(solution)/shard_map/ppermute | solution.py:37
  28.4 1.6 %collective-permute-start.8 = (bf16[64,1024]{1,0:T(8,128)(2,1)S(1)}, bf16[64,1024]{1,0:T(8,128)(2,1)S(1)}, u32[]{:S(2)}, u32[]{:S(2)}) collective-permute-start(bf16[64,1024]{1,0:T(8,128)(2,1)S(1)} %slice.73), channel_id=1, source_target_pairs={{0,1},{1,0},{2,3},{3,2},{4,5},{5,4},{6,7},{7,6},{8,9},{9,8},{10,11... | collective-permute-start | bytes 393224 | tf_op jit(solution)/shard_map/ppermute | solution.py:31
  30.0 0.5 %collective-permute-start.7 = (bf16[64,1024]{1,0:T(8,128)(2,1)S(1)}, bf16[64,1024]{1,0:T(8,128)(2,1)S(1)}, u32[]{:S(2)}, u32[]{:S(2)}) collective-permute-start(bf16[64,1024]{1,0:T(8,128)(2,1)S(1)} %slice.74), channel_id=1, source_target_pairs={{0,1},{1,0},{2,3},{3,2},{4,5},{5,4},{6,7},{7,6},{8,9},{9,8},{10,11... | collective-permute-start | bytes 393224 | tf_op jit(solution)/shard_map/ppermute | solution.py:31
  30.5 0.4 fusion.61
  30.9 0.4 fusion.7
  31.3 1.6 %collective-permute-start.9 = (bf16[128,1024]{1,0:T(8,128)(2,1)S(1)}, bf16[128,1024]{1,0:T(8,128)(2,1)S(1)}, u32[]{:S(2)}, u32[]{:S(2)}) collective-permute-start(bf16[128,1024]{1,0:T(8,128)(2,1)S(1)} %fusion.7), channel_id=1, source_target_pairs={{0,1},{1,0},{2,3},{3,2},{4,5},{5,4},{6,7},{7,6},{8,9},{9,8},{10,11... | collective-permute-start | bytes 786440 | tf_op jit(solution)/shard_map/ppermute | solution.py:31
  32.9 0.7 %fusion.34 = bf16[768,128]{0,1:T(8,128)(2,1)S(1)} fusion(bf16[128,1024]{1,0:T(8,128)(2,1)S(1)} %get-tuple-element.46, bf16[768,1024]{1,0:T(8,128)(2,1)S(1)} %copy-done, s32[768]{0:T(1024)S(1)} %get-tuple-element.61), kind=kOutput, calls=%fused_computation.47 | convolution fusion | flops 202014720 | bytes 2034688 | tf_op jit(solution)/shard_map/dot_general | solution.py:46
  33.7 0.4 fusion.62
  34.0 0.4 fusion.6
  34.4 0.3 collective-permute-done.8
  34.8 2.7 %collective-permute-start.11 = (bf16[64,1024]{1,0:T(8,128)(2,1)S(1)}, bf16[64,1024]{1,0:T(8,128)(2,1)S(1)}, u32[]{:S(2)}, u32[]{:S(2)}) collective-permute-start(bf16[64,1024]{1,0:T(8,128)(2,1)S(1)} %fusion.39), channel_id=1, source_target_pairs={{0,2},{1,3},{2,0},{3,1},{4,6},{5,7},{6,4},{7,5},{8,10},{9,11},{10,... | collective-permute-start | bytes 393224 | tf_op jit(solution)/shard_map/ppermute | solution.py:31
  37.4 0.1 collective-permute-done.7
  37.6 3.1 %collective-permute-start.12 = (bf16[64,1024]{1,0:T(8,128)(2,1)S(1)}, bf16[64,1024]{1,0:T(8,128)(2,1)S(1)}, u32[]{:S(2)}, u32[]{:S(2)}) collective-permute-start(bf16[64,1024]{1,0:T(8,128)(2,1)S(1)} %fusion.40), channel_id=1, source_target_pairs={{0,2},{1,3},{2,0},{3,1},{4,6},{5,7},{6,4},{7,5},{8,10},{9,11},{10,... | collective-permute-start | bytes 393224 | tf_op jit(solution)/shard_map/ppermute | solution.py:31
  40.6 0.7 %fusion.33 = bf16[768,128]{0,1:T(8,128)(2,1)S(1)} fusion(bf16[128,1024]{1,0:T(8,128)(2,1)S(1)} %get-tuple-element.52, bf16[768,1024]{1,0:T(8,128)(2,1)S(1)} %copy-done, s32[768]{0:T(1024)S(1)} %get-tuple-element.60), kind=kOutput, calls=%fused_computation.46 | convolution fusion | flops 202014720 | bytes 2034688 | tf_op jit(solution)/shard_map/dot_general | solution.py:46
  41.4 0.1 pad_maximum_fusion.1
  41.4 0.4 fusion.63
  41.8 1.0 %fusion.64 = f32[768,1024]{1,0:T(8,128)S(1)} fusion(bf16[768,512]{0,1:T(8,128)(2,1)S(1)} %pad_maximum_fusion.1, bf16[512,1024]{1,0:T(8,128)(2,1)S(1)} %constant_dynamic-update-slice_fusion), kind=kOutput, calls=%fused_computation.106 | convolution fusion | flops 805306368 | bytes 4980736 | tf_op jit(solution)/shard_map/dot_general | solution.py:152
  42.8 0.4 fusion.5
  43.2 1.9 %collective-permute-done.11 = bf16[64,1024]{1,0:T(8,128)(2,1)S(1)} collective-permute-done((bf16[64,1024]{1,0:T(8,128)(2,1)S(1)}, bf16[64,1024]{1,0:T(8,128)(2,1)S(1)}, u32[]{:S(2)}, u32[]{:S(2)}) %collective-permute-start.11) | collective-permute-done | bytes 131104 | tf_op jit(solution)/shard_map/ppermute | solution.py:31
  45.1 2.5 %collective-permute-done.10 = bf16[768,1024]{1,0:T(8,128)(2,1)S(1)} collective-permute-done((bf16[768,1024]{1,0:T(8,128)(2,1)S(1)}, bf16[768,1024]{1,0:T(8,128)(2,1)S(1)}, u32[]{:S(2)}, u32[]{:S(2)}) %collective-permute-start.10) | collective-permute-done | bytes 1572896 | tf_op jit(solution)/shard_map/ppermute | solution.py:37
  47.6 1.8 %add_convert_fusion = bf16[768,1024]{1,0:T(8,128)(2,1)} fusion(f32[768,1024]{1,0:T(8,128)S(1)} %fusion.64, bf16[768,1024]{1,0:T(8,128)(2,1)S(1)} %collective-permute-done.10), kind=kLoop, calls=%fused_computation | loop fusion | flops 2359296 | bytes 6291456 | tf_op jit(solution)/shard_map/convert_element_type | solution.py:163
  49.3 0.0 collective-permute-done.12
  49.3 0.0 collective-permute-done.9
  49.3 0.8 %add_convert_fusion.1 = bf16[128,1024]{1,0:T(8,128)(2,1)} fusion(f32[128,1024]{1,0:T(8,128)S(1)} %fusion.5, bf16[128,1024]{1,0:T(8,128)(2,1)S(1)} %collective-permute-done.9, bf16[64,1024]{1,0:T(8,128)(2,1)S(1)} %collective-permute-done.12, bf16[64,1024]{1,0:T(8,128)(2,1)S(1)} %collective-permute-done.11), kind=kLoop, calls=%fused_computation.54 | loop fusion | flops 1048576 | bytes 1310720 | tf_op jit(solution)/shard_map/convert_element_type | solution.py:170
  (13 shorter events, 0.3 us)
Async XLA Ops:
  0.6 20.8 %collective-permute-start = (bf16[768,1024]{1,0:T(8,128)(2,1)}, bf16[768,1024]{1,0:T(8,128)(2,1)S(1)}, u32[]{:S(2)}, u32[]{:S(2)}) collective-permute-start(bf16[768,1024]{1,0:T(8,128)(2,1)} %param.4), channel_id=1, source_target_pairs={{0,12},{4,0},{8,4},{12,8},{1,13},{5,1},{9,5},{13,9},{2,14},{6,2},{... | collective-permute-start | bytes 4718600 | tf_op jit(solution)/shard_map/ppermute | solution.py:37
  4.0 8.8 %collective-permute-start.3 = (bf16[64,1024]{1,0:T(8,128)(2,1)S(1)}, bf16[64,1024]{1,0:T(8,128)(2,1)S(1)}, u32[]{:S(2)}, u32[]{:S(2)}) collective-permute-start(bf16[64,1024]{1,0:T(8,128)(2,1)S(1)} %constant_dynamic-slice_fusion.8), channel_id=1, source_target_pairs={{0,2},{1,3},{2,0},{3,1},{4,6},{5,7},{6,4},{7,5},{8,10},{9,11},{10,... | collective-permute-start | bytes 393224 | tf_op jit(solution)/shard_map/ppermute | solution.py:31
  6.6 14.8 %collective-permute-start.2 = (bf16[128,1024]{1,0:T(8,128)(2,1)}, bf16[128,1024]{1,0:T(8,128)(2,1)S(1)}, u32[]{:S(2)}, u32[]{:S(2)}) collective-permute-start(bf16[128,1024]{1,0:T(8,128)(2,1)} %param.5), channel_id=1, source_target_pairs={{0,1},{1,0},{2,3},{3,2},{4,5},{5,4},{6,7},{7,6},{8,9},{9,8},{10,11... | collective-permute-start | bytes 786440 | tf_op jit(solution)/shard_map/ppermute | solution.py:31
  12.8 6.0 %collective-permute-start.5 = (bf16[64,1024]{1,0:T(8,128)(2,1)S(1)}, bf16[64,1024]{1,0:T(8,128)(2,1)S(1)}, u32[]{:S(2)}, u32[]{:S(2)}) collective-permute-start(bf16[64,1024]{1,0:T(8,128)(2,1)S(1)} %collective-permute-done.3), channel_id=1, source_target_pairs={{0,1},{1,0},{2,3},{3,2},{4,5},{5,4},{6,7},{7,6},{8,9},{9,8},{10,11... | collective-permute-start | bytes 393224 | tf_op jit(solution)/shard_map/ppermute | solution.py:31
  13.4 8.0 %collective-permute-start.4 = (bf16[64,1024]{1,0:T(8,128)(2,1)S(1)}, bf16[64,1024]{1,0:T(8,128)(2,1)S(1)}, u32[]{:S(2)}, u32[]{:S(2)}) collective-permute-start(bf16[64,1024]{1,0:T(8,128)(2,1)S(1)} %collective-permute-done.3), channel_id=1, source_target_pairs={{0,16},{16,0},{1,17},{17,1},{2,18},{18,2},{3,19},{19,3},{4,20},{20... | collective-permute-start | bytes 393224 | tf_op jit(solution)/shard_map/ppermute | solution.py:34
  15.7 5.8 %collective-permute-start.1 = (s32[768,8]{0,1:T(8,128)S(1)}, s32[768,8]{0,1:T(8,128)S(1)}, u32[]{:S(2)}, u32[]{:S(2)}) collective-permute-start(s32[768,8]{0,1:T(8,128)S(1)} %fusion.41), channel_id=1, source_target_pairs={{0,12},{4,0},{8,4},{12,8},{1,13},{5,1},{9,5},{13,9},{2,14},{6,2},{... | collective-permute-start | bytes 73736 | tf_op jit(solution)/shard_map/ppermute | solution.py:37
  18.8 5.0 %collective-permute-start.6 = (bf16[64,1024]{1,0:T(8,128)(2,1)S(1)}, bf16[64,1024]{1,0:T(8,128)(2,1)S(1)}, u32[]{:S(2)}, u32[]{:S(2)}) collective-permute-start(bf16[64,1024]{1,0:T(8,128)(2,1)S(1)} %collective-permute-done.5), channel_id=1, source_target_pairs={{0,16},{16,0},{1,17},{17,1},{2,18},{18,2},{3,19},{19,3},{4,20},{20... | collective-permute-start | bytes 393224 | tf_op jit(solution)/shard_map/ppermute | solution.py:34
  21.6 1.4 %copy-start = (bf16[768,1024]{1,0:T(8,128)(2,1)S(1)}, bf16[768,1024]{1,0:T(8,128)(2,1)}, u32[]{:S(2)}) copy-start(bf16[768,1024]{1,0:T(8,128)(2,1)} %param.4) | copy-start | bytes 4718596
  27.2 20.4 %collective-permute-start.10 = (bf16[768,1024]{1,0:T(8,128)(2,1)S(1)}, bf16[768,1024]{1,0:T(8,128)(2,1)S(1)}, u32[]{:S(2)}, u32[]{:S(2)}) collective-permute-start(bf16[768,1024]{1,0:T(8,128)(2,1)S(1)} %convolution_convert_fusion), channel_id=1, source_target_pairs={{0,4},{4,8},{8,12},{12,0},{1,5},{5,9},{9,13},{13,1},{2,6},{6,10},{... | collective-permute-start | bytes 4718600 | tf_op jit(solution)/shard_map/ppermute | solution.py:37
  28.4 6.3 %collective-permute-start.8 = (bf16[64,1024]{1,0:T(8,128)(2,1)S(1)}, bf16[64,1024]{1,0:T(8,128)(2,1)S(1)}, u32[]{:S(2)}, u32[]{:S(2)}) collective-permute-start(bf16[64,1024]{1,0:T(8,128)(2,1)S(1)} %slice.73), channel_id=1, source_target_pairs={{0,1},{1,0},{2,3},{3,2},{4,5},{5,4},{6,7},{7,6},{8,9},{9,8},{10,11... | collective-permute-start | bytes 393224 | tf_op jit(solution)/shard_map/ppermute | solution.py:31
  30.0 7.5 %collective-permute-start.7 = (bf16[64,1024]{1,0:T(8,128)(2,1)S(1)}, bf16[64,1024]{1,0:T(8,128)(2,1)S(1)}, u32[]{:S(2)}, u32[]{:S(2)}) collective-permute-start(bf16[64,1024]{1,0:T(8,128)(2,1)S(1)} %slice.74), channel_id=1, source_target_pairs={{0,1},{1,0},{2,3},{3,2},{4,5},{5,4},{6,7},{7,6},{8,9},{9,8},{10,11... | collective-permute-start | bytes 393224 | tf_op jit(solution)/shard_map/ppermute | solution.py:31
  31.3 18.0 %collective-permute-start.9 = (bf16[128,1024]{1,0:T(8,128)(2,1)S(1)}, bf16[128,1024]{1,0:T(8,128)(2,1)S(1)}, u32[]{:S(2)}, u32[]{:S(2)}) collective-permute-start(bf16[128,1024]{1,0:T(8,128)(2,1)S(1)} %fusion.7), channel_id=1, source_target_pairs={{0,1},{1,0},{2,3},{3,2},{4,5},{5,4},{6,7},{7,6},{8,9},{9,8},{10,11... | collective-permute-start | bytes 786440 | tf_op jit(solution)/shard_map/ppermute | solution.py:31
  34.8 10.4 %collective-permute-start.11 = (bf16[64,1024]{1,0:T(8,128)(2,1)S(1)}, bf16[64,1024]{1,0:T(8,128)(2,1)S(1)}, u32[]{:S(2)}, u32[]{:S(2)}) collective-permute-start(bf16[64,1024]{1,0:T(8,128)(2,1)S(1)} %fusion.39), channel_id=1, source_target_pairs={{0,2},{1,3},{2,0},{3,1},{4,6},{5,7},{6,4},{7,5},{8,10},{9,11},{10,... | collective-permute-start | bytes 393224 | tf_op jit(solution)/shard_map/ppermute | solution.py:31
  37.6 11.8 %collective-permute-start.12 = (bf16[64,1024]{1,0:T(8,128)(2,1)S(1)}, bf16[64,1024]{1,0:T(8,128)(2,1)S(1)}, u32[]{:S(2)}, u32[]{:S(2)}) collective-permute-start(bf16[64,1024]{1,0:T(8,128)(2,1)S(1)} %fusion.40), channel_id=1, source_target_pairs={{0,2},{1,3},{2,0},{3,1},{4,6},{5,7},{6,4},{7,5},{8,10},{9,11},{10,... | collective-permute-start | bytes 393224 | tf_op jit(solution)/shard_map/ppermute | solution.py:31

commit v22 on v21

--- a/solution.py
+++ b/solution.py
@@ -122,10 +122,10 @@
     d_next = jnp.concatenate([d_early, d_late], axis=1)
     last[0] = d_late
     add_next(late)
+    second = in_turn(g_w[late])
     theirs = jnp.dot(in_turn(d_next), joined, preferred_element_type=jnp.float32).astype(jnp.bfloat16)
     last[0] = theirs
     back = to_label(theirs, 1)
-    second = in_turn(g_w[late])
     for k in range(1, late):
         if k > 1:
             own_delta(k, piece_of(k))

time: 50.4 us -> 50.4 us (level)
  no operation moved by 1% of the time
where the time goes in v22:
time: 50.4 us; the launch traced here: 50.1 us
  starting transfers between devices  21.8 us (43%)
  waiting for transfers between devices  11.7 us (23%)
  matrix products  9.71 us (19%)
  other arithmetic  3.58 us (7%)
  local copies, waits for them, and re-layouts  2.49 us (5%)
  between operations  0.91 us (2%)
    ppermute x8, starting transfers between devices, to_dp(): return lax.ppermute(x, 'dp', [(i, i ^ k) for i in range(n_dp)])  14.5 us
    ppermute x8, waiting for transfers between devices, to_dp(): return lax.ppermute(x, 'dp', [(i, i ^ k) for i in range(n_dp)])  8.17 us
    dot_general x6, matrix products, delta_of(): lax.dot_general(rows, piece, (((1,), (1,)), ((), ())), preferred_element_...  4.61 us
    ppermute x3, starting transfers between devices, to_label(): lax.ppermute(x, 'label', [(i, (i + by) % n_label) for i in range(n_label)])  4.23 us
    ppermute x3, waiting for transfers between devices, to_label(): lax.ppermute(x, 'label', [(i, (i + by) % n_label) for i in range(n_label)])  3.47 us
    ppermute x2, starting transfers between devices, to_group(): return lax.ppermute(x, 'groups', [(i, i ^ 1) for i in range(n_groups)])  3.09 us
    dot_general x8, matrix products, grad_w_of(): lax.dot_general(delta, rows, (((0,), (0,)), ((), ())), preferred_element_...  3.05 us
    convert_element_type x1, other arithmetic, local(): grad_x = (grad_x + in_turn(back).astype(jnp.float32)).astype(jnp.bfloat16)  1.75 us
  transfers between devices with their start and end apart: 13, of which 7 were waited for; matrix products, arithmetic and copies ran while one was open for 23% of the time, Pallas kernels for 0%

profile of v22, /device:TPU:0, one launch (start us, length us, event | category | flops | bytes accessed | tf_op | source)
XLA Modules:
  0.0 50.1 jit_solution(5517488824393325743)
XLA Ops:
  0.6 2.4 %collective-permute-start = (bf16[768,1024]{1,0:T(8,128)(2,1)}, bf16[768,1024]{1,0:T(8,128)(2,1)S(1)}, u32[]{:S(2)}, u32[]{:S(2)}) collective-permute-start(bf16[768,1024]{1,0:T(8,128)(2,1)} %param.4), channel_id=1, source_target_pairs={{0,12},{4,0},{8,4},{12,8},{1,13},{5,1},{9,5},{13,9},{2,14},{6,2},{... | collective-permute-start | bytes 4718600 | tf_op jit(solution)/shard_map/ppermute | solution.py:37
  3.1 0.9 %constant_dynamic-slice_fusion.8 = bf16[64,1024]{1,0:T(8,128)(2,1)S(1)} fusion(bf16[128,1024]{1,0:T(8,128)(2,1)} %param.5, s32[]{:T(128)S(6)} %select_n.62), kind=kLoop, calls=%fused_computation.81 | loop fusion | bytes 262148 | tf_op jit(solution)/shard_map/dynamic_slice | solution.py:59
  4.0 2.7 %collective-permute-start.3 = (bf16[64,1024]{1,0:T(8,128)(2,1)S(1)}, bf16[64,1024]{1,0:T(8,128)(2,1)S(1)}, u32[]{:S(2)}, u32[]{:S(2)}) collective-permute-start(bf16[64,1024]{1,0:T(8,128)(2,1)S(1)} %constant_dynamic-slice_fusion.8), channel_id=1, source_target_pairs={{0,2},{1,3},{2,0},{3,1},{4,6},{5,7},{6,4},{7,5},{8,10},{9,11},{10,... | collective-permute-start | bytes 393224 | tf_op jit(solution)/shard_map/ppermute | solution.py:31
  6.6 1.6 %collective-permute-start.2 = (bf16[128,1024]{1,0:T(8,128)(2,1)}, bf16[128,1024]{1,0:T(8,128)(2,1)S(1)}, u32[]{:S(2)}, u32[]{:S(2)}) collective-permute-start(bf16[128,1024]{1,0:T(8,128)(2,1)} %param.5), channel_id=1, source_target_pairs={{0,1},{1,0},{2,3},{3,2},{4,5},{5,4},{6,7},{7,6},{8,9},{9,8},{10,11... | collective-permute-start | bytes 786440 | tf_op jit(solution)/shard_map/ppermute | solution.py:31
  8.2 4.6 %collective-permute-done.3 = bf16[64,1024]{1,0:T(8,128)(2,1)S(1)} collective-permute-done((bf16[64,1024]{1,0:T(8,128)(2,1)S(1)}, bf16[64,1024]{1,0:T(8,128)(2,1)S(1)}, u32[]{:S(2)}, u32[]{:S(2)}) %collective-permute-start.3) | collective-permute-done | bytes 131104 | tf_op jit(solution)/shard_map/ppermute | solution.py:31
  12.8 0.7 %collective-permute-start.5 = (bf16[64,1024]{1,0:T(8,128)(2,1)S(1)}, bf16[64,1024]{1,0:T(8,128)(2,1)S(1)}, u32[]{:S(2)}, u32[]{:S(2)}) collective-permute-start(bf16[64,1024]{1,0:T(8,128)(2,1)S(1)} %collective-permute-done.3), channel_id=1, source_target_pairs={{0,1},{1,0},{2,3},{3,2},{4,5},{5,4},{6,7},{7,6},{8,9},{9,8},{10,11... | collective-permute-start | bytes 393224 | tf_op jit(solution)/shard_map/ppermute | solution.py:31
  13.4 1.5 %collective-permute-start.4 = (bf16[64,1024]{1,0:T(8,128)(2,1)S(1)}, bf16[64,1024]{1,0:T(8,128)(2,1)S(1)}, u32[]{:S(2)}, u32[]{:S(2)}) collective-permute-start(bf16[64,1024]{1,0:T(8,128)(2,1)S(1)} %collective-permute-done.3), channel_id=1, source_target_pairs={{0,16},{16,0},{1,17},{17,1},{2,18},{18,2},{3,19},{19,3},{4,20},{20... | collective-permute-start | bytes 393224 | tf_op jit(solution)/shard_map/ppermute | solution.py:34
  15.0 0.7 %fusion.41 = s32[768,8]{0,1:T(8,128)S(1)} fusion(s32[768,8]{0,1:T(8,128)} %param.6, s32[768]{0:T(1024)} %param.7), kind=kLoop, calls=%fused_computation.67 | loop fusion | flops 12288 | bytes 52224 | tf_op jit(solution)/shard_map/jit(_where)/select_n | solution.py:23
  15.7 0.6 %collective-permute-start.1 = (s32[768,8]{0,1:T(8,128)S(1)}, s32[768,8]{0,1:T(8,128)S(1)}, u32[]{:S(2)}, u32[]{:S(2)}) collective-permute-start(s32[768,8]{0,1:T(8,128)S(1)} %fusion.41), channel_id=1, source_target_pairs={{0,12},{4,0},{8,4},{12,8},{1,13},{5,1},{9,5},{13,9},{2,14},{6,2},{... | collective-permute-start | bytes 73736 | tf_op jit(solution)/shard_map/ppermute | solution.py:37
  16.3 1.1 %dynamic_update_slice.18 = bf16[512,1024]{1,0:T(8,128)(2,1)S(1)} pad(bf16[128,1024]{1,0:T(8,128)(2,1)} %param.5, bf16[]{:T(256)} %constant.72.clone.1), padding=0_384x0_0 | pad | bytes 1310722 | tf_op jit(solution)/shard_map/dynamic_update_slice | solution.py:71
  17.5 1.3 %collective-permute-done.5 = bf16[64,1024]{1,0:T(8,128)(2,1)S(1)} collective-permute-done((bf16[64,1024]{1,0:T(8,128)(2,1)S(1)}, bf16[64,1024]{1,0:T(8,128)(2,1)S(1)}, u32[]{:S(2)}, u32[]{:S(2)}) %collective-permute-start.5) | collective-permute-done | bytes 131104 | tf_op jit(solution)/shard_map/ppermute | solution.py:31
  18.8 1.6 %collective-permute-start.6 = (bf16[64,1024]{1,0:T(8,128)(2,1)S(1)}, bf16[64,1024]{1,0:T(8,128)(2,1)S(1)}, u32[]{:S(2)}, u32[]{:S(2)}) collective-permute-start(bf16[64,1024]{1,0:T(8,128)(2,1)S(1)} %collective-permute-done.5), channel_id=1, source_target_pairs={{0,16},{16,0},{1,17},{17,1},{2,18},{18,2},{3,19},{19,3},{4,20},{20... | collective-permute-start | bytes 393224 | tf_op jit(solution)/shard_map/ppermute | solution.py:34
  20.4 1.1 %collective-permute-done.1 = s32[768,8]{0,1:T(8,128)S(1)} collective-permute-done((s32[768,8]{0,1:T(8,128)S(1)}, s32[768,8]{0,1:T(8,128)S(1)}, u32[]{:S(2)}, u32[]{:S(2)}) %collective-permute-start.1) | collective-permute-done | bytes 24608 | tf_op jit(solution)/shard_map/ppermute | solution.py:37
  21.5 0.0 collective-permute-done.4
  21.5 0.0 collective-permute-done.2
  21.5 0.0 collective-permute-done
  21.6 0.1 fusion.53
  21.6 0.0 copy-start
  21.7 1.1 %fusion.4 = bf16[768,384]{0,1:T(8,128)(2,1)S(1)} fusion(bf16[768,1024]{1,0:T(8,128)(2,1)S(1)} %collective-permute-done, bf16[512,1024]{1,0:T(8,128)(2,1)S(1)} %constant_dynamic-update-slice_fusion.2, s32[768]{0:T(1024)S(1)} %get-tuple-element.65, s32[768]{0:T(1024)S(1)} %get-tuple-element.66, s32[768]{0:T(1024)S(1)} %get-tuple-element.67, ...), kind=kOutput, calls=%fused_computation.7 | convolution fusion | flops 606633984 | bytes 2962432 | tf_op jit(solution)/shard_map/dot_general | solution.py:46
  22.8 0.3 copy-done
  23.1 0.7 %fusion.37 = bf16[768,128]{0,1:T(8,128)(2,1)S(1)} fusion(bf16[128,1024]{1,0:T(8,128)(2,1)S(1)} %slice.51, bf16[768,1024]{1,0:T(8,128)(2,1)S(1)} %copy-done, s32[768]{0:T(1024)S(1)} %get-tuple-element.63), kind=kOutput, calls=%fused_computation.50 | convolution fusion | flops 202014720 | bytes 2034688 | tf_op jit(solution)/shard_map/dot_general | solution.py:46
  23.8 0.0 collective-permute-done.6
  23.9 0.1 fusion.58
  23.9 0.7 %fusion.36 = bf16[768,128]{0,1:T(8,128)(2,1)S(1)} fusion(bf16[128,1024]{1,0:T(8,128)(2,1)S(1)} %get-tuple-element.41, bf16[768,1024]{1,0:T(8,128)(2,1)S(1)} %copy-done, s32[768]{0:T(1024)S(1)} %get-tuple-element.62), kind=kOutput, calls=%fused_computation.49 | convolution fusion | flops 202014720 | bytes 2034688 | tf_op jit(solution)/shard_map/dot_general | solution.py:46
  24.6 0.4 fusion.60
  25.0 0.7 %fusion.35 = bf16[768,128]{0,1:T(8,128)(2,1)S(1)} fusion(bf16[768,1024]{1,0:T(8,128)(2,1)S(1)} %collective-permute-done, bf16[128,1024]{1,0:T(8,128)(2,1)S(1)} %get-tuple-element.41, s32[768]{0:T(1024)S(1)} %get-tuple-element.64), kind=kOutput, calls=%fused_computation.48 | convolution fusion | flops 202014720 | bytes 2034688 | tf_op jit(solution)/shard_map/dot_general | solution.py:46
  25.7 0.4 fusion.8
  26.1 0.1 pad_maximum_fusion
  26.2 1.0 %convolution_convert_fusion = bf16[768,1024]{1,0:T(8,128)(2,1)S(1)} fusion(bf16[768,512]{0,1:T(8,128)(2,1)S(1)} %pad_maximum_fusion, bf16[512,1024]{1,0:T(8,128)(2,1)S(1)} %constant_dynamic-update-slice_fusion), kind=kOutput, calls=%fused_computation.1 | convolution fusion | flops 806092800 | bytes 3407872 | tf_op jit(solution)/shard_map/dot_general | solution.py:126
  27.2 1.2 %collective-permute-start.10 = (bf16[768,1024]{1,0:T(8,128)(2,1)S(1)}, bf16[768,1024]{1,0:T(8,128)(2,1)S(1)}, u32[]{:S(2)}, u32[]{:S(2)}) collective-permute-start(bf16[768,1024]{1,0:T(8,128)(2,1)S(1)} %convolution_convert_fusion), channel_id=1, source_target_pairs={{0,4},{4,8},{8,12},{12,0},{1,5},{5,9},{9,13},{13,1},{2,6},{6,10},{... | collective-permute-start | bytes 4718600 | tf_op jit(solution)/shard_map/ppermute | solution.py:37
  28.4 1.6 %collective-permute-start.8 = (bf16[64,1024]{1,0:T(8,128)(2,1)S(1)}, bf16[64,1024]{1,0:T(8,128)(2,1)S(1)}, u32[]{:S(2)}, u32[]{:S(2)}) collective-permute-start(bf16[64,1024]{1,0:T(8,128)(2,1)S(1)} %slice.73), channel_id=1, source_target_pairs={{0,1},{1,0},{2,3},{3,2},{4,5},{5,4},{6,7},{7,6},{8,9},{9,8},{10,11... | collective-permute-start | bytes 393224 | tf_op jit(solution)/shard_map/ppermute | solution.py:31
  30.1 0.4 collective-permute-start.7
  30.5 0.4 fusion.61
  30.9 0.4 fusion.7
  31.3 1.6 %collective-permute-start.9 = (bf16[128,1024]{1,0:T(8,128)(2,1)S(1)}, bf16[128,1024]{1,0:T(8,128)(2,1)S(1)}, u32[]{:S(2)}, u32[]{:S(2)}) collective-permute-start(bf16[128,1024]{1,0:T(8,128)(2,1)S(1)} %fusion.7), channel_id=1, source_target_pairs={{0,1},{1,0},{2,3},{3,2},{4,5},{5,4},{6,7},{7,6},{8,9},{9,8},{10,11... | collective-permute-start | bytes 786440 | tf_op jit(solution)/shard_map/ppermute | solution.py:31
  33.0 0.7 %fusion.34 = bf16[768,128]{0,1:T(8,128)(2,1)S(1)} fusion(bf16[128,1024]{1,0:T(8,128)(2,1)S(1)} %get-tuple-element.46, bf16[768,1024]{1,0:T(8,128)(2,1)S(1)} %copy-done, s32[768]{0:T(1024)S(1)} %get-tuple-element.61), kind=kOutput, calls=%fused_computation.47 | convolution fusion | flops 202014720 | bytes 2034688 | tf_op jit(solution)/shard_map/dot_general | solution.py:46
  33.7 0.4 fusion.62
  34.0 0.4 fusion.6
  34.4 0.4 collective-permute-done.8
  34.9 2.7 %collective-permute-start.11 = (bf16[64,1024]{1,0:T(8,128)(2,1)S(1)}, bf16[64,1024]{1,0:T(8,128)(2,1)S(1)}, u32[]{:S(2)}, u32[]{:S(2)}) collective-permute-start(bf16[64,1024]{1,0:T(8,128)(2,1)S(1)} %fusion.39), channel_id=1, source_target_pairs={{0,2},{1,3},{2,0},{3,1},{4,6},{5,7},{6,4},{7,5},{8,10},{9,11},{10,... | collective-permute-start | bytes 393224 | tf_op jit(solution)/shard_map/ppermute | solution.py:31
  37.5 0.1 collective-permute-done.7
  37.7 3.2 %collective-permute-start.12 = (bf16[64,1024]{1,0:T(8,128)(2,1)S(1)}, bf16[64,1024]{1,0:T(8,128)(2,1)S(1)}, u32[]{:S(2)}, u32[]{:S(2)}) collective-permute-start(bf16[64,1024]{1,0:T(8,128)(2,1)S(1)} %fusion.40), channel_id=1, source_target_pairs={{0,2},{1,3},{2,0},{3,1},{4,6},{5,7},{6,4},{7,5},{8,10},{9,11},{10,... | collective-permute-start | bytes 393224 | tf_op jit(solution)/shard_map/ppermute | solution.py:31
  40.9 0.7 %fusion.33 = bf16[768,128]{0,1:T(8,128)(2,1)S(1)} fusion(bf16[128,1024]{1,0:T(8,128)(2,1)S(1)} %get-tuple-element.52, bf16[768,1024]{1,0:T(8,128)(2,1)S(1)} %copy-done, s32[768]{0:T(1024)S(1)} %get-tuple-element.60), kind=kOutput, calls=%fused_computation.46 | convolution fusion | flops 202014720 | bytes 2034688 | tf_op jit(solution)/shard_map/dot_general | solution.py:46
  41.6 0.1 pad_maximum_fusion.1
  41.6 0.4 fusion.63
  42.0 1.0 %fusion.64 = f32[768,1024]{1,0:T(8,128)S(1)} fusion(bf16[768,512]{0,1:T(8,128)(2,1)S(1)} %pad_maximum_fusion.1, bf16[512,1024]{1,0:T(8,128)(2,1)S(1)} %constant_dynamic-update-slice_fusion), kind=kOutput, calls=%fused_computation.106 | convolution fusion | flops 805306368 | bytes 4980736 | tf_op jit(solution)/shard_map/dot_general | solution.py:152
  43.1 0.4 fusion.5
  43.4 1.8 %collective-permute-done.11 = bf16[64,1024]{1,0:T(8,128)(2,1)S(1)} collective-permute-done((bf16[64,1024]{1,0:T(8,128)(2,1)S(1)}, bf16[64,1024]{1,0:T(8,128)(2,1)S(1)}, u32[]{:S(2)}, u32[]{:S(2)}) %collective-permute-start.11) | collective-permute-done | bytes 131104 | tf_op jit(solution)/shard_map/ppermute | solution.py:31
  45.2 2.4 %collective-permute-done.10 = bf16[768,1024]{1,0:T(8,128)(2,1)S(1)} collective-permute-done((bf16[768,1024]{1,0:T(8,128)(2,1)S(1)}, bf16[768,1024]{1,0:T(8,128)(2,1)S(1)}, u32[]{:S(2)}, u32[]{:S(2)}) %collective-permute-start.10) | collective-permute-done | bytes 1572896 | tf_op jit(solution)/shard_map/ppermute | solution.py:37
  47.6 1.8 %add_convert_fusion = bf16[768,1024]{1,0:T(8,128)(2,1)} fusion(f32[768,1024]{1,0:T(8,128)S(1)} %fusion.64, bf16[768,1024]{1,0:T(8,128)(2,1)S(1)} %collective-permute-done.10), kind=kLoop, calls=%fused_computation | loop fusion | flops 2359296 | bytes 6291456 | tf_op jit(solution)/shard_map/convert_element_type | solution.py:163
  49.3 0.0 collective-permute-done.12
  49.3 0.0 collective-permute-done.9
  49.3 0.8 %add_convert_fusion.1 = bf16[128,1024]{1,0:T(8,128)(2,1)} fusion(f32[128,1024]{1,0:T(8,128)S(1)} %fusion.5, bf16[128,1024]{1,0:T(8,128)(2,1)S(1)} %collective-permute-done.9, bf16[64,1024]{1,0:T(8,128)(2,1)S(1)} %collective-permute-done.12, bf16[64,1024]{1,0:T(8,128)(2,1)S(1)} %collective-permute-done.11), kind=kLoop, calls=%fused_computation.54 | loop fusion | flops 1048576 | bytes 1310720 | tf_op jit(solution)/shard_map/convert_element_type | solution.py:170
  (13 shorter events, 0.3 us)
Async XLA Ops:
  0.6 20.8 %collective-permute-start = (bf16[768,1024]{1,0:T(8,128)(2,1)}, bf16[768,1024]{1,0:T(8,128)(2,1)S(1)}, u32[]{:S(2)}, u32[]{:S(2)}) collective-permute-start(bf16[768,1024]{1,0:T(8,128)(2,1)} %param.4), channel_id=1, source_target_pairs={{0,12},{4,0},{8,4},{12,8},{1,13},{5,1},{9,5},{13,9},{2,14},{6,2},{... | collective-permute-start | bytes 4718600 | tf_op jit(solution)/shard_map/ppermute | solution.py:37
  4.0 8.8 %collective-permute-start.3 = (bf16[64,1024]{1,0:T(8,128)(2,1)S(1)}, bf16[64,1024]{1,0:T(8,128)(2,1)S(1)}, u32[]{:S(2)}, u32[]{:S(2)}) collective-permute-start(bf16[64,1024]{1,0:T(8,128)(2,1)S(1)} %constant_dynamic-slice_fusion.8), channel_id=1, source_target_pairs={{0,2},{1,3},{2,0},{3,1},{4,6},{5,7},{6,4},{7,5},{8,10},{9,11},{10,... | collective-permute-start | bytes 393224 | tf_op jit(solution)/shard_map/ppermute | solution.py:31
  6.6 14.8 %collective-permute-start.2 = (bf16[128,1024]{1,0:T(8,128)(2,1)}, bf16[128,1024]{1,0:T(8,128)(2,1)S(1)}, u32[]{:S(2)}, u32[]{:S(2)}) collective-permute-start(bf16[128,1024]{1,0:T(8,128)(2,1)} %param.5), channel_id=1, source_target_pairs={{0,1},{1,0},{2,3},{3,2},{4,5},{5,4},{6,7},{7,6},{8,9},{9,8},{10,11... | collective-permute-start | bytes 786440 | tf_op jit(solution)/shard_map/ppermute | solution.py:31
  12.8 6.0 %collective-permute-start.5 = (bf16[64,1024]{1,0:T(8,128)(2,1)S(1)}, bf16[64,1024]{1,0:T(8,128)(2,1)S(1)}, u32[]{:S(2)}, u32[]{:S(2)}) collective-permute-start(bf16[64,1024]{1,0:T(8,128)(2,1)S(1)} %collective-permute-done.3), channel_id=1, source_target_pairs={{0,1},{1,0},{2,3},{3,2},{4,5},{5,4},{6,7},{7,6},{8,9},{9,8},{10,11... | collective-permute-start | bytes 393224 | tf_op jit(solution)/shard_map/ppermute | solution.py:31
  13.4 8.0 %collective-permute-start.4 = (bf16[64,1024]{1,0:T(8,128)(2,1)S(1)}, bf16[64,1024]{1,0:T(8,128)(2,1)S(1)}, u32[]{:S(2)}, u32[]{:S(2)}) collective-permute-start(bf16[64,1024]{1,0:T(8,128)(2,1)S(1)} %collective-permute-done.3), channel_id=1, source_target_pairs={{0,16},{16,0},{1,17},{17,1},{2,18},{18,2},{3,19},{19,3},{4,20},{20... | collective-permute-start | bytes 393224 | tf_op jit(solution)/shard_map/ppermute | solution.py:34
  15.7 5.8 %collective-permute-start.1 = (s32[768,8]{0,1:T(8,128)S(1)}, s32[768,8]{0,1:T(8,128)S(1)}, u32[]{:S(2)}, u32[]{:S(2)}) collective-permute-start(s32[768,8]{0,1:T(8,128)S(1)} %fusion.41), channel_id=1, source_target_pairs={{0,12},{4,0},{8,4},{12,8},{1,13},{5,1},{9,5},{13,9},{2,14},{6,2},{... | collective-permute-start | bytes 73736 | tf_op jit(solution)/shard_map/ppermute | solution.py:37
  18.8 5.0 %collective-permute-start.6 = (bf16[64,1024]{1,0:T(8,128)(2,1)S(1)}, bf16[64,1024]{1,0:T(8,128)(2,1)S(1)}, u32[]{:S(2)}, u32[]{:S(2)}) collective-permute-start(bf16[64,1024]{1,0:T(8,128)(2,1)S(1)} %collective-permute-done.5), channel_id=1, source_target_pairs={{0,16},{16,0},{1,17},{17,1},{2,18},{18,2},{3,19},{19,3},{4,20},{20... | collective-permute-start | bytes 393224 | tf_op jit(solution)/shard_map/ppermute | solution.py:34
  21.6 1.4 %copy-start = (bf16[768,1024]{1,0:T(8,128)(2,1)S(1)}, bf16[768,1024]{1,0:T(8,128)(2,1)}, u32[]{:S(2)}) copy-start(bf16[768,1024]{1,0:T(8,128)(2,1)} %param.4) | copy-start | bytes 4718596
  27.2 20.4 %collective-permute-start.10 = (bf16[768,1024]{1,0:T(8,128)(2,1)S(1)}, bf16[768,1024]{1,0:T(8,128)(2,1)S(1)}, u32[]{:S(2)}, u32[]{:S(2)}) collective-permute-start(bf16[768,1024]{1,0:T(8,128)(2,1)S(1)} %convolution_convert_fusion), channel_id=1, source_target_pairs={{0,4},{4,8},{8,12},{12,0},{1,5},{5,9},{9,13},{13,1},{2,6},{6,10},{... | collective-permute-start | bytes 4718600 | tf_op jit(solution)/shard_map/ppermute | solution.py:37
  28.4 6.4 %collective-permute-start.8 = (bf16[64,1024]{1,0:T(8,128)(2,1)S(1)}, bf16[64,1024]{1,0:T(8,128)(2,1)S(1)}, u32[]{:S(2)}, u32[]{:S(2)}) collective-permute-start(bf16[64,1024]{1,0:T(8,128)(2,1)S(1)} %slice.73), channel_id=1, source_target_pairs={{0,1},{1,0},{2,3},{3,2},{4,5},{5,4},{6,7},{7,6},{8,9},{9,8},{10,11... | collective-permute-start | bytes 393224 | tf_op jit(solution)/shard_map/ppermute | solution.py:31
  30.1 7.5 %collective-permute-start.7 = (bf16[64,1024]{1,0:T(8,128)(2,1)S(1)}, bf16[64,1024]{1,0:T(8,128)(2,1)S(1)}, u32[]{:S(2)}, u32[]{:S(2)}) collective-permute-start(bf16[64,1024]{1,0:T(8,128)(2,1)S(1)} %slice.74), channel_id=1, source_target_pairs={{0,1},{1,0},{2,3},{3,2},{4,5},{5,4},{6,7},{7,6},{8,9},{9,8},{10,11... | collective-permute-start | bytes 393224 | tf_op jit(solution)/shard_map/ppermute | solution.py:31
  31.3 18.0 %collective-permute-start.9 = (bf16[128,1024]{1,0:T(8,128)(2,1)S(1)}, bf16[128,1024]{1,0:T(8,128)(2,1)S(1)}, u32[]{:S(2)}, u32[]{:S(2)}) collective-permute-start(bf16[128,1024]{1,0:T(8,128)(2,1)S(1)} %fusion.7), channel_id=1, source_target_pairs={{0,1},{1,0},{2,3},{3,2},{4,5},{5,4},{6,7},{7,6},{8,9},{9,8},{10,11... | collective-permute-start | bytes 786440 | tf_op jit(solution)/shard_map/ppermute | solution.py:31
  34.9 10.4 %collective-permute-start.11 = (bf16[64,1024]{1,0:T(8,128)(2,1)S(1)}, bf16[64,1024]{1,0:T(8,128)(2,1)S(1)}, u32[]{:S(2)}, u32[]{:S(2)}) collective-permute-start(bf16[64,1024]{1,0:T(8,128)(2,1)S(1)} %fusion.39), channel_id=1, source_target_pairs={{0,2},{1,3},{2,0},{3,1},{4,6},{5,7},{6,4},{7,5},{8,10},{9,11},{10,... | collective-permute-start | bytes 393224 | tf_op jit(solution)/shard_map/ppermute | solution.py:31
  37.7 11.7 %collective-permute-start.12 = (bf16[64,1024]{1,0:T(8,128)(2,1)S(1)}, bf16[64,1024]{1,0:T(8,128)(2,1)S(1)}, u32[]{:S(2)}, u32[]{:S(2)}) collective-permute-start(bf16[64,1024]{1,0:T(8,128)(2,1)S(1)} %fusion.40), channel_id=1, source_target_pairs={{0,2},{1,3},{2,0},{3,1},{4,6},{5,7},{6,4},{7,5},{8,10},{9,11},{10,... | collective-permute-start | bytes 393224 | tf_op jit(solution)/shard_map/ppermute | solution.py:31

commit v23 on v22

--- a/solution.py
+++ b/solution.py
@@ -153,14 +153,14 @@
         in_turn(jnp.concatenate([d_own[k] for k in range(n_dp)], axis=1)),
         joined,
         preferred_element_type=jnp.float32,
-    )
+    ).astype(jnp.bfloat16)
     last[0] = grad_x
     add_next(0)
     for k in range(2, n_dp):
         if (k, 0) in moved:
             moved[k, 0] = in_turn(moved[k, 0])
             last[0] = moved[k, 0]
-    grad_x = (grad_x + in_turn(back).astype(jnp.float32)).astype(jnp.bfloat16)
+    grad_x = (grad_x.astype(jnp.float32) + in_turn(back).astype(jnp.float32)).astype(jnp.bfloat16)
     last[0] = grad_x
     grad_w = g_w[0] + in_turn(moved[1]).astype(jnp.float32)
     for k in range(2, n_dp):

time: 50.4 us -> 50.5 us (level)
  no operation moved by 1% of the time
where the time goes in v23:
time: 50.5 us; the launch traced here: 50.2 us
  starting transfers between devices  21.8 us (43%)
  waiting for transfers between devices  11.7 us (23%)
  matrix products  9.7 us (19%)
  other arithmetic  3.67 us (7%)
  local copies, waits for them, and re-layouts  2.49 us (5%)
  between operations  0.91 us (2%)
    ppermute x8, starting transfers between devices, to_dp(): return lax.ppermute(x, 'dp', [(i, i ^ k) for i in range(n_dp)])  14.5 us
    ppermute x8, waiting for transfers between devices, to_dp(): return lax.ppermute(x, 'dp', [(i, i ^ k) for i in range(n_dp)])  8.17 us
    dot_general x6, matrix products, delta_of(): lax.dot_general(rows, piece, (((1,), (1,)), ((), ())), preferred_element_...  4.62 us
    ppermute x3, starting transfers between devices, to_label(): lax.ppermute(x, 'label', [(i, (i + by) % n_label) for i in range(n_label)])  4.23 us
    ppermute x3, waiting for transfers between devices, to_label(): lax.ppermute(x, 'label', [(i, (i + by) % n_label) for i in range(n_label)])  3.47 us
    ppermute x2, starting transfers between devices, to_group(): return lax.ppermute(x, 'groups', [(i, i ^ 1) for i in range(n_groups)])  3.09 us
    dot_general x8, matrix products, grad_w_of(): lax.dot_general(delta, rows, (((0,), (0,)), ((), ())), preferred_element_...  3.05 us
    convert_element_type x1, other arithmetic, local(): (grad_x.astype(jnp.float32) + in_turn(back).astype(jnp.float32)).astype(j...  1.84 us
  transfers between devices with their start and end apart: 13, of which 7 were waited for; matrix products, arithmetic and copies ran while one was open for 23% of the time, Pallas kernels for 0%

profile of v23, /device:TPU:0, one launch (start us, length us, event | category | flops | bytes accessed | tf_op | source)
XLA Modules:
  0.0 50.2 jit_solution(12914856268741875636)
XLA Ops:
  0.6 2.4 %collective-permute-start = (bf16[768,1024]{1,0:T(8,128)(2,1)}, bf16[768,1024]{1,0:T(8,128)(2,1)S(1)}, u32[]{:S(2)}, u32[]{:S(2)}) collective-permute-start(bf16[768,1024]{1,0:T(8,128)(2,1)} %param.4), channel_id=1, source_target_pairs={{0,12},{4,0},{8,4},{12,8},{1,13},{5,1},{9,5},{13,9},{2,14},{6,2},{... | collective-permute-start | bytes 4718600 | tf_op jit(solution)/shard_map/ppermute | solution.py:37
  3.1 0.9 %constant_dynamic-slice_fusion.8 = bf16[64,1024]{1,0:T(8,128)(2,1)S(1)} fusion(bf16[128,1024]{1,0:T(8,128)(2,1)} %param.5, s32[]{:T(128)S(6)} %select_n.62), kind=kLoop, calls=%fused_computation.82 | loop fusion | bytes 262148 | tf_op jit(solution)/shard_map/dynamic_slice | solution.py:59
  4.0 2.7 %collective-permute-start.3 = (bf16[64,1024]{1,0:T(8,128)(2,1)S(1)}, bf16[64,1024]{1,0:T(8,128)(2,1)S(1)}, u32[]{:S(2)}, u32[]{:S(2)}) collective-permute-start(bf16[64,1024]{1,0:T(8,128)(2,1)S(1)} %constant_dynamic-slice_fusion.8), channel_id=1, source_target_pairs={{0,2},{1,3},{2,0},{3,1},{4,6},{5,7},{6,4},{7,5},{8,10},{9,11},{10,... | collective-permute-start | bytes 393224 | tf_op jit(solution)/shard_map/ppermute | solution.py:31
  6.6 1.6 %collective-permute-start.2 = (bf16[128,1024]{1,0:T(8,128)(2,1)}, bf16[128,1024]{1,0:T(8,128)(2,1)S(1)}, u32[]{:S(2)}, u32[]{:S(2)}) collective-permute-start(bf16[128,1024]{1,0:T(8,128)(2,1)} %param.5), channel_id=1, source_target_pairs={{0,1},{1,0},{2,3},{3,2},{4,5},{5,4},{6,7},{7,6},{8,9},{9,8},{10,11... | collective-permute-start | bytes 786440 | tf_op jit(solution)/shard_map/ppermute | solution.py:31
  8.2 4.6 %collective-permute-done.3 = bf16[64,1024]{1,0:T(8,128)(2,1)S(1)} collective-permute-done((bf16[64,1024]{1,0:T(8,128)(2,1)S(1)}, bf16[64,1024]{1,0:T(8,128)(2,1)S(1)}, u32[]{:S(2)}, u32[]{:S(2)}) %collective-permute-start.3) | collective-permute-done | bytes 131104 | tf_op jit(solution)/shard_map/ppermute | solution.py:31
  12.8 0.7 %collective-permute-start.5 = (bf16[64,1024]{1,0:T(8,128)(2,1)S(1)}, bf16[64,1024]{1,0:T(8,128)(2,1)S(1)}, u32[]{:S(2)}, u32[]{:S(2)}) collective-permute-start(bf16[64,1024]{1,0:T(8,128)(2,1)S(1)} %collective-permute-done.3), channel_id=1, source_target_pairs={{0,1},{1,0},{2,3},{3,2},{4,5},{5,4},{6,7},{7,6},{8,9},{9,8},{10,11... | collective-permute-start | bytes 393224 | tf_op jit(solution)/shard_map/ppermute | solution.py:31
  13.4 1.5 %collective-permute-start.4 = (bf16[64,1024]{1,0:T(8,128)(2,1)S(1)}, bf16[64,1024]{1,0:T(8,128)(2,1)S(1)}, u32[]{:S(2)}, u32[]{:S(2)}) collective-permute-start(bf16[64,1024]{1,0:T(8,128)(2,1)S(1)} %collective-permute-done.3), channel_id=1, source_target_pairs={{0,16},{16,0},{1,17},{17,1},{2,18},{18,2},{3,19},{19,3},{4,20},{20... | collective-permute-start | bytes 393224 | tf_op jit(solution)/shard_map/ppermute | solution.py:34
  15.0 0.7 %fusion.41 = s32[768,8]{0,1:T(8,128)S(1)} fusion(s32[768,8]{0,1:T(8,128)} %param.6, s32[768]{0:T(1024)} %param.7), kind=kLoop, calls=%fused_computation.68 | loop fusion | flops 12288 | bytes 52224 | tf_op jit(solution)/shard_map/jit(_where)/select_n | solution.py:23
  15.7 0.6 %collective-permute-start.1 = (s32[768,8]{0,1:T(8,128)S(1)}, s32[768,8]{0,1:T(8,128)S(1)}, u32[]{:S(2)}, u32[]{:S(2)}) collective-permute-start(s32[768,8]{0,1:T(8,128)S(1)} %fusion.41), channel_id=1, source_target_pairs={{0,12},{4,0},{8,4},{12,8},{1,13},{5,1},{9,5},{13,9},{2,14},{6,2},{... | collective-permute-start | bytes 73736 | tf_op jit(solution)/shard_map/ppermute | solution.py:37
  16.3 1.1 %dynamic_update_slice.18 = bf16[512,1024]{1,0:T(8,128)(2,1)S(1)} pad(bf16[128,1024]{1,0:T(8,128)(2,1)} %param.5, bf16[]{:T(256)} %constant.72.clone.1), padding=0_384x0_0 | pad | bytes 1310722 | tf_op jit(solution)/shard_map/dynamic_update_slice | solution.py:71
  17.5 1.3 %collective-permute-done.5 = bf16[64,1024]{1,0:T(8,128)(2,1)S(1)} collective-permute-done((bf16[64,1024]{1,0:T(8,128)(2,1)S(1)}, bf16[64,1024]{1,0:T(8,128)(2,1)S(1)}, u32[]{:S(2)}, u32[]{:S(2)}) %collective-permute-start.5) | collective-permute-done | bytes 131104 | tf_op jit(solution)/shard_map/ppermute | solution.py:31
  18.8 1.6 %collective-permute-start.6 = (bf16[64,1024]{1,0:T(8,128)(2,1)S(1)}, bf16[64,1024]{1,0:T(8,128)(2,1)S(1)}, u32[]{:S(2)}, u32[]{:S(2)}) collective-permute-start(bf16[64,1024]{1,0:T(8,128)(2,1)S(1)} %collective-permute-done.5), channel_id=1, source_target_pairs={{0,16},{16,0},{1,17},{17,1},{2,18},{18,2},{3,19},{19,3},{4,20},{20... | collective-permute-start | bytes 393224 | tf_op jit(solution)/shard_map/ppermute | solution.py:34
  20.4 1.1 %collective-permute-done.1 = s32[768,8]{0,1:T(8,128)S(1)} collective-permute-done((s32[768,8]{0,1:T(8,128)S(1)}, s32[768,8]{0,1:T(8,128)S(1)}, u32[]{:S(2)}, u32[]{:S(2)}) %collective-permute-start.1) | collective-permute-done | bytes 24608 | tf_op jit(solution)/shard_map/ppermute | solution.py:37
  21.5 0.0 collective-permute-done.4
  21.5 0.0 collective-permute-done.2
  21.5 0.0 collective-permute-done
  21.6 0.1 fusion.53
  21.6 0.0 copy-start
  21.7 1.1 %fusion.4 = bf16[768,384]{0,1:T(8,128)(2,1)S(1)} fusion(bf16[768,1024]{1,0:T(8,128)(2,1)S(1)} %collective-permute-done, bf16[512,1024]{1,0:T(8,128)(2,1)S(1)} %constant_dynamic-update-slice_fusion.2, s32[768]{0:T(1024)S(1)} %get-tuple-element.65, s32[768]{0:T(1024)S(1)} %get-tuple-element.66, s32[768]{0:T(1024)S(1)} %get-tuple-element.67, ...), kind=kOutput, calls=%fused_computation.8 | convolution fusion | flops 606633984 | bytes 2962432 | tf_op jit(solution)/shard_map/dot_general | solution.py:46
  22.8 0.3 copy-done
  23.1 0.7 %fusion.37 = bf16[768,128]{0,1:T(8,128)(2,1)S(1)} fusion(bf16[128,1024]{1,0:T(8,128)(2,1)S(1)} %slice.51, bf16[768,1024]{1,0:T(8,128)(2,1)S(1)} %copy-done, s32[768]{0:T(1024)S(1)} %get-tuple-element.63), kind=kOutput, calls=%fused_computation.51 | convolution fusion | flops 202014720 | bytes 2034688 | tf_op jit(solution)/shard_map/dot_general | solution.py:46
  23.8 0.0 collective-permute-done.6
  23.9 0.1 fusion.58
  23.9 0.7 %fusion.36 = bf16[768,128]{0,1:T(8,128)(2,1)S(1)} fusion(bf16[128,1024]{1,0:T(8,128)(2,1)S(1)} %get-tuple-element.41, bf16[768,1024]{1,0:T(8,128)(2,1)S(1)} %copy-done, s32[768]{0:T(1024)S(1)} %get-tuple-element.62), kind=kOutput, calls=%fused_computation.50 | convolution fusion | flops 202014720 | bytes 2034688 | tf_op jit(solution)/shard_map/dot_general | solution.py:46
  24.6 0.4 fusion.60
  25.0 0.7 %fusion.35 = bf16[768,128]{0,1:T(8,128)(2,1)S(1)} fusion(bf16[768,1024]{1,0:T(8,128)(2,1)S(1)} %collective-permute-done, bf16[128,1024]{1,0:T(8,128)(2,1)S(1)} %get-tuple-element.41, s32[768]{0:T(1024)S(1)} %get-tuple-element.64), kind=kOutput, calls=%fused_computation.49 | convolution fusion | flops 202014720 | bytes 2034688 | tf_op jit(solution)/shard_map/dot_general | solution.py:46
  25.7 0.4 fusion.8
  26.1 0.1 pad_maximum_fusion
  26.2 1.0 %convolution_convert_fusion.1 = bf16[768,1024]{1,0:T(8,128)(2,1)S(1)} fusion(bf16[768,512]{0,1:T(8,128)(2,1)S(1)} %pad_maximum_fusion, bf16[512,1024]{1,0:T(8,128)(2,1)S(1)} %constant_dynamic-update-slice_fusion), kind=kOutput, calls=%fused_computation.2 | convolution fusion | flops 806092800 | bytes 3407872 | tf_op jit(solution)/shard_map/dot_general | solution.py:126
  27.2 1.2 %collective-permute-start.10 = (bf16[768,1024]{1,0:T(8,128)(2,1)S(1)}, bf16[768,1024]{1,0:T(8,128)(2,1)S(1)}, u32[]{:S(2)}, u32[]{:S(2)}) collective-permute-start(bf16[768,1024]{1,0:T(8,128)(2,1)S(1)} %convolution_convert_fusion.1), channel_id=1, source_target_pairs={{0,4},{4,8},{8,12},{12,0},{1,5},{5,9},{9,13},{13,1},{2,6},{6,10},{... | collective-permute-start | bytes 4718600 | tf_op jit(solution)/shard_map/ppermute | solution.py:37
  28.4 1.6 %collective-permute-start.8 = (bf16[64,1024]{1,0:T(8,128)(2,1)S(1)}, bf16[64,1024]{1,0:T(8,128)(2,1)S(1)}, u32[]{:S(2)}, u32[]{:S(2)}) collective-permute-start(bf16[64,1024]{1,0:T(8,128)(2,1)S(1)} %slice.73), channel_id=1, source_target_pairs={{0,1},{1,0},{2,3},{3,2},{4,5},{5,4},{6,7},{7,6},{8,9},{9,8},{10,11... | collective-permute-start | bytes 393224 | tf_op jit(solution)/shard_map/ppermute | solution.py:31
  30.1 0.4 collective-permute-start.7
  30.5 0.4 fusion.61
  30.9 0.4 fusion.7
  31.3 1.6 %collective-permute-start.9 = (bf16[128,1024]{1,0:T(8,128)(2,1)S(1)}, bf16[128,1024]{1,0:T(8,128)(2,1)S(1)}, u32[]{:S(2)}, u32[]{:S(2)}) collective-permute-start(bf16[128,1024]{1,0:T(8,128)(2,1)S(1)} %fusion.7), channel_id=1, source_target_pairs={{0,1},{1,0},{2,3},{3,2},{4,5},{5,4},{6,7},{7,6},{8,9},{9,8},{10,11... | collective-permute-start | bytes 786440 | tf_op jit(solution)/shard_map/ppermute | solution.py:31
  33.0 0.7 %fusion.34 = bf16[768,128]{0,1:T(8,128)(2,1)S(1)} fusion(bf16[128,1024]{1,0:T(8,128)(2,1)S(1)} %get-tuple-element.46, bf16[768,1024]{1,0:T(8,128)(2,1)S(1)} %copy-done, s32[768]{0:T(1024)S(1)} %get-tuple-element.61), kind=kOutput, calls=%fused_computation.48 | convolution fusion | flops 202014720 | bytes 2034688 | tf_op jit(solution)/shard_map/dot_general | solution.py:46
  33.7 0.4 fusion.62
  34.0 0.4 fusion.6
  34.4 0.4 collective-permute-done.8
  34.8 2.7 %collective-permute-start.11 = (bf16[64,1024]{1,0:T(8,128)(2,1)S(1)}, bf16[64,1024]{1,0:T(8,128)(2,1)S(1)}, u32[]{:S(2)}, u32[]{:S(2)}) collective-permute-start(bf16[64,1024]{1,0:T(8,128)(2,1)S(1)} %fusion.39), channel_id=1, source_target_pairs={{0,2},{1,3},{2,0},{3,1},{4,6},{5,7},{6,4},{7,5},{8,10},{9,11},{10,... | collective-permute-start | bytes 393224 | tf_op jit(solution)/shard_map/ppermute | solution.py:31
  37.5 0.1 collective-permute-done.7
  37.7 3.2 %collective-permute-start.12 = (bf16[64,1024]{1,0:T(8,128)(2,1)S(1)}, bf16[64,1024]{1,0:T(8,128)(2,1)S(1)}, u32[]{:S(2)}, u32[]{:S(2)}) collective-permute-start(bf16[64,1024]{1,0:T(8,128)(2,1)S(1)} %fusion.40), channel_id=1, source_target_pairs={{0,2},{1,3},{2,0},{3,1},{4,6},{5,7},{6,4},{7,5},{8,10},{9,11},{10,... | collective-permute-start | bytes 393224 | tf_op jit(solution)/shard_map/ppermute | solution.py:31
  40.9 0.7 %fusion.33 = bf16[768,128]{0,1:T(8,128)(2,1)S(1)} fusion(bf16[128,1024]{1,0:T(8,128)(2,1)S(1)} %get-tuple-element.52, bf16[768,1024]{1,0:T(8,128)(2,1)S(1)} %copy-done, s32[768]{0:T(1024)S(1)} %get-tuple-element.60), kind=kOutput, calls=%fused_computation.47 | convolution fusion | flops 202014720 | bytes 2034688 | tf_op jit(solution)/shard_map/dot_general | solution.py:46
  41.6 0.1 pad_maximum_fusion.1
  41.6 0.4 fusion.63
  42.0 1.0 %convolution_convert_fusion = bf16[768,1024]{1,0:T(8,128)(2,1)S(1)} fusion(bf16[768,512]{0,1:T(8,128)(2,1)S(1)} %pad_maximum_fusion.1, bf16[512,1024]{1,0:T(8,128)(2,1)S(1)} %constant_dynamic-update-slice_fusion), kind=kOutput, calls=%fused_computation.1 | convolution fusion | flops 806092800 | bytes 3407872 | tf_op jit(solution)/shard_map/dot_general | solution.py:152
  43.1 0.4 fusion.5
  43.4 1.8 %collective-permute-done.11 = bf16[64,1024]{1,0:T(8,128)(2,1)S(1)} collective-permute-done((bf16[64,1024]{1,0:T(8,128)(2,1)S(1)}, bf16[64,1024]{1,0:T(8,128)(2,1)S(1)}, u32[]{:S(2)}, u32[]{:S(2)}) %collective-permute-start.11) | collective-permute-done | bytes 131104 | tf_op jit(solution)/shard_map/ppermute | solution.py:31
  45.2 2.4 %collective-permute-done.10 = bf16[768,1024]{1,0:T(8,128)(2,1)S(1)} collective-permute-done((bf16[768,1024]{1,0:T(8,128)(2,1)S(1)}, bf16[768,1024]{1,0:T(8,128)(2,1)S(1)}, u32[]{:S(2)}, u32[]{:S(2)}) %collective-permute-start.10) | collective-permute-done | bytes 1572896 | tf_op jit(solution)/shard_map/ppermute | solution.py:37
  47.6 1.8 %add_convert_fusion = bf16[768,1024]{1,0:T(8,128)(2,1)} fusion(bf16[768,1024]{1,0:T(8,128)(2,1)S(1)} %collective-permute-done.10, bf16[768,1024]{1,0:T(8,128)(2,1)S(1)} %convolution_convert_fusion), kind=kLoop, calls=%fused_computation | loop fusion | flops 3145728 | bytes 4718592 | tf_op jit(solution)/shard_map/convert_element_type | solution.py:163
  49.4 0.0 collective-permute-done.12
  49.4 0.0 collective-permute-done.9
  49.4 0.8 %add_convert_fusion.1 = bf16[128,1024]{1,0:T(8,128)(2,1)} fusion(f32[128,1024]{1,0:T(8,128)S(1)} %fusion.5, bf16[128,1024]{1,0:T(8,128)(2,1)S(1)} %collective-permute-done.9, bf16[64,1024]{1,0:T(8,128)(2,1)S(1)} %collective-permute-done.12, bf16[64,1024]{1,0:T(8,128)(2,1)S(1)} %collective-permute-done.11), kind=kLoop, calls=%fused_computation.55 | loop fusion | flops 1048576 | bytes 1310720 | tf_op jit(solution)/shard_map/convert_element_type | solution.py:170
  (13 shorter events, 0.3 us)
Async XLA Ops:
  0.6 20.8 %collective-permute-start = (bf16[768,1024]{1,0:T(8,128)(2,1)}, bf16[768,1024]{1,0:T(8,128)(2,1)S(1)}, u32[]{:S(2)}, u32[]{:S(2)}) collective-permute-start(bf16[768,1024]{1,0:T(8,128)(2,1)} %param.4), channel_id=1, source_target_pairs={{0,12},{4,0},{8,4},{12,8},{1,13},{5,1},{9,5},{13,9},{2,14},{6,2},{... | collective-permute-start | bytes 4718600 | tf_op jit(solution)/shard_map/ppermute | solution.py:37
  4.0 8.8 %collective-permute-start.3 = (bf16[64,1024]{1,0:T(8,128)(2,1)S(1)}, bf16[64,1024]{1,0:T(8,128)(2,1)S(1)}, u32[]{:S(2)}, u32[]{:S(2)}) collective-permute-start(bf16[64,1024]{1,0:T(8,128)(2,1)S(1)} %constant_dynamic-slice_fusion.8), channel_id=1, source_target_pairs={{0,2},{1,3},{2,0},{3,1},{4,6},{5,7},{6,4},{7,5},{8,10},{9,11},{10,... | collective-permute-start | bytes 393224 | tf_op jit(solution)/shard_map/ppermute | solution.py:31
  6.6 14.8 %collective-permute-start.2 = (bf16[128,1024]{1,0:T(8,128)(2,1)}, bf16[128,1024]{1,0:T(8,128)(2,1)S(1)}, u32[]{:S(2)}, u32[]{:S(2)}) collective-permute-start(bf16[128,1024]{1,0:T(8,128)(2,1)} %param.5), channel_id=1, source_target_pairs={{0,1},{1,0},{2,3},{3,2},{4,5},{5,4},{6,7},{7,6},{8,9},{9,8},{10,11... | collective-permute-start | bytes 786440 | tf_op jit(solution)/shard_map/ppermute | solution.py:31
  12.8 6.0 %collective-permute-start.5 = (bf16[64,1024]{1,0:T(8,128)(2,1)S(1)}, bf16[64,1024]{1,0:T(8,128)(2,1)S(1)}, u32[]{:S(2)}, u32[]{:S(2)}) collective-permute-start(bf16[64,1024]{1,0:T(8,128)(2,1)S(1)} %collective-permute-done.3), channel_id=1, source_target_pairs={{0,1},{1,0},{2,3},{3,2},{4,5},{5,4},{6,7},{7,6},{8,9},{9,8},{10,11... | collective-permute-start | bytes 393224 | tf_op jit(solution)/shard_map/ppermute | solution.py:31
  13.4 8.0 %collective-permute-start.4 = (bf16[64,1024]{1,0:T(8,128)(2,1)S(1)}, bf16[64,1024]{1,0:T(8,128)(2,1)S(1)}, u32[]{:S(2)}, u32[]{:S(2)}) collective-permute-start(bf16[64,1024]{1,0:T(8,128)(2,1)S(1)} %collective-permute-done.3), channel_id=1, source_target_pairs={{0,16},{16,0},{1,17},{17,1},{2,18},{18,2},{3,19},{19,3},{4,20},{20... | collective-permute-start | bytes 393224 | tf_op jit(solution)/shard_map/ppermute | solution.py:34
  15.7 5.8 %collective-permute-start.1 = (s32[768,8]{0,1:T(8,128)S(1)}, s32[768,8]{0,1:T(8,128)S(1)}, u32[]{:S(2)}, u32[]{:S(2)}) collective-permute-start(s32[768,8]{0,1:T(8,128)S(1)} %fusion.41), channel_id=1, source_target_pairs={{0,12},{4,0},{8,4},{12,8},{1,13},{5,1},{9,5},{13,9},{2,14},{6,2},{... | collective-permute-start | bytes 73736 | tf_op jit(solution)/shard_map/ppermute | solution.py:37
  18.8 5.0 %collective-permute-start.6 = (bf16[64,1024]{1,0:T(8,128)(2,1)S(1)}, bf16[64,1024]{1,0:T(8,128)(2,1)S(1)}, u32[]{:S(2)}, u32[]{:S(2)}) collective-permute-start(bf16[64,1024]{1,0:T(8,128)(2,1)S(1)} %collective-permute-done.5), channel_id=1, source_target_pairs={{0,16},{16,0},{1,17},{17,1},{2,18},{18,2},{3,19},{19,3},{4,20},{20... | collective-permute-start | bytes 393224 | tf_op jit(solution)/shard_map/ppermute | solution.py:34
  21.6 1.4 %copy-start = (bf16[768,1024]{1,0:T(8,128)(2,1)S(1)}, bf16[768,1024]{1,0:T(8,128)(2,1)}, u32[]{:S(2)}) copy-start(bf16[768,1024]{1,0:T(8,128)(2,1)} %param.4) | copy-start | bytes 4718596
  27.2 20.4 %collective-permute-start.10 = (bf16[768,1024]{1,0:T(8,128)(2,1)S(1)}, bf16[768,1024]{1,0:T(8,128)(2,1)S(1)}, u32[]{:S(2)}, u32[]{:S(2)}) collective-permute-start(bf16[768,1024]{1,0:T(8,128)(2,1)S(1)} %convolution_convert_fusion.1), channel_id=1, source_target_pairs={{0,4},{4,8},{8,12},{12,0},{1,5},{5,9},{9,13},{13,1},{2,6},{6,10},{... | collective-permute-start | bytes 4718600 | tf_op jit(solution)/shard_map/ppermute | solution.py:37
  28.4 6.4 %collective-permute-start.8 = (bf16[64,1024]{1,0:T(8,128)(2,1)S(1)}, bf16[64,1024]{1,0:T(8,128)(2,1)S(1)}, u32[]{:S(2)}, u32[]{:S(2)}) collective-permute-start(bf16[64,1024]{1,0:T(8,128)(2,1)S(1)} %slice.73), channel_id=1, source_target_pairs={{0,1},{1,0},{2,3},{3,2},{4,5},{5,4},{6,7},{7,6},{8,9},{9,8},{10,11... | collective-permute-start | bytes 393224 | tf_op jit(solution)/shard_map/ppermute | solution.py:31
  30.1 7.5 %collective-permute-start.7 = (bf16[64,1024]{1,0:T(8,128)(2,1)S(1)}, bf16[64,1024]{1,0:T(8,128)(2,1)S(1)}, u32[]{:S(2)}, u32[]{:S(2)}) collective-permute-start(bf16[64,1024]{1,0:T(8,128)(2,1)S(1)} %slice.74), channel_id=1, source_target_pairs={{0,1},{1,0},{2,3},{3,2},{4,5},{5,4},{6,7},{7,6},{8,9},{9,8},{10,11... | collective-permute-start | bytes 393224 | tf_op jit(solution)/shard_map/ppermute | solution.py:31
  31.3 18.1 %collective-permute-start.9 = (bf16[128,1024]{1,0:T(8,128)(2,1)S(1)}, bf16[128,1024]{1,0:T(8,128)(2,1)S(1)}, u32[]{:S(2)}, u32[]{:S(2)}) collective-permute-start(bf16[128,1024]{1,0:T(8,128)(2,1)S(1)} %fusion.7), channel_id=1, source_target_pairs={{0,1},{1,0},{2,3},{3,2},{4,5},{5,4},{6,7},{7,6},{8,9},{9,8},{10,11... | collective-permute-start | bytes 786440 | tf_op jit(solution)/shard_map/ppermute | solution.py:31
  34.8 10.4 %collective-permute-start.11 = (bf16[64,1024]{1,0:T(8,128)(2,1)S(1)}, bf16[64,1024]{1,0:T(8,128)(2,1)S(1)}, u32[]{:S(2)}, u32[]{:S(2)}) collective-permute-start(bf16[64,1024]{1,0:T(8,128)(2,1)S(1)} %fusion.39), channel_id=1, source_target_pairs={{0,2},{1,3},{2,0},{3,1},{4,6},{5,7},{6,4},{7,5},{8,10},{9,11},{10,... | collective-permute-start | bytes 393224 | tf_op jit(solution)/shard_map/ppermute | solution.py:31
  37.7 11.8 %collective-permute-start.12 = (bf16[64,1024]{1,0:T(8,128)(2,1)S(1)}, bf16[64,1024]{1,0:T(8,128)(2,1)S(1)}, u32[]{:S(2)}, u32[]{:S(2)}) collective-permute-start(bf16[64,1024]{1,0:T(8,128)(2,1)S(1)} %fusion.40), channel_id=1, source_target_pairs={{0,2},{1,3},{2,0},{3,1},{4,6},{5,7},{6,4},{7,5},{8,10},{9,11},{10,... | collective-permute-start | bytes 393224 | tf_op jit(solution)/shard_map/ppermute | solution.py:31
